TPU v7x, 32 devices: a whole 2x2x4 slice. The times are simulated.
32 devices in a mesh: row: 8 (over z, core), col: 4 (over y, x).
Axes of the slice: x: 2, y: 2, z: 4, core: 2. Of those that a mesh axis runs over, the one named last changes fastest.
Arguments:
- rhs: float32 [8, 1024, 1024], P('row', None, 'col'), may hold values from -6 to 6
- panel: float32 [8, 2, 1024, 1024], P('row', None, 'col'), may hold values from -0.125 to 0.125
- diag_inverse: float32 [2, 1024, 1024], P(None, 'row'), as said below
- flags: int32 [8, 2], P('row'), may hold values 0 or 1
- slot_block: int32 [8], replicated, may hold values from 0 to 7, each once
Outputs:
- result: float32 [8, 1024, 1024], P('row', None, 'col')
Inputs may be any that keep to these rules, and one draw needn't show every extreme that they name: `slot_block`: each block row 0 to 7 is held by exactly one slot. `diag_inverse`: lower triangular with a positive diagonal.
All inputs are finite; a program needn't handle non-finite values. No bound on the sum of `flags` on one device may be relied on, other than what follows from the above.
Results may differ from a plain program's by a relative error of at most 0.000078.
Values sent between devices are 32-bit elements; how exact they have to be, the bound alone decides.
No kernel may reach another device: no remote copies, remote signals or barrier semaphores. Data moves between devices by JAX's collectives and lax.ppermute only.
A program may use at most 64 MiB of HBM per device.

v0:
```python
import jax
import jax.numpy as jnp
from jax import lax
from jax.sharding import PartitionSpec as P


def broadcast(shard, axis, root):
    mine = lax.axis_index(axis) == root
    return lax.psum(jnp.where(mine, shard, jnp.zeros_like(shard)), axis)


def shards(rhs, panel, diag_inverse, flags, slot_block):
    highest = lax.Precision.HIGHEST
    rank = lax.axis_index("row")
    held = slot_block[rank]
    owners = (jnp.argmax(slot_block == 0), jnp.argmax(slot_block == 1))
    weights = flags[0].astype(jnp.float32)
    current = rhs[0]
    solved = []
    for step in range(2):
        pivot = broadcast(current, "row", owners[step])
        share = jnp.dot(diag_inverse[step], pivot, precision=highest)
        block_x = lax.all_gather(share, "row", axis=0, tiled=True)
        product = jnp.dot(
            lax.all_gather(panel[0, step], "col", axis=0, tiled=True), block_x, precision=highest
        )
        current = current - weights[step] * product
        solved.append(block_x)
    result = jnp.where(held == 0, solved[0], jnp.where(held == 1, solved[1], current))
    return result[None]


def solution(mesh):
    in_specs = (
        P("row", None, "col"),
        P("row", None, "col", None),
        P(None, "row", None),
        P("row", None),
        P(),
    )
    out_specs = P("row", None, "col")
    return jax.shard_map(shards, mesh=mesh, in_specs=in_specs, out_specs=out_specs, check_vma=False)
```

profile of v0, /device:TPU:0, one launch (start us, length us, event | category | flops | bytes accessed | tf_op | source)
XLA Modules:
  0.0 313.4 jit_solution(4280684929434325500)
XLA Ops:
  6.5 0.0 copy-start.1
  6.5 0.0 all-reduce.3.cloned.1.call-start
  6.5 1.5 compare_reduce_fusion.1
  8.1 1.6 copy.6
  10.3 1.0 bitcast_select_fusion
  11.4 0.0 copy-start.3
  11.4 0.0 copy-start.2
  11.4 0.0 all-reduce.3.cloned.1.call-update
  11.4 0.0 all-gather.7.cloned.1.call-start
  11.5 61.6 %all-reduce.3.cloned.1.call-done = f32[1024,256]{0,1:T(8,128)} async-done(((f32[1024,256]{0,1:T(8,128)}), f32[1024,256]{0,1:T(8,128)}) %all-reduce.3.cloned.1.call-update) | async-done | bytes 1048592 | tf_op jit(solution)/shard_map/psum | solution.py:9
  73.1 3.0 convolution_bitcast_fusion.1
  76.1 0.0 all-gather.7.cloned.1.call-update
  76.1 0.0 all-gather.11.cloned.1.call-start
  76.1 0.0 copy-done.1
  76.1 1.5 fusion.35
  77.6 0.0 all-gather.11.cloned.1.call-update
  77.7 0.0 all-reduce.5.cloned.1.call-start
  77.7 0.0 copy-done.3
  77.7 0.7 compare_reduce_fusion
  79.0 0.0 copy-done.2
  79.0 0.7 fusion.36
  79.7 19.5 %all-gather.7.cloned.1.call-done = f32[1024,256]{0,1:T(8,128)} async-done(((f32[128,256]{0,1:T(8,128)}), f32[1024,256]{0,1:T(8,128)}) %all-gather.7.cloned.1.call-update) | async-done | bytes 1048592 | tf_op jit(solution)/shard_map/all_gather | solution.py:23
  99.2 53.2 %all-gather.11.cloned.1.call-done = f32[1,1,1024,1024]{3,2,1,0:T(8,128)} async-done(((f32[1,1,256,1024]{3,2,1,0:T(8,128)}), f32[1,1,1024,1024]{3,2,1,0:T(8,128)}) %all-gather.11.cloned.1.call-update) | async-done | bytes 4194320 | tf_op jit(solution)/shard_map/all_gather | solution.py:25
  152.4 0.0 copy-start
  152.4 7.9 %broadcast_select_fusion = (f32[1024,256]{0,1:T(8,128)}, f32[1024,256]{0,1:T(8,128)S(1)}) fusion(pred[]{:T(512)S(6)} %eq.34, f32[1024,256]{0,1:T(8,128)} %all-gather.7.cloned.1.call-done, f32[1,1,1024,1024]{3,2,1,0:T(8,128)} %all-gather.11.cloned.1.call-done, f32[]{:T(128)} %bitcast.5, f32[1,1024,256]{1,2,0:T(8,128)S(1)} %copy.6), kind=kOutput, calls=%fused_computation.20 | convolution fusion | flops 3222011904 | bytes 8388613 | tf_op jit(solution)/shard_map/dot_general | solution.py:24
  160.2 0.0 all-reduce.5.cloned.1.call-update
  160.3 0.0 all-gather.13.cloned.1.call-start
  160.3 0.5 all-gather.13.cloned.1.call-update
  160.8 0.0 all-gather.9.cloned.1.call-start
  160.9 58.2 %all-reduce.5.cloned.1.call-done = f32[1024,256]{0,1:T(8,128)} async-done(((f32[1024,256]{0,1:T(8,128)}), f32[1024,256]{0,1:T(8,128)}) %all-reduce.5.cloned.1.call-update) | async-done | bytes 1048592 | tf_op jit(solution)/shard_map/psum | solution.py:9
  219.1 3.0 convolution_bitcast_fusion
  222.1 0.0 all-gather.9.cloned.1.call-update
  222.2 0.7 dynamic_slice.3
  224.1 48.4 %all-gather.13.cloned.1.call-done = f32[1,1,1024,1024]{3,2,1,0:T(8,128)} async-done(((f32[1,1,256,1024]{3,2,1,0:T(8,128)}), f32[1,1,1024,1024]{3,2,1,0:T(8,128)}) %all-gather.13.cloned.1.call-update) | async-done | bytes 4194320 | tf_op jit(solution)/shard_map/all_gather | solution.py:25
  272.5 25.5 %all-gather.9.cloned.1.call-done = f32[1024,256]{0,1:T(8,128)} async-done(((f32[128,256]{0,1:T(8,128)}), f32[1024,256]{0,1:T(8,128)}) %all-gather.9.cloned.1.call-update) | async-done | bytes 1048592 | tf_op jit(solution)/shard_map/all_gather | solution.py:23
  298.0 0.0 copy-done
  298.0 7.2 %fusion.28 = f32[1,1024,256]{1,2,0:T(8,128)S(1)} fusion(f32[1024,256]{0,1:T(8,128)S(1)} %copy-done, f32[1024,256]{0,1:T(8,128)} %all-gather.9.cloned.1.call-done, f32[1024,256]{0,1:T(8,128)S(1)} %get-tuple-element.14, f32[1,1,1024,1024]{3,2,1,0:T(8,128)} %all-gather.13.cloned.1.call-done, f32[]{:T(128)} %bitcast.10, pred[]{:T(512)} %bitcast.4, pred[]{:T(512)} %bitcast), kind=kOutput, calls=%fused_computation.12 | convolution fusion | flops 3222274048 | bytes 8388614 | tf_op jit(solution)/shard_map/dot_general | solution.py:24
  305.2 1.3 copy.7
  (1 shorter events, 0.0 us)
Async XLA Ops:
  6.5 69.6 %copy-start.1 = (f32[1,2,256,1024]{3,2,1,0:T(8,128)S(1)}, f32[1,2,256,1024]{3,2,1,0:T(8,128)}, u32[]{:S(2)}) copy-start(f32[1,2,256,1024]{3,2,1,0:T(8,128)} %param.6) | copy-start | bytes 6291460
  6.5 66.5 %all-reduce.3.cloned.1.call-start = ((), (), s32[]{:S(2)}) async-start(), calls=%async_computation | async-start | bytes 2097152 | tf_op jit(solution)/shard_map/psum | solution.py:9
  11.4 66.3 %copy-start.3 = (s32[8]{0:T(128)S(1)}, s32[8]{0:T(128)}, u32[]{:S(2)}) copy-start(s32[8]{0:T(128)} %param.9) | copy-start | bytes 100
  11.4 67.6 %copy-start.2 = (s32[1,2]{1,0:T(1,128)S(1)}, s32[1,2]{1,0:T(1,128)}, u32[]{:S(2)}) copy-start(s32[1,2]{1,0:T(1,128)} %param.8) | copy-start | bytes 28
  11.4 87.8 %all-gather.7.cloned.1.call-start = ((), (), s32[]{:S(2)}) async-start(), calls=%async_computation.1 | async-start | bytes 1179648 | tf_op jit(solution)/shard_map/all_gather | solution.py:23
  76.1 76.3 %all-gather.11.cloned.1.call-start = ((), (), s32[]{:S(2)}) async-start(), calls=%async_computation.4 | async-start | bytes 5242880 | tf_op jit(solution)/shard_map/all_gather | solution.py:25
  77.7 141.5 %all-reduce.5.cloned.1.call-start = ((), (), s32[]{:S(2)}) async-start(), calls=%async_computation.2 | async-start | bytes 2097152 | tf_op jit(solution)/shard_map/psum | solution.py:9
  152.4 145.6 %copy-start = (f32[1024,256]{0,1:T(8,128)S(1)}, f32[1024,256]{0,1:T(8,128)}, u32[]{:S(2)}) copy-start(f32[1024,256]{0,1:T(8,128)} %all-gather.7.cloned.1.call-done) | copy-start | bytes 3145732
  160.3 112.3 %all-gather.13.cloned.1.call-start = ((), (), s32[]{:S(2)}) async-start(), calls=%async_computation.5 | async-start | bytes 5242880 | tf_op jit(solution)/shard_map/all_gather | solution.py:25
  160.8 137.1 %all-gather.9.cloned.1.call-start = ((), (), s32[]{:S(2)}) async-start(), calls=%async_computation.3 | async-start | bytes 1179648 | tf_op jit(solution)/shard_map/all_gather | solution.py:23
Sparse Core Ops, SparseCore 0:
  11.5 61.4 all-reduce.2
  76.2 22.9 all-gather.6
  101.0 51.2 all-gather.10
  160.4 58.7 all-reduce.4
  220.8 51.6 all-gather.12
  274.0 23.9 all-gather.8
where the time goes:
time: 314 us; the launch traced here: 313 us
  waiting for transfers between devices  267 us (85%)
  matrix products  21.1 us (7%)
  between operations  16.1 us (5%)
  local copies, waits for them, and re-layouts  5.68 us (2%)
  other arithmetic  3.24 us (1%)
    psum x2, waiting for transfers between devices, broadcast(): return lax.psum(jnp.where(mine, shard, jnp.zeros_like(shard)), axis)  120 us
    all_gather x2, waiting for transfers between devices, shards(): lax.all_gather(panel[0, step], 'col', axis=0, tiled=True)  102 us
    all_gather x2, waiting for transfers between devices, shards(): block_x = lax.all_gather(share, 'row', axis=0, tiled=True)  44.9 us
    dot_general x2, matrix products, shards(): jnp.dot(lax.all_gather(panel[0, step], 'col', axis=0, tiled=True), block_...  15.1 us
  transfers between devices with their start and end apart: 6, of which 6 were waited for; matrix products, arithmetic and copies ran while one was open for 2% of the time, Pallas kernels for 0%

commit v1 on v0

v1 whole, which is shorter than its diff:
```python
import functools

import jax
import jax.numpy as jnp
from jax import lax
from jax.experimental import pallas as pl
from jax.experimental.pallas import tpu as pltpu
from jax.sharding import PartitionSpec as P

HIGH = lax.Precision.HIGH


def bit(index, b):
    return (index >> b) & 1


def swap(x, axis, b, size):
    return lax.ppermute(x, axis, [(i, i ^ (1 << b)) for i in range(size)])


def tie(value, *others):
    return lax.optimization_barrier((value, *others))


def join(low_first, a, b):
    return jnp.where(low_first, jnp.concatenate([a, b]), jnp.concatenate([b, a]))


def halves(x, b):
    half = x.shape[0] // 2
    return lax.dynamic_slice_in_dim(x, b * half, half), lax.dynamic_slice_in_dim(x, (1 - b) * half, half)


def scatter_step(x, b, size, owner, me):
    mine = bit(me, b)
    keep, send = halves(x, mine)
    return jnp.where(bit(owner, b) == mine, keep, swap(send, "row", b, size))


def cross_step(x, b, size, owner, me):
    return jnp.where(bit(owner, b) == bit(me, b), x, swap(x, "row", b, size))


def gather_step(x, b, size, me):
    return join(bit(me, b) == 0, x, swap(x, "row", b, size))


def split(x):
    high = x.astype(jnp.bfloat16)
    return high, (x - high.astype(jnp.float32)).astype(jnp.bfloat16)


def dot3(a, b):
    def dot(p, q):
        return jnp.dot(p, q, preferred_element_type=jnp.float32)

    return dot(a[0], b[0]) + (dot(a[0], b[1]) + dot(a[1], b[0]))


def prepare_body(step, ids, own, *refs):
    pieces, (high, low, panel, sems) = refs[:6], refs[6:]
    side = ids[1]
    half = pieces[0].shape[0]
    sources = [(own.at[0, step], side * 2)]
    for ref, (distance, part) in zip(pieces, ((1, 0), (2, 1), (1, 1), (2, 0), (3, 0), (3, 1))):
        sources.append((ref, (side ^ distance) * 2 + part))
    copies = []
    for index, (ref, place) in enumerate(sources):
        rows = pl.ds(pl.multiple_of(place * half, half), ref.shape[0])
        copy = pltpu.make_async_copy(ref, panel.at[rows], sems.at[index])
        copy.start()
        copies.append(copy)
    for copy in copies:
        copy.wait()
    for start in range(0, panel.shape[0], half):
        rows = pl.ds(start, half)
        high[rows], low[rows] = split(panel[rows])


def prepare(ids, panel, step, pieces):
    depth = panel.shape[3]
    vmem, anywhere = pl.BlockSpec(memory_space=pltpu.VMEM), pl.BlockSpec(memory_space=pl.ANY)
    return pl.pallas_call(
        functools.partial(prepare_body, step),
        out_shape=[jax.ShapeDtypeStruct((depth, depth), jnp.bfloat16)] * 2,
        in_specs=[pl.BlockSpec(memory_space=pltpu.SMEM)] + [anywhere] * 7,
        out_specs=[vmem] * 2,
        scratch_shapes=[pltpu.VMEM((depth, depth), jnp.float32), pltpu.SemaphoreType.DMA((7,))],
        compiler_params=pltpu.CompilerParams(vmem_limit_bytes=8 * 2**20),
        cost_estimate=pl.CostEstimate(flops=0, bytes_accessed=8 * depth * depth, transcendentals=0),
        name="prepare",
    )(ids, panel, *pieces)


def update_body(step, ids, weight, high, low, own_x, other_x, current, out, *rest):
    x = rest[-1]
    rank, held = ids[0], ids[2]
    core, z = bit(rank, 0), rank >> 1
    share = own_x.shape[0] // 4
    for distance in range(4):
        block = pl.ds(distance * share, share)
        place = (z ^ distance) * 2
        x[pl.ds(pl.multiple_of((place + core) * share, share), share)] = own_x[block]
        x[pl.ds(pl.multiple_of((place + 1 - core) * share, share), share)] = other_x[block]
    parts = split(x[...])
    size = out.shape[0] // 2
    for start in (0, size):
        rows = pl.ds(start, size)
        new = current[rows] - weight[0] * dot3((high[rows], low[rows]), parts)
        if step == 0:
            out[rows] = jnp.where(held == 0, x[rows], new)
        else:
            out[rows] = jnp.where(held == 0, current[rows], jnp.where(held == 1, x[rows], new))
    if step == 0:
        rest[0][...] = out[pl.ds(pl.multiple_of((1 - core) * size, size), size)]


def update(step, ids, weight, pair, own_x, other_x, current):
    rows, cols = current.shape
    depth = pair[0].shape[1]
    vmem, smem = pl.BlockSpec(memory_space=pltpu.VMEM), pl.BlockSpec(memory_space=pltpu.SMEM)
    counts = (rows, rows // 2) if step == 0 else (rows,)
    return pl.pallas_call(
        functools.partial(update_body, step),
        out_shape=[jax.ShapeDtypeStruct((count, cols), jnp.float32) for count in counts],
        in_specs=[smem, smem] + [vmem] * 5,
        out_specs=[vmem] * len(counts),
        scratch_shapes=[pltpu.VMEM((depth, cols), jnp.float32)],
        compiler_params=pltpu.CompilerParams(vmem_limit_bytes=8 * 2**20),
        cost_estimate=pl.CostEstimate(flops=6 * rows * depth * cols, bytes_accessed=4 * rows * (depth + 3 * cols), transcendentals=0),
        name="update",
    )(ids, weight, *pair, own_x, other_x, current)


def general(rows, cols, rhs, panel, diag_inverse, flags, slot_block):
    rank = lax.axis_index("row")
    owners = (jnp.argmax(slot_block == 0), jnp.argmax(slot_block == 1))
    weights = flags[0].astype(jnp.float32)
    bits = rows.bit_length() - 1
    current = rhs[0]
    solved = []
    for step in range(2):
        pivot = current
        for b in range(bits - 1):
            pivot = scatter_step(pivot, b, rows, owners[step], rank)
        pivot = cross_step(pivot, bits - 1, rows, owners[step], rank)
        for b in reversed(range(bits - 1)):
            pivot = gather_step(pivot, b, rows, rank)
        x = jnp.dot(diag_inverse[step], pivot, precision=HIGH)
        for b in range(bits):
            x = gather_step(x, b, rows, rank)
        whole = lax.all_gather(panel[0, step], "col", axis=0, tiled=True)
        current = current - weights[step] * jnp.dot(whole, x, precision=HIGH)
        solved.append(x)
    held = slot_block[rank]
    return jnp.where(held == 0, solved[0], jnp.where(held == 1, solved[1], current))[None]


def paced(rows, cols, rhs, panel, diag_inverse, flags, slot_block):
    rank, side = lax.axis_index("row"), lax.axis_index("col")
    owner = jnp.argmax(slot_block == 0)
    half = panel.shape[2] // 2
    core = bit(rank, 0)

    def near(one, two):
        return [swap(one, "col", 0, cols), swap(two, "col", 1, cols)]

    def far(one, two):
        return [swap(one, "col", 1, cols), swap(two, "col", 0, cols)]

    def block_halves(panel, step):
        return panel[0, step, :half], panel[0, step, half:]

    y = scatter_step(rhs[0], 0, rows, owner, rank)
    y, panel = tie(y, panel)
    top, bottom = block_halves(panel, 0)
    first0 = near(top, bottom)
    y = scatter_step(y, 1, rows, owner, rank)
    y, panel, flags, slot_block, rank_, side_ = tie(y, panel, flags, slot_block, rank, side)
    top, bottom = block_halves(panel, 0)
    second0 = near(bottom, top)
    weights = flags[0].astype(jnp.float32)
    ids = jnp.stack([rank_, side_, slot_block[rank_]])
    second = jnp.argmax(slot_block == 1)
    y = cross_step(y, 2, rows, owner, rank)
    y, ids, weight0, weight1, second, *first0 = tie(y, ids, weights[0:1], weights[1:2], second, *first0)
    far0 = far(*first0)
    y = gather_step(y, 1, rows, rank)
    y, *second0 = tie(y, *second0)
    other = swap(y, "row", 0, rows)
    other, *far0 = tie(other, *far0)
    y = join(core == 0, y, other)
    x = jnp.dot(diag_inverse[0], y, precision=HIGH)
    x2, x1 = swap(x, "row", 2, rows), swap(x, "row", 1, rows)
    x2, x1 = tie(x2, x1)
    pair = prepare(ids, panel, 0, [*first0, *second0, *far0])
    x3 = swap(x2, "row", 1, rows)
    x3, high, low = tie(x3, *pair)
    x = jnp.concatenate([x, x1, x2, x3])
    other = swap(x, "row", 0, rows)
    current, send = update(0, ids, weight0, (high, low), x, other, rhs[0])
    got = swap(send, "row", 0, rows)
    keep = lax.dynamic_slice_in_dim(current, core * send.shape[0], send.shape[0])
    y = jnp.where(bit(second, 0) == core, keep, got)
    y, panel = tie(y, panel)
    top, bottom = block_halves(panel, 1)
    first1 = near(top, bottom)
    y = scatter_step(y, 1, rows, second, rank)
    y, panel = tie(y, panel)
    top, bottom = block_halves(panel, 1)
    second1 = near(bottom, top)
    y = cross_step(y, 2, rows, second, rank)
    y, *first1 = tie(y, *first1)
    far1 = far(*first1)
    y = gather_step(y, 1, rows, rank)
    y, *second1 = tie(y, *second1)
    other = swap(y, "row", 0, rows)
    other, *far1 = tie(other, *far1)
    y = join(core == 0, y, other)
    x = jnp.dot(diag_inverse[1], y, precision=HIGH)
    x2, x1 = swap(x, "row", 2, rows), swap(x, "row", 1, rows)
    pair = prepare(ids, panel, 1, [*first1, *second1, *far1])
    x2, x1, *pair = tie(x2, x1, *pair)
    x3 = swap(x2, "row", 1, rows)
    x = jnp.concatenate([x, x1, x2, x3])
    other = swap(x, "row", 0, rows)
    (result,) = update(1, ids, weight1, pair, x, other, current)
    return result[None]


def solution(mesh):
    rows, cols = mesh.shape["row"], mesh.shape["col"]
    form = paced if (rows, cols) == (8, 4) else general

    def shards(*args):
        return form(rows, cols, *args)

    in_specs = (
        P("row", None, "col"),
        P("row", None, "col", None),
        P(None, "row", None),
        P("row", None),
        P(),
    )
    out_specs = P("row", None, "col")
    return jax.shard_map(shards, mesh=mesh, in_specs=in_specs, out_specs=out_specs, check_vma=False)
```

time: 314 us -> 129 us (0.41)
  waiting for transfers between devices: 267 us -> 58.4 us
  starting transfers between devices: 0.21 us -> 37.8 us
  matrix products: 21.1 us -> 2.57 us
  Pallas kernels: 0 us -> 12.6 us
  between operations: 16.1 us -> 4.03 us
  other arithmetic: 3.24 us -> 8.66 us
    all_gather x4 -> x0, waiting for transfers between devices: 147 us -> none  [the longest x2 102 us: shards(): lax.all_gather(panel[0, step], 'col', axis=0, tiled=True)]
    psum x2 -> x0, waiting for transfers between devices: 120 us -> none  [broadcast(): return lax.psum(jnp.where(mine, shard, jnp.zeros_like(shard)), axis)]
    ppermute x0 -> x30, waiting for transfers between devices: none -> 58.4 us  [swap(): return lax.ppermute(x, axis, [(i, i ^ 1 << b) for i in range(size)])]
    ppermute x0 -> x30, starting transfers between devices: none -> 37.8 us  [swap(): return lax.ppermute(x, axis, [(i, i ^ 1 << b) for i in range(size)])]
    dot_general x4 -> x2, matrix products: 21.1 us -> 2.57 us  [the longest x1 2.13 us: paced(): x = jnp.dot(diag_inverse[0], y, precision=HIGH)]
    pallas_call x0 -> x4, Pallas kernels: none -> 12.6 us  [the longest x2 7.89 us: update(): pl.pallas_call(functools.partial(update_body, step), out_shape=[jax.Shape...]
    select_n x1 -> x8, other arithmetic: 1.04 us -> 5.92 us  [the longest x2 1.92 us: join(): jnp.where(low_first, jnp.concatenate([a, b]), jnp.concatenate([b, a]))]
  transfers between devices with their start and end apart: 6 -> 30, of which waited for: 6 -> 19; matrix products, arithmetic and copies ran while one was open for 2% -> 8% of each run, Pallas kernels for 0% -> 4%
where the time goes in v1:
time: 129 us
  waiting for transfers between devices  58.4 us (45%)
  starting transfers between devices  37.8 us (29%)
  Pallas kernels  12.6 us (10%)
  other arithmetic  8.66 us (7%)
  local copies, waits for them, and re-layouts  4.81 us (4%)
  between operations  4.03 us (3%)
  matrix products  2.57 us (2%)
    ppermute x30, waiting for transfers between devices, swap(): return lax.ppermute(x, axis, [(i, i ^ 1 << b) for i in range(size)])  58.4 us
    ppermute x30, starting transfers between devices, swap(): return lax.ppermute(x, axis, [(i, i ^ 1 << b) for i in range(size)])  37.8 us
    pallas_call x2, Pallas kernels, update(): pl.pallas_call(functools.partial(update_body, step), out_shape=[jax.Shape...  7.89 us
    pallas_call x2, Pallas kernels, prepare(): pl.pallas_call(functools.partial(prepare_body, step), out_shape=[jax.Shap...  4.7 us
  transfers between devices with their start and end apart: 30, of which 19 were waited for; matrix products, arithmetic and copies ran while one was open for 8% of the time, Pallas kernels for 4%

profile of v1, /device:TPU:0, one launch (start us, length us, event | category | flops | bytes accessed | tf_op | source)
XLA Modules:
  0.0 128.9 jit_solution(10330001767702634316)
XLA Ops:
  0.0 1.2 dynamic-slice_bitcast_fusion
  1.7 1.3 %compare_reduce_fusion.1 = (pred[]{:T(512)}, s32[]{:T(128)}) fusion(s32[8]{0:T(128)} %param.9), kind=kLoop, calls=%fused_computation.40 | loop fusion | flops 57 | bytes 37 | tf_op jit(solution)/shard_map/paced/reduce | solution.py:161
  5.0 1.1 bitcast_select_fusion
  6.2 2.7 %collective-permute-start.1 = (f32[256,256]{1,0:T(8,128)S(1)}, f32[256,256]{1,0:T(8,128)S(1)}, u32[]{:S(2)}, u32[]{:S(2)}) collective-permute-start(f32[256,256]{1,0:T(8,128)S(1)} %constant_dynamic-slice_fusion.1), channel_id=1, source_target_pairs={{0,8},{4,12},{8,0},{12,4},{16,24},{20,28},{24,16},{28,20},{1,9},{5... | collective-permute-start | bytes 786440 | tf_op jit(solution)/shard_map/ppermute | solution.py:18
  8.8 1.1 slice_bitcast_fusion.6
  9.9 1.5 %collective-permute-start.4 = (f32[128,1024]{1,0:T(8,128)}, f32[128,1024]{1,0:T(8,128)S(1)}, u32[]{:S(2)}, u32[]{:S(2)}) collective-permute-start(f32[128,1024]{1,0:T(8,128)} %get-tuple-element.113), channel_id=1, source_target_pairs={{0,2},{1,3},{2,0},{3,1},{4,6},{5,7},{6,4},{7,5},{8,10},{9,11},{10,... | collective-permute-start | bytes 1572872 | tf_op jit(solution)/shard_map/ppermute | solution.py:18
  11.4 1.5 %collective-permute-start.3 = (f32[128,1024]{1,0:T(8,128)}, f32[128,1024]{1,0:T(8,128)S(1)}, u32[]{:S(2)}, u32[]{:S(2)}) collective-permute-start(f32[128,1024]{1,0:T(8,128)} %get-tuple-element.114), channel_id=1, source_target_pairs={{0,1},{1,0},{2,3},{3,2},{4,5},{5,4},{6,7},{7,6},{8,9},{9,8},{10,11... | collective-permute-start | bytes 1572872 | tf_op jit(solution)/shard_map/ppermute | solution.py:18
  12.9 2.9 %collective-permute-done.1 = f32[256,256]{1,0:T(8,128)S(1)} collective-permute-done((f32[256,256]{1,0:T(8,128)S(1)}, f32[256,256]{1,0:T(8,128)S(1)}, u32[]{:S(2)}, u32[]{:S(2)}) %collective-permute-start.1) | collective-permute-done | bytes 262176 | tf_op jit(solution)/shard_map/ppermute | solution.py:18
  16.4 2.8 %collective-permute-start.2 = (f32[256,256]{1,0:T(8,128)S(1)}, f32[256,256]{1,0:T(8,128)}, u32[]{:S(2)}, u32[]{:S(2)}) collective-permute-start(f32[256,256]{1,0:T(8,128)S(1)} %dynamic-slice_select_fusion.2), channel_id=1, source_target_pairs={{0,16},{4,20},{8,24},{12,28},{16,0},{20,4},{24,8},{28,12},{1,17},{... | collective-permute-start | bytes 786440 | tf_op jit(solution)/shard_map/ppermute | solution.py:18
  19.1 1.1 slice_bitcast_fusion.4
  20.2 1.5 %collective-permute-start.7 = (f32[128,1024]{1,0:T(8,128)}, f32[128,1024]{1,0:T(8,128)}, u32[]{:S(2)}, u32[]{:S(2)}) collective-permute-start(f32[128,1024]{1,0:T(8,128)} %get-tuple-element.111), channel_id=1, source_target_pairs={{0,2},{1,3},{2,0},{3,1},{4,6},{5,7},{6,4},{7,5},{8,10},{9,11},{10,... | collective-permute-start | bytes 1572872 | tf_op jit(solution)/shard_map/ppermute | solution.py:18
  21.7 1.5 %collective-permute-start.6 = (f32[128,1024]{1,0:T(8,128)}, f32[128,1024]{1,0:T(8,128)}, u32[]{:S(2)}, u32[]{:S(2)}) collective-permute-start(f32[128,1024]{1,0:T(8,128)} %get-tuple-element.112), channel_id=1, source_target_pairs={{0,1},{1,0},{2,3},{3,2},{4,5},{5,4},{6,7},{7,6},{8,9},{9,8},{10,11... | collective-permute-start | bytes 1572872 | tf_op jit(solution)/shard_map/ppermute | solution.py:18
  24.5 0.7 compare_reduce_fusion
  25.2 5.9 %collective-permute-done.2 = f32[256,256]{1,0:T(8,128)} collective-permute-done((f32[256,256]{1,0:T(8,128)S(1)}, f32[256,256]{1,0:T(8,128)}, u32[]{:S(2)}, u32[]{:S(2)}) %collective-permute-start.2) | collective-permute-done | bytes 262176 | tf_op jit(solution)/shard_map/ppermute | solution.py:18
  31.1 1.7 %broadcast_select_fusion.1 = f32[256,256]{1,0:T(8,128)} fusion(f32[256,256]{1,0:T(8,128)S(1)} %dynamic-slice_select_fusion.2, f32[256,256]{1,0:T(8,128)} %collective-permute-done.2, pred[]{:T(512)S(6)} %eq.36), kind=kLoop, calls=%fused_computation.38 | loop fusion | flops 65536 | bytes 786433 | tf_op jit(solution)/shard_map/jit(_where)/select_n | solution.py:41
  33.3 1.5 %collective-permute-start.9 = (f32[128,1024]{1,0:T(8,128)S(1)}, f32[128,1024]{1,0:T(8,128)}, u32[]{:S(2)}, u32[]{:S(2)}) collective-permute-start(f32[128,1024]{1,0:T(8,128)S(1)} %collective-permute-done.3.refs_0_), channel_id=1, source_target_pairs={{0,2},{1,3},{2,0},{3,1},{4,6},{5,7},{6,4},{7,5},{8,10},{9,11},{10,... | collective-permute-start | bytes 1572872 | tf_op jit(solution)/shard_map/ppermute | solution.py:18
  34.9 1.5 %collective-permute-start.10 = (f32[128,1024]{1,0:T(8,128)S(1)}, f32[128,1024]{1,0:T(8,128)}, u32[]{:S(2)}, u32[]{:S(2)}) collective-permute-start(f32[128,1024]{1,0:T(8,128)S(1)} %collective-permute-done.4.refs_1_), channel_id=1, source_target_pairs={{0,1},{1,0},{2,3},{3,2},{4,5},{5,4},{6,7},{7,6},{8,9},{9,8},{10,11... | collective-permute-start | bytes 1572872 | tf_op jit(solution)/shard_map/ppermute | solution.py:18
  36.3 3.9 %collective-permute-done.5 = f32[256,256]{1,0:T(8,128)S(1)} collective-permute-done((f32[256,256]{1,0:T(8,128)}, f32[256,256]{1,0:T(8,128)S(1)}, u32[]{:S(2)}, u32[]{:S(2)}) %collective-permute-start.5) | collective-permute-done | bytes 262176 | tf_op jit(solution)/shard_map/ppermute | solution.py:18
  40.3 1.9 %maximum_select_fusion.4 = f32[512,256]{1,0:T(8,128)} fusion(f32[256,256]{1,0:T(8,128)S(1)} %collective-permute-done.5, f32[256,256]{1,0:T(8,128)} %broadcast_select_fusion.1, pred[]{:T(512)S(6)} %eq.41), kind=kLoop, calls=%fused_computation.14 | loop fusion | flops 393216 | bytes 1048577 | tf_op jit(solution)/shard_map/jit(_where)/select_n | solution.py:26
  42.2 4.8 %collective-permute-done.9.refs_4_ = f32[128,1024]{1,0:T(8,128)} collective-permute-done((f32[128,1024]{1,0:T(8,128)S(1)}, f32[128,1024]{1,0:T(8,128)}, u32[]{:S(2)}, u32[]{:S(2)}) %collective-permute-start.9) | collective-permute-done | bytes 524320 | tf_op jit(solution)/shard_map/ppermute | solution.py:18
  47.0 1.2 collective-permute-done.10.refs_5_
  48.3 2.1 %convolution_bitcast_fusion.1 = f32[128,256]{1,0:T(8,128)S(1)} fusion(f32[512,256]{1,0:T(8,128)} %collective-permute-done.8, f32[512,256]{1,0:T(8,128)} %maximum_select_fusion.4, f32[2,128,1024]{2,1,0:T(8,128)} %param.7, pred[]{:T(512)S(6)} %eq.40), kind=kOutput, calls=%fused_computation.1 | convolution fusion | flops 202113024 | bytes 1703937 | tf_op jit(solution)/shard_map/dot_general | solution.py:193
  50.9 2.5 %collective-permute-start.11 = (f32[128,256]{1,0:T(8,128)S(1)}, f32[128,256]{1,0:T(8,128)S(1)}, u32[]{:S(2)}, u32[]{:S(2)}) collective-permute-start(f32[128,256]{1,0:T(8,128)S(1)} %convolution_bitcast_fusion.1), channel_id=1, source_target_pairs={{0,16},{4,20},{8,24},{12,28},{16,0},{20,4},{24,8},{28,12},{1,17},{... | collective-permute-start | bytes 393224 | tf_op jit(solution)/shard_map/ppermute | solution.py:18
  53.4 2.5 %collective-permute-done.12 = f32[128,256]{1,0:T(8,128)S(1)} collective-permute-done((f32[128,256]{1,0:T(8,128)S(1)}, f32[128,256]{1,0:T(8,128)S(1)}, u32[]{:S(2)}, u32[]{:S(2)}) %collective-permute-start.12) | collective-permute-done | bytes 131104 | tf_op jit(solution)/shard_map/ppermute | solution.py:18
  55.9 1.9 %collective-permute-done.11 = f32[128,256]{1,0:T(8,128)S(1)} collective-permute-done((f32[128,256]{1,0:T(8,128)S(1)}, f32[128,256]{1,0:T(8,128)S(1)}, u32[]{:S(2)}, u32[]{:S(2)}) %collective-permute-start.11) | collective-permute-done | bytes 131104 | tf_op jit(solution)/shard_map/ppermute | solution.py:18
  57.8 2.0 %collective-permute-start.13 = (f32[128,256]{1,0:T(8,128)S(1)}, f32[128,256]{1,0:T(8,128)S(1)}, u32[]{:S(2)}, u32[]{:S(2)}) collective-permute-start(f32[128,256]{1,0:T(8,128)S(1)} %collective-permute-done.11), channel_id=1, source_target_pairs={{0,8},{4,12},{8,0},{12,4},{16,24},{20,28},{24,16},{28,20},{1,9},{5... | collective-permute-start | bytes 393224 | tf_op jit(solution)/shard_map/ppermute | solution.py:18
  59.7 3.0 %prepare.2 = (bf16[1024,1024]{1,0:T(8,128)(2,1)S(1)}, bf16[1024,1024]{1,0:T(8,128)(2,1)S(1)}) custom-call(s32[3]{0:T(128)S(1)} %pad_add_fusion.ids, f32[1,2,256,1024]{3,2,1,0:T(8,128)S(1)} %copy-done, f32[128,1024]{1,0:T(8,128)S(1)} %collective-permute-done.3.refs_0_, f32[128,1024]{1,0:T(8,128)S(1)} %collective-permute-done.4.refs_1_, ...), custom_call_target="tpu_custom_call" | custom-call | bytes 8388608 | tf_op jit(solution)/shard_map/prepare/pallas_call | solution.py:83
  62.9 1.9 %collective-permute-done.14.other_x = f32[512,256]{1,0:T(8,128)S(1)} collective-permute-done((f32[512,256]{1,0:T(8,128)S(1)}, f32[512,256]{1,0:T(8,128)S(1)}, u32[]{:S(2)}, u32[]{:S(2)}) %collective-permute-start.14) | collective-permute-done | bytes 524320 | tf_op jit(solution)/shard_map/ppermute | solution.py:18
  64.8 3.9 %update.2 = (f32[1024,256]{1,0:T(8,128)S(1)}, f32[512,256]{1,0:T(8,128)}) custom-call(s32[3]{0:T(128)S(1)} %pad_add_fusion.ids, f32[1]{0:T(128)} %bitcast.4.weight, bf16[1024,1024]{1,0:T(8,128)(2,1)S(1)} %get-tuple-element.82.high, bf16[1024,1024]{1,0:T(8,128)(2,1)S(1)} %get-tuple-element.83.low, f32[512,256]{1,0:T(8,128)S(1)} %pad_maximum_fusion.own_x, ...), custom_call_target="tpu_custom_call" | custom-call | flops 1610612736 | bytes 7340032 | tf_op jit(solution)/shard_map/update/pallas_call | solution.py:123
  71.0 1.1 dynamic-slice_select_fusion
  72.2 2.0 %collective-permute-start.16 = (f32[256,256]{1,0:T(8,128)S(1)}, f32[256,256]{1,0:T(8,128)S(1)}, u32[]{:S(2)}, u32[]{:S(2)}) collective-permute-start(f32[256,256]{1,0:T(8,128)S(1)} %constant_dynamic-slice_fusion), channel_id=1, source_target_pairs={{0,8},{4,12},{8,0},{12,4},{16,24},{20,28},{24,16},{28,20},{1,9},{5... | collective-permute-start | bytes 786440 | tf_op jit(solution)/shard_map/ppermute | solution.py:18
  74.9 1.5 %collective-permute-start.18 = (f32[128,1024]{1,0:T(8,128)S(1)}, f32[128,1024]{1,0:T(8,128)S(1)}, u32[]{:S(2)}, u32[]{:S(2)}) collective-permute-start(f32[128,1024]{1,0:T(8,128)S(1)} %get-tuple-element.110), channel_id=1, source_target_pairs={{0,1},{1,0},{2,3},{3,2},{4,5},{5,4},{6,7},{7,6},{8,9},{9,8},{10,11... | collective-permute-start | bytes 1572872 | tf_op jit(solution)/shard_map/ppermute | solution.py:18
  76.4 3.3 %collective-permute-done.16 = f32[256,256]{1,0:T(8,128)S(1)} collective-permute-done((f32[256,256]{1,0:T(8,128)S(1)}, f32[256,256]{1,0:T(8,128)S(1)}, u32[]{:S(2)}, u32[]{:S(2)}) %collective-permute-start.16) | collective-permute-done | bytes 262176 | tf_op jit(solution)/shard_map/ppermute | solution.py:18
  79.8 2.8 %collective-permute-start.17 = (f32[256,256]{1,0:T(8,128)S(1)}, f32[256,256]{1,0:T(8,128)S(1)}, u32[]{:S(2)}, u32[]{:S(2)}) collective-permute-start(f32[256,256]{1,0:T(8,128)S(1)} %dynamic-slice_select_fusion.1), channel_id=1, source_target_pairs={{0,16},{4,20},{8,24},{12,28},{16,0},{20,4},{24,8},{28,12},{1,17},{... | collective-permute-start | bytes 786440 | tf_op jit(solution)/shard_map/ppermute | solution.py:18
  83.3 1.5 %collective-permute-start.21 = (f32[128,1024]{1,0:T(8,128)S(1)}, f32[128,1024]{1,0:T(8,128)S(1)}, u32[]{:S(2)}, u32[]{:S(2)}) collective-permute-start(f32[128,1024]{1,0:T(8,128)S(1)} %get-tuple-element.108), channel_id=1, source_target_pairs={{0,1},{1,0},{2,3},{3,2},{4,5},{5,4},{6,7},{7,6},{8,9},{9,8},{10,11... | collective-permute-start | bytes 1572872 | tf_op jit(solution)/shard_map/ppermute | solution.py:18
  84.8 8.2 %collective-permute-done.17 = f32[256,256]{1,0:T(8,128)S(1)} collective-permute-done((f32[256,256]{1,0:T(8,128)S(1)}, f32[256,256]{1,0:T(8,128)S(1)}, u32[]{:S(2)}, u32[]{:S(2)}) %collective-permute-start.17) | collective-permute-done | bytes 262176 | tf_op jit(solution)/shard_map/ppermute | solution.py:18
  93.1 0.8 collective-permute-start.20
  94.4 1.5 %collective-permute-start.25 = (f32[128,1024]{1,0:T(8,128)S(1)}, f32[128,1024]{1,0:T(8,128)S(1)}, u32[]{:S(2)}, u32[]{:S(2)}) collective-permute-start(f32[128,1024]{1,0:T(8,128)S(1)} %collective-permute-done.19.refs_1_), channel_id=1, source_target_pairs={{0,1},{1,0},{2,3},{3,2},{4,5},{5,4},{6,7},{7,6},{8,9},{9,8},{10,11... | collective-permute-start | bytes 1572872 | tf_op jit(solution)/shard_map/ppermute | solution.py:18
  95.9 4.4 %collective-permute-done.20 = f32[256,256]{1,0:T(8,128)S(1)} collective-permute-done((f32[256,256]{1,0:T(8,128)S(1)}, f32[256,256]{1,0:T(8,128)S(1)}, u32[]{:S(2)}, u32[]{:S(2)}) %collective-permute-start.20) | collective-permute-done | bytes 262176 | tf_op jit(solution)/shard_map/ppermute | solution.py:18
  100.5 8.9 %collective-permute-done.24.refs_4_ = f32[128,1024]{1,0:T(8,128)S(1)} collective-permute-done((f32[128,1024]{1,0:T(8,128)S(1)}, f32[128,1024]{1,0:T(8,128)S(1)}, u32[]{:S(2)}, u32[]{:S(2)}) %collective-permute-start.24) | collective-permute-done | bytes 524320 | tf_op jit(solution)/shard_map/ppermute | solution.py:18
  110.6 2.7 %collective-permute-start.26 = (f32[128,256]{1,0:T(8,128)S(1)}, f32[128,256]{1,0:T(8,128)S(1)}, u32[]{:S(2)}, u32[]{:S(2)}) collective-permute-start(f32[128,256]{1,0:T(8,128)S(1)} %convolution_bitcast_fusion), channel_id=1, source_target_pairs={{0,16},{4,20},{8,24},{12,28},{16,0},{20,4},{24,8},{28,12},{1,17},{... | collective-permute-start | bytes 393224 | tf_op jit(solution)/shard_map/ppermute | solution.py:18
  113.3 1.7 %prepare.3 = (bf16[1024,1024]{1,0:T(8,128)(2,1)S(1)}, bf16[1024,1024]{1,0:T(8,128)(2,1)S(1)}) custom-call(s32[3]{0:T(128)S(1)} %pad_add_fusion.ids, f32[1,2,256,1024]{3,2,1,0:T(8,128)S(1)} %copy-done, f32[128,1024]{1,0:T(8,128)S(1)} %collective-permute-done.18.refs_0_, f32[128,1024]{1,0:T(8,128)S(1)} %collective-permute-done.19.refs_1_, ...), custom_call_target="tpu_custom_call" | custom-call | bytes 8388608 | tf_op jit(solution)/shard_map/prepare/pallas_call | solution.py:83
  115.0 0.9 collective-permute-done.27
  115.8 2.0 %collective-permute-done.26 = f32[128,256]{1,0:T(8,128)S(1)} collective-permute-done((f32[128,256]{1,0:T(8,128)S(1)}, f32[128,256]{1,0:T(8,128)S(1)}, u32[]{:S(2)}, u32[]{:S(2)}) %collective-permute-start.26) | collective-permute-done | bytes 131104 | tf_op jit(solution)/shard_map/ppermute | solution.py:18
  117.9 2.2 %collective-permute-start.28 = (f32[128,256]{1,0:T(8,128)S(1)}, f32[128,256]{1,0:T(8,128)S(1)}, u32[]{:S(2)}, u32[]{:S(2)}) collective-permute-start(f32[128,256]{1,0:T(8,128)S(1)} %collective-permute-done.26), channel_id=1, source_target_pairs={{0,8},{4,12},{8,0},{12,4},{16,24},{20,28},{24,16},{28,20},{1,9},{5... | collective-permute-start | bytes 393224 | tf_op jit(solution)/shard_map/ppermute | solution.py:18
  120.0 2.9 %collective-permute-done.28 = f32[128,256]{1,0:T(8,128)S(1)} collective-permute-done((f32[128,256]{1,0:T(8,128)S(1)}, f32[128,256]{1,0:T(8,128)S(1)}, u32[]{:S(2)}, u32[]{:S(2)}) %collective-permute-start.28) | collective-permute-done | bytes 131104 | tf_op jit(solution)/shard_map/ppermute | solution.py:18
  123.1 1.9 %collective-permute-done.29.other_x = f32[512,256]{1,0:T(8,128)S(1)} collective-permute-done((f32[512,256]{1,0:T(8,128)S(1)}, f32[512,256]{1,0:T(8,128)S(1)}, u32[]{:S(2)}, u32[]{:S(2)}) %collective-permute-start.29) | collective-permute-done | bytes 524320 | tf_op jit(solution)/shard_map/ppermute | solution.py:18
  125.0 3.9 %update.3 = f32[1024,256]{1,0:T(8,128)} custom-call(s32[3]{0:T(128)S(1)} %pad_add_fusion.ids, f32[1]{0:T(128)} %bitcast.5.weight, bf16[1024,1024]{1,0:T(8,128)(2,1)S(1)} %get-tuple-element.103.high, bf16[1024,1024]{1,0:T(8,128)(2,1)S(1)} %get-tuple-element.104.low, f32[512,256]{1,0:T(8,128)S(1)} %pad_maximum_fusion.1.own_x, ...), custom_call_target="tpu_custom_call" | custom-call | flops 1610612736 | bytes 7340032 | tf_op jit(solution)/shard_map/update/pallas_call | solution.py:123
  (51 shorter events, 7.5 us)
Async XLA Ops:
  0.0 8.8 %copy-start = (f32[1,2,256,1024]{3,2,1,0:T(8,128)S(1)}, f32[1,2,256,1024]{3,2,1,0:T(8,128)}, u32[]{:S(2)}) copy-start(f32[1,2,256,1024]{3,2,1,0:T(8,128)} %own.1) | copy-start | bytes 6291460
  1.2 3.7 %collective-permute-start = (f32[512,256]{1,0:T(8,128)S(1)}, f32[512,256]{1,0:T(8,128)S(1)}, u32[]{:S(2)}, u32[]{:S(2)}) collective-permute-start(f32[512,256]{1,0:T(8,128)S(1)} %dynamic-slice_bitcast_fusion), channel_id=1, source_target_pairs={{0,4},{4,0},{8,12},{12,8},{16,20},{20,16},{24,28},{28,24},{1,5},{5... | collective-permute-start | bytes 1572872 | tf_op jit(solution)/shard_map/ppermute | solution.py:18
  6.1 9.7 %copy-start.3 = (s32[1,2]{1,0:T(1,128)S(1)}, s32[1,2]{1,0:T(1,128)}, u32[]{:S(2)}) copy-start(s32[1,2]{1,0:T(1,128)} %param.8) | copy-start | bytes 28
  6.1 17.1 %copy-start.4 = (s32[8]{0:T(128)S(1)}, s32[8]{0:T(128)}, u32[]{:S(2)}) copy-start(s32[8]{0:T(128)} %param.9) | copy-start | bytes 100
  6.2 9.6 %collective-permute-start.1 = (f32[256,256]{1,0:T(8,128)S(1)}, f32[256,256]{1,0:T(8,128)S(1)}, u32[]{:S(2)}, u32[]{:S(2)}) collective-permute-start(f32[256,256]{1,0:T(8,128)S(1)} %constant_dynamic-slice_fusion.1), channel_id=1, source_target_pairs={{0,8},{4,12},{8,0},{12,4},{16,24},{20,28},{24,16},{28,20},{1,9},{5... | collective-permute-start | bytes 786440 | tf_op jit(solution)/shard_map/ppermute | solution.py:18
  9.9 22.9 %collective-permute-start.4 = (f32[128,1024]{1,0:T(8,128)}, f32[128,1024]{1,0:T(8,128)S(1)}, u32[]{:S(2)}, u32[]{:S(2)}) collective-permute-start(f32[128,1024]{1,0:T(8,128)} %get-tuple-element.113), channel_id=1, source_target_pairs={{0,2},{1,3},{2,0},{3,1},{4,6},{5,7},{6,4},{7,5},{8,10},{9,11},{10,... | collective-permute-start | bytes 1572872 | tf_op jit(solution)/shard_map/ppermute | solution.py:18
  11.4 21.4 %collective-permute-start.3 = (f32[128,1024]{1,0:T(8,128)}, f32[128,1024]{1,0:T(8,128)S(1)}, u32[]{:S(2)}, u32[]{:S(2)}) collective-permute-start(f32[128,1024]{1,0:T(8,128)} %get-tuple-element.114), channel_id=1, source_target_pairs={{0,1},{1,0},{2,3},{3,2},{4,5},{5,4},{6,7},{7,6},{8,9},{9,8},{10,11... | collective-permute-start | bytes 1572872 | tf_op jit(solution)/shard_map/ppermute | solution.py:18
  16.4 14.7 %collective-permute-start.2 = (f32[256,256]{1,0:T(8,128)S(1)}, f32[256,256]{1,0:T(8,128)}, u32[]{:S(2)}, u32[]{:S(2)}) collective-permute-start(f32[256,256]{1,0:T(8,128)S(1)} %dynamic-slice_select_fusion.2), channel_id=1, source_target_pairs={{0,16},{4,20},{8,24},{12,28},{16,0},{20,4},{24,8},{28,12},{1,17},{... | collective-permute-start | bytes 786440 | tf_op jit(solution)/shard_map/ppermute | solution.py:18
  20.2 21.9 %collective-permute-start.7 = (f32[128,1024]{1,0:T(8,128)}, f32[128,1024]{1,0:T(8,128)}, u32[]{:S(2)}, u32[]{:S(2)}) collective-permute-start(f32[128,1024]{1,0:T(8,128)} %get-tuple-element.111), channel_id=1, source_target_pairs={{0,2},{1,3},{2,0},{3,1},{4,6},{5,7},{6,4},{7,5},{8,10},{9,11},{10,... | collective-permute-start | bytes 1572872 | tf_op jit(solution)/shard_map/ppermute | solution.py:18
  21.7 20.4 %collective-permute-start.6 = (f32[128,1024]{1,0:T(8,128)}, f32[128,1024]{1,0:T(8,128)}, u32[]{:S(2)}, u32[]{:S(2)}) collective-permute-start(f32[128,1024]{1,0:T(8,128)} %get-tuple-element.112), channel_id=1, source_target_pairs={{0,1},{1,0},{2,3},{3,2},{4,5},{5,4},{6,7},{7,6},{8,9},{9,8},{10,11... | collective-permute-start | bytes 1572872 | tf_op jit(solution)/shard_map/ppermute | solution.py:18
  32.8 7.5 %collective-permute-start.5 = (f32[256,256]{1,0:T(8,128)}, f32[256,256]{1,0:T(8,128)S(1)}, u32[]{:S(2)}, u32[]{:S(2)}) collective-permute-start(f32[256,256]{1,0:T(8,128)} %broadcast_select_fusion.1), channel_id=1, source_target_pairs={{0,8},{4,12},{8,0},{12,4},{16,24},{20,28},{24,16},{28,20},{1,9},{5... | collective-permute-start | bytes 786440 | tf_op jit(solution)/shard_map/ppermute | solution.py:18
  33.3 13.7 %collective-permute-start.9 = (f32[128,1024]{1,0:T(8,128)S(1)}, f32[128,1024]{1,0:T(8,128)}, u32[]{:S(2)}, u32[]{:S(2)}) collective-permute-start(f32[128,1024]{1,0:T(8,128)S(1)} %collective-permute-done.3.refs_0_), channel_id=1, source_target_pairs={{0,2},{1,3},{2,0},{3,1},{4,6},{5,7},{6,4},{7,5},{8,10},{9,11},{10,... | collective-permute-start | bytes 1572872 | tf_op jit(solution)/shard_map/ppermute | solution.py:18
  34.9 13.4 %collective-permute-start.10 = (f32[128,1024]{1,0:T(8,128)S(1)}, f32[128,1024]{1,0:T(8,128)}, u32[]{:S(2)}, u32[]{:S(2)}) collective-permute-start(f32[128,1024]{1,0:T(8,128)S(1)} %collective-permute-done.4.refs_1_), channel_id=1, source_target_pairs={{0,1},{1,0},{2,3},{3,2},{4,5},{5,4},{6,7},{7,6},{8,9},{9,8},{10,11... | collective-permute-start | bytes 1572872 | tf_op jit(solution)/shard_map/ppermute | solution.py:18
  42.2 6.1 %collective-permute-start.8 = (f32[512,256]{1,0:T(8,128)}, f32[512,256]{1,0:T(8,128)}, u32[]{:S(2)}, u32[]{:S(2)}) collective-permute-start(f32[512,256]{1,0:T(8,128)} %maximum_select_fusion.4), channel_id=1, source_target_pairs={{0,4},{4,0},{8,12},{12,8},{16,20},{20,16},{24,28},{28,24},{1,5},{5... | collective-permute-start | bytes 1572872 | tf_op jit(solution)/shard_map/ppermute | solution.py:18
  50.4 14.4 %copy-start.1 = (f32[1,1024,256]{2,1,0:T(8,128)S(1)}, f32[1,1024,256]{2,1,0:T(8,128)}, u32[]{:S(2)}) copy-start(f32[1,1024,256]{2,1,0:T(8,128)} %param.5) | copy-start | bytes 3145732
  50.4 5.5 %collective-permute-start.12 = (f32[128,256]{1,0:T(8,128)S(1)}, f32[128,256]{1,0:T(8,128)S(1)}, u32[]{:S(2)}, u32[]{:S(2)}) collective-permute-start(f32[128,256]{1,0:T(8,128)S(1)} %convolution_bitcast_fusion.1), channel_id=1, source_target_pairs={{0,8},{4,12},{8,0},{12,4},{16,24},{20,28},{24,16},{28,20},{1,9},{5... | collective-permute-start | bytes 393224 | tf_op jit(solution)/shard_map/ppermute | solution.py:18
  50.9 6.9 %collective-permute-start.11 = (f32[128,256]{1,0:T(8,128)S(1)}, f32[128,256]{1,0:T(8,128)S(1)}, u32[]{:S(2)}, u32[]{:S(2)}) collective-permute-start(f32[128,256]{1,0:T(8,128)S(1)} %convolution_bitcast_fusion.1), channel_id=1, source_target_pairs={{0,16},{4,20},{8,24},{12,28},{16,0},{20,4},{24,8},{28,12},{1,17},{... | collective-permute-start | bytes 393224 | tf_op jit(solution)/shard_map/ppermute | solution.py:18
  57.8 5.0 %collective-permute-start.13 = (f32[128,256]{1,0:T(8,128)S(1)}, f32[128,256]{1,0:T(8,128)S(1)}, u32[]{:S(2)}, u32[]{:S(2)}) collective-permute-start(f32[128,256]{1,0:T(8,128)S(1)} %collective-permute-done.11), channel_id=1, source_target_pairs={{0,8},{4,12},{8,0},{12,4},{16,24},{20,28},{24,16},{28,20},{1,9},{5... | collective-permute-start | bytes 393224 | tf_op jit(solution)/shard_map/ppermute | solution.py:18
  62.8 2.0 %collective-permute-start.14 = (f32[512,256]{1,0:T(8,128)S(1)}, f32[512,256]{1,0:T(8,128)S(1)}, u32[]{:S(2)}, u32[]{:S(2)}) collective-permute-start(f32[512,256]{1,0:T(8,128)S(1)} %pad_maximum_fusion.own_x), channel_id=1, source_target_pairs={{0,4},{4,0},{8,12},{12,8},{16,20},{20,16},{24,28},{28,24},{1,5},{5... | collective-permute-start | bytes 1572872 | tf_op jit(solution)/shard_map/ppermute | solution.py:18
  68.8 2.3 %collective-permute-start.15 = (f32[512,256]{1,0:T(8,128)}, f32[512,256]{1,0:T(8,128)}, u32[]{:S(2)}, u32[]{:S(2)}) collective-permute-start(f32[512,256]{1,0:T(8,128)} %get-tuple-element.87), channel_id=1, source_target_pairs={{0,4},{4,0},{8,12},{12,8},{16,20},{20,16},{24,28},{28,24},{1,5},{5... | collective-permute-start | bytes 1572872 | tf_op jit(solution)/shard_map/ppermute | solution.py:18
  72.2 7.6 %collective-permute-start.16 = (f32[256,256]{1,0:T(8,128)S(1)}, f32[256,256]{1,0:T(8,128)S(1)}, u32[]{:S(2)}, u32[]{:S(2)}) collective-permute-start(f32[256,256]{1,0:T(8,128)S(1)} %constant_dynamic-slice_fusion), channel_id=1, source_target_pairs={{0,8},{4,12},{8,0},{12,4},{16,24},{20,28},{24,16},{28,20},{1,9},{5... | collective-permute-start | bytes 786440 | tf_op jit(solution)/shard_map/ppermute | solution.py:18
  74.3 18.8 %collective-permute-start.19 = (f32[128,1024]{1,0:T(8,128)S(1)}, f32[128,1024]{1,0:T(8,128)S(1)}, u32[]{:S(2)}, u32[]{:S(2)}) collective-permute-start(f32[128,1024]{1,0:T(8,128)S(1)} %get-tuple-element.109), channel_id=1, source_target_pairs={{0,2},{1,3},{2,0},{3,1},{4,6},{5,7},{6,4},{7,5},{8,10},{9,11},{10,... | collective-permute-start | bytes 1572872 | tf_op jit(solution)/shard_map/ppermute | solution.py:18
  74.9 18.1 %collective-permute-start.18 = (f32[128,1024]{1,0:T(8,128)S(1)}, f32[128,1024]{1,0:T(8,128)S(1)}, u32[]{:S(2)}, u32[]{:S(2)}) collective-permute-start(f32[128,1024]{1,0:T(8,128)S(1)} %get-tuple-element.110), channel_id=1, source_target_pairs={{0,1},{1,0},{2,3},{3,2},{4,5},{5,4},{6,7},{7,6},{8,9},{9,8},{10,11... | collective-permute-start | bytes 1572872 | tf_op jit(solution)/shard_map/ppermute | solution.py:18
  79.8 30.0 %copy-start.2 = (f32[2,128,1024]{2,1,0:T(8,128)S(1)}, f32[2,128,1024]{2,1,0:T(8,128)}, u32[]{:S(2)}) copy-start(f32[2,128,1024]{2,1,0:T(8,128)} %param.7) | copy-start | bytes 3145732
  79.8 13.2 %collective-permute-start.17 = (f32[256,256]{1,0:T(8,128)S(1)}, f32[256,256]{1,0:T(8,128)S(1)}, u32[]{:S(2)}, u32[]{:S(2)}) collective-permute-start(f32[256,256]{1,0:T(8,128)S(1)} %dynamic-slice_select_fusion.1), channel_id=1, source_target_pairs={{0,16},{4,20},{8,24},{12,28},{16,0},{20,4},{24,8},{28,12},{1,17},{... | collective-permute-start | bytes 786440 | tf_op jit(solution)/shard_map/ppermute | solution.py:18
  82.6 17.7 %collective-permute-start.22 = (f32[128,1024]{1,0:T(8,128)S(1)}, f32[128,1024]{1,0:T(8,128)S(1)}, u32[]{:S(2)}, u32[]{:S(2)}) collective-permute-start(f32[128,1024]{1,0:T(8,128)S(1)} %get-tuple-element.107), channel_id=1, source_target_pairs={{0,2},{1,3},{2,0},{3,1},{4,6},{5,7},{6,4},{7,5},{8,10},{9,11},{10,... | collective-permute-start | bytes 1572872 | tf_op jit(solution)/shard_map/ppermute | solution.py:18
  83.3 17.2 %collective-permute-start.21 = (f32[128,1024]{1,0:T(8,128)S(1)}, f32[128,1024]{1,0:T(8,128)S(1)}, u32[]{:S(2)}, u32[]{:S(2)}) collective-permute-start(f32[128,1024]{1,0:T(8,128)S(1)} %get-tuple-element.108), channel_id=1, source_target_pairs={{0,1},{1,0},{2,3},{3,2},{4,5},{5,4},{6,7},{7,6},{8,9},{9,8},{10,11... | collective-permute-start | bytes 1572872 | tf_op jit(solution)/shard_map/ppermute | solution.py:18
  93.1 7.3 %collective-permute-start.20 = (f32[256,256]{1,0:T(8,128)S(1)}, f32[256,256]{1,0:T(8,128)S(1)}, u32[]{:S(2)}, u32[]{:S(2)}) collective-permute-start(f32[256,256]{1,0:T(8,128)S(1)} %broadcast_select_fusion), channel_id=1, source_target_pairs={{0,8},{4,12},{8,0},{12,4},{16,24},{20,28},{24,16},{28,20},{1,9},{5... | collective-permute-start | bytes 786440 | tf_op jit(solution)/shard_map/ppermute | solution.py:18
  93.8 15.6 %collective-permute-start.24 = (f32[128,1024]{1,0:T(8,128)S(1)}, f32[128,1024]{1,0:T(8,128)S(1)}, u32[]{:S(2)}, u32[]{:S(2)}) collective-permute-start(f32[128,1024]{1,0:T(8,128)S(1)} %collective-permute-done.18.refs_0_), channel_id=1, source_target_pairs={{0,2},{1,3},{2,0},{3,1},{4,6},{5,7},{6,4},{7,5},{8,10},{9,11},{10,... | collective-permute-start | bytes 1572872 | tf_op jit(solution)/shard_map/ppermute | solution.py:18
  94.4 15.3 %collective-permute-start.25 = (f32[128,1024]{1,0:T(8,128)S(1)}, f32[128,1024]{1,0:T(8,128)S(1)}, u32[]{:S(2)}, u32[]{:S(2)}) collective-permute-start(f32[128,1024]{1,0:T(8,128)S(1)} %collective-permute-done.19.refs_1_), channel_id=1, source_target_pairs={{0,1},{1,0},{2,3},{3,2},{4,5},{5,4},{6,7},{7,6},{8,9},{9,8},{10,11... | collective-permute-start | bytes 1572872 | tf_op jit(solution)/shard_map/ppermute | solution.py:18
  100.5 9.3 %collective-permute-start.23 = (f32[512,256]{1,0:T(8,128)S(1)}, f32[512,256]{1,0:T(8,128)S(1)}, u32[]{:S(2)}, u32[]{:S(2)}) collective-permute-start(f32[512,256]{1,0:T(8,128)S(1)} %maximum_select_fusion.5), channel_id=1, source_target_pairs={{0,4},{4,0},{8,12},{12,8},{16,20},{20,16},{24,28},{28,24},{1,5},{5... | collective-permute-start | bytes 1572872 | tf_op jit(solution)/shard_map/ppermute | solution.py:18
  110.2 5.6 %collective-permute-start.27 = (f32[128,256]{1,0:T(8,128)S(1)}, f32[128,256]{1,0:T(8,128)S(1)}, u32[]{:S(2)}, u32[]{:S(2)}) collective-permute-start(f32[128,256]{1,0:T(8,128)S(1)} %convolution_bitcast_fusion), channel_id=1, source_target_pairs={{0,8},{4,12},{8,0},{12,4},{16,24},{20,28},{24,16},{28,20},{1,9},{5... | collective-permute-start | bytes 393224 | tf_op jit(solution)/shard_map/ppermute | solution.py:18
  110.6 7.3 %collective-permute-start.26 = (f32[128,256]{1,0:T(8,128)S(1)}, f32[128,256]{1,0:T(8,128)S(1)}, u32[]{:S(2)}, u32[]{:S(2)}) collective-permute-start(f32[128,256]{1,0:T(8,128)S(1)} %convolution_bitcast_fusion), channel_id=1, source_target_pairs={{0,16},{4,20},{8,24},{12,28},{16,0},{20,4},{24,8},{28,12},{1,17},{... | collective-permute-start | bytes 393224 | tf_op jit(solution)/shard_map/ppermute | solution.py:18
  117.9 5.1 %collective-permute-start.28 = (f32[128,256]{1,0:T(8,128)S(1)}, f32[128,256]{1,0:T(8,128)S(1)}, u32[]{:S(2)}, u32[]{:S(2)}) collective-permute-start(f32[128,256]{1,0:T(8,128)S(1)} %collective-permute-done.26), channel_id=1, source_target_pairs={{0,8},{4,12},{8,0},{12,4},{16,24},{20,28},{24,16},{28,20},{1,9},{5... | collective-permute-start | bytes 393224 | tf_op jit(solution)/shard_map/ppermute | solution.py:18
  123.0 2.0 %collective-permute-start.29 = (f32[512,256]{1,0:T(8,128)S(1)}, f32[512,256]{1,0:T(8,128)S(1)}, u32[]{:S(2)}, u32[]{:S(2)}) collective-permute-start(f32[512,256]{1,0:T(8,128)S(1)} %pad_maximum_fusion.1.own_x), channel_id=1, source_target_pairs={{0,4},{4,0},{8,12},{12,8},{16,20},{20,16},{24,28},{28,24},{1,5},{5... | collective-permute-start | bytes 1572872 | tf_op jit(solution)/shard_map/ppermute | solution.py:18

commit v2 on v0

v2 whole, which is shorter than its diff:
```python
import functools

import jax
import jax.numpy as jnp
from jax import lax
from jax.experimental import pallas as pl
from jax.experimental.pallas import tpu as pltpu
from jax.sharding import PartitionSpec as P

HIGH = lax.Precision.HIGH
PREPARE_BYTES = 4 * 2**20
UPDATE_BYTES = 5 * 2**20


def bit(index, b):
    return (index >> b) & 1


def swap(x, axis, b, size):
    return lax.ppermute(x, axis, [(i, i ^ (1 << b)) for i in range(size)])


def tie(value, *others):
    return lax.optimization_barrier((value, *others))


def join(low_first, a, b):
    return jnp.where(low_first, jnp.concatenate([a, b]), jnp.concatenate([b, a]))


def halves(x, b):
    half = x.shape[0] // 2
    return lax.dynamic_slice_in_dim(x, b * half, half), lax.dynamic_slice_in_dim(x, (1 - b) * half, half)


def scatter_step(x, b, size, owner, me):
    mine = bit(me, b)
    keep, send = halves(x, mine)
    return jnp.where(bit(owner, b) == mine, keep, swap(send, "row", b, size))


def cross_step(x, b, size, owner, me):
    return jnp.where(bit(owner, b) == bit(me, b), x, swap(x, "row", b, size))


def gather_step(x, b, size, me):
    return join(bit(me, b) == 0, x, swap(x, "row", b, size))


def split(x):
    high = x.astype(jnp.bfloat16)
    return high, (x - high.astype(jnp.float32)).astype(jnp.bfloat16)


def dot3(a, b):
    def dot(p, q):
        return jnp.dot(p, q, preferred_element_type=jnp.float32)

    return dot(a[0], b[0]) + (dot(a[0], b[1]) + dot(a[1], b[0]))


def prepare_body(own_top, own_bottom, *refs):
    pieces, (high, low, slots, sems) = refs[:6], refs[6:]
    side = lax.axis_index("col")
    half = pieces[0].shape[0]
    sources = [(own_top, side * 2), (own_bottom, side * 2 + 1)]
    for ref, (distance, part) in zip(pieces, ((1, 0), (2, 1), (1, 1), (2, 0), (3, 0), (3, 1))):
        sources.append((ref, (side ^ distance) * 2 + part))
    groups = [sources[start:start + 2] for start in range(0, 8, 2)]

    def fetch(index):
        copies = []
        start = 0
        for member, (ref, _) in enumerate(groups[index]):
            into = slots.at[index % 2, pl.ds(start, ref.shape[0])]
            copies.append(pltpu.make_async_copy(ref, into, sems.at[index % 2, member]))
            start += ref.shape[0]
        for copy in copies:
            copy.start()
        return copies

    flying = [fetch(0), fetch(1)]
    for index, group in enumerate(groups):
        for copy in flying[index]:
            copy.wait()
        start = 0
        for ref, place in group:
            rows = pl.ds(pl.multiple_of(place * half, half), ref.shape[0])
            high[rows], low[rows] = split(slots[index % 2, pl.ds(start, ref.shape[0])])
            start += ref.shape[0]
        if index + 2 < len(groups):
            flying.append(fetch(index + 2))


def prepare(pieces):
    half, depth = pieces[0].shape
    vmem, anywhere = pl.BlockSpec(memory_space=pltpu.VMEM), pl.BlockSpec(memory_space=pl.ANY)
    return pl.pallas_call(
        prepare_body,
        out_shape=[jax.ShapeDtypeStruct((depth, depth), jnp.bfloat16)] * 2,
        in_specs=[anywhere] * 8,
        out_specs=[vmem] * 2,
        scratch_shapes=[pltpu.VMEM((2, 2 * half, depth), jnp.float32), pltpu.SemaphoreType.DMA((2, 2))],
        compiler_params=pltpu.CompilerParams(vmem_limit_bytes=PREPARE_BYTES),
        cost_estimate=pl.CostEstimate(flops=0, bytes_accessed=16 * depth * depth, transcendentals=0),
        name="prepare",
    )(*pieces)


def assemble(x, blocks, rank):
    core, z = bit(rank, 0), rank >> 1
    share = blocks[0].shape[0]
    for index, ref in enumerate(blocks):
        place = (z ^ (index & 3)) * 2 + (core ^ (index >> 2))
        x[pl.ds(pl.multiple_of(place * share, share), share)] = ref[...]


def first_body(flags, slot_block, high, low, *refs):
    blocks, (rhs, keep, send, x, current, sem) = refs[:8], refs[8:]
    copy = pltpu.make_async_copy(rhs.at[0], current, sem)
    copy.start()
    rank = lax.axis_index("row")
    core = bit(rank, 0)
    assemble(x, blocks, rank)
    parts = split(x[...])
    weight = flags[0, 0].astype(jnp.float32)
    size = keep.shape[0]
    copy.wait()
    for out, part in ((send, 1 - core), (keep, core)):
        rows = pl.ds(pl.multiple_of(part * size, size), size)
        new = current[rows] - weight * dot3((high[rows], low[rows]), parts)
        out[...] = jnp.where(slot_block[rank] == 0, x[rows], new)


def second_body(flags, slot_block, high, low, *refs):
    blocks, (keep, send, out, x) = refs[:8], refs[8:]
    rank = lax.axis_index("row")
    core, held = bit(rank, 0), slot_block[rank]
    assemble(x, blocks, rank)
    parts = split(x[...])
    weight = flags[0, 1].astype(jnp.float32)
    size = keep.shape[0]
    for current, part in ((keep, core), (send, 1 - core)):
        rows = pl.ds(pl.multiple_of(part * size, size), size)
        new = current[...] - weight * dot3((high[rows], low[rows]), parts)
        out[rows] = jnp.where(held == 0, current[...], jnp.where(held == 1, x[rows], new))


def solve_body(step, inverse, *refs):
    quarters, (out, y) = refs[:4], refs[4:]
    rank = lax.axis_index("row")
    size = quarters[0].shape[0]
    core, z = bit(rank, 0), bit(rank, 1)
    for index, ref in enumerate(quarters):
        place = (core ^ (index >> 1)) * 2 + (z ^ (index & 1))
        y[pl.ds(pl.multiple_of(place * size, size), size)] = ref[...]
    out[...] = dot3(split(inverse[step]), split(y[...]))


def solve(step, inverse, quarters):
    _, rows, depth = inverse.shape
    cols = quarters[0].shape[1]
    vmem = pl.BlockSpec(memory_space=pltpu.VMEM)
    return pl.pallas_call(
        functools.partial(solve_body, step),
        out_shape=jax.ShapeDtypeStruct((rows, cols), jnp.float32),
        in_specs=[vmem] * 5,
        out_specs=vmem,
        scratch_shapes=[pltpu.VMEM((depth, cols), jnp.float32)],
        compiler_params=pltpu.CompilerParams(vmem_limit_bytes=UPDATE_BYTES),
        cost_estimate=pl.CostEstimate(flops=6 * rows * depth * cols, bytes_accessed=4 * (rows * depth + depth * cols), transcendentals=0),
        name="solve",
    )(inverse, *quarters)


def update(step, flags, slot_block, pair, blocks, current):
    depth = pair[0].shape[1]
    rows, cols = pair[0].shape[0], blocks[0].shape[1]
    vmem, smem = pl.BlockSpec(memory_space=pltpu.VMEM), pl.BlockSpec(memory_space=pltpu.SMEM)
    counts = (rows // 2, rows // 2) if step == 0 else (rows,)
    scratch = [pltpu.VMEM((depth, cols), jnp.float32)]
    if step == 0:
        scratch += [pltpu.VMEM((rows, cols), jnp.float32), pltpu.SemaphoreType.DMA]
    return pl.pallas_call(
        first_body if step == 0 else second_body,
        out_shape=[jax.ShapeDtypeStruct((count, cols), jnp.float32) for count in counts],
        in_specs=[smem, smem] + [vmem] * 10 + ([pl.BlockSpec(memory_space=pl.ANY)] if step == 0 else [vmem] * 2),
        out_specs=[vmem] * len(counts),
        scratch_shapes=scratch,
        compiler_params=pltpu.CompilerParams(vmem_limit_bytes=UPDATE_BYTES),
        cost_estimate=pl.CostEstimate(flops=6 * rows * depth * cols, bytes_accessed=4 * rows * (depth + 3 * cols), transcendentals=0),
        name="update",
    )(flags, slot_block, *pair, *blocks, *current)


def general(rows, cols, rhs, panel, diag_inverse, flags, slot_block):
    rank = lax.axis_index("row")
    owners = (jnp.argmax(slot_block == 0), jnp.argmax(slot_block == 1))
    weights = flags[0].astype(jnp.float32)
    bits = rows.bit_length() - 1
    current = rhs[0]
    solved = []
    for step in range(2):
        pivot = current
        for b in range(bits - 1):
            pivot = scatter_step(pivot, b, rows, owners[step], rank)
        pivot = cross_step(pivot, bits - 1, rows, owners[step], rank)
        for b in reversed(range(bits - 1)):
            pivot = gather_step(pivot, b, rows, rank)
        x = jnp.dot(diag_inverse[step], pivot, precision=HIGH)
        for b in range(bits):
            x = gather_step(x, b, rows, rank)
        whole = lax.all_gather(panel[0, step], "col", axis=0, tiled=True)
        current = current - weights[step] * jnp.dot(whole, x, precision=HIGH)
        solved.append(x)
    held = slot_block[rank]
    return jnp.where(held == 0, solved[0], jnp.where(held == 1, solved[1], current))[None]


def paced(rows, cols, rhs, panel, diag_inverse, flags, slot_block):
    rank = lax.axis_index("row")
    owner, second = jnp.argmax(slot_block == 0), jnp.argmax(slot_block == 1)
    half = panel.shape[2] // 2
    core = bit(rank, 0)

    def near(one, two):
        return [swap(one, "col", 0, cols), swap(two, "col", 1, cols)]

    def far(one, two):
        return [swap(one, "col", 1, cols), swap(two, "col", 0, cols)]

    def solved(step, y, block, first, owner):
        y = scatter_step(y, 1, rows, owner, rank)
        y, top, bottom = tie(y, *block)
        second = near(bottom, top)
        y = cross_step(y, 2, rows, owner, rank)
        y, *first = tie(y, *first)
        pieces = far(*first)
        other = swap(y, "row", 0, rows)
        beside = swap(y, "row", 1, rows)
        beside, other, *second = tie(beside, other, *second)
        last = swap(beside, "row", 0, rows)
        x = solve(step, diag_inverse, [y, beside, other, last])
        x2, x1 = swap(x, "row", 2, rows), swap(x, "row", 1, rows)
        x2, x1, *pieces = tie(x2, x1, *pieces)
        high, low = prepare([*block, *first, *second, *pieces])
        x3 = swap(x2, "row", 1, rows)
        across = [swap(part, "row", 0, rows) for part in (x, x1, x2)]
        x3, high, low, *across = tie(x3, high, low, *across)
        return [x, x1, x2, x3, *across, swap(x3, "row", 0, rows)], (high, low)

    y = scatter_step(rhs[0], 0, rows, owner, rank)
    y, panel = tie(y, panel)
    cut = [panel[0, step, start:start + half] for step in range(2) for start in (0, half)]
    cut = lax.optimization_barrier(cut)
    blocks, pair = solved(0, y, cut[:2], near(*cut[:2]), owner)
    first = near(*cut[2:])
    keep, send = update(0, flags, slot_block, pair, blocks, [rhs])
    keep, send, *first = tie(keep, send, *first)
    got = swap(send, "row", 0, rows)
    y = jnp.where(bit(second, 0) == core, keep, got)
    blocks, pair = solved(1, y, cut[2:], first, second)
    (result,) = update(1, flags, slot_block, pair, blocks, [keep, send])
    return result[None]


def solution(mesh):
    rows, cols = mesh.shape["row"], mesh.shape["col"]
    form = paced if (rows, cols) == (8, 4) else general

    def shards(*args):
        return form(rows, cols, *args)

    in_specs = (
        P("row", None, "col"),
        P("row", None, "col", None),
        P(None, "row", None),
        P("row", None),
        P(),
    )
    out_specs = P("row", None, "col")
    return jax.shard_map(shards, mesh=mesh, in_specs=in_specs, out_specs=out_specs, check_vma=False)
```

time: 314 us -> 128 us (0.41)
  waiting for transfers between devices: 267 us -> 58.1 us
  starting transfers between devices: 0.21 us -> 45 us
  matrix products: 21.1 us -> 0 us
  between operations: 16.1 us -> 3.85 us
  Pallas kernels: 0 us -> 11.4 us
    all_gather x4 -> x0, waiting for transfers between devices: 147 us -> none  [the longest x2 102 us: shards(): lax.all_gather(panel[0, step], 'col', axis=0, tiled=True)]
    psum x2 -> x0, waiting for transfers between devices: 120 us -> none  [broadcast(): return lax.psum(jnp.where(mine, shard, jnp.zeros_like(shard)), axis)]
    ppermute x0 -> x38, waiting for transfers between devices: none -> 58.1 us  [swap(): return lax.ppermute(x, axis, [(i, i ^ 1 << b) for i in range(size)])]
    ppermute x0 -> x38, starting transfers between devices: none -> 45 us  [swap(): return lax.ppermute(x, axis, [(i, i ^ 1 << b) for i in range(size)])]
    dot_general x4 -> x0, matrix products: 21.1 us -> none  [the longest x2 15.1 us: shards(): jnp.dot(lax.all_gather(panel[0, step], 'col', axis=0, tiled=True), block_...]
    pallas_call x0 -> x6, Pallas kernels: none -> 11.4 us  [the longest x2 7.43 us: update(): pl.pallas_call(first_body if step == 0 else second_body, out_shape=[jax.S...]
  transfers between devices with their start and end apart: 6 -> 38, of which waited for: 6 -> 18; matrix products, arithmetic and copies ran while one was open for 2% -> 2% of each run, Pallas kernels for 0% -> 6%
where the time goes in v2:
time: 128 us; the launch traced here: 127 us
  waiting for transfers between devices  58.1 us (45%)
  starting transfers between devices  45 us (35%)
  Pallas kernels  11.4 us (9%)
  other arithmetic  5.36 us (4%)
  between operations  3.85 us (3%)
  local copies, waits for them, and re-layouts  3.69 us (3%)
    ppermute x38, waiting for transfers between devices, swap(): return lax.ppermute(x, axis, [(i, i ^ 1 << b) for i in range(size)])  58.1 us
    ppermute x38, starting transfers between devices, swap(): return lax.ppermute(x, axis, [(i, i ^ 1 << b) for i in range(size)])  45 us
    pallas_call x2, Pallas kernels, update(): pl.pallas_call(first_body if step == 0 else second_body, out_shape=[jax.S...  7.43 us
    pallas_call x2, Pallas kernels, prepare(): pl.pallas_call(prepare_body, out_shape=[jax.ShapeDtypeStruct((depth, dept...  3.01 us
  transfers between devices with their start and end apart: 38, of which 18 were waited for; matrix products, arithmetic and copies ran while one was open for 2% of the time, Pallas kernels for 6%

profile of v2, /device:TPU:0, one launch (start us, length us, event | category | flops | bytes accessed | tf_op | source)
XLA Modules:
  0.0 127.4 jit_solution(6790073885058412802)
XLA Ops:
  0.0 1.1 dynamic-slice_bitcast_fusion
  1.6 1.3 %compare_reduce_fusion = (pred[]{:T(512)}, s32[]{:T(128)}) fusion(s32[8]{0:T(128)} %slot_block.3), kind=kLoop, calls=%fused_computation.11 | loop fusion | flops 57 | bytes 37 | tf_op jit(solution)/shard_map/paced/reduce | solution.py:222
  4.1 1.3 bitcast_select_fusion
  5.4 2.7 %collective-permute-start.1 = (f32[256,256]{1,0:T(8,128)S(1)}, f32[256,256]{1,0:T(8,128)S(1)}, u32[]{:S(2)}, u32[]{:S(2)}) collective-permute-start(f32[256,256]{1,0:T(8,128)S(1)} %constant_dynamic-slice_fusion.1), channel_id=1, source_target_pairs={{0,8},{4,12},{8,0},{12,4},{16,24},{20,28},{24,16},{28,20},{1,9},{5... | collective-permute-start | bytes 786440 | tf_op jit(solution)/shard_map/ppermute | solution.py:20
  8.2 1.6 %collective-permute-start.3 = (f32[128,1024]{1,0:T(8,128)S(1)}, f32[128,1024]{1,0:T(8,128)}, u32[]{:S(2)}, u32[]{:S(2)}) collective-permute-start(f32[128,1024]{1,0:T(8,128)S(1)} %get-tuple-element.72.own_top), channel_id=1, source_target_pairs={{0,1},{1,0},{2,3},{3,2},{4,5},{5,4},{6,7},{7,6},{8,9},{9,8},{10,11... | collective-permute-start | bytes 1572872 | tf_op jit(solution)/shard_map/ppermute | solution.py:20
  9.8 1.5 %collective-permute-start.4 = (f32[128,1024]{1,0:T(8,128)S(1)}, f32[128,1024]{1,0:T(8,128)}, u32[]{:S(2)}, u32[]{:S(2)}) collective-permute-start(f32[128,1024]{1,0:T(8,128)S(1)} %get-tuple-element.71.own_bottom), channel_id=1, source_target_pairs={{0,2},{1,3},{2,0},{3,1},{4,6},{5,7},{6,4},{7,5},{8,10},{9,11},{10,... | collective-permute-start | bytes 1572872 | tf_op jit(solution)/shard_map/ppermute | solution.py:20
  11.3 3.7 %collective-permute-done.1 = f32[256,256]{1,0:T(8,128)S(1)} collective-permute-done((f32[256,256]{1,0:T(8,128)S(1)}, f32[256,256]{1,0:T(8,128)S(1)}, u32[]{:S(2)}, u32[]{:S(2)}) %collective-permute-start.1) | collective-permute-done | bytes 262176 | tf_op jit(solution)/shard_map/ppermute | solution.py:20
  15.0 2.8 %collective-permute-start.2 = (f32[256,256]{1,0:T(8,128)S(1)}, f32[256,256]{1,0:T(8,128)}, u32[]{:S(2)}, u32[]{:S(2)}) collective-permute-start(f32[256,256]{1,0:T(8,128)S(1)} %dynamic-slice_select_fusion.1), channel_id=1, source_target_pairs={{0,16},{4,20},{8,24},{12,28},{16,0},{20,4},{24,8},{28,12},{1,17},{... | collective-permute-start | bytes 786440 | tf_op jit(solution)/shard_map/ppermute | solution.py:20
  18.4 1.6 %collective-permute-start.7 = (f32[128,1024]{1,0:T(8,128)S(1)}, f32[128,1024]{1,0:T(8,128)S(1)}, u32[]{:S(2)}, u32[]{:S(2)}) collective-permute-start(f32[128,1024]{1,0:T(8,128)S(1)} %get-tuple-element.71.own_bottom), channel_id=1, source_target_pairs={{0,1},{1,0},{2,3},{3,2},{4,5},{5,4},{6,7},{7,6},{8,9},{9,8},{10,11... | collective-permute-start | bytes 1572872 | tf_op jit(solution)/shard_map/ppermute | solution.py:20
  20.0 1.5 %collective-permute-start.8 = (f32[128,1024]{1,0:T(8,128)S(1)}, f32[128,1024]{1,0:T(8,128)S(1)}, u32[]{:S(2)}, u32[]{:S(2)}) collective-permute-start(f32[128,1024]{1,0:T(8,128)S(1)} %get-tuple-element.72.own_top), channel_id=1, source_target_pairs={{0,2},{1,3},{2,0},{3,1},{4,6},{5,7},{6,4},{7,5},{8,10},{9,11},{10,... | collective-permute-start | bytes 1572872 | tf_op jit(solution)/shard_map/ppermute | solution.py:20
  21.5 8.4 %collective-permute-done.2 = f32[256,256]{1,0:T(8,128)} collective-permute-done((f32[256,256]{1,0:T(8,128)S(1)}, f32[256,256]{1,0:T(8,128)}, u32[]{:S(2)}, u32[]{:S(2)}) %collective-permute-start.2) | collective-permute-done | bytes 262176 | tf_op jit(solution)/shard_map/ppermute | solution.py:20
  30.6 1.5 %collective-permute-start.12 = (f32[128,1024]{1,0:T(8,128)}, f32[128,1024]{1,0:T(8,128)S(1)}, u32[]{:S(2)}, u32[]{:S(2)}) collective-permute-start(f32[128,1024]{1,0:T(8,128)} %collective-permute-done.3.refs_0_), channel_id=1, source_target_pairs={{0,2},{1,3},{2,0},{3,1},{4,6},{5,7},{6,4},{7,5},{8,10},{9,11},{10,... | collective-permute-start | bytes 1572872 | tf_op jit(solution)/shard_map/ppermute | solution.py:20
  32.1 5.3 %collective-permute-done.5.refs_1_ = f32[256,256]{1,0:T(8,128)S(1)} collective-permute-done((f32[256,256]{1,0:T(8,128)S(1)}, f32[256,256]{1,0:T(8,128)S(1)}, u32[]{:S(2)}, u32[]{:S(2)}) %collective-permute-start.5) | collective-permute-done | bytes 262176 | tf_op jit(solution)/shard_map/ppermute | solution.py:20
  37.5 1.3 collective-permute-start.13
  38.8 1.5 %collective-permute-done.9.refs_3_ = f32[256,256]{1,0:T(8,128)S(1)} collective-permute-done((f32[256,256]{1,0:T(8,128)S(1)}, f32[256,256]{1,0:T(8,128)S(1)}, u32[]{:S(2)}, u32[]{:S(2)}) %collective-permute-start.9) | collective-permute-done | bytes 262176 | tf_op jit(solution)/shard_map/ppermute | solution.py:20
  40.9 4.4 %collective-permute-start.10 = (f32[128,256]{1,0:T(8,128)S(1)}, f32[128,256]{1,0:T(8,128)S(1)}, u32[]{:S(2)}, u32[]{:S(2)}) collective-permute-start(f32[128,256]{1,0:T(8,128)S(1)} %solve.2.refs_0_), channel_id=1, source_target_pairs={{0,16},{4,20},{8,24},{12,28},{16,0},{20,4},{24,8},{28,12},{1,17},{... | collective-permute-start | bytes 393224 | tf_op jit(solution)/shard_map/ppermute | solution.py:20
  45.2 1.7 %collective-permute-start.11 = (f32[128,256]{1,0:T(8,128)S(1)}, f32[128,256]{1,0:T(8,128)S(1)}, u32[]{:S(2)}, u32[]{:S(2)}) collective-permute-start(f32[128,256]{1,0:T(8,128)S(1)} %solve.2.refs_0_), channel_id=1, source_target_pairs={{0,8},{4,12},{8,0},{12,4},{16,24},{20,28},{24,16},{28,20},{1,9},{5... | collective-permute-start | bytes 393224 | tf_op jit(solution)/shard_map/ppermute | solution.py:20
  47.5 2.3 %collective-permute-done.13.refs_5_ = f32[128,1024]{1,0:T(8,128)S(1)} collective-permute-done((f32[128,1024]{1,0:T(8,128)}, f32[128,1024]{1,0:T(8,128)S(1)}, u32[]{:S(2)}, u32[]{:S(2)}) %collective-permute-start.13) | collective-permute-done | bytes 524320 | tf_op jit(solution)/shard_map/ppermute | solution.py:20
  49.8 1.3 %collective-permute-start.20 = (f32[128,1024]{1,0:T(8,128)S(1)}, f32[128,1024]{1,0:T(8,128)S(1)}, u32[]{:S(2)}, u32[]{:S(2)}) collective-permute-start(f32[128,1024]{1,0:T(8,128)S(1)} %get-tuple-element.101.own_bottom), channel_id=1, source_target_pairs={{0,2},{1,3},{2,0},{3,1},{4,6},{5,7},{6,4},{7,5},{8,10},{9,11},{10,... | collective-permute-start | bytes 1572872 | tf_op jit(solution)/shard_map/ppermute | solution.py:20
  51.1 0.8 collective-permute-done.10.refs_2_
  52.0 3.2 %collective-permute-start.14 = (f32[128,256]{1,0:T(8,128)S(1)}, f32[128,256]{1,0:T(8,128)S(1)}, u32[]{:S(2)}, u32[]{:S(2)}) collective-permute-start(f32[128,256]{1,0:T(8,128)S(1)} %collective-permute-done.10.refs_2_), channel_id=1, source_target_pairs={{0,8},{4,12},{8,0},{12,4},{16,24},{20,28},{24,16},{28,20},{1,9},{5... | collective-permute-start | bytes 393224 | tf_op jit(solution)/shard_map/ppermute | solution.py:20
  55.7 1.9 %prepare.2 = (bf16[1024,1024]{1,0:T(8,128)(2,1)S(1)}, bf16[1024,1024]{1,0:T(8,128)(2,1)S(1)}) custom-call(f32[128,1024]{1,0:T(8,128)S(1)} %get-tuple-element.72.own_top, f32[128,1024]{1,0:T(8,128)S(1)} %get-tuple-element.71.own_bottom, f32[128,1024]{1,0:T(8,128)} %collective-permute-done.3.refs_0_, f32[128,1024]{1,0:T(8,128)} %collective-permute-done.4.refs_1_, ...), custom_call_target="tpu_custom_call" | custom-call | bytes 16777216 | tf_op jit(solution)/shard_map/prepare/pallas_call | solution.py:98
  58.2 1.3 %collective-permute-done.18.refs_7_ = f32[128,256]{1,0:T(8,128)S(1)} collective-permute-done((f32[128,256]{1,0:T(8,128)S(1)}, f32[128,256]{1,0:T(8,128)S(1)}, u32[]{:S(2)}, u32[]{:S(2)}) %collective-permute-start.18) | collective-permute-done | bytes 131104 | tf_op jit(solution)/shard_map/ppermute | solution.py:20
  59.5 3.5 %update.2 = (f32[512,256]{1,0:T(8,128)S(1)}, f32[512,256]{1,0:T(8,128)}) custom-call(s32[1,2]{1,0:T(1,128)S(1)} %copy-done.6, s32[8]{0:T(128)S(1)} %copy-done.7, bf16[1024,1024]{1,0:T(8,128)(2,1)S(1)} %get-tuple-element.85.high, bf16[1024,1024]{1,0:T(8,128)(2,1)S(1)} %get-tuple-element.86.low, f32[128,256]{1,0:T(8,128)S(1)} %solve.2.refs_0_, ...), custom_call_target="tpu_custom_call" | custom-call | flops 1610612736 | bytes 7340032 | tf_op jit(solution)/shard_map/update/pallas_call | solution.py:184
  63.1 0.8 copy-done.2
  63.9 0.8 copy-done.4
  64.8 0.7 compare_reduce_fusion.1
  66.1 0.8 collective-permute-done.21
  67.0 0.8 copy-done.9
  67.8 2.1 %collective-permute-start.22 = (f32[256,256]{1,0:T(8,128)S(1)}, f32[256,256]{1,0:T(8,128)}, u32[]{:S(2)}, u32[]{:S(2)}) collective-permute-start(f32[256,256]{1,0:T(8,128)S(1)} %constant_dynamic-slice_fusion), channel_id=1, source_target_pairs={{0,8},{4,12},{8,0},{12,4},{16,24},{20,28},{24,16},{28,20},{1,9},{5... | collective-permute-start | bytes 786440 | tf_op jit(solution)/shard_map/ppermute | solution.py:20
  70.5 6.2 %collective-permute-done.22 = f32[256,256]{1,0:T(8,128)} collective-permute-done((f32[256,256]{1,0:T(8,128)S(1)}, f32[256,256]{1,0:T(8,128)}, u32[]{:S(2)}, u32[]{:S(2)}) %collective-permute-start.22) | collective-permute-done | bytes 262176 | tf_op jit(solution)/shard_map/ppermute | solution.py:20
  76.8 1.0 dynamic-slice_select_fusion
  77.8 5.2 %collective-permute-start.23 = (f32[256,256]{1,0:T(8,128)S(1)}, f32[256,256]{1,0:T(8,128)}, u32[]{:S(2)}, u32[]{:S(2)}) collective-permute-start(f32[256,256]{1,0:T(8,128)S(1)} %dynamic-slice_select_fusion), channel_id=1, source_target_pairs={{0,16},{4,20},{8,24},{12,28},{16,0},{20,4},{24,8},{28,12},{1,17},{... | collective-permute-start | bytes 786440 | tf_op jit(solution)/shard_map/ppermute | solution.py:20
  83.6 1.5 %collective-permute-start.26 = (f32[128,1024]{1,0:T(8,128)S(1)}, f32[128,1024]{1,0:T(8,128)S(1)}, u32[]{:S(2)}, u32[]{:S(2)}) collective-permute-start(f32[128,1024]{1,0:T(8,128)S(1)} %get-tuple-element.101.own_bottom), channel_id=1, source_target_pairs={{0,1},{1,0},{2,3},{3,2},{4,5},{5,4},{6,7},{7,6},{8,9},{9,8},{10,11... | collective-permute-start | bytes 1572872 | tf_op jit(solution)/shard_map/ppermute | solution.py:20
  85.7 9.6 %collective-permute-done.23 = f32[256,256]{1,0:T(8,128)} collective-permute-done((f32[256,256]{1,0:T(8,128)S(1)}, f32[256,256]{1,0:T(8,128)}, u32[]{:S(2)}, u32[]{:S(2)}) %collective-permute-start.23) | collective-permute-done | bytes 262176 | tf_op jit(solution)/shard_map/ppermute | solution.py:20
  95.3 1.0 broadcast_select_fusion.2.refs_0_
  96.3 0.7 collective-permute-start.24
  97.5 6.7 %collective-permute-done.24.refs_1_ = f32[256,256]{1,0:T(8,128)S(1)} collective-permute-done((f32[256,256]{1,0:T(8,128)S(1)}, f32[256,256]{1,0:T(8,128)S(1)}, u32[]{:S(2)}, u32[]{:S(2)}) %collective-permute-start.24) | collective-permute-done | bytes 262176 | tf_op jit(solution)/shard_map/ppermute | solution.py:20
  104.1 1.5 %collective-permute-start.32 = (f32[128,1024]{1,0:T(8,128)}, f32[128,1024]{1,0:T(8,128)S(1)}, u32[]{:S(2)}, u32[]{:S(2)}) collective-permute-start(f32[128,1024]{1,0:T(8,128)} %copy-done.4), channel_id=1, source_target_pairs={{0,1},{1,0},{2,3},{3,2},{4,5},{5,4},{6,7},{7,6},{8,9},{9,8},{10,11... | collective-permute-start | bytes 1572872 | tf_op jit(solution)/shard_map/ppermute | solution.py:20
  105.7 1.5 %collective-permute-done.28.refs_3_ = f32[256,256]{1,0:T(8,128)S(1)} collective-permute-done((f32[256,256]{1,0:T(8,128)S(1)}, f32[256,256]{1,0:T(8,128)S(1)}, u32[]{:S(2)}, u32[]{:S(2)}) %collective-permute-start.28) | collective-permute-done | bytes 262176 | tf_op jit(solution)/shard_map/ppermute | solution.py:20
  107.7 1.9 %collective-permute-start.29 = (f32[128,256]{1,0:T(8,128)S(1)}, f32[128,256]{1,0:T(8,128)S(1)}, u32[]{:S(2)}, u32[]{:S(2)}) collective-permute-start(f32[128,256]{1,0:T(8,128)S(1)} %solve.3.refs_0_), channel_id=1, source_target_pairs={{0,16},{4,20},{8,24},{12,28},{16,0},{20,4},{24,8},{28,12},{1,17},{... | collective-permute-start | bytes 393224 | tf_op jit(solution)/shard_map/ppermute | solution.py:20
  109.6 1.7 %collective-permute-start.30 = (f32[128,256]{1,0:T(8,128)S(1)}, f32[128,256]{1,0:T(8,128)S(1)}, u32[]{:S(2)}, u32[]{:S(2)}) collective-permute-start(f32[128,256]{1,0:T(8,128)S(1)} %solve.3.refs_0_), channel_id=1, source_target_pairs={{0,8},{4,12},{8,0},{12,4},{16,24},{20,28},{24,16},{28,20},{1,9},{5... | collective-permute-start | bytes 393224 | tf_op jit(solution)/shard_map/ppermute | solution.py:20
  111.4 5.5 %collective-permute-done.32.refs_5_ = f32[128,1024]{1,0:T(8,128)S(1)} collective-permute-done((f32[128,1024]{1,0:T(8,128)}, f32[128,1024]{1,0:T(8,128)S(1)}, u32[]{:S(2)}, u32[]{:S(2)}) %collective-permute-start.32) | collective-permute-done | bytes 524320 | tf_op jit(solution)/shard_map/ppermute | solution.py:20
  117.1 1.3 %collective-permute-start.33 = (f32[128,256]{1,0:T(8,128)S(1)}, f32[128,256]{1,0:T(8,128)S(1)}, u32[]{:S(2)}, u32[]{:S(2)}) collective-permute-start(f32[128,256]{1,0:T(8,128)S(1)} %collective-permute-done.29.refs_2_), channel_id=1, source_target_pairs={{0,8},{4,12},{8,0},{12,4},{16,24},{20,28},{24,16},{28,20},{1,9},{5... | collective-permute-start | bytes 393224 | tf_op jit(solution)/shard_map/ppermute | solution.py:20
  118.9 1.1 prepare.3
  120.0 2.1 %collective-permute-done.33.refs_3_ = f32[128,256]{1,0:T(8,128)S(1)} collective-permute-done((f32[128,256]{1,0:T(8,128)S(1)}, f32[128,256]{1,0:T(8,128)S(1)}, u32[]{:S(2)}, u32[]{:S(2)}) %collective-permute-start.33) | collective-permute-done | bytes 131104 | tf_op jit(solution)/shard_map/ppermute | solution.py:20
  122.1 1.3 %collective-permute-done.37.refs_7_ = f32[128,256]{1,0:T(8,128)S(1)} collective-permute-done((f32[128,256]{1,0:T(8,128)S(1)}, f32[128,256]{1,0:T(8,128)S(1)}, u32[]{:S(2)}, u32[]{:S(2)}) %collective-permute-start.37) | collective-permute-done | bytes 131104 | tf_op jit(solution)/shard_map/ppermute | solution.py:20
  123.4 3.9 %update.3 = f32[1024,256]{1,0:T(8,128)} custom-call(s32[1,2]{1,0:T(1,128)S(1)} %copy-done.6, s32[8]{0:T(128)S(1)} %copy-done.7, bf16[1024,1024]{1,0:T(8,128)(2,1)S(1)} %get-tuple-element.115.high, bf16[1024,1024]{1,0:T(8,128)(2,1)S(1)} %get-tuple-element.116.low, f32[128,256]{1,0:T(8,128)S(1)} %solve.3.refs_0_, ...), custom_call_target="tpu_custom_call" | custom-call | flops 1610612736 | bytes 7340032 | tf_op jit(solution)/shard_map/update/pallas_call | solution.py:184
  (66 shorter events, 6.1 us)
Async XLA Ops:
  1.1 3.0 %collective-permute-start = (f32[512,256]{1,0:T(8,128)S(1)}, f32[512,256]{1,0:T(8,128)S(1)}, u32[]{:S(2)}, u32[]{:S(2)}) collective-permute-start(f32[512,256]{1,0:T(8,128)S(1)} %dynamic-slice_bitcast_fusion), channel_id=1, source_target_pairs={{0,4},{4,0},{8,12},{12,8},{16,20},{20,16},{24,28},{28,24},{1,5},{5... | collective-permute-start | bytes 1572872 | tf_op jit(solution)/shard_map/ppermute | solution.py:20
  4.1 4.0 %copy-start.8 = (f32[1,2,256,1024]{3,2,1,0:T(8,128)S(1)}, f32[1,2,256,1024]{3,2,1,0:T(8,128)}, u32[]{:S(2)}) copy-start(f32[1,2,256,1024]{3,2,1,0:T(8,128)} %param.6) | copy-start | bytes 6291460
  5.4 35.0 %copy-start = (f32[2,128,1024]{2,1,0:T(8,128)S(1)}, f32[2,128,1024]{2,1,0:T(8,128)}, u32[]{:S(2)}) copy-start(f32[2,128,1024]{2,1,0:T(8,128)} %inverse.3) | copy-start | bytes 3145732
  5.4 9.6 %collective-permute-start.1 = (f32[256,256]{1,0:T(8,128)S(1)}, f32[256,256]{1,0:T(8,128)S(1)}, u32[]{:S(2)}, u32[]{:S(2)}) collective-permute-start(f32[256,256]{1,0:T(8,128)S(1)} %constant_dynamic-slice_fusion.1), channel_id=1, source_target_pairs={{0,8},{4,12},{8,0},{12,4},{16,24},{20,28},{24,16},{28,20},{1,9},{5... | collective-permute-start | bytes 786440 | tf_op jit(solution)/shard_map/ppermute | solution.py:20
  8.2 21.8 %collective-permute-start.3 = (f32[128,1024]{1,0:T(8,128)S(1)}, f32[128,1024]{1,0:T(8,128)}, u32[]{:S(2)}, u32[]{:S(2)}) collective-permute-start(f32[128,1024]{1,0:T(8,128)S(1)} %get-tuple-element.72.own_top), channel_id=1, source_target_pairs={{0,1},{1,0},{2,3},{3,2},{4,5},{5,4},{6,7},{7,6},{8,9},{9,8},{10,11... | collective-permute-start | bytes 1572872 | tf_op jit(solution)/shard_map/ppermute | solution.py:20
  9.8 20.3 %collective-permute-start.4 = (f32[128,1024]{1,0:T(8,128)S(1)}, f32[128,1024]{1,0:T(8,128)}, u32[]{:S(2)}, u32[]{:S(2)}) collective-permute-start(f32[128,1024]{1,0:T(8,128)S(1)} %get-tuple-element.71.own_bottom), channel_id=1, source_target_pairs={{0,2},{1,3},{2,0},{3,1},{4,6},{5,7},{6,4},{7,5},{8,10},{9,11},{10,... | collective-permute-start | bytes 1572872 | tf_op jit(solution)/shard_map/ppermute | solution.py:20
  15.0 14.9 %collective-permute-start.2 = (f32[256,256]{1,0:T(8,128)S(1)}, f32[256,256]{1,0:T(8,128)}, u32[]{:S(2)}, u32[]{:S(2)}) collective-permute-start(f32[256,256]{1,0:T(8,128)S(1)} %dynamic-slice_select_fusion.1), channel_id=1, source_target_pairs={{0,16},{4,20},{8,24},{12,28},{16,0},{20,4},{24,8},{28,12},{1,17},{... | collective-permute-start | bytes 786440 | tf_op jit(solution)/shard_map/ppermute | solution.py:20
  18.4 20.3 %collective-permute-start.7 = (f32[128,1024]{1,0:T(8,128)S(1)}, f32[128,1024]{1,0:T(8,128)S(1)}, u32[]{:S(2)}, u32[]{:S(2)}) collective-permute-start(f32[128,1024]{1,0:T(8,128)S(1)} %get-tuple-element.71.own_bottom), channel_id=1, source_target_pairs={{0,1},{1,0},{2,3},{3,2},{4,5},{5,4},{6,7},{7,6},{8,9},{9,8},{10,11... | collective-permute-start | bytes 1572872 | tf_op jit(solution)/shard_map/ppermute | solution.py:20
  20.0 18.7 %collective-permute-start.8 = (f32[128,1024]{1,0:T(8,128)S(1)}, f32[128,1024]{1,0:T(8,128)S(1)}, u32[]{:S(2)}, u32[]{:S(2)}) collective-permute-start(f32[128,1024]{1,0:T(8,128)S(1)} %get-tuple-element.72.own_top), channel_id=1, source_target_pairs={{0,2},{1,3},{2,0},{3,1},{4,6},{5,7},{6,4},{7,5},{8,10},{9,11},{10,... | collective-permute-start | bytes 1572872 | tf_op jit(solution)/shard_map/ppermute | solution.py:20
  30.0 7.4 %collective-permute-start.5 = (f32[256,256]{1,0:T(8,128)S(1)}, f32[256,256]{1,0:T(8,128)S(1)}, u32[]{:S(2)}, u32[]{:S(2)}) collective-permute-start(f32[256,256]{1,0:T(8,128)S(1)} %broadcast_select_fusion.1.refs_0_), channel_id=1, source_target_pairs={{0,8},{4,12},{8,0},{12,4},{16,24},{20,28},{24,16},{28,20},{1,9},{5... | collective-permute-start | bytes 786440 | tf_op jit(solution)/shard_map/ppermute | solution.py:20
  30.6 8.1 %collective-permute-start.6 = (f32[256,256]{1,0:T(8,128)S(1)}, f32[256,256]{1,0:T(8,128)S(1)}, u32[]{:S(2)}, u32[]{:S(2)}) collective-permute-start(f32[256,256]{1,0:T(8,128)S(1)} %broadcast_select_fusion.1.refs_0_), channel_id=1, source_target_pairs={{0,4},{4,0},{8,12},{12,8},{16,20},{20,16},{24,28},{28,24},{1,5},{5... | collective-permute-start | bytes 786440 | tf_op jit(solution)/shard_map/ppermute | solution.py:20
  30.6 16.4 %collective-permute-start.12 = (f32[128,1024]{1,0:T(8,128)}, f32[128,1024]{1,0:T(8,128)S(1)}, u32[]{:S(2)}, u32[]{:S(2)}) collective-permute-start(f32[128,1024]{1,0:T(8,128)} %collective-permute-done.3.refs_0_), channel_id=1, source_target_pairs={{0,2},{1,3},{2,0},{3,1},{4,6},{5,7},{6,4},{7,5},{8,10},{9,11},{10,... | collective-permute-start | bytes 1572872 | tf_op jit(solution)/shard_map/ppermute | solution.py:20
  37.5 12.3 %collective-permute-start.13 = (f32[128,1024]{1,0:T(8,128)}, f32[128,1024]{1,0:T(8,128)S(1)}, u32[]{:S(2)}, u32[]{:S(2)}) collective-permute-start(f32[128,1024]{1,0:T(8,128)} %collective-permute-done.4.refs_1_), channel_id=1, source_target_pairs={{0,1},{1,0},{2,3},{3,2},{4,5},{5,4},{6,7},{7,6},{8,9},{9,8},{10,11... | collective-permute-start | bytes 1572872 | tf_op jit(solution)/shard_map/ppermute | solution.py:20
  38.7 1.6 %collective-permute-start.9 = (f32[256,256]{1,0:T(8,128)S(1)}, f32[256,256]{1,0:T(8,128)S(1)}, u32[]{:S(2)}, u32[]{:S(2)}) collective-permute-start(f32[256,256]{1,0:T(8,128)S(1)} %collective-permute-done.5.refs_1_), channel_id=1, source_target_pairs={{0,4},{4,0},{8,12},{12,8},{16,20},{20,16},{24,28},{28,24},{1,5},{5... | collective-permute-start | bytes 786440 | tf_op jit(solution)/shard_map/ppermute | solution.py:20
  40.8 18.7 %copy-start.1 = (f32[1,1024,256]{2,1,0:T(8,128)S(1)}, f32[1,1024,256]{2,1,0:T(8,128)}, u32[]{:S(2)}) copy-start(f32[1,1024,256]{2,1,0:T(8,128)} %refs_8_.1) | copy-start | bytes 3145732
  40.8 18.7 %copy-start.6 = (s32[1,2]{1,0:T(1,128)S(1)}, s32[1,2]{1,0:T(1,128)}, u32[]{:S(2)}) copy-start(s32[1,2]{1,0:T(1,128)} %flags.3) | copy-start | bytes 28
  40.9 18.7 %copy-start.7 = (s32[8]{0:T(128)S(1)}, s32[8]{0:T(128)}, u32[]{:S(2)}) copy-start(s32[8]{0:T(128)} %slot_block.3) | copy-start | bytes 100
  40.9 11.1 %collective-permute-start.10 = (f32[128,256]{1,0:T(8,128)S(1)}, f32[128,256]{1,0:T(8,128)S(1)}, u32[]{:S(2)}, u32[]{:S(2)}) collective-permute-start(f32[128,256]{1,0:T(8,128)S(1)} %solve.2.refs_0_), channel_id=1, source_target_pairs={{0,16},{4,20},{8,24},{12,28},{16,0},{20,4},{24,8},{28,12},{1,17},{... | collective-permute-start | bytes 393224 | tf_op jit(solution)/shard_map/ppermute | solution.py:20
  45.2 6.8 %collective-permute-start.11 = (f32[128,256]{1,0:T(8,128)S(1)}, f32[128,256]{1,0:T(8,128)S(1)}, u32[]{:S(2)}, u32[]{:S(2)}) collective-permute-start(f32[128,256]{1,0:T(8,128)S(1)} %solve.2.refs_0_), channel_id=1, source_target_pairs={{0,8},{4,12},{8,0},{12,4},{16,24},{20,28},{24,16},{28,20},{1,9},{5... | collective-permute-start | bytes 393224 | tf_op jit(solution)/shard_map/ppermute | solution.py:20
  47.0 8.3 %collective-permute-start.15 = (f32[128,256]{1,0:T(8,128)S(1)}, f32[128,256]{1,0:T(8,128)S(1)}, u32[]{:S(2)}, u32[]{:S(2)}) collective-permute-start(f32[128,256]{1,0:T(8,128)S(1)} %solve.2.refs_0_), channel_id=1, source_target_pairs={{0,4},{4,0},{8,12},{12,8},{16,20},{20,16},{24,28},{28,24},{1,5},{5... | collective-permute-start | bytes 393224 | tf_op jit(solution)/shard_map/ppermute | solution.py:20
  47.0 16.1 %collective-permute-start.19 = (f32[128,1024]{1,0:T(8,128)S(1)}, f32[128,1024]{1,0:T(8,128)S(1)}, u32[]{:S(2)}, u32[]{:S(2)}) collective-permute-start(f32[128,1024]{1,0:T(8,128)S(1)} %get-tuple-element.102.own_top), channel_id=1, source_target_pairs={{0,1},{1,0},{2,3},{3,2},{4,5},{5,4},{6,7},{7,6},{8,9},{9,8},{10,11... | collective-permute-start | bytes 1572872 | tf_op jit(solution)/shard_map/ppermute | solution.py:20
  49.8 13.3 %collective-permute-start.20 = (f32[128,1024]{1,0:T(8,128)S(1)}, f32[128,1024]{1,0:T(8,128)S(1)}, u32[]{:S(2)}, u32[]{:S(2)}) collective-permute-start(f32[128,1024]{1,0:T(8,128)S(1)} %get-tuple-element.101.own_bottom), channel_id=1, source_target_pairs={{0,2},{1,3},{2,0},{3,1},{4,6},{5,7},{6,4},{7,5},{8,10},{9,11},{10,... | collective-permute-start | bytes 1572872 | tf_op jit(solution)/shard_map/ppermute | solution.py:20
  52.0 6.1 %collective-permute-start.14 = (f32[128,256]{1,0:T(8,128)S(1)}, f32[128,256]{1,0:T(8,128)S(1)}, u32[]{:S(2)}, u32[]{:S(2)}) collective-permute-start(f32[128,256]{1,0:T(8,128)S(1)} %collective-permute-done.10.refs_2_), channel_id=1, source_target_pairs={{0,8},{4,12},{8,0},{12,4},{16,24},{20,28},{24,16},{28,20},{1,9},{5... | collective-permute-start | bytes 393224 | tf_op jit(solution)/shard_map/ppermute | solution.py:20
  55.2 2.9 %collective-permute-start.16 = (f32[128,256]{1,0:T(8,128)S(1)}, f32[128,256]{1,0:T(8,128)S(1)}, u32[]{:S(2)}, u32[]{:S(2)}) collective-permute-start(f32[128,256]{1,0:T(8,128)S(1)} %collective-permute-done.11.refs_1_), channel_id=1, source_target_pairs={{0,4},{4,0},{8,12},{12,8},{16,20},{20,16},{24,28},{28,24},{1,5},{5... | collective-permute-start | bytes 393224 | tf_op jit(solution)/shard_map/ppermute | solution.py:20
  55.2 2.9 %collective-permute-start.17 = (f32[128,256]{1,0:T(8,128)S(1)}, f32[128,256]{1,0:T(8,128)S(1)}, u32[]{:S(2)}, u32[]{:S(2)}) collective-permute-start(f32[128,256]{1,0:T(8,128)S(1)} %collective-permute-done.10.refs_2_), channel_id=1, source_target_pairs={{0,4},{4,0},{8,12},{12,8},{16,20},{20,16},{24,28},{28,24},{1,5},{5... | collective-permute-start | bytes 393224 | tf_op jit(solution)/shard_map/ppermute | solution.py:20
  58.2 1.4 %collective-permute-start.18 = (f32[128,256]{1,0:T(8,128)S(1)}, f32[128,256]{1,0:T(8,128)S(1)}, u32[]{:S(2)}, u32[]{:S(2)}) collective-permute-start(f32[128,256]{1,0:T(8,128)S(1)} %collective-permute-done.14.refs_3_), channel_id=1, source_target_pairs={{0,4},{4,0},{8,12},{12,8},{16,20},{20,16},{24,28},{28,24},{1,5},{5... | collective-permute-start | bytes 393224 | tf_op jit(solution)/shard_map/ppermute | solution.py:20
  63.1 0.8 copy-start.2
  63.9 0.8 copy-start.4
  64.7 32.3 %copy-start.3 = (f32[128,1024]{1,0:T(8,128)S(1)}, f32[128,1024]{1,0:T(8,128)}, u32[]{:S(2)}) copy-start(f32[128,1024]{1,0:T(8,128)} %copy-done.2) | copy-start | bytes 1572868
  64.7 2.3 %collective-permute-start.21 = (f32[512,256]{1,0:T(8,128)}, f32[512,256]{1,0:T(8,128)}, u32[]{:S(2)}, u32[]{:S(2)}) collective-permute-start(f32[512,256]{1,0:T(8,128)} %get-tuple-element.96.refs_9_), channel_id=1, source_target_pairs={{0,4},{4,0},{8,12},{12,8},{16,20},{20,16},{24,28},{28,24},{1,5},{5... | collective-permute-start | bytes 1572872 | tf_op jit(solution)/shard_map/ppermute | solution.py:20
  67.0 0.8 copy-start.9
  67.8 8.9 %collective-permute-start.22 = (f32[256,256]{1,0:T(8,128)S(1)}, f32[256,256]{1,0:T(8,128)}, u32[]{:S(2)}, u32[]{:S(2)}) collective-permute-start(f32[256,256]{1,0:T(8,128)S(1)} %constant_dynamic-slice_fusion), channel_id=1, source_target_pairs={{0,8},{4,12},{8,0},{12,4},{16,24},{20,28},{24,16},{28,20},{1,9},{5... | collective-permute-start | bytes 786440 | tf_op jit(solution)/shard_map/ppermute | solution.py:20
  77.8 17.5 %collective-permute-start.23 = (f32[256,256]{1,0:T(8,128)S(1)}, f32[256,256]{1,0:T(8,128)}, u32[]{:S(2)}, u32[]{:S(2)}) collective-permute-start(f32[256,256]{1,0:T(8,128)S(1)} %dynamic-slice_select_fusion), channel_id=1, source_target_pairs={{0,16},{4,20},{8,24},{12,28},{16,0},{20,4},{24,8},{28,12},{1,17},{... | collective-permute-start | bytes 786440 | tf_op jit(solution)/shard_map/ppermute | solution.py:20
  83.6 35.4 %copy-start.5 = (f32[128,1024]{1,0:T(8,128)S(1)}, f32[128,1024]{1,0:T(8,128)}, u32[]{:S(2)}) copy-start(f32[128,1024]{1,0:T(8,128)} %copy-done.4) | copy-start | bytes 1572868
  83.6 22.0 %collective-permute-start.26 = (f32[128,1024]{1,0:T(8,128)S(1)}, f32[128,1024]{1,0:T(8,128)S(1)}, u32[]{:S(2)}, u32[]{:S(2)}) collective-permute-start(f32[128,1024]{1,0:T(8,128)S(1)} %get-tuple-element.101.own_bottom), channel_id=1, source_target_pairs={{0,1},{1,0},{2,3},{3,2},{4,5},{5,4},{6,7},{7,6},{8,9},{9,8},{10,11... | collective-permute-start | bytes 1572872 | tf_op jit(solution)/shard_map/ppermute | solution.py:20
  85.1 20.5 %collective-permute-start.27 = (f32[128,1024]{1,0:T(8,128)S(1)}, f32[128,1024]{1,0:T(8,128)S(1)}, u32[]{:S(2)}, u32[]{:S(2)}) collective-permute-start(f32[128,1024]{1,0:T(8,128)S(1)} %get-tuple-element.102.own_top), channel_id=1, source_target_pairs={{0,2},{1,3},{2,0},{3,1},{4,6},{5,7},{6,4},{7,5},{8,10},{9,11},{10,... | collective-permute-start | bytes 1572872 | tf_op jit(solution)/shard_map/ppermute | solution.py:20
  96.3 7.9 %collective-permute-start.24 = (f32[256,256]{1,0:T(8,128)S(1)}, f32[256,256]{1,0:T(8,128)S(1)}, u32[]{:S(2)}, u32[]{:S(2)}) collective-permute-start(f32[256,256]{1,0:T(8,128)S(1)} %broadcast_select_fusion.2.refs_0_), channel_id=1, source_target_pairs={{0,8},{4,12},{8,0},{12,4},{16,24},{20,28},{24,16},{28,20},{1,9},{5... | collective-permute-start | bytes 786440 | tf_op jit(solution)/shard_map/ppermute | solution.py:20
  96.9 8.7 %collective-permute-start.25 = (f32[256,256]{1,0:T(8,128)S(1)}, f32[256,256]{1,0:T(8,128)S(1)}, u32[]{:S(2)}, u32[]{:S(2)}) collective-permute-start(f32[256,256]{1,0:T(8,128)S(1)} %broadcast_select_fusion.2.refs_0_), channel_id=1, source_target_pairs={{0,4},{4,0},{8,12},{12,8},{16,20},{20,16},{24,28},{28,24},{1,5},{5... | collective-permute-start | bytes 786440 | tf_op jit(solution)/shard_map/ppermute | solution.py:20
  97.0 14.4 %collective-permute-start.31 = (f32[128,1024]{1,0:T(8,128)S(1)}, f32[128,1024]{1,0:T(8,128)S(1)}, u32[]{:S(2)}, u32[]{:S(2)}) collective-permute-start(f32[128,1024]{1,0:T(8,128)S(1)} %copy-done.3), channel_id=1, source_target_pairs={{0,2},{1,3},{2,0},{3,1},{4,6},{5,7},{6,4},{7,5},{8,10},{9,11},{10,... | collective-permute-start | bytes 1572872 | tf_op jit(solution)/shard_map/ppermute | solution.py:20
  104.1 12.7 %collective-permute-start.32 = (f32[128,1024]{1,0:T(8,128)}, f32[128,1024]{1,0:T(8,128)S(1)}, u32[]{:S(2)}, u32[]{:S(2)}) collective-permute-start(f32[128,1024]{1,0:T(8,128)} %copy-done.4), channel_id=1, source_target_pairs={{0,1},{1,0},{2,3},{3,2},{4,5},{5,4},{6,7},{7,6},{8,9},{9,8},{10,11... | collective-permute-start | bytes 1572872 | tf_op jit(solution)/shard_map/ppermute | solution.py:20
  105.6 1.6 %collective-permute-start.28 = (f32[256,256]{1,0:T(8,128)S(1)}, f32[256,256]{1,0:T(8,128)S(1)}, u32[]{:S(2)}, u32[]{:S(2)}) collective-permute-start(f32[256,256]{1,0:T(8,128)S(1)} %collective-permute-done.24.refs_1_), channel_id=1, source_target_pairs={{0,4},{4,0},{8,12},{12,8},{16,20},{20,16},{24,28},{28,24},{1,5},{5... | collective-permute-start | bytes 786440 | tf_op jit(solution)/shard_map/ppermute | solution.py:20
  107.7 9.4 %collective-permute-start.29 = (f32[128,256]{1,0:T(8,128)S(1)}, f32[128,256]{1,0:T(8,128)S(1)}, u32[]{:S(2)}, u32[]{:S(2)}) collective-permute-start(f32[128,256]{1,0:T(8,128)S(1)} %solve.3.refs_0_), channel_id=1, source_target_pairs={{0,16},{4,20},{8,24},{12,28},{16,0},{20,4},{24,8},{28,12},{1,17},{... | collective-permute-start | bytes 393224 | tf_op jit(solution)/shard_map/ppermute | solution.py:20
  109.6 7.5 %collective-permute-start.30 = (f32[128,256]{1,0:T(8,128)S(1)}, f32[128,256]{1,0:T(8,128)S(1)}, u32[]{:S(2)}, u32[]{:S(2)}) collective-permute-start(f32[128,256]{1,0:T(8,128)S(1)} %solve.3.refs_0_), channel_id=1, source_target_pairs={{0,8},{4,12},{8,0},{12,4},{16,24},{20,28},{24,16},{28,20},{1,9},{5... | collective-permute-start | bytes 393224 | tf_op jit(solution)/shard_map/ppermute | solution.py:20
  111.4 8.7 %collective-permute-start.34 = (f32[128,256]{1,0:T(8,128)S(1)}, f32[128,256]{1,0:T(8,128)S(1)}, u32[]{:S(2)}, u32[]{:S(2)}) collective-permute-start(f32[128,256]{1,0:T(8,128)S(1)} %solve.3.refs_0_), channel_id=1, source_target_pairs={{0,4},{4,0},{8,12},{12,8},{16,20},{20,16},{24,28},{28,24},{1,5},{5... | collective-permute-start | bytes 393224 | tf_op jit(solution)/shard_map/ppermute | solution.py:20
  117.1 5.0 %collective-permute-start.33 = (f32[128,256]{1,0:T(8,128)S(1)}, f32[128,256]{1,0:T(8,128)S(1)}, u32[]{:S(2)}, u32[]{:S(2)}) collective-permute-start(f32[128,256]{1,0:T(8,128)S(1)} %collective-permute-done.29.refs_2_), channel_id=1, source_target_pairs={{0,8},{4,12},{8,0},{12,4},{16,24},{20,28},{24,16},{28,20},{1,9},{5... | collective-permute-start | bytes 393224 | tf_op jit(solution)/shard_map/ppermute | solution.py:20
  118.4 3.7 %collective-permute-start.35 = (f32[128,256]{1,0:T(8,128)S(1)}, f32[128,256]{1,0:T(8,128)S(1)}, u32[]{:S(2)}, u32[]{:S(2)}) collective-permute-start(f32[128,256]{1,0:T(8,128)S(1)} %collective-permute-done.30.refs_1_), channel_id=1, source_target_pairs={{0,4},{4,0},{8,12},{12,8},{16,20},{20,16},{24,28},{28,24},{1,5},{5... | collective-permute-start | bytes 393224 | tf_op jit(solution)/shard_map/ppermute | solution.py:20
  118.4 3.7 %collective-permute-start.36 = (f32[128,256]{1,0:T(8,128)S(1)}, f32[128,256]{1,0:T(8,128)S(1)}, u32[]{:S(2)}, u32[]{:S(2)}) collective-permute-start(f32[128,256]{1,0:T(8,128)S(1)} %collective-permute-done.29.refs_2_), channel_id=1, source_target_pairs={{0,4},{4,0},{8,12},{12,8},{16,20},{20,16},{24,28},{28,24},{1,5},{5... | collective-permute-start | bytes 393224 | tf_op jit(solution)/shard_map/ppermute | solution.py:20
  122.1 1.4 %collective-permute-start.37 = (f32[128,256]{1,0:T(8,128)S(1)}, f32[128,256]{1,0:T(8,128)S(1)}, u32[]{:S(2)}, u32[]{:S(2)}) collective-permute-start(f32[128,256]{1,0:T(8,128)S(1)} %collective-permute-done.33.refs_3_), channel_id=1, source_target_pairs={{0,4},{4,0},{8,12},{12,8},{16,20},{20,16},{24,28},{28,24},{1,5},{5... | collective-permute-start | bytes 393224 | tf_op jit(solution)/shard_map/ppermute | solution.py:20

commit v3 on v2

--- a/solution.py
+++ b/solution.py
@@ -59,14 +59,14 @@
     return dot(a[0], b[0]) + (dot(a[0], b[1]) + dot(a[1], b[0]))
 
 
-def prepare_body(own_top, own_bottom, *refs):
+def prepare_body(step, own, *refs):
     pieces, (high, low, slots, sems) = refs[:6], refs[6:]
     side = lax.axis_index("col")
     half = pieces[0].shape[0]
-    sources = [(own_top, side * 2), (own_bottom, side * 2 + 1)]
+    sources = [(own.at[0, step], side * 2)]
     for ref, (distance, part) in zip(pieces, ((1, 0), (2, 1), (1, 1), (2, 0), (3, 0), (3, 1))):
         sources.append((ref, (side ^ distance) * 2 + part))
-    groups = [sources[start:start + 2] for start in range(0, 8, 2)]
+    groups = [sources[0:1], sources[1:3], sources[3:5], sources[5:7]]
 
     def fetch(index):
         copies = []
@@ -92,19 +92,19 @@
             flying.append(fetch(index + 2))
 
 
-def prepare(pieces):
-    half, depth = pieces[0].shape
+def prepare(panel, step, pieces):
+    depth = panel.shape[3]
     vmem, anywhere = pl.BlockSpec(memory_space=pltpu.VMEM), pl.BlockSpec(memory_space=pl.ANY)
     return pl.pallas_call(
-        prepare_body,
+        functools.partial(prepare_body, step),
         out_shape=[jax.ShapeDtypeStruct((depth, depth), jnp.bfloat16)] * 2,
-        in_specs=[anywhere] * 8,
+        in_specs=[anywhere] * 7,
         out_specs=[vmem] * 2,
-        scratch_shapes=[pltpu.VMEM((2, 2 * half, depth), jnp.float32), pltpu.SemaphoreType.DMA((2, 2))],
+        scratch_shapes=[pltpu.VMEM((2, panel.shape[2], depth), jnp.float32), pltpu.SemaphoreType.DMA((2, 2))],
         compiler_params=pltpu.CompilerParams(vmem_limit_bytes=PREPARE_BYTES),
         cost_estimate=pl.CostEstimate(flops=0, bytes_accessed=16 * depth * depth, transcendentals=0),
         name="prepare",
-    )(*pieces)
+    )(panel, *pieces)
 
 
 def assemble(x, blocks, rank):
@@ -168,7 +168,7 @@
         out_specs=vmem,
         scratch_shapes=[pltpu.VMEM((depth, cols), jnp.float32)],
         compiler_params=pltpu.CompilerParams(vmem_limit_bytes=UPDATE_BYTES),
-        cost_estimate=pl.CostEstimate(flops=6 * rows * depth * cols, bytes_accessed=4 * (rows * depth + depth * cols), transcendentals=0),
+        cost_estimate=pl.CostEstimate(flops=2 * rows * depth * cols, bytes_accessed=4 * rows * cols, transcendentals=0),
         name="solve",
     )(inverse, *quarters)
 
@@ -229,37 +229,40 @@
     def far(one, two):
         return [swap(one, "col", 1, cols), swap(two, "col", 0, cols)]
 
-    def solved(step, y, block, first, owner):
+    def block_halves(panel, step):
+        return panel[0, step, :half], panel[0, step, half:]
+
+    def solved(step, y, panel, owner):
+        y, panel = tie(y, panel)
+        first = near(*block_halves(panel, step))
         y = scatter_step(y, 1, rows, owner, rank)
-        y, top, bottom = tie(y, *block)
+        y, panel = tie(y, panel)
+        top, bottom = block_halves(panel, step)
         second = near(bottom, top)
         y = cross_step(y, 2, rows, owner, rank)
         y, *first = tie(y, *first)
         pieces = far(*first)
-        other = swap(y, "row", 0, rows)
         beside = swap(y, "row", 1, rows)
-        beside, other, *second = tie(beside, other, *second)
-        last = swap(beside, "row", 0, rows)
+        beside, y, *second = tie(beside, y, *second)
+        other, last = swap(y, "row", 0, rows), swap(beside, "row", 0, rows)
         x = solve(step, diag_inverse, [y, beside, other, last])
         x2, x1 = swap(x, "row", 2, rows), swap(x, "row", 1, rows)
         x2, x1, *pieces = tie(x2, x1, *pieces)
-        high, low = prepare([*block, *first, *second, *pieces])
+        high, low = prepare(panel, step, [*first, *second, *pieces])
         x3 = swap(x2, "row", 1, rows)
-        across = [swap(part, "row", 0, rows) for part in (x, x1, x2)]
+        across = [swap(block, "row", 0, rows) for block in (x, x1, x2)]
         x3, high, low, *across = tie(x3, high, low, *across)
         return [x, x1, x2, x3, *across, swap(x3, "row", 0, rows)], (high, low)
 
-    y = scatter_step(rhs[0], 0, rows, owner, rank)
-    y, panel = tie(y, panel)
-    cut = [panel[0, step, start:start + half] for step in range(2) for start in (0, half)]
-    cut = lax.optimization_barrier(cut)
-    blocks, pair = solved(0, y, cut[:2], near(*cut[:2]), owner)
-    first = near(*cut[2:])
+    keep, send = halves(rhs[0], core)
+    got = swap(send, "row", 0, rows)
+    keep, send = tie(keep, send)
+    y = jnp.where(bit(owner, 0) == core, keep, got)
+    blocks, pair = solved(0, y, panel, owner)
     keep, send = update(0, flags, slot_block, pair, blocks, [rhs])
-    keep, send, *first = tie(keep, send, *first)
     got = swap(send, "row", 0, rows)
     y = jnp.where(bit(second, 0) == core, keep, got)
-    blocks, pair = solved(1, y, cut[2:], first, second)
+    blocks, pair = solved(1, y, panel, second)
     (result,) = update(1, flags, slot_block, pair, blocks, [keep, send])
     return result[None]
 

time: 128 us -> 117 us (0.914)
  waiting for transfers between devices: 58.1 us -> 44.6 us
  local copies, waits for them, and re-layouts: 3.69 us -> 7.48 us
  other arithmetic: 5.36 us -> 3.63 us
    ppermute x38, waiting for transfers between devices: 58.1 us -> 44.6 us  [swap(): return lax.ppermute(x, axis, [(i, i ^ 1 << b) for i in range(size)])]
    squeeze x1 -> x4, local copies, waits for them, and re-layouts: 0.14 us -> 4.38 us  [block_halves(): return (panel[0, step, :half], panel[0, step, half:])]
    select_n x3 -> x2, other arithmetic: 2.28 us -> 0.07 us  [scatter_step(): return jnp.where(bit(owner, b) == mine, keep, swap(send, 'row', b, size))]
    unnamed x20 -> x14, local copies, waits for them, and re-layouts: 2.43 us -> 0.84 us
  transfers between devices with their start and end apart: 38 -> 38, of which waited for: 18 -> 22; matrix products, arithmetic and copies ran while one was open for 2% -> 6% of each run, Pallas kernels for 6% -> 4%
where the time goes in v3:
time: 117 us
  starting transfers between devices  45.2 us (39%)
  waiting for transfers between devices  44.6 us (38%)
  Pallas kernels  12.4 us (11%)
  local copies, waits for them, and re-layouts  7.48 us (6%)
  between operations  3.64 us (3%)
  other arithmetic  3.63 us (3%)
    ppermute x38, starting transfers between devices, swap(): return lax.ppermute(x, axis, [(i, i ^ 1 << b) for i in range(size)])  45.2 us
    ppermute x38, waiting for transfers between devices, swap(): return lax.ppermute(x, axis, [(i, i ^ 1 << b) for i in range(size)])  44.6 us
    pallas_call x2, Pallas kernels, update(): pl.pallas_call(first_body if step == 0 else second_body, out_shape=[jax.S...  7.38 us
    squeeze x4, local copies, waits for them, and re-layouts, block_halves(): return (panel[0, step, :half], panel[0, step, half:])  4.38 us
    pallas_call x2, Pallas kernels, prepare(): pl.pallas_call(functools.partial(prepare_body, step), out_shape=[jax.Shap...  4.03 us
  transfers between devices with their start and end apart: 38, of which 22 were waited for; matrix products, arithmetic and copies ran while one was open for 6% of the time, Pallas kernels for 4%

profile of v3, /device:TPU:0, one launch (start us, length us, event | category | flops | bytes accessed | tf_op | source)
XLA Modules:
  0.0 116.9 jit_solution(13117196563539425747)
XLA Ops:
  0.0 2.2 %dynamic-slice_bitcast_fusion = (f32[512,256]{1,0:T(8,128)}, f32[512,256]{1,0:T(8,128)S(1)}) fusion(f32[1,1024,256]{2,1,0:T(8,128)} %refs_8_.1, s32[]{:T(128)S(6)} %select_n.67, s32[]{:T(128)S(6)} %select_n.66), kind=kLoop, calls=%fused_computation.8 | loop fusion | bytes 2097160 | tf_op jit(solution)/shard_map/dynamic_slice | solution.py:33
  4.7 2.9 %collective-permute-start.1 = (f32[256,256]{1,0:T(8,128)S(1)}, f32[256,256]{1,0:T(8,128)S(1)}, u32[]{:S(2)}, u32[]{:S(2)}) collective-permute-start(f32[256,256]{1,0:T(8,128)S(1)} %constant_dynamic-slice_fusion.1), channel_id=1, source_target_pairs={{0,8},{4,12},{8,0},{12,4},{16,24},{20,28},{24,16},{28,20},{1,9},{5... | collective-permute-start | bytes 786440 | tf_op jit(solution)/shard_map/ppermute | solution.py:20
  7.5 1.1 slice_bitcast_fusion.6
  8.6 1.5 %collective-permute-start.3 = (f32[128,1024]{1,0:T(8,128)}, f32[128,1024]{1,0:T(8,128)}, u32[]{:S(2)}, u32[]{:S(2)}) collective-permute-start(f32[128,1024]{1,0:T(8,128)} %get-tuple-element.114), channel_id=1, source_target_pairs={{0,1},{1,0},{2,3},{3,2},{4,5},{5,4},{6,7},{7,6},{8,9},{9,8},{10,11... | collective-permute-start | bytes 1572872 | tf_op jit(solution)/shard_map/ppermute | solution.py:20
  10.1 1.5 %collective-permute-start.4 = (f32[128,1024]{1,0:T(8,128)}, f32[128,1024]{1,0:T(8,128)}, u32[]{:S(2)}, u32[]{:S(2)}) collective-permute-start(f32[128,1024]{1,0:T(8,128)} %get-tuple-element.113), channel_id=1, source_target_pairs={{0,2},{1,3},{2,0},{3,1},{4,6},{5,7},{6,4},{7,5},{8,10},{9,11},{10,... | collective-permute-start | bytes 1572872 | tf_op jit(solution)/shard_map/ppermute | solution.py:20
  11.6 2.7 %collective-permute-done.1 = f32[256,256]{1,0:T(8,128)S(1)} collective-permute-done((f32[256,256]{1,0:T(8,128)S(1)}, f32[256,256]{1,0:T(8,128)S(1)}, u32[]{:S(2)}, u32[]{:S(2)}) %collective-permute-start.1) | collective-permute-done | bytes 262176 | tf_op jit(solution)/shard_map/ppermute | solution.py:20
  14.3 2.8 %collective-permute-start.2 = (f32[256,256]{1,0:T(8,128)S(1)}, f32[256,256]{1,0:T(8,128)}, u32[]{:S(2)}, u32[]{:S(2)}) collective-permute-start(f32[256,256]{1,0:T(8,128)S(1)} %dynamic-slice_select_fusion.1), channel_id=1, source_target_pairs={{0,16},{4,20},{8,24},{12,28},{16,0},{20,4},{24,8},{28,12},{1,17},{... | collective-permute-start | bytes 786440 | tf_op jit(solution)/shard_map/ppermute | solution.py:20
  17.2 1.1 slice_bitcast_fusion.4
  18.2 1.5 %collective-permute-start.6 = (f32[128,1024]{1,0:T(8,128)}, f32[128,1024]{1,0:T(8,128)}, u32[]{:S(2)}, u32[]{:S(2)}) collective-permute-start(f32[128,1024]{1,0:T(8,128)} %get-tuple-element.112), channel_id=1, source_target_pairs={{0,1},{1,0},{2,3},{3,2},{4,5},{5,4},{6,7},{7,6},{8,9},{9,8},{10,11... | collective-permute-start | bytes 1572872 | tf_op jit(solution)/shard_map/ppermute | solution.py:20
  19.7 1.5 %collective-permute-start.7 = (f32[128,1024]{1,0:T(8,128)}, f32[128,1024]{1,0:T(8,128)}, u32[]{:S(2)}, u32[]{:S(2)}) collective-permute-start(f32[128,1024]{1,0:T(8,128)} %get-tuple-element.111), channel_id=1, source_target_pairs={{0,2},{1,3},{2,0},{3,1},{4,6},{5,7},{6,4},{7,5},{8,10},{9,11},{10,... | collective-permute-start | bytes 1572872 | tf_op jit(solution)/shard_map/ppermute | solution.py:20
  21.8 7.3 %collective-permute-done.2 = f32[256,256]{1,0:T(8,128)} collective-permute-done((f32[256,256]{1,0:T(8,128)S(1)}, f32[256,256]{1,0:T(8,128)}, u32[]{:S(2)}, u32[]{:S(2)}) %collective-permute-start.2) | collective-permute-done | bytes 262176 | tf_op jit(solution)/shard_map/ppermute | solution.py:20
  29.7 1.5 %collective-permute-start.12 = (f32[128,1024]{1,0:T(8,128)}, f32[128,1024]{1,0:T(8,128)S(1)}, u32[]{:S(2)}, u32[]{:S(2)}) collective-permute-start(f32[128,1024]{1,0:T(8,128)} %collective-permute-done.3.refs_0_), channel_id=1, source_target_pairs={{0,2},{1,3},{2,0},{3,1},{4,6},{5,7},{6,4},{7,5},{8,10},{9,11},{10,... | collective-permute-start | bytes 1572872 | tf_op jit(solution)/shard_map/ppermute | solution.py:20
  31.2 1.5 %collective-permute-start.13 = (f32[128,1024]{1,0:T(8,128)}, f32[128,1024]{1,0:T(8,128)S(1)}, u32[]{:S(2)}, u32[]{:S(2)}) collective-permute-start(f32[128,1024]{1,0:T(8,128)} %collective-permute-done.4.refs_1_), channel_id=1, source_target_pairs={{0,1},{1,0},{2,3},{3,2},{4,5},{5,4},{6,7},{7,6},{8,9},{9,8},{10,11... | collective-permute-start | bytes 1572872 | tf_op jit(solution)/shard_map/ppermute | solution.py:20
  32.7 3.9 %collective-permute-done.5.refs_1_ = f32[256,256]{1,0:T(8,128)S(1)} collective-permute-done((f32[256,256]{1,0:T(8,128)S(1)}, f32[256,256]{1,0:T(8,128)S(1)}, u32[]{:S(2)}, u32[]{:S(2)}) %collective-permute-start.5) | collective-permute-done | bytes 262176 | tf_op jit(solution)/shard_map/ppermute | solution.py:20
  37.1 1.0 collective-permute-done.8.refs_2_
  39.1 4.0 %collective-permute-start.10 = (f32[128,256]{1,0:T(8,128)S(1)}, f32[128,256]{1,0:T(8,128)S(1)}, u32[]{:S(2)}, u32[]{:S(2)}) collective-permute-start(f32[128,256]{1,0:T(8,128)S(1)} %solve.2.refs_0_), channel_id=1, source_target_pairs={{0,16},{4,20},{8,24},{12,28},{16,0},{20,4},{24,8},{28,12},{1,17},{... | collective-permute-start | bytes 393224 | tf_op jit(solution)/shard_map/ppermute | solution.py:20
  43.1 1.7 %collective-permute-start.11 = (f32[128,256]{1,0:T(8,128)S(1)}, f32[128,256]{1,0:T(8,128)S(1)}, u32[]{:S(2)}, u32[]{:S(2)}) collective-permute-start(f32[128,256]{1,0:T(8,128)S(1)} %solve.2.refs_0_), channel_id=1, source_target_pairs={{0,8},{4,12},{8,0},{12,4},{16,24},{20,28},{24,16},{28,20},{1,9},{5... | collective-permute-start | bytes 393224 | tf_op jit(solution)/shard_map/ppermute | solution.py:20
  44.8 1.5 %collective-permute-done.12.refs_4_ = f32[128,1024]{1,0:T(8,128)S(1)} collective-permute-done((f32[128,1024]{1,0:T(8,128)}, f32[128,1024]{1,0:T(8,128)S(1)}, u32[]{:S(2)}, u32[]{:S(2)}) %collective-permute-start.12) | collective-permute-done | bytes 524320 | tf_op jit(solution)/shard_map/ppermute | solution.py:20
  46.4 3.4 %collective-permute-done.10.refs_2_ = f32[128,256]{1,0:T(8,128)S(1)} collective-permute-done((f32[128,256]{1,0:T(8,128)S(1)}, f32[128,256]{1,0:T(8,128)S(1)}, u32[]{:S(2)}, u32[]{:S(2)}) %collective-permute-start.10) | collective-permute-done | bytes 131104 | tf_op jit(solution)/shard_map/ppermute | solution.py:20
  49.9 1.6 %collective-permute-start.14 = (f32[128,256]{1,0:T(8,128)S(1)}, f32[128,256]{1,0:T(8,128)S(1)}, u32[]{:S(2)}, u32[]{:S(2)}) collective-permute-start(f32[128,256]{1,0:T(8,128)S(1)} %collective-permute-done.10.refs_2_), channel_id=1, source_target_pairs={{0,8},{4,12},{8,0},{12,4},{16,24},{20,28},{24,16},{28,20},{1,9},{5... | collective-permute-start | bytes 393224 | tf_op jit(solution)/shard_map/ppermute | solution.py:20
  52.0 2.0 %prepare.2 = (bf16[1024,1024]{1,0:T(8,128)(2,1)S(1)}, bf16[1024,1024]{1,0:T(8,128)(2,1)S(1)}) custom-call(f32[1,2,256,1024]{3,2,1,0:T(8,128)S(1)} %copy-done, f32[128,1024]{1,0:T(8,128)} %collective-permute-done.3.refs_0_, f32[128,1024]{1,0:T(8,128)} %collective-permute-done.4.refs_1_, f32[128,1024]{1,0:T(8,128)} %collective-permute-done.6.refs_2_, ...), custom_call_target="tpu_custom_call" | custom-call | bytes 16777216 | tf_op jit(solution)/shard_map/prepare/pallas_call | solution.py:98
  54.9 1.3 %collective-permute-done.18.refs_7_ = f32[128,256]{1,0:T(8,128)S(1)} collective-permute-done((f32[128,256]{1,0:T(8,128)S(1)}, f32[128,256]{1,0:T(8,128)S(1)}, u32[]{:S(2)}, u32[]{:S(2)}) %collective-permute-start.18) | collective-permute-done | bytes 131104 | tf_op jit(solution)/shard_map/ppermute | solution.py:20
  56.2 3.5 %update.2 = (f32[512,256]{1,0:T(8,128)S(1)}, f32[512,256]{1,0:T(8,128)}) custom-call(s32[1,2]{1,0:T(1,128)S(1)} %copy-done.5, s32[8]{0:T(128)S(1)} %copy-done.6, bf16[1024,1024]{1,0:T(8,128)(2,1)S(1)} %get-tuple-element.76.high, bf16[1024,1024]{1,0:T(8,128)(2,1)S(1)} %get-tuple-element.77.low, f32[128,256]{1,0:T(8,128)S(1)} %solve.2.refs_0_, ...), custom_call_target="tpu_custom_call" | custom-call | flops 1610612736 | bytes 7340032 | tf_op jit(solution)/shard_map/update/pallas_call | solution.py:184
  62.8 1.1 broadcast_select_fusion.1
  63.9 1.6 %collective-permute-start.20 = (f32[256,256]{1,0:T(8,128)S(1)}, f32[256,256]{1,0:T(8,128)S(1)}, u32[]{:S(2)}, u32[]{:S(2)}) collective-permute-start(f32[256,256]{1,0:T(8,128)S(1)} %constant_dynamic-slice_fusion), channel_id=1, source_target_pairs={{0,8},{4,12},{8,0},{12,4},{16,24},{20,28},{24,16},{28,20},{1,9},{5... | collective-permute-start | bytes 786440 | tf_op jit(solution)/shard_map/ppermute | solution.py:20
  65.6 1.1 slice_bitcast_fusion.2
  66.7 1.5 %collective-permute-start.22 = (f32[128,1024]{1,0:T(8,128)}, f32[128,1024]{1,0:T(8,128)}, u32[]{:S(2)}, u32[]{:S(2)}) collective-permute-start(f32[128,1024]{1,0:T(8,128)} %get-tuple-element.110), channel_id=1, source_target_pairs={{0,1},{1,0},{2,3},{3,2},{4,5},{5,4},{6,7},{7,6},{8,9},{9,8},{10,11... | collective-permute-start | bytes 1572872 | tf_op jit(solution)/shard_map/ppermute | solution.py:20
  68.2 1.5 %collective-permute-start.23 = (f32[128,1024]{1,0:T(8,128)}, f32[128,1024]{1,0:T(8,128)}, u32[]{:S(2)}, u32[]{:S(2)}) collective-permute-start(f32[128,1024]{1,0:T(8,128)} %get-tuple-element.109), channel_id=1, source_target_pairs={{0,2},{1,3},{2,0},{3,1},{4,6},{5,7},{6,4},{7,5},{8,10},{9,11},{10,... | collective-permute-start | bytes 1572872 | tf_op jit(solution)/shard_map/ppermute | solution.py:20
  69.7 2.7 %collective-permute-done.20 = f32[256,256]{1,0:T(8,128)S(1)} collective-permute-done((f32[256,256]{1,0:T(8,128)S(1)}, f32[256,256]{1,0:T(8,128)S(1)}, u32[]{:S(2)}, u32[]{:S(2)}) %collective-permute-start.20) | collective-permute-done | bytes 262176 | tf_op jit(solution)/shard_map/ppermute | solution.py:20
  72.4 2.7 %collective-permute-start.21 = (f32[256,256]{1,0:T(8,128)S(1)}, f32[256,256]{1,0:T(8,128)}, u32[]{:S(2)}, u32[]{:S(2)}) collective-permute-start(f32[256,256]{1,0:T(8,128)S(1)} %dynamic-slice_select_fusion), channel_id=1, source_target_pairs={{0,16},{4,20},{8,24},{12,28},{16,0},{20,4},{24,8},{28,12},{1,17},{... | collective-permute-start | bytes 786440 | tf_op jit(solution)/shard_map/ppermute | solution.py:20
  75.1 1.1 slice_bitcast_fusion
  76.2 1.5 %collective-permute-start.25 = (f32[128,1024]{1,0:T(8,128)}, f32[128,1024]{1,0:T(8,128)}, u32[]{:S(2)}, u32[]{:S(2)}) collective-permute-start(f32[128,1024]{1,0:T(8,128)} %get-tuple-element.108), channel_id=1, source_target_pairs={{0,1},{1,0},{2,3},{3,2},{4,5},{5,4},{6,7},{7,6},{8,9},{9,8},{10,11... | collective-permute-start | bytes 1572872 | tf_op jit(solution)/shard_map/ppermute | solution.py:20
  77.7 1.5 %collective-permute-start.26 = (f32[128,1024]{1,0:T(8,128)}, f32[128,1024]{1,0:T(8,128)}, u32[]{:S(2)}, u32[]{:S(2)}) collective-permute-start(f32[128,1024]{1,0:T(8,128)} %get-tuple-element.107), channel_id=1, source_target_pairs={{0,2},{1,3},{2,0},{3,1},{4,6},{5,7},{6,4},{7,5},{8,10},{9,11},{10,... | collective-permute-start | bytes 1572872 | tf_op jit(solution)/shard_map/ppermute | solution.py:20
  79.8 7.0 %collective-permute-done.21 = f32[256,256]{1,0:T(8,128)} collective-permute-done((f32[256,256]{1,0:T(8,128)S(1)}, f32[256,256]{1,0:T(8,128)}, u32[]{:S(2)}, u32[]{:S(2)}) %collective-permute-start.21) | collective-permute-done | bytes 262176 | tf_op jit(solution)/shard_map/ppermute | solution.py:20
  86.7 1.0 broadcast_select_fusion.3.refs_0_
  88.4 1.5 %collective-permute-start.31 = (f32[128,1024]{1,0:T(8,128)}, f32[128,1024]{1,0:T(8,128)S(1)}, u32[]{:S(2)}, u32[]{:S(2)}) collective-permute-start(f32[128,1024]{1,0:T(8,128)} %collective-permute-done.22.refs_0_), channel_id=1, source_target_pairs={{0,2},{1,3},{2,0},{3,1},{4,6},{5,7},{6,4},{7,5},{8,10},{9,11},{10,... | collective-permute-start | bytes 1572872 | tf_op jit(solution)/shard_map/ppermute | solution.py:20
  89.9 1.5 %collective-permute-start.32 = (f32[128,1024]{1,0:T(8,128)}, f32[128,1024]{1,0:T(8,128)S(1)}, u32[]{:S(2)}, u32[]{:S(2)}) collective-permute-start(f32[128,1024]{1,0:T(8,128)} %collective-permute-done.23.refs_1_), channel_id=1, source_target_pairs={{0,1},{1,0},{2,3},{3,2},{4,5},{5,4},{6,7},{7,6},{8,9},{9,8},{10,11... | collective-permute-start | bytes 1572872 | tf_op jit(solution)/shard_map/ppermute | solution.py:20
  91.9 2.6 %collective-permute-done.26.refs_3_ = f32[128,1024]{1,0:T(8,128)} collective-permute-done((f32[128,1024]{1,0:T(8,128)}, f32[128,1024]{1,0:T(8,128)}, u32[]{:S(2)}, u32[]{:S(2)}) %collective-permute-start.26) | collective-permute-done | bytes 524320 | tf_op jit(solution)/shard_map/ppermute | solution.py:20
  95.4 1.0 collective-permute-done.27.refs_2_
  97.3 2.6 %collective-permute-start.29 = (f32[128,256]{1,0:T(8,128)S(1)}, f32[128,256]{1,0:T(8,128)S(1)}, u32[]{:S(2)}, u32[]{:S(2)}) collective-permute-start(f32[128,256]{1,0:T(8,128)S(1)} %solve.3.refs_0_), channel_id=1, source_target_pairs={{0,16},{4,20},{8,24},{12,28},{16,0},{20,4},{24,8},{28,12},{1,17},{... | collective-permute-start | bytes 393224 | tf_op jit(solution)/shard_map/ppermute | solution.py:20
  99.9 1.7 %collective-permute-start.30 = (f32[128,256]{1,0:T(8,128)S(1)}, f32[128,256]{1,0:T(8,128)S(1)}, u32[]{:S(2)}, u32[]{:S(2)}) collective-permute-start(f32[128,256]{1,0:T(8,128)S(1)} %solve.3.refs_0_), channel_id=1, source_target_pairs={{0,8},{4,12},{8,0},{12,4},{16,24},{20,28},{24,16},{28,20},{1,9},{5... | collective-permute-start | bytes 393224 | tf_op jit(solution)/shard_map/ppermute | solution.py:20
  101.6 2.6 %collective-permute-done.31.refs_4_ = f32[128,1024]{1,0:T(8,128)S(1)} collective-permute-done((f32[128,1024]{1,0:T(8,128)}, f32[128,1024]{1,0:T(8,128)S(1)}, u32[]{:S(2)}, u32[]{:S(2)}) %collective-permute-start.31) | collective-permute-done | bytes 524320 | tf_op jit(solution)/shard_map/ppermute | solution.py:20
  104.3 2.4 %collective-permute-done.29.refs_2_ = f32[128,256]{1,0:T(8,128)S(1)} collective-permute-done((f32[128,256]{1,0:T(8,128)S(1)}, f32[128,256]{1,0:T(8,128)S(1)}, u32[]{:S(2)}, u32[]{:S(2)}) %collective-permute-start.29) | collective-permute-done | bytes 131104 | tf_op jit(solution)/shard_map/ppermute | solution.py:20
  106.7 1.6 %collective-permute-start.33 = (f32[128,256]{1,0:T(8,128)S(1)}, f32[128,256]{1,0:T(8,128)S(1)}, u32[]{:S(2)}, u32[]{:S(2)}) collective-permute-start(f32[128,256]{1,0:T(8,128)S(1)} %collective-permute-done.29.refs_2_), channel_id=1, source_target_pairs={{0,8},{4,12},{8,0},{12,4},{16,24},{20,28},{24,16},{28,20},{1,9},{5... | collective-permute-start | bytes 393224 | tf_op jit(solution)/shard_map/ppermute | solution.py:20
  108.8 2.0 %prepare.3 = (bf16[1024,1024]{1,0:T(8,128)(2,1)S(1)}, bf16[1024,1024]{1,0:T(8,128)(2,1)S(1)}) custom-call(f32[1,2,256,1024]{3,2,1,0:T(8,128)S(1)} %copy-done, f32[128,1024]{1,0:T(8,128)} %collective-permute-done.22.refs_0_, f32[128,1024]{1,0:T(8,128)} %collective-permute-done.23.refs_1_, f32[128,1024]{1,0:T(8,128)} %collective-permute-done.25.refs_2_, ...), custom_call_target="tpu_custom_call" | custom-call | bytes 16777216 | tf_op jit(solution)/shard_map/prepare/pallas_call | solution.py:98
  110.8 0.8 collective-permute-done.33.refs_3_
  111.7 1.3 %collective-permute-done.37.refs_7_ = f32[128,256]{1,0:T(8,128)S(1)} collective-permute-done((f32[128,256]{1,0:T(8,128)S(1)}, f32[128,256]{1,0:T(8,128)S(1)}, u32[]{:S(2)}, u32[]{:S(2)}) %collective-permute-start.37) | collective-permute-done | bytes 131104 | tf_op jit(solution)/shard_map/ppermute | solution.py:20
  113.0 3.9 %update.3 = f32[1024,256]{1,0:T(8,128)} custom-call(s32[1,2]{1,0:T(1,128)S(1)} %copy-done.5, s32[8]{0:T(128)S(1)} %copy-done.6, bf16[1024,1024]{1,0:T(8,128)(2,1)S(1)} %get-tuple-element.101.high, bf16[1024,1024]{1,0:T(8,128)(2,1)S(1)} %get-tuple-element.102.low, f32[128,256]{1,0:T(8,128)S(1)} %solve.3.refs_0_, ...), custom_call_target="tpu_custom_call" | custom-call | flops 1610612736 | bytes 7340032 | tf_op jit(solution)/shard_map/update/pallas_call | solution.py:184
  (63 shorter events, 10.1 us)
Async XLA Ops:
  0.0 2.7 %copy-start.6 = (s32[8]{0:T(128)S(1)}, s32[8]{0:T(128)}, u32[]{:S(2)}) copy-start(s32[8]{0:T(128)} %slot_block.3) | copy-start | bytes 100
  0.0 7.5 %copy-start = (f32[1,2,256,1024]{3,2,1,0:T(8,128)S(1)}, f32[1,2,256,1024]{3,2,1,0:T(8,128)}, u32[]{:S(2)}) copy-start(f32[1,2,256,1024]{3,2,1,0:T(8,128)} %own.1) | copy-start | bytes 6291460
  2.2 2.3 %collective-permute-start = (f32[512,256]{1,0:T(8,128)}, f32[512,256]{1,0:T(8,128)S(1)}, u32[]{:S(2)}, u32[]{:S(2)}) collective-permute-start(f32[512,256]{1,0:T(8,128)} %get-tuple-element.115), channel_id=1, source_target_pairs={{0,4},{4,0},{8,12},{12,8},{16,20},{20,16},{24,28},{28,24},{1,5},{5... | collective-permute-start | bytes 1572872 | tf_op jit(solution)/shard_map/ppermute | solution.py:20
  4.7 9.6 %collective-permute-start.1 = (f32[256,256]{1,0:T(8,128)S(1)}, f32[256,256]{1,0:T(8,128)S(1)}, u32[]{:S(2)}, u32[]{:S(2)}) collective-permute-start(f32[256,256]{1,0:T(8,128)S(1)} %constant_dynamic-slice_fusion.1), channel_id=1, source_target_pairs={{0,8},{4,12},{8,0},{12,4},{16,24},{20,28},{24,16},{28,20},{1,9},{5... | collective-permute-start | bytes 786440 | tf_op jit(solution)/shard_map/ppermute | solution.py:20
  8.6 29.9 %copy-start.1 = (f32[2,128,1024]{2,1,0:T(8,128)S(1)}, f32[2,128,1024]{2,1,0:T(8,128)}, u32[]{:S(2)}) copy-start(f32[2,128,1024]{2,1,0:T(8,128)} %inverse.3) | copy-start | bytes 3145732
  8.6 20.5 %collective-permute-start.3 = (f32[128,1024]{1,0:T(8,128)}, f32[128,1024]{1,0:T(8,128)}, u32[]{:S(2)}, u32[]{:S(2)}) collective-permute-start(f32[128,1024]{1,0:T(8,128)} %get-tuple-element.114), channel_id=1, source_target_pairs={{0,1},{1,0},{2,3},{3,2},{4,5},{5,4},{6,7},{7,6},{8,9},{9,8},{10,11... | collective-permute-start | bytes 1572872 | tf_op jit(solution)/shard_map/ppermute | solution.py:20
  10.1 19.1 %collective-permute-start.4 = (f32[128,1024]{1,0:T(8,128)}, f32[128,1024]{1,0:T(8,128)}, u32[]{:S(2)}, u32[]{:S(2)}) collective-permute-start(f32[128,1024]{1,0:T(8,128)} %get-tuple-element.113), channel_id=1, source_target_pairs={{0,2},{1,3},{2,0},{3,1},{4,6},{5,7},{6,4},{7,5},{8,10},{9,11},{10,... | collective-permute-start | bytes 1572872 | tf_op jit(solution)/shard_map/ppermute | solution.py:20
  14.3 14.8 %collective-permute-start.2 = (f32[256,256]{1,0:T(8,128)S(1)}, f32[256,256]{1,0:T(8,128)}, u32[]{:S(2)}, u32[]{:S(2)}) collective-permute-start(f32[256,256]{1,0:T(8,128)S(1)} %dynamic-slice_select_fusion.1), channel_id=1, source_target_pairs={{0,16},{4,20},{8,24},{12,28},{16,0},{20,4},{24,8},{28,12},{1,17},{... | collective-permute-start | bytes 786440 | tf_op jit(solution)/shard_map/ppermute | solution.py:20
  18.2 18.4 %collective-permute-start.6 = (f32[128,1024]{1,0:T(8,128)}, f32[128,1024]{1,0:T(8,128)}, u32[]{:S(2)}, u32[]{:S(2)}) collective-permute-start(f32[128,1024]{1,0:T(8,128)} %get-tuple-element.112), channel_id=1, source_target_pairs={{0,1},{1,0},{2,3},{3,2},{4,5},{5,4},{6,7},{7,6},{8,9},{9,8},{10,11... | collective-permute-start | bytes 1572872 | tf_op jit(solution)/shard_map/ppermute | solution.py:20
  19.7 16.9 %collective-permute-start.7 = (f32[128,1024]{1,0:T(8,128)}, f32[128,1024]{1,0:T(8,128)}, u32[]{:S(2)}, u32[]{:S(2)}) collective-permute-start(f32[128,1024]{1,0:T(8,128)} %get-tuple-element.111), channel_id=1, source_target_pairs={{0,2},{1,3},{2,0},{3,1},{4,6},{5,7},{6,4},{7,5},{8,10},{9,11},{10,... | collective-permute-start | bytes 1572872 | tf_op jit(solution)/shard_map/ppermute | solution.py:20
  29.2 7.4 %collective-permute-start.5 = (f32[256,256]{1,0:T(8,128)S(1)}, f32[256,256]{1,0:T(8,128)S(1)}, u32[]{:S(2)}, u32[]{:S(2)}) collective-permute-start(f32[256,256]{1,0:T(8,128)S(1)} %broadcast_select_fusion.2.refs_0_), channel_id=1, source_target_pairs={{0,8},{4,12},{8,0},{12,4},{16,24},{20,28},{24,16},{28,20},{1,9},{5... | collective-permute-start | bytes 786440 | tf_op jit(solution)/shard_map/ppermute | solution.py:20
  29.7 16.7 %collective-permute-start.12 = (f32[128,1024]{1,0:T(8,128)}, f32[128,1024]{1,0:T(8,128)S(1)}, u32[]{:S(2)}, u32[]{:S(2)}) collective-permute-start(f32[128,1024]{1,0:T(8,128)} %collective-permute-done.3.refs_0_), channel_id=1, source_target_pairs={{0,2},{1,3},{2,0},{3,1},{4,6},{5,7},{6,4},{7,5},{8,10},{9,11},{10,... | collective-permute-start | bytes 1572872 | tf_op jit(solution)/shard_map/ppermute | solution.py:20
  31.2 15.2 %collective-permute-start.13 = (f32[128,1024]{1,0:T(8,128)}, f32[128,1024]{1,0:T(8,128)S(1)}, u32[]{:S(2)}, u32[]{:S(2)}) collective-permute-start(f32[128,1024]{1,0:T(8,128)} %collective-permute-done.4.refs_1_), channel_id=1, source_target_pairs={{0,1},{1,0},{2,3},{3,2},{4,5},{5,4},{6,7},{7,6},{8,9},{9,8},{10,11... | collective-permute-start | bytes 1572872 | tf_op jit(solution)/shard_map/ppermute | solution.py:20
  36.6 1.5 %collective-permute-start.8 = (f32[256,256]{1,0:T(8,128)S(1)}, f32[256,256]{1,0:T(8,128)S(1)}, u32[]{:S(2)}, u32[]{:S(2)}) collective-permute-start(f32[256,256]{1,0:T(8,128)S(1)} %broadcast_select_fusion.2.refs_0_), channel_id=1, source_target_pairs={{0,4},{4,0},{8,12},{12,8},{16,20},{20,16},{24,28},{28,24},{1,5},{5... | collective-permute-start | bytes 786440 | tf_op jit(solution)/shard_map/ppermute | solution.py:20
  36.6 1.9 %collective-permute-start.9 = (f32[256,256]{1,0:T(8,128)S(1)}, f32[256,256]{1,0:T(8,128)S(1)}, u32[]{:S(2)}, u32[]{:S(2)}) collective-permute-start(f32[256,256]{1,0:T(8,128)S(1)} %collective-permute-done.5.refs_1_), channel_id=1, source_target_pairs={{0,4},{4,0},{8,12},{12,8},{16,20},{20,16},{24,28},{28,24},{1,5},{5... | collective-permute-start | bytes 786440 | tf_op jit(solution)/shard_map/ppermute | solution.py:20
  39.0 17.2 %copy-start.2 = (f32[1,1024,256]{2,1,0:T(8,128)S(1)}, f32[1,1024,256]{2,1,0:T(8,128)}, u32[]{:S(2)}) copy-start(f32[1,1024,256]{2,1,0:T(8,128)} %refs_8_.1) | copy-start | bytes 3145732
  39.0 17.2 %copy-start.5 = (s32[1,2]{1,0:T(1,128)S(1)}, s32[1,2]{1,0:T(1,128)}, u32[]{:S(2)}) copy-start(s32[1,2]{1,0:T(1,128)} %flags.3) | copy-start | bytes 28
  39.1 10.7 %collective-permute-start.10 = (f32[128,256]{1,0:T(8,128)S(1)}, f32[128,256]{1,0:T(8,128)S(1)}, u32[]{:S(2)}, u32[]{:S(2)}) collective-permute-start(f32[128,256]{1,0:T(8,128)S(1)} %solve.2.refs_0_), channel_id=1, source_target_pairs={{0,16},{4,20},{8,24},{12,28},{16,0},{20,4},{24,8},{28,12},{1,17},{... | collective-permute-start | bytes 393224 | tf_op jit(solution)/shard_map/ppermute | solution.py:20
  43.1 6.8 %collective-permute-start.11 = (f32[128,256]{1,0:T(8,128)S(1)}, f32[128,256]{1,0:T(8,128)S(1)}, u32[]{:S(2)}, u32[]{:S(2)}) collective-permute-start(f32[128,256]{1,0:T(8,128)S(1)} %solve.2.refs_0_), channel_id=1, source_target_pairs={{0,8},{4,12},{8,0},{12,4},{16,24},{20,28},{24,16},{28,20},{1,9},{5... | collective-permute-start | bytes 393224 | tf_op jit(solution)/shard_map/ppermute | solution.py:20
  44.8 9.2 %collective-permute-start.15 = (f32[128,256]{1,0:T(8,128)S(1)}, f32[128,256]{1,0:T(8,128)S(1)}, u32[]{:S(2)}, u32[]{:S(2)}) collective-permute-start(f32[128,256]{1,0:T(8,128)S(1)} %solve.2.refs_0_), channel_id=1, source_target_pairs={{0,4},{4,0},{8,12},{12,8},{16,20},{20,16},{24,28},{28,24},{1,5},{5... | collective-permute-start | bytes 393224 | tf_op jit(solution)/shard_map/ppermute | solution.py:20
  49.9 5.0 %collective-permute-start.14 = (f32[128,256]{1,0:T(8,128)S(1)}, f32[128,256]{1,0:T(8,128)S(1)}, u32[]{:S(2)}, u32[]{:S(2)}) collective-permute-start(f32[128,256]{1,0:T(8,128)S(1)} %collective-permute-done.10.refs_2_), channel_id=1, source_target_pairs={{0,8},{4,12},{8,0},{12,4},{16,24},{20,28},{24,16},{28,20},{1,9},{5... | collective-permute-start | bytes 393224 | tf_op jit(solution)/shard_map/ppermute | solution.py:20
  51.5 3.4 %collective-permute-start.16 = (f32[128,256]{1,0:T(8,128)S(1)}, f32[128,256]{1,0:T(8,128)S(1)}, u32[]{:S(2)}, u32[]{:S(2)}) collective-permute-start(f32[128,256]{1,0:T(8,128)S(1)} %collective-permute-done.11.refs_1_), channel_id=1, source_target_pairs={{0,4},{4,0},{8,12},{12,8},{16,20},{20,16},{24,28},{28,24},{1,5},{5... | collective-permute-start | bytes 393224 | tf_op jit(solution)/shard_map/ppermute | solution.py:20
  51.5 3.4 %collective-permute-start.17 = (f32[128,256]{1,0:T(8,128)S(1)}, f32[128,256]{1,0:T(8,128)S(1)}, u32[]{:S(2)}, u32[]{:S(2)}) collective-permute-start(f32[128,256]{1,0:T(8,128)S(1)} %collective-permute-done.10.refs_2_), channel_id=1, source_target_pairs={{0,4},{4,0},{8,12},{12,8},{16,20},{20,16},{24,28},{28,24},{1,5},{5... | collective-permute-start | bytes 393224 | tf_op jit(solution)/shard_map/ppermute | solution.py:20
  54.8 1.4 %collective-permute-start.18 = (f32[128,256]{1,0:T(8,128)S(1)}, f32[128,256]{1,0:T(8,128)S(1)}, u32[]{:S(2)}, u32[]{:S(2)}) collective-permute-start(f32[128,256]{1,0:T(8,128)S(1)} %collective-permute-done.14.refs_3_), channel_id=1, source_target_pairs={{0,4},{4,0},{8,12},{12,8},{16,20},{20,16},{24,28},{28,24},{1,5},{5... | collective-permute-start | bytes 393224 | tf_op jit(solution)/shard_map/ppermute | solution.py:20
  59.7 0.8 copy-start.3
  60.5 2.3 %collective-permute-start.19 = (f32[512,256]{1,0:T(8,128)}, f32[512,256]{1,0:T(8,128)}, u32[]{:S(2)}, u32[]{:S(2)}) collective-permute-start(f32[512,256]{1,0:T(8,128)} %get-tuple-element.83.refs_9_), channel_id=1, source_target_pairs={{0,4},{4,0},{8,12},{12,8},{16,20},{20,16},{24,28},{28,24},{1,5},{5... | collective-permute-start | bytes 1572872 | tf_op jit(solution)/shard_map/ppermute | solution.py:20
  63.9 8.4 %collective-permute-start.20 = (f32[256,256]{1,0:T(8,128)S(1)}, f32[256,256]{1,0:T(8,128)S(1)}, u32[]{:S(2)}, u32[]{:S(2)}) collective-permute-start(f32[256,256]{1,0:T(8,128)S(1)} %constant_dynamic-slice_fusion), channel_id=1, source_target_pairs={{0,8},{4,12},{8,0},{12,4},{16,24},{20,28},{24,16},{28,20},{1,9},{5... | collective-permute-start | bytes 786440 | tf_op jit(solution)/shard_map/ppermute | solution.py:20
  66.7 21.0 %collective-permute-start.22 = (f32[128,1024]{1,0:T(8,128)}, f32[128,1024]{1,0:T(8,128)}, u32[]{:S(2)}, u32[]{:S(2)}) collective-permute-start(f32[128,1024]{1,0:T(8,128)} %get-tuple-element.110), channel_id=1, source_target_pairs={{0,1},{1,0},{2,3},{3,2},{4,5},{5,4},{6,7},{7,6},{8,9},{9,8},{10,11... | collective-permute-start | bytes 1572872 | tf_op jit(solution)/shard_map/ppermute | solution.py:20
  68.2 19.6 %collective-permute-start.23 = (f32[128,1024]{1,0:T(8,128)}, f32[128,1024]{1,0:T(8,128)}, u32[]{:S(2)}, u32[]{:S(2)}) collective-permute-start(f32[128,1024]{1,0:T(8,128)} %get-tuple-element.109), channel_id=1, source_target_pairs={{0,2},{1,3},{2,0},{3,1},{4,6},{5,7},{6,4},{7,5},{8,10},{9,11},{10,... | collective-permute-start | bytes 1572872 | tf_op jit(solution)/shard_map/ppermute | solution.py:20
  72.4 14.3 %collective-permute-start.21 = (f32[256,256]{1,0:T(8,128)S(1)}, f32[256,256]{1,0:T(8,128)}, u32[]{:S(2)}, u32[]{:S(2)}) collective-permute-start(f32[256,256]{1,0:T(8,128)S(1)} %dynamic-slice_select_fusion), channel_id=1, source_target_pairs={{0,16},{4,20},{8,24},{12,28},{16,0},{20,4},{24,8},{28,12},{1,17},{... | collective-permute-start | bytes 786440 | tf_op jit(solution)/shard_map/ppermute | solution.py:20
  76.2 15.7 %collective-permute-start.25 = (f32[128,1024]{1,0:T(8,128)}, f32[128,1024]{1,0:T(8,128)}, u32[]{:S(2)}, u32[]{:S(2)}) collective-permute-start(f32[128,1024]{1,0:T(8,128)} %get-tuple-element.108), channel_id=1, source_target_pairs={{0,1},{1,0},{2,3},{3,2},{4,5},{5,4},{6,7},{7,6},{8,9},{9,8},{10,11... | collective-permute-start | bytes 1572872 | tf_op jit(solution)/shard_map/ppermute | solution.py:20
  77.7 16.9 %collective-permute-start.26 = (f32[128,1024]{1,0:T(8,128)}, f32[128,1024]{1,0:T(8,128)}, u32[]{:S(2)}, u32[]{:S(2)}) collective-permute-start(f32[128,1024]{1,0:T(8,128)} %get-tuple-element.107), channel_id=1, source_target_pairs={{0,2},{1,3},{2,0},{3,1},{4,6},{5,7},{6,4},{7,5},{8,10},{9,11},{10,... | collective-permute-start | bytes 1572872 | tf_op jit(solution)/shard_map/ppermute | solution.py:20
  87.7 7.2 %collective-permute-start.24 = (f32[256,256]{1,0:T(8,128)S(1)}, f32[256,256]{1,0:T(8,128)S(1)}, u32[]{:S(2)}, u32[]{:S(2)}) collective-permute-start(f32[256,256]{1,0:T(8,128)S(1)} %broadcast_select_fusion.3.refs_0_), channel_id=1, source_target_pairs={{0,8},{4,12},{8,0},{12,4},{16,24},{20,28},{24,16},{28,20},{1,9},{5... | collective-permute-start | bytes 786440 | tf_op jit(solution)/shard_map/ppermute | solution.py:20
  88.4 15.9 %collective-permute-start.31 = (f32[128,1024]{1,0:T(8,128)}, f32[128,1024]{1,0:T(8,128)S(1)}, u32[]{:S(2)}, u32[]{:S(2)}) collective-permute-start(f32[128,1024]{1,0:T(8,128)} %collective-permute-done.22.refs_0_), channel_id=1, source_target_pairs={{0,2},{1,3},{2,0},{3,1},{4,6},{5,7},{6,4},{7,5},{8,10},{9,11},{10,... | collective-permute-start | bytes 1572872 | tf_op jit(solution)/shard_map/ppermute | solution.py:20
  89.9 14.3 %collective-permute-start.32 = (f32[128,1024]{1,0:T(8,128)}, f32[128,1024]{1,0:T(8,128)S(1)}, u32[]{:S(2)}, u32[]{:S(2)}) collective-permute-start(f32[128,1024]{1,0:T(8,128)} %collective-permute-done.23.refs_1_), channel_id=1, source_target_pairs={{0,1},{1,0},{2,3},{3,2},{4,5},{5,4},{6,7},{7,6},{8,9},{9,8},{10,11... | collective-permute-start | bytes 1572872 | tf_op jit(solution)/shard_map/ppermute | solution.py:20
  94.9 1.5 %collective-permute-start.27 = (f32[256,256]{1,0:T(8,128)S(1)}, f32[256,256]{1,0:T(8,128)S(1)}, u32[]{:S(2)}, u32[]{:S(2)}) collective-permute-start(f32[256,256]{1,0:T(8,128)S(1)} %broadcast_select_fusion.3.refs_0_), channel_id=1, source_target_pairs={{0,4},{4,0},{8,12},{12,8},{16,20},{20,16},{24,28},{28,24},{1,5},{5... | collective-permute-start | bytes 786440 | tf_op jit(solution)/shard_map/ppermute | solution.py:20
  94.9 1.9 %collective-permute-start.28 = (f32[256,256]{1,0:T(8,128)S(1)}, f32[256,256]{1,0:T(8,128)S(1)}, u32[]{:S(2)}, u32[]{:S(2)}) collective-permute-start(f32[256,256]{1,0:T(8,128)S(1)} %collective-permute-done.24.refs_1_), channel_id=1, source_target_pairs={{0,4},{4,0},{8,12},{12,8},{16,20},{20,16},{24,28},{28,24},{1,5},{5... | collective-permute-start | bytes 786440 | tf_op jit(solution)/shard_map/ppermute | solution.py:20
  97.3 15.7 %copy-start.4 = (f32[512,256]{1,0:T(8,128)S(1)}, f32[512,256]{1,0:T(8,128)}, u32[]{:S(2)}) copy-start(f32[512,256]{1,0:T(8,128)} %copy-done.3) | copy-start | bytes 1572868
  97.3 9.4 %collective-permute-start.29 = (f32[128,256]{1,0:T(8,128)S(1)}, f32[128,256]{1,0:T(8,128)S(1)}, u32[]{:S(2)}, u32[]{:S(2)}) collective-permute-start(f32[128,256]{1,0:T(8,128)S(1)} %solve.3.refs_0_), channel_id=1, source_target_pairs={{0,16},{4,20},{8,24},{12,28},{16,0},{20,4},{24,8},{28,12},{1,17},{... | collective-permute-start | bytes 393224 | tf_op jit(solution)/shard_map/ppermute | solution.py:20
  99.9 6.8 %collective-permute-start.30 = (f32[128,256]{1,0:T(8,128)S(1)}, f32[128,256]{1,0:T(8,128)S(1)}, u32[]{:S(2)}, u32[]{:S(2)}) collective-permute-start(f32[128,256]{1,0:T(8,128)S(1)} %solve.3.refs_0_), channel_id=1, source_target_pairs={{0,8},{4,12},{8,0},{12,4},{16,24},{20,28},{24,16},{28,20},{1,9},{5... | collective-permute-start | bytes 393224 | tf_op jit(solution)/shard_map/ppermute | solution.py:20
  101.6 9.2 %collective-permute-start.34 = (f32[128,256]{1,0:T(8,128)S(1)}, f32[128,256]{1,0:T(8,128)S(1)}, u32[]{:S(2)}, u32[]{:S(2)}) collective-permute-start(f32[128,256]{1,0:T(8,128)S(1)} %solve.3.refs_0_), channel_id=1, source_target_pairs={{0,4},{4,0},{8,12},{12,8},{16,20},{20,16},{24,28},{28,24},{1,5},{5... | collective-permute-start | bytes 393224 | tf_op jit(solution)/shard_map/ppermute | solution.py:20
  106.7 5.0 %collective-permute-start.33 = (f32[128,256]{1,0:T(8,128)S(1)}, f32[128,256]{1,0:T(8,128)S(1)}, u32[]{:S(2)}, u32[]{:S(2)}) collective-permute-start(f32[128,256]{1,0:T(8,128)S(1)} %collective-permute-done.29.refs_2_), channel_id=1, source_target_pairs={{0,8},{4,12},{8,0},{12,4},{16,24},{20,28},{24,16},{28,20},{1,9},{5... | collective-permute-start | bytes 393224 | tf_op jit(solution)/shard_map/ppermute | solution.py:20
  108.3 3.4 %collective-permute-start.35 = (f32[128,256]{1,0:T(8,128)S(1)}, f32[128,256]{1,0:T(8,128)S(1)}, u32[]{:S(2)}, u32[]{:S(2)}) collective-permute-start(f32[128,256]{1,0:T(8,128)S(1)} %collective-permute-done.30.refs_1_), channel_id=1, source_target_pairs={{0,4},{4,0},{8,12},{12,8},{16,20},{20,16},{24,28},{28,24},{1,5},{5... | collective-permute-start | bytes 393224 | tf_op jit(solution)/shard_map/ppermute | solution.py:20
  108.3 3.4 %collective-permute-start.36 = (f32[128,256]{1,0:T(8,128)S(1)}, f32[128,256]{1,0:T(8,128)S(1)}, u32[]{:S(2)}, u32[]{:S(2)}) collective-permute-start(f32[128,256]{1,0:T(8,128)S(1)} %collective-permute-done.29.refs_2_), channel_id=1, source_target_pairs={{0,4},{4,0},{8,12},{12,8},{16,20},{20,16},{24,28},{28,24},{1,5},{5... | collective-permute-start | bytes 393224 | tf_op jit(solution)/shard_map/ppermute | solution.py:20
  111.7 1.4 %collective-permute-start.37 = (f32[128,256]{1,0:T(8,128)S(1)}, f32[128,256]{1,0:T(8,128)S(1)}, u32[]{:S(2)}, u32[]{:S(2)}) collective-permute-start(f32[128,256]{1,0:T(8,128)S(1)} %collective-permute-done.33.refs_3_), channel_id=1, source_target_pairs={{0,4},{4,0},{8,12},{12,8},{16,20},{20,16},{24,28},{28,24},{1,5},{5... | collective-permute-start | bytes 393224 | tf_op jit(solution)/shard_map/ppermute | solution.py:20

commit v4 on v3

--- a/solution.py
+++ b/solution.py
@@ -59,14 +59,14 @@
     return dot(a[0], b[0]) + (dot(a[0], b[1]) + dot(a[1], b[0]))
 
 
-def prepare_body(step, own, *refs):
+def prepare_body(own_top, own_bottom, *refs):
     pieces, (high, low, slots, sems) = refs[:6], refs[6:]
     side = lax.axis_index("col")
     half = pieces[0].shape[0]
-    sources = [(own.at[0, step], side * 2)]
+    sources = [(own_top, side * 2), (own_bottom, side * 2 + 1)]
     for ref, (distance, part) in zip(pieces, ((1, 0), (2, 1), (1, 1), (2, 0), (3, 0), (3, 1))):
         sources.append((ref, (side ^ distance) * 2 + part))
-    groups = [sources[0:1], sources[1:3], sources[3:5], sources[5:7]]
+    groups = [sources[start:start + 2] for start in range(0, 8, 2)]
 
     def fetch(index):
         copies = []
@@ -92,19 +92,19 @@
             flying.append(fetch(index + 2))
 
 
-def prepare(panel, step, pieces):
-    depth = panel.shape[3]
+def prepare(pieces):
+    half, depth = pieces[0].shape
     vmem, anywhere = pl.BlockSpec(memory_space=pltpu.VMEM), pl.BlockSpec(memory_space=pl.ANY)
     return pl.pallas_call(
-        functools.partial(prepare_body, step),
+        prepare_body,
         out_shape=[jax.ShapeDtypeStruct((depth, depth), jnp.bfloat16)] * 2,
-        in_specs=[anywhere] * 7,
+        in_specs=[anywhere] * 8,
         out_specs=[vmem] * 2,
-        scratch_shapes=[pltpu.VMEM((2, panel.shape[2], depth), jnp.float32), pltpu.SemaphoreType.DMA((2, 2))],
+        scratch_shapes=[pltpu.VMEM((2, 2 * half, depth), jnp.float32), pltpu.SemaphoreType.DMA((2, 2))],
         compiler_params=pltpu.CompilerParams(vmem_limit_bytes=PREPARE_BYTES),
         cost_estimate=pl.CostEstimate(flops=0, bytes_accessed=16 * depth * depth, transcendentals=0),
         name="prepare",
-    )(panel, *pieces)
+    )(*pieces)
 
 
 def assemble(x, blocks, rank):
@@ -146,7 +146,7 @@
         out[rows] = jnp.where(held == 0, current[...], jnp.where(held == 1, x[rows], new))
 
 
-def solve_body(step, inverse, *refs):
+def solve_body(inverse, *refs):
     quarters, (out, y) = refs[:4], refs[4:]
     rank = lax.axis_index("row")
     size = quarters[0].shape[0]
@@ -154,15 +154,15 @@
     for index, ref in enumerate(quarters):
         place = (core ^ (index >> 1)) * 2 + (z ^ (index & 1))
         y[pl.ds(pl.multiple_of(place * size, size), size)] = ref[...]
-    out[...] = dot3(split(inverse[step]), split(y[...]))
-
-
-def solve(step, inverse, quarters):
-    _, rows, depth = inverse.shape
+    out[...] = dot3(split(inverse[...]), split(y[...]))
+
+
+def solve(inverse, quarters):
+    rows, depth = inverse.shape
     cols = quarters[0].shape[1]
     vmem = pl.BlockSpec(memory_space=pltpu.VMEM)
     return pl.pallas_call(
-        functools.partial(solve_body, step),
+        solve_body,
         out_shape=jax.ShapeDtypeStruct((rows, cols), jnp.float32),
         in_specs=[vmem] * 5,
         out_specs=vmem,
@@ -234,21 +234,21 @@
 
     def solved(step, y, panel, owner):
         y, panel = tie(y, panel)
-        first = near(*block_halves(panel, step))
+        block = tie(*block_halves(panel, step))
+        first = near(*block)
         y = scatter_step(y, 1, rows, owner, rank)
-        y, panel = tie(y, panel)
-        top, bottom = block_halves(panel, step)
-        second = near(bottom, top)
+        y, *block = tie(y, *block)
+        second = near(*block[::-1])
         y = cross_step(y, 2, rows, owner, rank)
-        y, *first = tie(y, *first)
+        y, inverse, *first = tie(y, diag_inverse, *first)
         pieces = far(*first)
         beside = swap(y, "row", 1, rows)
         beside, y, *second = tie(beside, y, *second)
         other, last = swap(y, "row", 0, rows), swap(beside, "row", 0, rows)
-        x = solve(step, diag_inverse, [y, beside, other, last])
+        x = solve(inverse[step], [y, beside, other, last])
         x2, x1 = swap(x, "row", 2, rows), swap(x, "row", 1, rows)
         x2, x1, *pieces = tie(x2, x1, *pieces)
-        high, low = prepare(panel, step, [*first, *second, *pieces])
+        high, low = prepare([*block, *first, *second, *pieces])
         x3 = swap(x2, "row", 1, rows)
         across = [swap(block, "row", 0, rows) for block in (x, x1, x2)]
         x3, high, low, *across = tie(x3, high, low, *across)

time: 117 us -> 114 us (0.974)
  waiting for transfers between devices: 44.6 us -> 50.1 us
  starting transfers between devices: 45.2 us -> 40.4 us
  Pallas kernels: 12.4 us -> 9.98 us
  local copies, waits for them, and re-layouts: 7.48 us -> 5.8 us
    ppermute x38, waiting for transfers between devices: 44.6 us -> 50.1 us  [swap(): return lax.ppermute(x, axis, [(i, i ^ 1 << b) for i in range(size)])]
    ppermute x38, starting transfers between devices: 45.2 us -> 40.4 us  [swap(): return lax.ppermute(x, axis, [(i, i ^ 1 << b) for i in range(size)])]
    squeeze x4 -> x2, local copies, waits for them, and re-layouts: 4.38 us -> 1.37 us  [block_halves(): return (panel[0, step, :half], panel[0, step, half:])]
    squeeze x0 -> x2, local copies, waits for them, and re-layouts: none -> 2.15 us  [solved(): x = solve(inverse[step], [y, beside, other, last])]
    pallas_call x2, Pallas kernels: 7.38 us -> 6.12 us  [update(): pl.pallas_call(first_body if step == 0 else second_body, out_shape=[jax.S...]
  transfers between devices with their start and end apart: 38 -> 38, of which waited for: 22 -> 18; matrix products, arithmetic and copies ran while one was open for 6% -> 6% of each run, Pallas kernels for 4% -> 3%
where the time goes in v4:
time: 114 us; the launch traced here: 113 us
  waiting for transfers between devices  50.1 us (44%)
  starting transfers between devices  40.4 us (35%)
  Pallas kernels  9.98 us (9%)
  local copies, waits for them, and re-layouts  5.8 us (5%)
  between operations  3.68 us (3%)
  other arithmetic  3.46 us (3%)
    ppermute x38, waiting for transfers between devices, swap(): return lax.ppermute(x, axis, [(i, i ^ 1 << b) for i in range(size)])  50.1 us
    ppermute x38, starting transfers between devices, swap(): return lax.ppermute(x, axis, [(i, i ^ 1 << b) for i in range(size)])  40.4 us
    pallas_call x2, Pallas kernels, update(): pl.pallas_call(first_body if step == 0 else second_body, out_shape=[jax.S...  6.12 us
    pallas_call x2, Pallas kernels, prepare(): pl.pallas_call(prepare_body, out_shape=[jax.ShapeDtypeStruct((depth, dept...  2.91 us
  transfers between devices with their start and end apart: 38, of which 18 were waited for; matrix products, arithmetic and copies ran while one was open for 6% of the time, Pallas kernels for 3%

profile of v4, /device:TPU:0, one launch (start us, length us, event | category | flops | bytes accessed | tf_op | source)
XLA Modules:
  0.0 113.4 jit_solution(1325381985981118565)
XLA Ops:
  0.0 2.2 %dynamic-slice_bitcast_fusion = (f32[512,256]{1,0:T(8,128)}, f32[512,256]{1,0:T(8,128)S(1)}) fusion(f32[1,1024,256]{2,1,0:T(8,128)} %refs_8_.1, s32[]{:T(128)S(6)} %select_n.67, s32[]{:T(128)S(6)} %select_n.66), kind=kLoop, calls=%fused_computation.6 | loop fusion | bytes 2097160 | tf_op jit(solution)/shard_map/dynamic_slice | solution.py:33
  2.7 0.7 compare_reduce_fusion
  4.6 2.9 %collective-permute-start.1 = (f32[256,256]{1,0:T(8,128)S(1)}, f32[256,256]{1,0:T(8,128)S(1)}, u32[]{:S(2)}, u32[]{:S(2)}) collective-permute-start(f32[256,256]{1,0:T(8,128)S(1)} %constant_dynamic-slice_fusion.1), channel_id=1, source_target_pairs={{0,8},{4,12},{8,0},{12,4},{16,24},{20,28},{24,16},{28,20},{1,9},{5... | collective-permute-start | bytes 786440 | tf_op jit(solution)/shard_map/ppermute | solution.py:20
  7.6 1.6 %collective-permute-start.3 = (f32[128,1024]{1,0:T(8,128)S(1)}, f32[128,1024]{1,0:T(8,128)S(1)}, u32[]{:S(2)}, u32[]{:S(2)}) collective-permute-start(f32[128,1024]{1,0:T(8,128)S(1)} %get-tuple-element.75.own_top), channel_id=1, source_target_pairs={{0,1},{1,0},{2,3},{3,2},{4,5},{5,4},{6,7},{7,6},{8,9},{9,8},{10,11... | collective-permute-start | bytes 1572872 | tf_op jit(solution)/shard_map/ppermute | solution.py:20
  9.2 1.5 %collective-permute-start.4 = (f32[128,1024]{1,0:T(8,128)S(1)}, f32[128,1024]{1,0:T(8,128)S(1)}, u32[]{:S(2)}, u32[]{:S(2)}) collective-permute-start(f32[128,1024]{1,0:T(8,128)S(1)} %get-tuple-element.74.own_bottom), channel_id=1, source_target_pairs={{0,2},{1,3},{2,0},{3,1},{4,6},{5,7},{6,4},{7,5},{8,10},{9,11},{10,... | collective-permute-start | bytes 1572872 | tf_op jit(solution)/shard_map/ppermute | solution.py:20
  10.7 3.5 %collective-permute-done.1 = f32[256,256]{1,0:T(8,128)S(1)} collective-permute-done((f32[256,256]{1,0:T(8,128)S(1)}, f32[256,256]{1,0:T(8,128)S(1)}, u32[]{:S(2)}, u32[]{:S(2)}) %collective-permute-start.1) | collective-permute-done | bytes 262176 | tf_op jit(solution)/shard_map/ppermute | solution.py:20
  14.3 2.8 %collective-permute-start.2 = (f32[256,256]{1,0:T(8,128)S(1)}, f32[256,256]{1,0:T(8,128)}, u32[]{:S(2)}, u32[]{:S(2)}) collective-permute-start(f32[256,256]{1,0:T(8,128)S(1)} %dynamic-slice_select_fusion.1), channel_id=1, source_target_pairs={{0,16},{4,20},{8,24},{12,28},{16,0},{20,4},{24,8},{28,12},{1,17},{... | collective-permute-start | bytes 786440 | tf_op jit(solution)/shard_map/ppermute | solution.py:20
  17.1 1.5 %collective-permute-start.6 = (f32[128,1024]{1,0:T(8,128)S(1)}, f32[128,1024]{1,0:T(8,128)S(1)}, u32[]{:S(2)}, u32[]{:S(2)}) collective-permute-start(f32[128,1024]{1,0:T(8,128)S(1)} %get-tuple-element.74.own_bottom), channel_id=1, source_target_pairs={{0,1},{1,0},{2,3},{3,2},{4,5},{5,4},{6,7},{7,6},{8,9},{9,8},{10,11... | collective-permute-start | bytes 1572872 | tf_op jit(solution)/shard_map/ppermute | solution.py:20
  18.6 1.5 %collective-permute-start.7 = (f32[128,1024]{1,0:T(8,128)S(1)}, f32[128,1024]{1,0:T(8,128)S(1)}, u32[]{:S(2)}, u32[]{:S(2)}) collective-permute-start(f32[128,1024]{1,0:T(8,128)S(1)} %get-tuple-element.75.own_top), channel_id=1, source_target_pairs={{0,2},{1,3},{2,0},{3,1},{4,6},{5,7},{6,4},{7,5},{8,10},{9,11},{10,... | collective-permute-start | bytes 1572872 | tf_op jit(solution)/shard_map/ppermute | solution.py:20
  20.7 8.2 %collective-permute-done.2 = f32[256,256]{1,0:T(8,128)} collective-permute-done((f32[256,256]{1,0:T(8,128)S(1)}, f32[256,256]{1,0:T(8,128)}, u32[]{:S(2)}, u32[]{:S(2)}) %collective-permute-start.2) | collective-permute-done | bytes 262176 | tf_op jit(solution)/shard_map/ppermute | solution.py:20
  28.9 1.0 broadcast_select_fusion.2.refs_0_
  30.4 1.5 %collective-permute-start.12 = (f32[128,1024]{1,0:T(8,128)S(1)}, f32[128,1024]{1,0:T(8,128)S(1)}, u32[]{:S(2)}, u32[]{:S(2)}) collective-permute-start(f32[128,1024]{1,0:T(8,128)S(1)} %collective-permute-done.3.refs_0_), channel_id=1, source_target_pairs={{0,2},{1,3},{2,0},{3,1},{4,6},{5,7},{6,4},{7,5},{8,10},{9,11},{10,... | collective-permute-start | bytes 1572872 | tf_op jit(solution)/shard_map/ppermute | solution.py:20
  31.9 1.5 %collective-permute-start.13 = (f32[128,1024]{1,0:T(8,128)S(1)}, f32[128,1024]{1,0:T(8,128)S(1)}, u32[]{:S(2)}, u32[]{:S(2)}) collective-permute-start(f32[128,1024]{1,0:T(8,128)S(1)} %collective-permute-done.4.refs_1_), channel_id=1, source_target_pairs={{0,1},{1,0},{2,3},{3,2},{4,5},{5,4},{6,7},{7,6},{8,9},{9,8},{10,11... | collective-permute-start | bytes 1572872 | tf_op jit(solution)/shard_map/ppermute | solution.py:20
  33.4 3.9 %collective-permute-done.5.refs_1_ = f32[256,256]{1,0:T(8,128)S(1)} collective-permute-done((f32[256,256]{1,0:T(8,128)S(1)}, f32[256,256]{1,0:T(8,128)S(1)}, u32[]{:S(2)}, u32[]{:S(2)}) %collective-permute-start.5) | collective-permute-done | bytes 262176 | tf_op jit(solution)/shard_map/ppermute | solution.py:20
  37.8 1.1 slice_bitcast_fusion.3.inverse
  39.7 2.2 %collective-permute-start.10 = (f32[128,256]{1,0:T(8,128)S(1)}, f32[128,256]{1,0:T(8,128)S(1)}, u32[]{:S(2)}, u32[]{:S(2)}) collective-permute-start(f32[128,256]{1,0:T(8,128)S(1)} %solve.2.refs_0_), channel_id=1, source_target_pairs={{0,16},{4,20},{8,24},{12,28},{16,0},{20,4},{24,8},{28,12},{1,17},{... | collective-permute-start | bytes 393224 | tf_op jit(solution)/shard_map/ppermute | solution.py:20
  41.9 1.7 %collective-permute-start.11 = (f32[128,256]{1,0:T(8,128)S(1)}, f32[128,256]{1,0:T(8,128)S(1)}, u32[]{:S(2)}, u32[]{:S(2)}) collective-permute-start(f32[128,256]{1,0:T(8,128)S(1)} %solve.2.refs_0_), channel_id=1, source_target_pairs={{0,8},{4,12},{8,0},{12,4},{16,24},{20,28},{24,16},{28,20},{1,9},{5... | collective-permute-start | bytes 393224 | tf_op jit(solution)/shard_map/ppermute | solution.py:20
  43.6 1.5 %collective-permute-done.12.refs_4_ = f32[128,1024]{1,0:T(8,128)S(1)} collective-permute-done((f32[128,1024]{1,0:T(8,128)S(1)}, f32[128,1024]{1,0:T(8,128)S(1)}, u32[]{:S(2)}, u32[]{:S(2)}) %collective-permute-start.12) | collective-permute-done | bytes 524320 | tf_op jit(solution)/shard_map/ppermute | solution.py:20
  45.2 3.9 %collective-permute-done.10.refs_2_ = f32[128,256]{1,0:T(8,128)S(1)} collective-permute-done((f32[128,256]{1,0:T(8,128)S(1)}, f32[128,256]{1,0:T(8,128)S(1)}, u32[]{:S(2)}, u32[]{:S(2)}) %collective-permute-start.10) | collective-permute-done | bytes 131104 | tf_op jit(solution)/shard_map/ppermute | solution.py:20
  49.1 1.1 %collective-permute-start.14 = (f32[128,256]{1,0:T(8,128)S(1)}, f32[128,256]{1,0:T(8,128)S(1)}, u32[]{:S(2)}, u32[]{:S(2)}) collective-permute-start(f32[128,256]{1,0:T(8,128)S(1)} %collective-permute-done.10.refs_2_), channel_id=1, source_target_pairs={{0,8},{4,12},{8,0},{12,4},{16,24},{20,28},{24,16},{28,20},{1,9},{5... | collective-permute-start | bytes 393224 | tf_op jit(solution)/shard_map/ppermute | solution.py:20
  50.8 1.1 prepare.2
  51.9 2.2 %collective-permute-done.14.refs_3_ = f32[128,256]{1,0:T(8,128)S(1)} collective-permute-done((f32[128,256]{1,0:T(8,128)S(1)}, f32[128,256]{1,0:T(8,128)S(1)}, u32[]{:S(2)}, u32[]{:S(2)}) %collective-permute-start.14) | collective-permute-done | bytes 131104 | tf_op jit(solution)/shard_map/ppermute | solution.py:20
  54.1 1.3 %collective-permute-done.18.refs_7_ = f32[128,256]{1,0:T(8,128)S(1)} collective-permute-done((f32[128,256]{1,0:T(8,128)S(1)}, f32[128,256]{1,0:T(8,128)S(1)}, u32[]{:S(2)}, u32[]{:S(2)}) %collective-permute-start.18) | collective-permute-done | bytes 131104 | tf_op jit(solution)/shard_map/ppermute | solution.py:20
  55.5 2.7 %update.2 = (f32[512,256]{1,0:T(8,128)S(1)}, f32[512,256]{1,0:T(8,128)S(1)}) custom-call(s32[1,2]{1,0:T(1,128)S(1)} %copy-done.1, s32[8]{0:T(128)S(1)} %copy-done.2, bf16[1024,1024]{1,0:T(8,128)(2,1)S(1)} %get-tuple-element.88.high, bf16[1024,1024]{1,0:T(8,128)(2,1)S(1)} %get-tuple-element.89.low, f32[128,256]{1,0:T(8,128)S(1)} %solve.2.refs_0_, ...), custom_call_target="tpu_custom_call" | custom-call | flops 1610612736 | bytes 7340032 | tf_op jit(solution)/shard_map/update/pallas_call | solution.py:184
  60.2 1.2 %collective-permute-start.20 = (f32[256,256]{1,0:T(8,128)S(1)}, f32[256,256]{1,0:T(8,128)S(1)}, u32[]{:S(2)}, u32[]{:S(2)}) collective-permute-start(f32[256,256]{1,0:T(8,128)S(1)} %constant_dynamic-slice_fusion), channel_id=1, source_target_pairs={{0,8},{4,12},{8,0},{12,4},{16,24},{20,28},{24,16},{28,20},{1,9},{5... | collective-permute-start | bytes 786440 | tf_op jit(solution)/shard_map/ppermute | solution.py:20
  61.5 1.3 %slice_bitcast_fusion.1 = (f32[128,1024]{1,0:T(8,128)S(1)}, f32[128,1024]{1,0:T(8,128)S(1)}) fusion(f32[1,2,256,1024]{3,2,1,0:T(8,128)} %param.6), kind=kLoop, calls=%fused_computation.1 | loop fusion | bytes 2097152 | tf_op jit(solution)/shard_map/squeeze | solution.py:233
  62.7 1.6 %collective-permute-start.22 = (f32[128,1024]{1,0:T(8,128)S(1)}, f32[128,1024]{1,0:T(8,128)S(1)}, u32[]{:S(2)}, u32[]{:S(2)}) collective-permute-start(f32[128,1024]{1,0:T(8,128)S(1)} %get-tuple-element.104.own_top), channel_id=1, source_target_pairs={{0,1},{1,0},{2,3},{3,2},{4,5},{5,4},{6,7},{7,6},{8,9},{9,8},{10,11... | collective-permute-start | bytes 1572872 | tf_op jit(solution)/shard_map/ppermute | solution.py:20
  64.3 1.5 %collective-permute-start.23 = (f32[128,1024]{1,0:T(8,128)S(1)}, f32[128,1024]{1,0:T(8,128)S(1)}, u32[]{:S(2)}, u32[]{:S(2)}) collective-permute-start(f32[128,1024]{1,0:T(8,128)S(1)} %get-tuple-element.103.own_bottom), channel_id=1, source_target_pairs={{0,2},{1,3},{2,0},{3,1},{4,6},{5,7},{6,4},{7,5},{8,10},{9,11},{10,... | collective-permute-start | bytes 1572872 | tf_op jit(solution)/shard_map/ppermute | solution.py:20
  65.8 3.1 %collective-permute-done.20 = f32[256,256]{1,0:T(8,128)S(1)} collective-permute-done((f32[256,256]{1,0:T(8,128)S(1)}, f32[256,256]{1,0:T(8,128)S(1)}, u32[]{:S(2)}, u32[]{:S(2)}) %collective-permute-start.20) | collective-permute-done | bytes 262176 | tf_op jit(solution)/shard_map/ppermute | solution.py:20
  68.9 2.3 %collective-permute-start.21 = (f32[256,256]{1,0:T(8,128)S(1)}, f32[256,256]{1,0:T(8,128)}, u32[]{:S(2)}, u32[]{:S(2)}) collective-permute-start(f32[256,256]{1,0:T(8,128)S(1)} %dynamic-slice_select_fusion), channel_id=1, source_target_pairs={{0,16},{4,20},{8,24},{12,28},{16,0},{20,4},{24,8},{28,12},{1,17},{... | collective-permute-start | bytes 786440 | tf_op jit(solution)/shard_map/ppermute | solution.py:20
  71.2 1.5 %collective-permute-start.25 = (f32[128,1024]{1,0:T(8,128)S(1)}, f32[128,1024]{1,0:T(8,128)}, u32[]{:S(2)}, u32[]{:S(2)}) collective-permute-start(f32[128,1024]{1,0:T(8,128)S(1)} %get-tuple-element.103.own_bottom), channel_id=1, source_target_pairs={{0,1},{1,0},{2,3},{3,2},{4,5},{5,4},{6,7},{7,6},{8,9},{9,8},{10,11... | collective-permute-start | bytes 1572872 | tf_op jit(solution)/shard_map/ppermute | solution.py:20
  72.7 1.5 %collective-permute-start.26 = (f32[128,1024]{1,0:T(8,128)S(1)}, f32[128,1024]{1,0:T(8,128)}, u32[]{:S(2)}, u32[]{:S(2)}) collective-permute-start(f32[128,1024]{1,0:T(8,128)S(1)} %get-tuple-element.104.own_top), channel_id=1, source_target_pairs={{0,2},{1,3},{2,0},{3,1},{4,6},{5,7},{6,4},{7,5},{8,10},{9,11},{10,... | collective-permute-start | bytes 1572872 | tf_op jit(solution)/shard_map/ppermute | solution.py:20
  74.8 8.6 %collective-permute-done.21 = f32[256,256]{1,0:T(8,128)} collective-permute-done((f32[256,256]{1,0:T(8,128)S(1)}, f32[256,256]{1,0:T(8,128)}, u32[]{:S(2)}, u32[]{:S(2)}) %collective-permute-start.21) | collective-permute-done | bytes 262176 | tf_op jit(solution)/shard_map/ppermute | solution.py:20
  83.4 1.0 broadcast_select_fusion.3.refs_0_
  84.6 1.5 %collective-permute-start.31 = (f32[128,1024]{1,0:T(8,128)S(1)}, f32[128,1024]{1,0:T(8,128)S(1)}, u32[]{:S(2)}, u32[]{:S(2)}) collective-permute-start(f32[128,1024]{1,0:T(8,128)S(1)} %collective-permute-done.22.refs_0_), channel_id=1, source_target_pairs={{0,2},{1,3},{2,0},{3,1},{4,6},{5,7},{6,4},{7,5},{8,10},{9,11},{10,... | collective-permute-start | bytes 1572872 | tf_op jit(solution)/shard_map/ppermute | solution.py:20
  86.2 1.5 %collective-permute-start.32 = (f32[128,1024]{1,0:T(8,128)S(1)}, f32[128,1024]{1,0:T(8,128)S(1)}, u32[]{:S(2)}, u32[]{:S(2)}) collective-permute-start(f32[128,1024]{1,0:T(8,128)S(1)} %collective-permute-done.23.refs_1_), channel_id=1, source_target_pairs={{0,1},{1,0},{2,3},{3,2},{4,5},{5,4},{6,7},{7,6},{8,9},{9,8},{10,11... | collective-permute-start | bytes 1572872 | tf_op jit(solution)/shard_map/ppermute | solution.py:20
  88.0 2.4 %collective-permute-done.26.refs_3_ = f32[128,1024]{1,0:T(8,128)} collective-permute-done((f32[128,1024]{1,0:T(8,128)S(1)}, f32[128,1024]{1,0:T(8,128)}, u32[]{:S(2)}, u32[]{:S(2)}) %collective-permute-start.26) | collective-permute-done | bytes 524320 | tf_op jit(solution)/shard_map/ppermute | solution.py:20
  90.5 1.4 %collective-permute-done.24.refs_1_ = f32[256,256]{1,0:T(8,128)S(1)} collective-permute-done((f32[256,256]{1,0:T(8,128)S(1)}, f32[256,256]{1,0:T(8,128)S(1)}, u32[]{:S(2)}, u32[]{:S(2)}) %collective-permute-start.24) | collective-permute-done | bytes 262176 | tf_op jit(solution)/shard_map/ppermute | solution.py:20
  92.4 1.1 slice_bitcast_fusion.inverse
  94.2 1.9 %collective-permute-start.29 = (f32[128,256]{1,0:T(8,128)S(1)}, f32[128,256]{1,0:T(8,128)S(1)}, u32[]{:S(2)}, u32[]{:S(2)}) collective-permute-start(f32[128,256]{1,0:T(8,128)S(1)} %solve.3.refs_0_), channel_id=1, source_target_pairs={{0,16},{4,20},{8,24},{12,28},{16,0},{20,4},{24,8},{28,12},{1,17},{... | collective-permute-start | bytes 393224 | tf_op jit(solution)/shard_map/ppermute | solution.py:20
  96.1 1.7 %collective-permute-start.30 = (f32[128,256]{1,0:T(8,128)S(1)}, f32[128,256]{1,0:T(8,128)S(1)}, u32[]{:S(2)}, u32[]{:S(2)}) collective-permute-start(f32[128,256]{1,0:T(8,128)S(1)} %solve.3.refs_0_), channel_id=1, source_target_pairs={{0,8},{4,12},{8,0},{12,4},{16,24},{20,28},{24,16},{28,20},{1,9},{5... | collective-permute-start | bytes 393224 | tf_op jit(solution)/shard_map/ppermute | solution.py:20
  97.9 2.5 %collective-permute-done.31.refs_4_ = f32[128,1024]{1,0:T(8,128)S(1)} collective-permute-done((f32[128,1024]{1,0:T(8,128)S(1)}, f32[128,1024]{1,0:T(8,128)S(1)}, u32[]{:S(2)}, u32[]{:S(2)}) %collective-permute-start.31) | collective-permute-done | bytes 524320 | tf_op jit(solution)/shard_map/ppermute | solution.py:20
  100.4 3.2 %collective-permute-done.29.refs_2_ = f32[128,256]{1,0:T(8,128)S(1)} collective-permute-done((f32[128,256]{1,0:T(8,128)S(1)}, f32[128,256]{1,0:T(8,128)S(1)}, u32[]{:S(2)}, u32[]{:S(2)}) %collective-permute-start.29) | collective-permute-done | bytes 131104 | tf_op jit(solution)/shard_map/ppermute | solution.py:20
  103.6 0.9 collective-permute-start.33
  105.0 1.8 %prepare.3 = (bf16[1024,1024]{1,0:T(8,128)(2,1)S(1)}, bf16[1024,1024]{1,0:T(8,128)(2,1)S(1)}) custom-call(f32[128,1024]{1,0:T(8,128)S(1)} %get-tuple-element.104.own_top, f32[128,1024]{1,0:T(8,128)S(1)} %get-tuple-element.103.own_bottom, f32[128,1024]{1,0:T(8,128)S(1)} %collective-permute-done.22.refs_0_, f32[128,1024]{1,0:T(8,128)S(1)} %collective-permute-done.23.refs_1_, ...), custom_call_target="tpu_custom_call" | custom-call | bytes 16777216 | tf_op jit(solution)/shard_map/prepare/pallas_call | solution.py:98
  106.9 1.7 %collective-permute-done.33.refs_3_ = f32[128,256]{1,0:T(8,128)S(1)} collective-permute-done((f32[128,256]{1,0:T(8,128)S(1)}, f32[128,256]{1,0:T(8,128)S(1)}, u32[]{:S(2)}, u32[]{:S(2)}) %collective-permute-start.33) | collective-permute-done | bytes 131104 | tf_op jit(solution)/shard_map/ppermute | solution.py:20
  108.6 1.3 %collective-permute-done.37.refs_7_ = f32[128,256]{1,0:T(8,128)S(1)} collective-permute-done((f32[128,256]{1,0:T(8,128)S(1)}, f32[128,256]{1,0:T(8,128)S(1)}, u32[]{:S(2)}, u32[]{:S(2)}) %collective-permute-start.37) | collective-permute-done | bytes 131104 | tf_op jit(solution)/shard_map/ppermute | solution.py:20
  110.0 3.4 %update.3 = f32[1024,256]{1,0:T(8,128)} custom-call(s32[1,2]{1,0:T(1,128)S(1)} %copy-done.1, s32[8]{0:T(128)S(1)} %copy-done.2, bf16[1024,1024]{1,0:T(8,128)(2,1)S(1)} %get-tuple-element.117.high, bf16[1024,1024]{1,0:T(8,128)(2,1)S(1)} %get-tuple-element.118.low, f32[128,256]{1,0:T(8,128)S(1)} %solve.3.refs_0_, ...), custom_call_target="tpu_custom_call" | custom-call | flops 1610612736 | bytes 7340032 | tf_op jit(solution)/shard_map/update/pallas_call | solution.py:184
  (57 shorter events, 6.5 us)
Async XLA Ops:
  0.0 2.7 %copy-start.2 = (s32[8]{0:T(128)S(1)}, s32[8]{0:T(128)}, u32[]{:S(2)}) copy-start(s32[8]{0:T(128)} %slot_block.3) | copy-start | bytes 100
  0.0 7.5 %copy-start.3 = (f32[1,2,256,1024]{3,2,1,0:T(8,128)S(1)}, f32[1,2,256,1024]{3,2,1,0:T(8,128)}, u32[]{:S(2)}) copy-start(f32[1,2,256,1024]{3,2,1,0:T(8,128)} %param.6) | copy-start | bytes 6291460
  2.2 2.3 %collective-permute-start = (f32[512,256]{1,0:T(8,128)}, f32[512,256]{1,0:T(8,128)S(1)}, u32[]{:S(2)}, u32[]{:S(2)}) collective-permute-start(f32[512,256]{1,0:T(8,128)} %get-tuple-element.127), channel_id=1, source_target_pairs={{0,4},{4,0},{8,12},{12,8},{16,20},{20,16},{24,28},{28,24},{1,5},{5... | collective-permute-start | bytes 1572872 | tf_op jit(solution)/shard_map/ppermute | solution.py:20
  4.6 9.6 %collective-permute-start.1 = (f32[256,256]{1,0:T(8,128)S(1)}, f32[256,256]{1,0:T(8,128)S(1)}, u32[]{:S(2)}, u32[]{:S(2)}) collective-permute-start(f32[256,256]{1,0:T(8,128)S(1)} %constant_dynamic-slice_fusion.1), channel_id=1, source_target_pairs={{0,8},{4,12},{8,0},{12,4},{16,24},{20,28},{24,16},{28,20},{1,9},{5... | collective-permute-start | bytes 786440 | tf_op jit(solution)/shard_map/ppermute | solution.py:20
  7.6 22.2 %collective-permute-start.3 = (f32[128,1024]{1,0:T(8,128)S(1)}, f32[128,1024]{1,0:T(8,128)S(1)}, u32[]{:S(2)}, u32[]{:S(2)}) collective-permute-start(f32[128,1024]{1,0:T(8,128)S(1)} %get-tuple-element.75.own_top), channel_id=1, source_target_pairs={{0,1},{1,0},{2,3},{3,2},{4,5},{5,4},{6,7},{7,6},{8,9},{9,8},{10,11... | collective-permute-start | bytes 1572872 | tf_op jit(solution)/shard_map/ppermute | solution.py:20
  9.2 20.7 %collective-permute-start.4 = (f32[128,1024]{1,0:T(8,128)S(1)}, f32[128,1024]{1,0:T(8,128)S(1)}, u32[]{:S(2)}, u32[]{:S(2)}) collective-permute-start(f32[128,1024]{1,0:T(8,128)S(1)} %get-tuple-element.74.own_bottom), channel_id=1, source_target_pairs={{0,2},{1,3},{2,0},{3,1},{4,6},{5,7},{6,4},{7,5},{8,10},{9,11},{10,... | collective-permute-start | bytes 1572872 | tf_op jit(solution)/shard_map/ppermute | solution.py:20
  14.3 14.6 %collective-permute-start.2 = (f32[256,256]{1,0:T(8,128)S(1)}, f32[256,256]{1,0:T(8,128)}, u32[]{:S(2)}, u32[]{:S(2)}) collective-permute-start(f32[256,256]{1,0:T(8,128)S(1)} %dynamic-slice_select_fusion.1), channel_id=1, source_target_pairs={{0,16},{4,20},{8,24},{12,28},{16,0},{20,4},{24,8},{28,12},{1,17},{... | collective-permute-start | bytes 786440 | tf_op jit(solution)/shard_map/ppermute | solution.py:20
  17.1 20.2 %collective-permute-start.6 = (f32[128,1024]{1,0:T(8,128)S(1)}, f32[128,1024]{1,0:T(8,128)S(1)}, u32[]{:S(2)}, u32[]{:S(2)}) collective-permute-start(f32[128,1024]{1,0:T(8,128)S(1)} %get-tuple-element.74.own_bottom), channel_id=1, source_target_pairs={{0,1},{1,0},{2,3},{3,2},{4,5},{5,4},{6,7},{7,6},{8,9},{9,8},{10,11... | collective-permute-start | bytes 1572872 | tf_op jit(solution)/shard_map/ppermute | solution.py:20
  18.6 18.7 %collective-permute-start.7 = (f32[128,1024]{1,0:T(8,128)S(1)}, f32[128,1024]{1,0:T(8,128)S(1)}, u32[]{:S(2)}, u32[]{:S(2)}) collective-permute-start(f32[128,1024]{1,0:T(8,128)S(1)} %get-tuple-element.75.own_top), channel_id=1, source_target_pairs={{0,2},{1,3},{2,0},{3,1},{4,6},{5,7},{6,4},{7,5},{8,10},{9,11},{10,... | collective-permute-start | bytes 1572872 | tf_op jit(solution)/shard_map/ppermute | solution.py:20
  29.9 7.4 %collective-permute-start.5 = (f32[256,256]{1,0:T(8,128)S(1)}, f32[256,256]{1,0:T(8,128)S(1)}, u32[]{:S(2)}, u32[]{:S(2)}) collective-permute-start(f32[256,256]{1,0:T(8,128)S(1)} %broadcast_select_fusion.2.refs_0_), channel_id=1, source_target_pairs={{0,8},{4,12},{8,0},{12,4},{16,24},{20,28},{24,16},{28,20},{1,9},{5... | collective-permute-start | bytes 786440 | tf_op jit(solution)/shard_map/ppermute | solution.py:20
  30.4 14.8 %collective-permute-start.12 = (f32[128,1024]{1,0:T(8,128)S(1)}, f32[128,1024]{1,0:T(8,128)S(1)}, u32[]{:S(2)}, u32[]{:S(2)}) collective-permute-start(f32[128,1024]{1,0:T(8,128)S(1)} %collective-permute-done.3.refs_0_), channel_id=1, source_target_pairs={{0,2},{1,3},{2,0},{3,1},{4,6},{5,7},{6,4},{7,5},{8,10},{9,11},{10,... | collective-permute-start | bytes 1572872 | tf_op jit(solution)/shard_map/ppermute | solution.py:20
  31.9 13.3 %collective-permute-start.13 = (f32[128,1024]{1,0:T(8,128)S(1)}, f32[128,1024]{1,0:T(8,128)S(1)}, u32[]{:S(2)}, u32[]{:S(2)}) collective-permute-start(f32[128,1024]{1,0:T(8,128)S(1)} %collective-permute-done.4.refs_1_), channel_id=1, source_target_pairs={{0,1},{1,0},{2,3},{3,2},{4,5},{5,4},{6,7},{7,6},{8,9},{9,8},{10,11... | collective-permute-start | bytes 1572872 | tf_op jit(solution)/shard_map/ppermute | solution.py:20
  37.3 1.6 %collective-permute-start.8 = (f32[256,256]{1,0:T(8,128)S(1)}, f32[256,256]{1,0:T(8,128)S(1)}, u32[]{:S(2)}, u32[]{:S(2)}) collective-permute-start(f32[256,256]{1,0:T(8,128)S(1)} %broadcast_select_fusion.2.refs_0_), channel_id=1, source_target_pairs={{0,4},{4,0},{8,12},{12,8},{16,20},{20,16},{24,28},{28,24},{1,5},{5... | collective-permute-start | bytes 786440 | tf_op jit(solution)/shard_map/ppermute | solution.py:20
  37.3 1.9 %collective-permute-start.9 = (f32[256,256]{1,0:T(8,128)S(1)}, f32[256,256]{1,0:T(8,128)S(1)}, u32[]{:S(2)}, u32[]{:S(2)}) collective-permute-start(f32[256,256]{1,0:T(8,128)S(1)} %collective-permute-done.5.refs_1_), channel_id=1, source_target_pairs={{0,4},{4,0},{8,12},{12,8},{16,20},{20,16},{24,28},{28,24},{1,5},{5... | collective-permute-start | bytes 786440 | tf_op jit(solution)/shard_map/ppermute | solution.py:20
  39.7 15.7 %copy-start = (f32[1,1024,256]{2,1,0:T(8,128)S(1)}, f32[1,1024,256]{2,1,0:T(8,128)}, u32[]{:S(2)}) copy-start(f32[1,1024,256]{2,1,0:T(8,128)} %refs_8_.1) | copy-start | bytes 3145732
  39.7 15.7 %copy-start.1 = (s32[1,2]{1,0:T(1,128)S(1)}, s32[1,2]{1,0:T(1,128)}, u32[]{:S(2)}) copy-start(s32[1,2]{1,0:T(1,128)} %flags.3) | copy-start | bytes 28
  39.7 9.4 %collective-permute-start.10 = (f32[128,256]{1,0:T(8,128)S(1)}, f32[128,256]{1,0:T(8,128)S(1)}, u32[]{:S(2)}, u32[]{:S(2)}) collective-permute-start(f32[128,256]{1,0:T(8,128)S(1)} %solve.2.refs_0_), channel_id=1, source_target_pairs={{0,16},{4,20},{8,24},{12,28},{16,0},{20,4},{24,8},{28,12},{1,17},{... | collective-permute-start | bytes 393224 | tf_op jit(solution)/shard_map/ppermute | solution.py:20
  41.9 7.2 %collective-permute-start.11 = (f32[128,256]{1,0:T(8,128)S(1)}, f32[128,256]{1,0:T(8,128)S(1)}, u32[]{:S(2)}, u32[]{:S(2)}) collective-permute-start(f32[128,256]{1,0:T(8,128)S(1)} %solve.2.refs_0_), channel_id=1, source_target_pairs={{0,8},{4,12},{8,0},{12,4},{16,24},{20,28},{24,16},{28,20},{1,9},{5... | collective-permute-start | bytes 393224 | tf_op jit(solution)/shard_map/ppermute | solution.py:20
  43.6 8.2 %collective-permute-start.15 = (f32[128,256]{1,0:T(8,128)S(1)}, f32[128,256]{1,0:T(8,128)S(1)}, u32[]{:S(2)}, u32[]{:S(2)}) collective-permute-start(f32[128,256]{1,0:T(8,128)S(1)} %solve.2.refs_0_), channel_id=1, source_target_pairs={{0,4},{4,0},{8,12},{12,8},{16,20},{20,16},{24,28},{28,24},{1,5},{5... | collective-permute-start | bytes 393224 | tf_op jit(solution)/shard_map/ppermute | solution.py:20
  49.1 5.0 %collective-permute-start.14 = (f32[128,256]{1,0:T(8,128)S(1)}, f32[128,256]{1,0:T(8,128)S(1)}, u32[]{:S(2)}, u32[]{:S(2)}) collective-permute-start(f32[128,256]{1,0:T(8,128)S(1)} %collective-permute-done.10.refs_2_), channel_id=1, source_target_pairs={{0,8},{4,12},{8,0},{12,4},{16,24},{20,28},{24,16},{28,20},{1,9},{5... | collective-permute-start | bytes 393224 | tf_op jit(solution)/shard_map/ppermute | solution.py:20
  50.3 3.8 %collective-permute-start.16 = (f32[128,256]{1,0:T(8,128)S(1)}, f32[128,256]{1,0:T(8,128)S(1)}, u32[]{:S(2)}, u32[]{:S(2)}) collective-permute-start(f32[128,256]{1,0:T(8,128)S(1)} %collective-permute-done.11.refs_1_), channel_id=1, source_target_pairs={{0,4},{4,0},{8,12},{12,8},{16,20},{20,16},{24,28},{28,24},{1,5},{5... | collective-permute-start | bytes 393224 | tf_op jit(solution)/shard_map/ppermute | solution.py:20
  50.3 3.8 %collective-permute-start.17 = (f32[128,256]{1,0:T(8,128)S(1)}, f32[128,256]{1,0:T(8,128)S(1)}, u32[]{:S(2)}, u32[]{:S(2)}) collective-permute-start(f32[128,256]{1,0:T(8,128)S(1)} %collective-permute-done.10.refs_2_), channel_id=1, source_target_pairs={{0,4},{4,0},{8,12},{12,8},{16,20},{20,16},{24,28},{28,24},{1,5},{5... | collective-permute-start | bytes 393224 | tf_op jit(solution)/shard_map/ppermute | solution.py:20
  54.1 1.4 %collective-permute-start.18 = (f32[128,256]{1,0:T(8,128)S(1)}, f32[128,256]{1,0:T(8,128)S(1)}, u32[]{:S(2)}, u32[]{:S(2)}) collective-permute-start(f32[128,256]{1,0:T(8,128)S(1)} %collective-permute-done.14.refs_3_), channel_id=1, source_target_pairs={{0,4},{4,0},{8,12},{12,8},{16,20},{20,16},{24,28},{28,24},{1,5},{5... | collective-permute-start | bytes 393224 | tf_op jit(solution)/shard_map/ppermute | solution.py:20
  58.1 2.0 %collective-permute-start.19 = (f32[512,256]{1,0:T(8,128)S(1)}, f32[512,256]{1,0:T(8,128)S(1)}, u32[]{:S(2)}, u32[]{:S(2)}) collective-permute-start(f32[512,256]{1,0:T(8,128)S(1)} %get-tuple-element.95.refs_9_), channel_id=1, source_target_pairs={{0,4},{4,0},{8,12},{12,8},{16,20},{20,16},{24,28},{28,24},{1,5},{5... | collective-permute-start | bytes 1572872 | tf_op jit(solution)/shard_map/ppermute | solution.py:20
  60.2 8.6 %collective-permute-start.20 = (f32[256,256]{1,0:T(8,128)S(1)}, f32[256,256]{1,0:T(8,128)S(1)}, u32[]{:S(2)}, u32[]{:S(2)}) collective-permute-start(f32[256,256]{1,0:T(8,128)S(1)} %constant_dynamic-slice_fusion), channel_id=1, source_target_pairs={{0,8},{4,12},{8,0},{12,4},{16,24},{20,28},{24,16},{28,20},{1,9},{5... | collective-permute-start | bytes 786440 | tf_op jit(solution)/shard_map/ppermute | solution.py:20
  62.7 21.6 %collective-permute-start.22 = (f32[128,1024]{1,0:T(8,128)S(1)}, f32[128,1024]{1,0:T(8,128)S(1)}, u32[]{:S(2)}, u32[]{:S(2)}) collective-permute-start(f32[128,1024]{1,0:T(8,128)S(1)} %get-tuple-element.104.own_top), channel_id=1, source_target_pairs={{0,1},{1,0},{2,3},{3,2},{4,5},{5,4},{6,7},{7,6},{8,9},{9,8},{10,11... | collective-permute-start | bytes 1572872 | tf_op jit(solution)/shard_map/ppermute | solution.py:20
  64.3 20.1 %collective-permute-start.23 = (f32[128,1024]{1,0:T(8,128)S(1)}, f32[128,1024]{1,0:T(8,128)S(1)}, u32[]{:S(2)}, u32[]{:S(2)}) collective-permute-start(f32[128,1024]{1,0:T(8,128)S(1)} %get-tuple-element.103.own_bottom), channel_id=1, source_target_pairs={{0,2},{1,3},{2,0},{3,1},{4,6},{5,7},{6,4},{7,5},{8,10},{9,11},{10,... | collective-permute-start | bytes 1572872 | tf_op jit(solution)/shard_map/ppermute | solution.py:20
  68.9 14.4 %collective-permute-start.21 = (f32[256,256]{1,0:T(8,128)S(1)}, f32[256,256]{1,0:T(8,128)}, u32[]{:S(2)}, u32[]{:S(2)}) collective-permute-start(f32[256,256]{1,0:T(8,128)S(1)} %dynamic-slice_select_fusion), channel_id=1, source_target_pairs={{0,16},{4,20},{8,24},{12,28},{16,0},{20,4},{24,8},{28,12},{1,17},{... | collective-permute-start | bytes 786440 | tf_op jit(solution)/shard_map/ppermute | solution.py:20
  71.2 16.8 %collective-permute-start.25 = (f32[128,1024]{1,0:T(8,128)S(1)}, f32[128,1024]{1,0:T(8,128)}, u32[]{:S(2)}, u32[]{:S(2)}) collective-permute-start(f32[128,1024]{1,0:T(8,128)S(1)} %get-tuple-element.103.own_bottom), channel_id=1, source_target_pairs={{0,1},{1,0},{2,3},{3,2},{4,5},{5,4},{6,7},{7,6},{8,9},{9,8},{10,11... | collective-permute-start | bytes 1572872 | tf_op jit(solution)/shard_map/ppermute | solution.py:20
  72.7 17.8 %collective-permute-start.26 = (f32[128,1024]{1,0:T(8,128)S(1)}, f32[128,1024]{1,0:T(8,128)}, u32[]{:S(2)}, u32[]{:S(2)}) collective-permute-start(f32[128,1024]{1,0:T(8,128)S(1)} %get-tuple-element.104.own_top), channel_id=1, source_target_pairs={{0,2},{1,3},{2,0},{3,1},{4,6},{5,7},{6,4},{7,5},{8,10},{9,11},{10,... | collective-permute-start | bytes 1572872 | tf_op jit(solution)/shard_map/ppermute | solution.py:20
  84.4 7.5 %collective-permute-start.24 = (f32[256,256]{1,0:T(8,128)S(1)}, f32[256,256]{1,0:T(8,128)S(1)}, u32[]{:S(2)}, u32[]{:S(2)}) collective-permute-start(f32[256,256]{1,0:T(8,128)S(1)} %broadcast_select_fusion.3.refs_0_), channel_id=1, source_target_pairs={{0,8},{4,12},{8,0},{12,4},{16,24},{20,28},{24,16},{28,20},{1,9},{5... | collective-permute-start | bytes 786440 | tf_op jit(solution)/shard_map/ppermute | solution.py:20
  84.6 15.8 %collective-permute-start.31 = (f32[128,1024]{1,0:T(8,128)S(1)}, f32[128,1024]{1,0:T(8,128)S(1)}, u32[]{:S(2)}, u32[]{:S(2)}) collective-permute-start(f32[128,1024]{1,0:T(8,128)S(1)} %collective-permute-done.22.refs_0_), channel_id=1, source_target_pairs={{0,2},{1,3},{2,0},{3,1},{4,6},{5,7},{6,4},{7,5},{8,10},{9,11},{10,... | collective-permute-start | bytes 1572872 | tf_op jit(solution)/shard_map/ppermute | solution.py:20
  86.2 14.2 %collective-permute-start.32 = (f32[128,1024]{1,0:T(8,128)S(1)}, f32[128,1024]{1,0:T(8,128)S(1)}, u32[]{:S(2)}, u32[]{:S(2)}) collective-permute-start(f32[128,1024]{1,0:T(8,128)S(1)} %collective-permute-done.23.refs_1_), channel_id=1, source_target_pairs={{0,1},{1,0},{2,3},{3,2},{4,5},{5,4},{6,7},{7,6},{8,9},{9,8},{10,11... | collective-permute-start | bytes 1572872 | tf_op jit(solution)/shard_map/ppermute | solution.py:20
  91.8 1.6 %collective-permute-start.27 = (f32[256,256]{1,0:T(8,128)S(1)}, f32[256,256]{1,0:T(8,128)S(1)}, u32[]{:S(2)}, u32[]{:S(2)}) collective-permute-start(f32[256,256]{1,0:T(8,128)S(1)} %broadcast_select_fusion.3.refs_0_), channel_id=1, source_target_pairs={{0,4},{4,0},{8,12},{12,8},{16,20},{20,16},{24,28},{28,24},{1,5},{5... | collective-permute-start | bytes 786440 | tf_op jit(solution)/shard_map/ppermute | solution.py:20
  91.8 1.9 %collective-permute-start.28 = (f32[256,256]{1,0:T(8,128)S(1)}, f32[256,256]{1,0:T(8,128)S(1)}, u32[]{:S(2)}, u32[]{:S(2)}) collective-permute-start(f32[256,256]{1,0:T(8,128)S(1)} %collective-permute-done.24.refs_1_), channel_id=1, source_target_pairs={{0,4},{4,0},{8,12},{12,8},{16,20},{20,16},{24,28},{28,24},{1,5},{5... | collective-permute-start | bytes 786440 | tf_op jit(solution)/shard_map/ppermute | solution.py:20
  94.2 9.4 %collective-permute-start.29 = (f32[128,256]{1,0:T(8,128)S(1)}, f32[128,256]{1,0:T(8,128)S(1)}, u32[]{:S(2)}, u32[]{:S(2)}) collective-permute-start(f32[128,256]{1,0:T(8,128)S(1)} %solve.3.refs_0_), channel_id=1, source_target_pairs={{0,16},{4,20},{8,24},{12,28},{16,0},{20,4},{24,8},{28,12},{1,17},{... | collective-permute-start | bytes 393224 | tf_op jit(solution)/shard_map/ppermute | solution.py:20
  96.1 7.5 %collective-permute-start.30 = (f32[128,256]{1,0:T(8,128)S(1)}, f32[128,256]{1,0:T(8,128)S(1)}, u32[]{:S(2)}, u32[]{:S(2)}) collective-permute-start(f32[128,256]{1,0:T(8,128)S(1)} %solve.3.refs_0_), channel_id=1, source_target_pairs={{0,8},{4,12},{8,0},{12,4},{16,24},{20,28},{24,16},{28,20},{1,9},{5... | collective-permute-start | bytes 393224 | tf_op jit(solution)/shard_map/ppermute | solution.py:20
  97.9 9.0 %collective-permute-start.34 = (f32[128,256]{1,0:T(8,128)S(1)}, f32[128,256]{1,0:T(8,128)S(1)}, u32[]{:S(2)}, u32[]{:S(2)}) collective-permute-start(f32[128,256]{1,0:T(8,128)S(1)} %solve.3.refs_0_), channel_id=1, source_target_pairs={{0,4},{4,0},{8,12},{12,8},{16,20},{20,16},{24,28},{28,24},{1,5},{5... | collective-permute-start | bytes 393224 | tf_op jit(solution)/shard_map/ppermute | solution.py:20
  103.6 5.0 %collective-permute-start.33 = (f32[128,256]{1,0:T(8,128)S(1)}, f32[128,256]{1,0:T(8,128)S(1)}, u32[]{:S(2)}, u32[]{:S(2)}) collective-permute-start(f32[128,256]{1,0:T(8,128)S(1)} %collective-permute-done.29.refs_2_), channel_id=1, source_target_pairs={{0,8},{4,12},{8,0},{12,4},{16,24},{20,28},{24,16},{28,20},{1,9},{5... | collective-permute-start | bytes 393224 | tf_op jit(solution)/shard_map/ppermute | solution.py:20
  104.5 4.1 %collective-permute-start.35 = (f32[128,256]{1,0:T(8,128)S(1)}, f32[128,256]{1,0:T(8,128)S(1)}, u32[]{:S(2)}, u32[]{:S(2)}) collective-permute-start(f32[128,256]{1,0:T(8,128)S(1)} %collective-permute-done.30.refs_1_), channel_id=1, source_target_pairs={{0,4},{4,0},{8,12},{12,8},{16,20},{20,16},{24,28},{28,24},{1,5},{5... | collective-permute-start | bytes 393224 | tf_op jit(solution)/shard_map/ppermute | solution.py:20
  104.5 4.1 %collective-permute-start.36 = (f32[128,256]{1,0:T(8,128)S(1)}, f32[128,256]{1,0:T(8,128)S(1)}, u32[]{:S(2)}, u32[]{:S(2)}) collective-permute-start(f32[128,256]{1,0:T(8,128)S(1)} %collective-permute-done.29.refs_2_), channel_id=1, source_target_pairs={{0,4},{4,0},{8,12},{12,8},{16,20},{20,16},{24,28},{28,24},{1,5},{5... | collective-permute-start | bytes 393224 | tf_op jit(solution)/shard_map/ppermute | solution.py:20
  108.6 1.4 %collective-permute-start.37 = (f32[128,256]{1,0:T(8,128)S(1)}, f32[128,256]{1,0:T(8,128)S(1)}, u32[]{:S(2)}, u32[]{:S(2)}) collective-permute-start(f32[128,256]{1,0:T(8,128)S(1)} %collective-permute-done.33.refs_3_), channel_id=1, source_target_pairs={{0,4},{4,0},{8,12},{12,8},{16,20},{20,16},{24,28},{28,24},{1,5},{5... | collective-permute-start | bytes 393224 | tf_op jit(solution)/shard_map/ppermute | solution.py:20

commit v5 on v4

--- a/solution.py
+++ b/solution.py
@@ -147,30 +147,31 @@
 
 
 def solve_body(inverse, *refs):
-    quarters, (out, y) = refs[:4], refs[4:]
-    rank = lax.axis_index("row")
-    size = quarters[0].shape[0]
+    chunks, (out, y) = refs[:8], refs[8:]
+    rank = lax.axis_index("row")
+    size = chunks[0].shape[0]
     core, z = bit(rank, 0), bit(rank, 1)
-    for index, ref in enumerate(quarters):
-        place = (core ^ (index >> 1)) * 2 + (z ^ (index & 1))
+    for index, ref in enumerate(chunks):
+        quarter = (core ^ (index >> 2)) * 2 + (z ^ ((index >> 1) & 1))
+        place = quarter * 2 + (index & 1)
         y[pl.ds(pl.multiple_of(place * size, size), size)] = ref[...]
     out[...] = dot3(split(inverse[...]), split(y[...]))
 
 
-def solve(inverse, quarters):
+def solve(inverse, chunks):
     rows, depth = inverse.shape
-    cols = quarters[0].shape[1]
+    cols = chunks[0].shape[1]
     vmem = pl.BlockSpec(memory_space=pltpu.VMEM)
     return pl.pallas_call(
         solve_body,
         out_shape=jax.ShapeDtypeStruct((rows, cols), jnp.float32),
-        in_specs=[vmem] * 5,
+        in_specs=[vmem] * 9,
         out_specs=vmem,
         scratch_shapes=[pltpu.VMEM((depth, cols), jnp.float32)],
         compiler_params=pltpu.CompilerParams(vmem_limit_bytes=UPDATE_BYTES),
         cost_estimate=pl.CostEstimate(flops=2 * rows * depth * cols, bytes_accessed=4 * rows * cols, transcendentals=0),
         name="solve",
-    )(inverse, *quarters)
+    )(inverse, *chunks)
 
 
 def update(step, flags, slot_block, pair, blocks, current):
@@ -236,16 +237,21 @@
         y, panel = tie(y, panel)
         block = tie(*block_halves(panel, step))
         first = near(*block)
-        y = scatter_step(y, 1, rows, owner, rank)
-        y, *block = tie(y, *block)
+        keep, send = halves(y, bit(rank, 1))
+        size = keep.shape[0] // 2
+        parts = tie(*[half[start:start + size] for half in (send, keep) for start in (0, size)])
+        own = []
+        for send, keep in zip(parts[:2], parts[2:]):
+            own.append(jnp.where(bit(owner, 1) == bit(rank, 1), keep, swap(send, "row", 1, rows)))
+        own[1], *block = tie(own[1], *block)
         second = near(*block[::-1])
-        y = cross_step(y, 2, rows, owner, rank)
-        y, inverse, *first = tie(y, diag_inverse, *first)
+        own = [cross_step(chunk, 2, rows, owner, rank) for chunk in own]
+        own[1], *first = tie(own[1], *first)
         pieces = far(*first)
-        beside = swap(y, "row", 1, rows)
-        beside, y, *second = tie(beside, y, *second)
-        other, last = swap(y, "row", 0, rows), swap(beside, "row", 0, rows)
-        x = solve(inverse[step], [y, beside, other, last])
+        own[0], inverse = tie(own[0], diag_inverse)
+        beside = [swap(chunk, "row", 1, rows) for chunk in own]
+        *chunks, second[0], second[1] = tie(*own, *beside, *second)
+        x = solve(inverse[step], chunks + [swap(chunk, "row", 0, rows) for chunk in chunks])
         x2, x1 = swap(x, "row", 2, rows), swap(x, "row", 1, rows)
         x2, x1, *pieces = tie(x2, x1, *pieces)
         high, low = prepare([*block, *first, *second, *pieces])

time: 114 us -> 122 us (1.070)
  waiting for transfers between devices: 50.1 us -> 63.7 us
  local copies, waits for them, and re-layouts: 5.8 us -> 2.55 us
  starting transfers between devices: 40.4 us -> 39.1 us
    ppermute x38 -> x48, waiting for transfers between devices: 50.1 us -> 63.7 us  [swap(): return lax.ppermute(x, axis, [(i, i ^ 1 << b) for i in range(size)])]
    squeeze x2, local copies, waits for them, and re-layouts: 2.15 us -> 0.07 us  [solved(): inverse[step]]
    select_n x2 -> x4, other arithmetic: 1.96 us -> 0.07 us  [cross_step(): return jnp.where(bit(owner, b) == bit(me, b), x, swap(x, 'row', b, size))]
    ppermute x38 -> x48, starting transfers between devices: 40.4 us -> 39.1 us  [swap(): return lax.ppermute(x, axis, [(i, i ^ 1 << b) for i in range(size)])]
    squeeze x2, local copies, waits for them, and re-layouts: 1.37 us -> 0.14 us  [block_halves(): return (panel[0, step, :half], panel[0, step, half:])]
  transfers between devices with their start and end apart: 38 -> 48, of which waited for: 18 -> 25; matrix products, arithmetic and copies ran while one was open for 6% -> 1% of each run, Pallas kernels for 3% -> 3%
where the time goes in v5:
time: 122 us; the launch traced here: 121 us
  waiting for transfers between devices  63.7 us (52%)
  starting transfers between devices  39.1 us (32%)
  Pallas kernels  9.16 us (8%)
  between operations  4.13 us (3%)
  other arithmetic  2.68 us (2%)
  local copies, waits for them, and re-layouts  2.55 us (2%)
    ppermute x48, waiting for transfers between devices, swap(): return lax.ppermute(x, axis, [(i, i ^ 1 << b) for i in range(size)])  63.7 us
    ppermute x48, starting transfers between devices, swap(): return lax.ppermute(x, axis, [(i, i ^ 1 << b) for i in range(size)])  39.1 us
    pallas_call x2, Pallas kernels, update(): pl.pallas_call(first_body if step == 0 else second_body, out_shape=[jax.S...  6.07 us
  transfers between devices with their start and end apart: 48, of which 25 were waited for; matrix products, arithmetic and copies ran while one was open for 1% of the time, Pallas kernels for 3%

profile of v5, /device:TPU:0, one launch (start us, length us, event | category | flops | bytes accessed | tf_op | source)
XLA Modules:
  0.0 121.4 jit_solution(11790273096796913012)
XLA Ops:
  0.0 2.2 %dynamic-slice_bitcast_fusion = (f32[512,256]{1,0:T(8,128)}, f32[512,256]{1,0:T(8,128)S(1)}) fusion(f32[1,1024,256]{2,1,0:T(8,128)} %refs_8_.1, s32[]{:T(128)S(6)} %select_n.83, s32[]{:T(128)S(6)} %select_n.82), kind=kLoop, calls=%fused_computation.6 | loop fusion | bytes 2097160 | tf_op jit(solution)/shard_map/dynamic_slice | solution.py:33
  2.7 0.7 compare_reduce_fusion
  5.5 2.6 %collective-permute-start.3 = (f32[128,256]{1,0:T(8,128)S(1)}, f32[128,256]{1,0:T(8,128)S(1)}, u32[]{:S(2)}, u32[]{:S(2)}) collective-permute-start(f32[128,256]{1,0:T(8,128)S(1)} %get-tuple-element.87), channel_id=1, source_target_pairs={{0,8},{4,12},{8,0},{12,4},{16,24},{20,28},{24,16},{28,20},{1,9},{5... | collective-permute-start | bytes 393224 | tf_op jit(solution)/shard_map/ppermute | solution.py:20
  8.2 1.9 %collective-permute-start.5 = (f32[128,1024]{1,0:T(8,128)S(1)}, f32[128,1024]{1,0:T(8,128)S(1)}, u32[]{:S(2)}, u32[]{:S(2)}) collective-permute-start(f32[128,1024]{1,0:T(8,128)S(1)} %get-tuple-element.94.own_top), channel_id=1, source_target_pairs={{0,1},{1,0},{2,3},{3,2},{4,5},{5,4},{6,7},{7,6},{8,9},{9,8},{10,11... | collective-permute-start | bytes 1572872 | tf_op jit(solution)/shard_map/ppermute | solution.py:20
  10.2 1.5 %collective-permute-start.6 = (f32[128,1024]{1,0:T(8,128)S(1)}, f32[128,1024]{1,0:T(8,128)S(1)}, u32[]{:S(2)}, u32[]{:S(2)}) collective-permute-start(f32[128,1024]{1,0:T(8,128)S(1)} %get-tuple-element.93.own_bottom), channel_id=1, source_target_pairs={{0,2},{1,3},{2,0},{3,1},{4,6},{5,7},{6,4},{7,5},{8,10},{9,11},{10,... | collective-permute-start | bytes 1572872 | tf_op jit(solution)/shard_map/ppermute | solution.py:20
  11.7 3.4 %collective-permute-done.1 = f32[128,256]{1,0:T(8,128)S(1)} collective-permute-done((f32[128,256]{1,0:T(8,128)S(1)}, f32[128,256]{1,0:T(8,128)S(1)}, u32[]{:S(2)}, u32[]{:S(2)}) %collective-permute-start.1) | collective-permute-done | bytes 131104 | tf_op jit(solution)/shard_map/ppermute | solution.py:20
  15.1 2.8 %collective-permute-start.2 = (f32[128,256]{1,0:T(8,128)S(1)}, f32[128,256]{1,0:T(8,128)S(1)}, u32[]{:S(2)}, u32[]{:S(2)}) collective-permute-start(f32[128,256]{1,0:T(8,128)S(1)} %broadcast_select_fusion.3), channel_id=1, source_target_pairs={{0,16},{4,20},{8,24},{12,28},{16,0},{20,4},{24,8},{28,12},{1,17},{... | collective-permute-start | bytes 393224 | tf_op jit(solution)/shard_map/ppermute | solution.py:20
  18.2 1.7 %collective-permute-start.10 = (f32[128,1024]{1,0:T(8,128)S(1)}, f32[128,1024]{1,0:T(8,128)S(1)}, u32[]{:S(2)}, u32[]{:S(2)}) collective-permute-start(f32[128,1024]{1,0:T(8,128)S(1)} %get-tuple-element.94.own_top), channel_id=1, source_target_pairs={{0,2},{1,3},{2,0},{3,1},{4,6},{5,7},{6,4},{7,5},{8,10},{9,11},{10,... | collective-permute-start | bytes 1572872 | tf_op jit(solution)/shard_map/ppermute | solution.py:20
  19.9 8.2 %collective-permute-done.2 = f32[128,256]{1,0:T(8,128)S(1)} collective-permute-done((f32[128,256]{1,0:T(8,128)S(1)}, f32[128,256]{1,0:T(8,128)S(1)}, u32[]{:S(2)}, u32[]{:S(2)}) %collective-permute-start.2) | collective-permute-done | bytes 131104 | tf_op jit(solution)/shard_map/ppermute | solution.py:20
  28.0 1.6 %collective-permute-start.9 = (f32[128,1024]{1,0:T(8,128)S(1)}, f32[128,1024]{1,0:T(8,128)S(1)}, u32[]{:S(2)}, u32[]{:S(2)}) collective-permute-start(f32[128,1024]{1,0:T(8,128)S(1)} %get-tuple-element.93.own_bottom), channel_id=1, source_target_pairs={{0,1},{1,0},{2,3},{3,2},{4,5},{5,4},{6,7},{7,6},{8,9},{9,8},{10,11... | collective-permute-start | bytes 1572872 | tf_op jit(solution)/shard_map/ppermute | solution.py:20
  29.8 0.6 collective-permute-start.7
  30.5 1.5 %collective-permute-start.8 = (f32[128,256]{1,0:T(8,128)S(1)}, f32[128,256]{1,0:T(8,128)S(1)}, u32[]{:S(2)}, u32[]{:S(2)}) collective-permute-start(f32[128,256]{1,0:T(8,128)S(1)} %broadcast_select_fusion.4.refs_1_), channel_id=1, source_target_pairs={{0,8},{4,12},{8,0},{12,4},{16,24},{20,28},{24,16},{28,20},{1,9},{5... | collective-permute-start | bytes 393224 | tf_op jit(solution)/shard_map/ppermute | solution.py:20
  31.9 1.5 %collective-permute-start.17 = (f32[128,1024]{1,0:T(8,128)S(1)}, f32[128,1024]{1,0:T(8,128)S(1)}, u32[]{:S(2)}, u32[]{:S(2)}) collective-permute-start(f32[128,1024]{1,0:T(8,128)S(1)} %collective-permute-done.5.refs_0_), channel_id=1, source_target_pairs={{0,2},{1,3},{2,0},{3,1},{4,6},{5,7},{6,4},{7,5},{8,10},{9,11},{10,... | collective-permute-start | bytes 1572872 | tf_op jit(solution)/shard_map/ppermute | solution.py:20
  33.4 2.3 %collective-permute-done.7.refs_2_ = f32[128,256]{1,0:T(8,128)S(1)} collective-permute-done((f32[128,256]{1,0:T(8,128)S(1)}, f32[128,256]{1,0:T(8,128)S(1)}, u32[]{:S(2)}, u32[]{:S(2)}) %collective-permute-start.7) | collective-permute-done | bytes 131104 | tf_op jit(solution)/shard_map/ppermute | solution.py:20
  35.7 1.5 %collective-permute-start.18 = (f32[128,1024]{1,0:T(8,128)S(1)}, f32[128,1024]{1,0:T(8,128)S(1)}, u32[]{:S(2)}, u32[]{:S(2)}) collective-permute-start(f32[128,1024]{1,0:T(8,128)S(1)} %collective-permute-done.6.refs_1_), channel_id=1, source_target_pairs={{0,1},{1,0},{2,3},{3,2},{4,5},{5,4},{6,7},{7,6},{8,9},{9,8},{10,11... | collective-permute-start | bytes 1572872 | tf_op jit(solution)/shard_map/ppermute | solution.py:20
  37.2 5.7 %collective-permute-done.9.refs_2_ = f32[128,1024]{1,0:T(8,128)S(1)} collective-permute-done((f32[128,1024]{1,0:T(8,128)S(1)}, f32[128,1024]{1,0:T(8,128)S(1)}, u32[]{:S(2)}, u32[]{:S(2)}) %collective-permute-start.9) | collective-permute-done | bytes 524320 | tf_op jit(solution)/shard_map/ppermute | solution.py:20
  43.4 0.8 collective-permute-done.11.refs_4_
  44.8 0.8 collective-permute-done.14.refs_7_
  46.2 3.0 %collective-permute-start.16 = (f32[128,256]{1,0:T(8,128)S(1)}, f32[128,256]{1,0:T(8,128)S(1)}, u32[]{:S(2)}, u32[]{:S(2)}) collective-permute-start(f32[128,256]{1,0:T(8,128)S(1)} %solve.2.refs_0_), channel_id=1, source_target_pairs={{0,8},{4,12},{8,0},{12,4},{16,24},{20,28},{24,16},{28,20},{1,9},{5... | collective-permute-start | bytes 393224 | tf_op jit(solution)/shard_map/ppermute | solution.py:20
  49.2 6.2 %collective-permute-done.15.refs_2_ = f32[128,256]{1,0:T(8,128)S(1)} collective-permute-done((f32[128,256]{1,0:T(8,128)S(1)}, f32[128,256]{1,0:T(8,128)S(1)}, u32[]{:S(2)}, u32[]{:S(2)}) %collective-permute-start.15) | collective-permute-done | bytes 131104 | tf_op jit(solution)/shard_map/ppermute | solution.py:20
  56.1 1.1 prepare.2
  57.2 3.6 %collective-permute-done.19.refs_3_ = f32[128,256]{1,0:T(8,128)S(1)} collective-permute-done((f32[128,256]{1,0:T(8,128)S(1)}, f32[128,256]{1,0:T(8,128)S(1)}, u32[]{:S(2)}, u32[]{:S(2)}) %collective-permute-start.19) | collective-permute-done | bytes 131104 | tf_op jit(solution)/shard_map/ppermute | solution.py:20
  60.8 1.3 %collective-permute-done.23.refs_7_ = f32[128,256]{1,0:T(8,128)S(1)} collective-permute-done((f32[128,256]{1,0:T(8,128)S(1)}, f32[128,256]{1,0:T(8,128)S(1)}, u32[]{:S(2)}, u32[]{:S(2)}) %collective-permute-start.23) | collective-permute-done | bytes 131104 | tf_op jit(solution)/shard_map/ppermute | solution.py:20
  62.2 2.7 %update.2 = (f32[512,256]{1,0:T(8,128)S(1)}, f32[512,256]{1,0:T(8,128)S(1)}) custom-call(s32[1,2]{1,0:T(1,128)S(1)} %copy-done.1, s32[8]{0:T(128)S(1)} %copy-done.2, bf16[1024,1024]{1,0:T(8,128)(2,1)S(1)} %get-tuple-element.109.high, bf16[1024,1024]{1,0:T(8,128)(2,1)S(1)} %get-tuple-element.110.low, f32[128,256]{1,0:T(8,128)S(1)} %solve.2.refs_0_, ...), custom_call_target="tpu_custom_call" | custom-call | flops 1610612736 | bytes 7340032 | tf_op jit(solution)/shard_map/update/pallas_call | solution.py:185
  65.1 0.7 compare_reduce_fusion.1
  67.6 1.1 broadcast_select_fusion.1
  69.2 1.6 %collective-permute-start.29 = (f32[128,1024]{1,0:T(8,128)S(1)}, f32[128,1024]{1,0:T(8,128)S(1)}, u32[]{:S(2)}, u32[]{:S(2)}) collective-permute-start(f32[128,1024]{1,0:T(8,128)S(1)} %get-tuple-element.130.own_top), channel_id=1, source_target_pairs={{0,1},{1,0},{2,3},{3,2},{4,5},{5,4},{6,7},{7,6},{8,9},{9,8},{10,11... | collective-permute-start | bytes 1572872 | tf_op jit(solution)/shard_map/ppermute | solution.py:20
  70.8 1.5 %collective-permute-start.30 = (f32[128,1024]{1,0:T(8,128)S(1)}, f32[128,1024]{1,0:T(8,128)S(1)}, u32[]{:S(2)}, u32[]{:S(2)}) collective-permute-start(f32[128,1024]{1,0:T(8,128)S(1)} %get-tuple-element.129.own_bottom), channel_id=1, source_target_pairs={{0,2},{1,3},{2,0},{3,1},{4,6},{5,7},{6,4},{7,5},{8,10},{9,11},{10,... | collective-permute-start | bytes 1572872 | tf_op jit(solution)/shard_map/ppermute | solution.py:20
  72.3 1.7 %collective-permute-start.27 = (f32[128,256]{1,0:T(8,128)S(1)}, f32[128,256]{1,0:T(8,128)S(1)}, u32[]{:S(2)}, u32[]{:S(2)}) collective-permute-start(f32[128,256]{1,0:T(8,128)S(1)} %get-tuple-element.123), channel_id=1, source_target_pairs={{0,8},{4,12},{8,0},{12,4},{16,24},{20,28},{24,16},{28,20},{1,9},{5... | collective-permute-start | bytes 393224 | tf_op jit(solution)/shard_map/ppermute | solution.py:20
  74.4 3.3 %collective-permute-done.27 = f32[128,256]{1,0:T(8,128)S(1)} collective-permute-done((f32[128,256]{1,0:T(8,128)S(1)}, f32[128,256]{1,0:T(8,128)S(1)}, u32[]{:S(2)}, u32[]{:S(2)}) %collective-permute-start.27) | collective-permute-done | bytes 131104 | tf_op jit(solution)/shard_map/ppermute | solution.py:20
  77.7 1.7 %collective-permute-start.28 = (f32[128,256]{1,0:T(8,128)S(1)}, f32[128,256]{1,0:T(8,128)S(1)}, u32[]{:S(2)}, u32[]{:S(2)}) collective-permute-start(f32[128,256]{1,0:T(8,128)S(1)} %broadcast_select_fusion.6), channel_id=1, source_target_pairs={{0,16},{4,20},{8,24},{12,28},{16,0},{20,4},{24,8},{28,12},{1,17},{... | collective-permute-start | bytes 393224 | tf_op jit(solution)/shard_map/ppermute | solution.py:20
  79.5 0.8 collective-permute-start.33
  80.3 5.6 %collective-permute-done.26 = f32[128,256]{1,0:T(8,128)S(1)} collective-permute-done((f32[128,256]{1,0:T(8,128)S(1)}, f32[128,256]{1,0:T(8,128)S(1)}, u32[]{:S(2)}, u32[]{:S(2)}) %collective-permute-start.26) | collective-permute-done | bytes 131104 | tf_op jit(solution)/shard_map/ppermute | solution.py:20
  85.8 1.4 %collective-permute-start.34 = (f32[128,1024]{1,0:T(8,128)S(1)}, f32[128,1024]{1,0:T(8,128)S(1)}, u32[]{:S(2)}, u32[]{:S(2)}) collective-permute-start(f32[128,1024]{1,0:T(8,128)S(1)} %get-tuple-element.130.own_top), channel_id=1, source_target_pairs={{0,2},{1,3},{2,0},{3,1},{4,6},{5,7},{6,4},{7,5},{8,10},{9,11},{10,... | collective-permute-start | bytes 1572872 | tf_op jit(solution)/shard_map/ppermute | solution.py:20
  87.4 2.1 %collective-permute-start.32 = (f32[128,256]{1,0:T(8,128)S(1)}, f32[128,256]{1,0:T(8,128)S(1)}, u32[]{:S(2)}, u32[]{:S(2)}) collective-permute-start(f32[128,256]{1,0:T(8,128)S(1)} %broadcast_select_fusion.8.refs_1_), channel_id=1, source_target_pairs={{0,8},{4,12},{8,0},{12,4},{16,24},{20,28},{24,16},{28,20},{1,9},{5... | collective-permute-start | bytes 393224 | tf_op jit(solution)/shard_map/ppermute | solution.py:20
  89.4 1.3 %collective-permute-start.41 = (f32[128,1024]{1,0:T(8,128)S(1)}, f32[128,1024]{1,0:T(8,128)S(1)}, u32[]{:S(2)}, u32[]{:S(2)}) collective-permute-start(f32[128,1024]{1,0:T(8,128)S(1)} %collective-permute-done.29.refs_0_), channel_id=1, source_target_pairs={{0,2},{1,3},{2,0},{3,1},{4,6},{5,7},{6,4},{7,5},{8,10},{9,11},{10,... | collective-permute-start | bytes 1572872 | tf_op jit(solution)/shard_map/ppermute | solution.py:20
  90.7 2.0 %collective-permute-done.31.refs_2_ = f32[128,256]{1,0:T(8,128)S(1)} collective-permute-done((f32[128,256]{1,0:T(8,128)S(1)}, f32[128,256]{1,0:T(8,128)S(1)}, u32[]{:S(2)}, u32[]{:S(2)}) %collective-permute-start.31) | collective-permute-done | bytes 131104 | tf_op jit(solution)/shard_map/ppermute | solution.py:20
  92.8 1.3 %collective-permute-start.42 = (f32[128,1024]{1,0:T(8,128)S(1)}, f32[128,1024]{1,0:T(8,128)S(1)}, u32[]{:S(2)}, u32[]{:S(2)}) collective-permute-start(f32[128,1024]{1,0:T(8,128)S(1)} %collective-permute-done.30.refs_1_), channel_id=1, source_target_pairs={{0,1},{1,0},{2,3},{3,2},{4,5},{5,4},{6,7},{7,6},{8,9},{9,8},{10,11... | collective-permute-start | bytes 1572872 | tf_op jit(solution)/shard_map/ppermute | solution.py:20
  94.2 5.8 %collective-permute-done.34.refs_3_ = f32[128,1024]{1,0:T(8,128)S(1)} collective-permute-done((f32[128,1024]{1,0:T(8,128)S(1)}, f32[128,1024]{1,0:T(8,128)S(1)}, u32[]{:S(2)}, u32[]{:S(2)}) %collective-permute-start.34) | collective-permute-done | bytes 524320 | tf_op jit(solution)/shard_map/ppermute | solution.py:20
  100.5 0.8 collective-permute-done.35.refs_4_
  101.8 0.8 collective-permute-done.38.refs_7_
  103.5 0.9 collective-permute-start.40
  104.4 6.5 %collective-permute-done.39.refs_2_ = f32[128,256]{1,0:T(8,128)S(1)} collective-permute-done((f32[128,256]{1,0:T(8,128)S(1)}, f32[128,256]{1,0:T(8,128)S(1)}, u32[]{:S(2)}, u32[]{:S(2)}) %collective-permute-start.39) | collective-permute-done | bytes 131104 | tf_op jit(solution)/shard_map/ppermute | solution.py:20
  110.9 0.8 collective-permute-done.40.refs_1_
  112.4 1.1 prepare.3
  113.5 3.1 %collective-permute-done.43.refs_3_ = f32[128,256]{1,0:T(8,128)S(1)} collective-permute-done((f32[128,256]{1,0:T(8,128)S(1)}, f32[128,256]{1,0:T(8,128)S(1)}, u32[]{:S(2)}, u32[]{:S(2)}) %collective-permute-start.43) | collective-permute-done | bytes 131104 | tf_op jit(solution)/shard_map/ppermute | solution.py:20
  116.6 1.3 %collective-permute-done.47.refs_7_ = f32[128,256]{1,0:T(8,128)S(1)} collective-permute-done((f32[128,256]{1,0:T(8,128)S(1)}, f32[128,256]{1,0:T(8,128)S(1)}, u32[]{:S(2)}, u32[]{:S(2)}) %collective-permute-start.47) | collective-permute-done | bytes 131104 | tf_op jit(solution)/shard_map/ppermute | solution.py:20
  118.0 3.4 %update.3 = f32[1024,256]{1,0:T(8,128)} custom-call(s32[1,2]{1,0:T(1,128)S(1)} %copy-done.1, s32[8]{0:T(128)S(1)} %copy-done.2, bf16[1024,1024]{1,0:T(8,128)(2,1)S(1)} %get-tuple-element.145.high, bf16[1024,1024]{1,0:T(8,128)(2,1)S(1)} %get-tuple-element.146.low, f32[128,256]{1,0:T(8,128)S(1)} %solve.3.refs_0_, ...), custom_call_target="tpu_custom_call" | custom-call | flops 1610612736 | bytes 7340032 | tf_op jit(solution)/shard_map/update/pallas_call | solution.py:185
  (85 shorter events, 7.5 us)
Async XLA Ops:
  2.2 3.1 %collective-permute-start = (f32[512,256]{1,0:T(8,128)}, f32[512,256]{1,0:T(8,128)S(1)}, u32[]{:S(2)}, u32[]{:S(2)}) collective-permute-start(f32[512,256]{1,0:T(8,128)} %get-tuple-element.155), channel_id=1, source_target_pairs={{0,4},{4,0},{8,12},{12,8},{16,20},{20,16},{24,28},{28,24},{1,5},{5... | collective-permute-start | bytes 1572872 | tf_op jit(solution)/shard_map/ppermute | solution.py:20
  5.5 12.5 %collective-permute-start.3 = (f32[128,256]{1,0:T(8,128)S(1)}, f32[128,256]{1,0:T(8,128)S(1)}, u32[]{:S(2)}, u32[]{:S(2)}) collective-permute-start(f32[128,256]{1,0:T(8,128)S(1)} %get-tuple-element.87), channel_id=1, source_target_pairs={{0,8},{4,12},{8,0},{12,4},{16,24},{20,28},{24,16},{28,20},{1,9},{5... | collective-permute-start | bytes 393224 | tf_op jit(solution)/shard_map/ppermute | solution.py:20
  8.1 7.0 %collective-permute-start.1 = (f32[128,256]{1,0:T(8,128)S(1)}, f32[128,256]{1,0:T(8,128)S(1)}, u32[]{:S(2)}, u32[]{:S(2)}) collective-permute-start(f32[128,256]{1,0:T(8,128)S(1)} %get-tuple-element.83), channel_id=1, source_target_pairs={{0,8},{4,12},{8,0},{12,4},{16,24},{20,28},{24,16},{28,20},{1,9},{5... | collective-permute-start | bytes 393224 | tf_op jit(solution)/shard_map/ppermute | solution.py:20
  8.2 22.2 %collective-permute-start.5 = (f32[128,1024]{1,0:T(8,128)S(1)}, f32[128,1024]{1,0:T(8,128)S(1)}, u32[]{:S(2)}, u32[]{:S(2)}) collective-permute-start(f32[128,1024]{1,0:T(8,128)S(1)} %get-tuple-element.94.own_top), channel_id=1, source_target_pairs={{0,1},{1,0},{2,3},{3,2},{4,5},{5,4},{6,7},{7,6},{8,9},{9,8},{10,11... | collective-permute-start | bytes 1572872 | tf_op jit(solution)/shard_map/ppermute | solution.py:20
  10.2 20.3 %collective-permute-start.6 = (f32[128,1024]{1,0:T(8,128)S(1)}, f32[128,1024]{1,0:T(8,128)S(1)}, u32[]{:S(2)}, u32[]{:S(2)}) collective-permute-start(f32[128,1024]{1,0:T(8,128)S(1)} %get-tuple-element.93.own_bottom), channel_id=1, source_target_pairs={{0,2},{1,3},{2,0},{3,1},{4,6},{5,7},{6,4},{7,5},{8,10},{9,11},{10,... | collective-permute-start | bytes 1572872 | tf_op jit(solution)/shard_map/ppermute | solution.py:20
  15.1 12.9 %collective-permute-start.2 = (f32[128,256]{1,0:T(8,128)S(1)}, f32[128,256]{1,0:T(8,128)S(1)}, u32[]{:S(2)}, u32[]{:S(2)}) collective-permute-start(f32[128,256]{1,0:T(8,128)S(1)} %broadcast_select_fusion.3), channel_id=1, source_target_pairs={{0,16},{4,20},{8,24},{12,28},{16,0},{20,4},{24,8},{28,12},{1,17},{... | collective-permute-start | bytes 393224 | tf_op jit(solution)/shard_map/ppermute | solution.py:20
  17.9 11.9 %collective-permute-start.4 = (f32[128,256]{1,0:T(8,128)S(1)}, f32[128,256]{1,0:T(8,128)S(1)}, u32[]{:S(2)}, u32[]{:S(2)}) collective-permute-start(f32[128,256]{1,0:T(8,128)S(1)} %broadcast_select_fusion.2), channel_id=1, source_target_pairs={{0,16},{4,20},{8,24},{12,28},{16,0},{20,4},{24,8},{28,12},{1,17},{... | collective-permute-start | bytes 393224 | tf_op jit(solution)/shard_map/ppermute | solution.py:20
  18.2 19.0 %collective-permute-start.10 = (f32[128,1024]{1,0:T(8,128)S(1)}, f32[128,1024]{1,0:T(8,128)S(1)}, u32[]{:S(2)}, u32[]{:S(2)}) collective-permute-start(f32[128,1024]{1,0:T(8,128)S(1)} %get-tuple-element.94.own_top), channel_id=1, source_target_pairs={{0,2},{1,3},{2,0},{3,1},{4,6},{5,7},{6,4},{7,5},{8,10},{9,11},{10,... | collective-permute-start | bytes 1572872 | tf_op jit(solution)/shard_map/ppermute | solution.py:20
  28.0 14.9 %collective-permute-start.9 = (f32[128,1024]{1,0:T(8,128)S(1)}, f32[128,1024]{1,0:T(8,128)S(1)}, u32[]{:S(2)}, u32[]{:S(2)}) collective-permute-start(f32[128,1024]{1,0:T(8,128)S(1)} %get-tuple-element.93.own_bottom), channel_id=1, source_target_pairs={{0,1},{1,0},{2,3},{3,2},{4,5},{5,4},{6,7},{7,6},{8,9},{9,8},{10,11... | collective-permute-start | bytes 1572872 | tf_op jit(solution)/shard_map/ppermute | solution.py:20
  29.8 5.9 %collective-permute-start.7 = (f32[128,256]{1,0:T(8,128)S(1)}, f32[128,256]{1,0:T(8,128)S(1)}, u32[]{:S(2)}, u32[]{:S(2)}) collective-permute-start(f32[128,256]{1,0:T(8,128)S(1)} %broadcast_select_fusion.5.refs_0_), channel_id=1, source_target_pairs={{0,8},{4,12},{8,0},{12,4},{16,24},{20,28},{24,16},{28,20},{1,9},{5... | collective-permute-start | bytes 393224 | tf_op jit(solution)/shard_map/ppermute | solution.py:20
  30.5 6.7 %collective-permute-start.8 = (f32[128,256]{1,0:T(8,128)S(1)}, f32[128,256]{1,0:T(8,128)S(1)}, u32[]{:S(2)}, u32[]{:S(2)}) collective-permute-start(f32[128,256]{1,0:T(8,128)S(1)} %broadcast_select_fusion.4.refs_1_), channel_id=1, source_target_pairs={{0,8},{4,12},{8,0},{12,4},{16,24},{20,28},{24,16},{28,20},{1,9},{5... | collective-permute-start | bytes 393224 | tf_op jit(solution)/shard_map/ppermute | solution.py:20
  31.9 23.6 %collective-permute-start.17 = (f32[128,1024]{1,0:T(8,128)S(1)}, f32[128,1024]{1,0:T(8,128)S(1)}, u32[]{:S(2)}, u32[]{:S(2)}) collective-permute-start(f32[128,1024]{1,0:T(8,128)S(1)} %collective-permute-done.5.refs_0_), channel_id=1, source_target_pairs={{0,2},{1,3},{2,0},{3,1},{4,6},{5,7},{6,4},{7,5},{8,10},{9,11},{10,... | collective-permute-start | bytes 1572872 | tf_op jit(solution)/shard_map/ppermute | solution.py:20
  35.7 19.8 %collective-permute-start.18 = (f32[128,1024]{1,0:T(8,128)S(1)}, f32[128,1024]{1,0:T(8,128)S(1)}, u32[]{:S(2)}, u32[]{:S(2)}) collective-permute-start(f32[128,1024]{1,0:T(8,128)S(1)} %collective-permute-done.6.refs_1_), channel_id=1, source_target_pairs={{0,1},{1,0},{2,3},{3,2},{4,5},{5,4},{6,7},{7,6},{8,9},{9,8},{10,11... | collective-permute-start | bytes 1572872 | tf_op jit(solution)/shard_map/ppermute | solution.py:20
  42.9 1.3 %collective-permute-start.11 = (f32[128,256]{1,0:T(8,128)S(1)}, f32[128,256]{1,0:T(8,128)S(1)}, u32[]{:S(2)}, u32[]{:S(2)}) collective-permute-start(f32[128,256]{1,0:T(8,128)S(1)} %broadcast_select_fusion.5.refs_0_), channel_id=1, source_target_pairs={{0,4},{4,0},{8,12},{12,8},{16,20},{20,16},{24,28},{28,24},{1,5},{5... | collective-permute-start | bytes 393224 | tf_op jit(solution)/shard_map/ppermute | solution.py:20
  42.9 1.5 %collective-permute-start.12 = (f32[128,256]{1,0:T(8,128)S(1)}, f32[128,256]{1,0:T(8,128)S(1)}, u32[]{:S(2)}, u32[]{:S(2)}) collective-permute-start(f32[128,256]{1,0:T(8,128)S(1)} %broadcast_select_fusion.4.refs_1_), channel_id=1, source_target_pairs={{0,4},{4,0},{8,12},{12,8},{16,20},{20,16},{24,28},{28,24},{1,5},{5... | collective-permute-start | bytes 393224 | tf_op jit(solution)/shard_map/ppermute | solution.py:20
  43.4 1.3 %collective-permute-start.13 = (f32[128,256]{1,0:T(8,128)S(1)}, f32[128,256]{1,0:T(8,128)S(1)}, u32[]{:S(2)}, u32[]{:S(2)}) collective-permute-start(f32[128,256]{1,0:T(8,128)S(1)} %collective-permute-done.7.refs_2_), channel_id=1, source_target_pairs={{0,4},{4,0},{8,12},{12,8},{16,20},{20,16},{24,28},{28,24},{1,5},{5... | collective-permute-start | bytes 393224 | tf_op jit(solution)/shard_map/ppermute | solution.py:20
  44.2 1.3 %collective-permute-start.14 = (f32[128,256]{1,0:T(8,128)S(1)}, f32[128,256]{1,0:T(8,128)S(1)}, u32[]{:S(2)}, u32[]{:S(2)}) collective-permute-start(f32[128,256]{1,0:T(8,128)S(1)} %collective-permute-done.8.refs_3_), channel_id=1, source_target_pairs={{0,4},{4,0},{8,12},{12,8},{16,20},{20,16},{24,28},{28,24},{1,5},{5... | collective-permute-start | bytes 393224 | tf_op jit(solution)/shard_map/ppermute | solution.py:20
  46.1 9.2 %collective-permute-start.15 = (f32[128,256]{1,0:T(8,128)S(1)}, f32[128,256]{1,0:T(8,128)S(1)}, u32[]{:S(2)}, u32[]{:S(2)}) collective-permute-start(f32[128,256]{1,0:T(8,128)S(1)} %solve.2.refs_0_), channel_id=1, source_target_pairs={{0,16},{4,20},{8,24},{12,28},{16,0},{20,4},{24,8},{28,12},{1,17},{... | collective-permute-start | bytes 393224 | tf_op jit(solution)/shard_map/ppermute | solution.py:20
  46.2 9.3 %collective-permute-start.16 = (f32[128,256]{1,0:T(8,128)S(1)}, f32[128,256]{1,0:T(8,128)S(1)}, u32[]{:S(2)}, u32[]{:S(2)}) collective-permute-start(f32[128,256]{1,0:T(8,128)S(1)} %solve.2.refs_0_), channel_id=1, source_target_pairs={{0,8},{4,12},{8,0},{12,4},{16,24},{20,28},{24,16},{28,20},{1,9},{5... | collective-permute-start | bytes 393224 | tf_op jit(solution)/shard_map/ppermute | solution.py:20
  49.2 8.0 %collective-permute-start.20 = (f32[128,256]{1,0:T(8,128)S(1)}, f32[128,256]{1,0:T(8,128)S(1)}, u32[]{:S(2)}, u32[]{:S(2)}) collective-permute-start(f32[128,256]{1,0:T(8,128)S(1)} %solve.2.refs_0_), channel_id=1, source_target_pairs={{0,4},{4,0},{8,12},{12,8},{16,20},{20,16},{24,28},{28,24},{1,5},{5... | collective-permute-start | bytes 393224 | tf_op jit(solution)/shard_map/ppermute | solution.py:20
  55.5 5.3 %collective-permute-start.19 = (f32[128,256]{1,0:T(8,128)S(1)}, f32[128,256]{1,0:T(8,128)S(1)}, u32[]{:S(2)}, u32[]{:S(2)}) collective-permute-start(f32[128,256]{1,0:T(8,128)S(1)} %collective-permute-done.15.refs_2_), channel_id=1, source_target_pairs={{0,8},{4,12},{8,0},{12,4},{16,24},{20,28},{24,16},{28,20},{1,9},{5... | collective-permute-start | bytes 393224 | tf_op jit(solution)/shard_map/ppermute | solution.py:20
  55.5 5.3 %collective-permute-start.21 = (f32[128,256]{1,0:T(8,128)S(1)}, f32[128,256]{1,0:T(8,128)S(1)}, u32[]{:S(2)}, u32[]{:S(2)}) collective-permute-start(f32[128,256]{1,0:T(8,128)S(1)} %collective-permute-done.16.refs_1_), channel_id=1, source_target_pairs={{0,4},{4,0},{8,12},{12,8},{16,20},{20,16},{24,28},{28,24},{1,5},{5... | collective-permute-start | bytes 393224 | tf_op jit(solution)/shard_map/ppermute | solution.py:20
  55.6 5.2 %collective-permute-start.22 = (f32[128,256]{1,0:T(8,128)S(1)}, f32[128,256]{1,0:T(8,128)S(1)}, u32[]{:S(2)}, u32[]{:S(2)}) collective-permute-start(f32[128,256]{1,0:T(8,128)S(1)} %collective-permute-done.15.refs_2_), channel_id=1, source_target_pairs={{0,4},{4,0},{8,12},{12,8},{16,20},{20,16},{24,28},{28,24},{1,5},{5... | collective-permute-start | bytes 393224 | tf_op jit(solution)/shard_map/ppermute | solution.py:20
  60.8 1.4 %collective-permute-start.23 = (f32[128,256]{1,0:T(8,128)S(1)}, f32[128,256]{1,0:T(8,128)S(1)}, u32[]{:S(2)}, u32[]{:S(2)}) collective-permute-start(f32[128,256]{1,0:T(8,128)S(1)} %collective-permute-done.19.refs_3_), channel_id=1, source_target_pairs={{0,4},{4,0},{8,12},{12,8},{16,20},{20,16},{24,28},{28,24},{1,5},{5... | collective-permute-start | bytes 393224 | tf_op jit(solution)/shard_map/ppermute | solution.py:20
  64.8 2.8 %collective-permute-start.24 = (f32[512,256]{1,0:T(8,128)S(1)}, f32[512,256]{1,0:T(8,128)}, u32[]{:S(2)}, u32[]{:S(2)}) collective-permute-start(f32[512,256]{1,0:T(8,128)S(1)} %get-tuple-element.116.refs_9_), channel_id=1, source_target_pairs={{0,4},{4,0},{8,12},{12,8},{16,20},{20,16},{24,28},{28,24},{1,5},{5... | collective-permute-start | bytes 1572872 | tf_op jit(solution)/shard_map/ppermute | solution.py:20
  68.8 5.5 %collective-permute-start.25 = (f32[128,256]{1,0:T(8,128)S(1)}, f32[128,256]{1,0:T(8,128)S(1)}, u32[]{:S(2)}, u32[]{:S(2)}) collective-permute-start(f32[128,256]{1,0:T(8,128)S(1)} %get-tuple-element.119), channel_id=1, source_target_pairs={{0,8},{4,12},{8,0},{12,4},{16,24},{20,28},{24,16},{28,20},{1,9},{5... | collective-permute-start | bytes 393224 | tf_op jit(solution)/shard_map/ppermute | solution.py:20
  69.2 18.1 %collective-permute-start.29 = (f32[128,1024]{1,0:T(8,128)S(1)}, f32[128,1024]{1,0:T(8,128)S(1)}, u32[]{:S(2)}, u32[]{:S(2)}) collective-permute-start(f32[128,1024]{1,0:T(8,128)S(1)} %get-tuple-element.130.own_top), channel_id=1, source_target_pairs={{0,1},{1,0},{2,3},{3,2},{4,5},{5,4},{6,7},{7,6},{8,9},{9,8},{10,11... | collective-permute-start | bytes 1572872 | tf_op jit(solution)/shard_map/ppermute | solution.py:20
  70.8 16.6 %collective-permute-start.30 = (f32[128,1024]{1,0:T(8,128)S(1)}, f32[128,1024]{1,0:T(8,128)S(1)}, u32[]{:S(2)}, u32[]{:S(2)}) collective-permute-start(f32[128,1024]{1,0:T(8,128)S(1)} %get-tuple-element.129.own_bottom), channel_id=1, source_target_pairs={{0,2},{1,3},{2,0},{3,1},{4,6},{5,7},{6,4},{7,5},{8,10},{9,11},{10,... | collective-permute-start | bytes 1572872 | tf_op jit(solution)/shard_map/ppermute | solution.py:20
  72.3 5.4 %collective-permute-start.27 = (f32[128,256]{1,0:T(8,128)S(1)}, f32[128,256]{1,0:T(8,128)S(1)}, u32[]{:S(2)}, u32[]{:S(2)}) collective-permute-start(f32[128,256]{1,0:T(8,128)S(1)} %get-tuple-element.123), channel_id=1, source_target_pairs={{0,8},{4,12},{8,0},{12,4},{16,24},{20,28},{24,16},{28,20},{1,9},{5... | collective-permute-start | bytes 393224 | tf_op jit(solution)/shard_map/ppermute | solution.py:20
  74.3 11.5 %collective-permute-start.26 = (f32[128,256]{1,0:T(8,128)S(1)}, f32[128,256]{1,0:T(8,128)S(1)}, u32[]{:S(2)}, u32[]{:S(2)}) collective-permute-start(f32[128,256]{1,0:T(8,128)S(1)} %broadcast_select_fusion.7), channel_id=1, source_target_pairs={{0,16},{4,20},{8,24},{12,28},{16,0},{20,4},{24,8},{28,12},{1,17},{... | collective-permute-start | bytes 393224 | tf_op jit(solution)/shard_map/ppermute | solution.py:20
  77.7 9.5 %collective-permute-start.28 = (f32[128,256]{1,0:T(8,128)S(1)}, f32[128,256]{1,0:T(8,128)S(1)}, u32[]{:S(2)}, u32[]{:S(2)}) collective-permute-start(f32[128,256]{1,0:T(8,128)S(1)} %broadcast_select_fusion.6), channel_id=1, source_target_pairs={{0,16},{4,20},{8,24},{12,28},{16,0},{20,4},{24,8},{28,12},{1,17},{... | collective-permute-start | bytes 393224 | tf_op jit(solution)/shard_map/ppermute | solution.py:20
  79.5 14.7 %collective-permute-start.33 = (f32[128,1024]{1,0:T(8,128)S(1)}, f32[128,1024]{1,0:T(8,128)S(1)}, u32[]{:S(2)}, u32[]{:S(2)}) collective-permute-start(f32[128,1024]{1,0:T(8,128)S(1)} %get-tuple-element.129.own_bottom), channel_id=1, source_target_pairs={{0,1},{1,0},{2,3},{3,2},{4,5},{5,4},{6,7},{7,6},{8,9},{9,8},{10,11... | collective-permute-start | bytes 1572872 | tf_op jit(solution)/shard_map/ppermute | solution.py:20
  85.8 14.1 %collective-permute-start.34 = (f32[128,1024]{1,0:T(8,128)S(1)}, f32[128,1024]{1,0:T(8,128)S(1)}, u32[]{:S(2)}, u32[]{:S(2)}) collective-permute-start(f32[128,1024]{1,0:T(8,128)S(1)} %get-tuple-element.130.own_top), channel_id=1, source_target_pairs={{0,2},{1,3},{2,0},{3,1},{4,6},{5,7},{6,4},{7,5},{8,10},{9,11},{10,... | collective-permute-start | bytes 1572872 | tf_op jit(solution)/shard_map/ppermute | solution.py:20
  87.2 5.5 %collective-permute-start.31 = (f32[128,256]{1,0:T(8,128)S(1)}, f32[128,256]{1,0:T(8,128)S(1)}, u32[]{:S(2)}, u32[]{:S(2)}) collective-permute-start(f32[128,256]{1,0:T(8,128)S(1)} %broadcast_select_fusion.9.refs_0_), channel_id=1, source_target_pairs={{0,8},{4,12},{8,0},{12,4},{16,24},{20,28},{24,16},{28,20},{1,9},{5... | collective-permute-start | bytes 393224 | tf_op jit(solution)/shard_map/ppermute | solution.py:20
  87.4 6.8 %collective-permute-start.32 = (f32[128,256]{1,0:T(8,128)S(1)}, f32[128,256]{1,0:T(8,128)S(1)}, u32[]{:S(2)}, u32[]{:S(2)}) collective-permute-start(f32[128,256]{1,0:T(8,128)S(1)} %broadcast_select_fusion.8.refs_1_), channel_id=1, source_target_pairs={{0,8},{4,12},{8,0},{12,4},{16,24},{20,28},{24,16},{28,20},{1,9},{5... | collective-permute-start | bytes 393224 | tf_op jit(solution)/shard_map/ppermute | solution.py:20
  89.4 22.2 %collective-permute-start.41 = (f32[128,1024]{1,0:T(8,128)S(1)}, f32[128,1024]{1,0:T(8,128)S(1)}, u32[]{:S(2)}, u32[]{:S(2)}) collective-permute-start(f32[128,1024]{1,0:T(8,128)S(1)} %collective-permute-done.29.refs_0_), channel_id=1, source_target_pairs={{0,2},{1,3},{2,0},{3,1},{4,6},{5,7},{6,4},{7,5},{8,10},{9,11},{10,... | collective-permute-start | bytes 1572872 | tf_op jit(solution)/shard_map/ppermute | solution.py:20
  92.8 18.9 %collective-permute-start.42 = (f32[128,1024]{1,0:T(8,128)S(1)}, f32[128,1024]{1,0:T(8,128)S(1)}, u32[]{:S(2)}, u32[]{:S(2)}) collective-permute-start(f32[128,1024]{1,0:T(8,128)S(1)} %collective-permute-done.30.refs_1_), channel_id=1, source_target_pairs={{0,1},{1,0},{2,3},{3,2},{4,5},{5,4},{6,7},{7,6},{8,9},{9,8},{10,11... | collective-permute-start | bytes 1572872 | tf_op jit(solution)/shard_map/ppermute | solution.py:20
  100.0 1.3 %collective-permute-start.35 = (f32[128,256]{1,0:T(8,128)S(1)}, f32[128,256]{1,0:T(8,128)S(1)}, u32[]{:S(2)}, u32[]{:S(2)}) collective-permute-start(f32[128,256]{1,0:T(8,128)S(1)} %broadcast_select_fusion.9.refs_0_), channel_id=1, source_target_pairs={{0,4},{4,0},{8,12},{12,8},{16,20},{20,16},{24,28},{28,24},{1,5},{5... | collective-permute-start | bytes 393224 | tf_op jit(solution)/shard_map/ppermute | solution.py:20
  100.0 1.5 %collective-permute-start.36 = (f32[128,256]{1,0:T(8,128)S(1)}, f32[128,256]{1,0:T(8,128)S(1)}, u32[]{:S(2)}, u32[]{:S(2)}) collective-permute-start(f32[128,256]{1,0:T(8,128)S(1)} %broadcast_select_fusion.8.refs_1_), channel_id=1, source_target_pairs={{0,4},{4,0},{8,12},{12,8},{16,20},{20,16},{24,28},{28,24},{1,5},{5... | collective-permute-start | bytes 393224 | tf_op jit(solution)/shard_map/ppermute | solution.py:20
  100.5 1.3 %collective-permute-start.37 = (f32[128,256]{1,0:T(8,128)S(1)}, f32[128,256]{1,0:T(8,128)S(1)}, u32[]{:S(2)}, u32[]{:S(2)}) collective-permute-start(f32[128,256]{1,0:T(8,128)S(1)} %collective-permute-done.31.refs_2_), channel_id=1, source_target_pairs={{0,4},{4,0},{8,12},{12,8},{16,20},{20,16},{24,28},{28,24},{1,5},{5... | collective-permute-start | bytes 393224 | tf_op jit(solution)/shard_map/ppermute | solution.py:20
  101.3 1.3 %collective-permute-start.38 = (f32[128,256]{1,0:T(8,128)S(1)}, f32[128,256]{1,0:T(8,128)S(1)}, u32[]{:S(2)}, u32[]{:S(2)}) collective-permute-start(f32[128,256]{1,0:T(8,128)S(1)} %collective-permute-done.32.refs_3_), channel_id=1, source_target_pairs={{0,4},{4,0},{8,12},{12,8},{16,20},{20,16},{24,28},{28,24},{1,5},{5... | collective-permute-start | bytes 393224 | tf_op jit(solution)/shard_map/ppermute | solution.py:20
  103.1 7.7 %collective-permute-start.39 = (f32[128,256]{1,0:T(8,128)S(1)}, f32[128,256]{1,0:T(8,128)S(1)}, u32[]{:S(2)}, u32[]{:S(2)}) collective-permute-start(f32[128,256]{1,0:T(8,128)S(1)} %solve.3.refs_0_), channel_id=1, source_target_pairs={{0,16},{4,20},{8,24},{12,28},{16,0},{20,4},{24,8},{28,12},{1,17},{... | collective-permute-start | bytes 393224 | tf_op jit(solution)/shard_map/ppermute | solution.py:20
  103.5 8.2 %collective-permute-start.40 = (f32[128,256]{1,0:T(8,128)S(1)}, f32[128,256]{1,0:T(8,128)S(1)}, u32[]{:S(2)}, u32[]{:S(2)}) collective-permute-start(f32[128,256]{1,0:T(8,128)S(1)} %solve.3.refs_0_), channel_id=1, source_target_pairs={{0,8},{4,12},{8,0},{12,4},{16,24},{20,28},{24,16},{28,20},{1,9},{5... | collective-permute-start | bytes 393224 | tf_op jit(solution)/shard_map/ppermute | solution.py:20
  104.4 9.1 %collective-permute-start.44 = (f32[128,256]{1,0:T(8,128)S(1)}, f32[128,256]{1,0:T(8,128)S(1)}, u32[]{:S(2)}, u32[]{:S(2)}) collective-permute-start(f32[128,256]{1,0:T(8,128)S(1)} %solve.3.refs_0_), channel_id=1, source_target_pairs={{0,4},{4,0},{8,12},{12,8},{16,20},{20,16},{24,28},{28,24},{1,5},{5... | collective-permute-start | bytes 393224 | tf_op jit(solution)/shard_map/ppermute | solution.py:20
  111.6 5.0 %collective-permute-start.43 = (f32[128,256]{1,0:T(8,128)S(1)}, f32[128,256]{1,0:T(8,128)S(1)}, u32[]{:S(2)}, u32[]{:S(2)}) collective-permute-start(f32[128,256]{1,0:T(8,128)S(1)} %collective-permute-done.39.refs_2_), channel_id=1, source_target_pairs={{0,8},{4,12},{8,0},{12,4},{16,24},{20,28},{24,16},{28,20},{1,9},{5... | collective-permute-start | bytes 393224 | tf_op jit(solution)/shard_map/ppermute | solution.py:20
  111.9 4.7 %collective-permute-start.45 = (f32[128,256]{1,0:T(8,128)S(1)}, f32[128,256]{1,0:T(8,128)S(1)}, u32[]{:S(2)}, u32[]{:S(2)}) collective-permute-start(f32[128,256]{1,0:T(8,128)S(1)} %collective-permute-done.40.refs_1_), channel_id=1, source_target_pairs={{0,4},{4,0},{8,12},{12,8},{16,20},{20,16},{24,28},{28,24},{1,5},{5... | collective-permute-start | bytes 393224 | tf_op jit(solution)/shard_map/ppermute | solution.py:20
  111.9 4.7 %collective-permute-start.46 = (f32[128,256]{1,0:T(8,128)S(1)}, f32[128,256]{1,0:T(8,128)S(1)}, u32[]{:S(2)}, u32[]{:S(2)}) collective-permute-start(f32[128,256]{1,0:T(8,128)S(1)} %collective-permute-done.39.refs_2_), channel_id=1, source_target_pairs={{0,4},{4,0},{8,12},{12,8},{16,20},{20,16},{24,28},{28,24},{1,5},{5... | collective-permute-start | bytes 393224 | tf_op jit(solution)/shard_map/ppermute | solution.py:20
  116.6 1.4 %collective-permute-start.47 = (f32[128,256]{1,0:T(8,128)S(1)}, f32[128,256]{1,0:T(8,128)S(1)}, u32[]{:S(2)}, u32[]{:S(2)}) collective-permute-start(f32[128,256]{1,0:T(8,128)S(1)} %collective-permute-done.43.refs_3_), channel_id=1, source_target_pairs={{0,4},{4,0},{8,12},{12,8},{16,20},{20,16},{24,28},{28,24},{1,5},{5... | collective-permute-start | bytes 393224 | tf_op jit(solution)/shard_map/ppermute | solution.py:20
  (6 other events, 114.6 us)

commit v6 on v4

--- a/solution.py
+++ b/solution.py
@@ -133,17 +133,22 @@
 
 
 def second_body(flags, slot_block, high, low, *refs):
-    blocks, (keep, send, out, x) = refs[:8], refs[8:]
+    blocks, (keep, send, out, x, rows_out, sems) = refs[:8], refs[8:]
     rank = lax.axis_index("row")
     core, held = bit(rank, 0), slot_block[rank]
     assemble(x, blocks, rank)
     parts = split(x[...])
     weight = flags[0, 1].astype(jnp.float32)
     size = keep.shape[0]
-    for current, part in ((keep, core), (send, 1 - core)):
+    copies = []
+    for index, (current, part) in enumerate(((keep, core), (send, 1 - core))):
         rows = pl.ds(pl.multiple_of(part * size, size), size)
         new = current[...] - weight * dot3((high[rows], low[rows]), parts)
-        out[rows] = jnp.where(held == 0, current[...], jnp.where(held == 1, x[rows], new))
+        rows_out[index] = jnp.where(held == 0, current[...], jnp.where(held == 1, x[rows], new))
+        copies.append(pltpu.make_async_copy(rows_out.at[index], out.at[rows], sems.at[index]))
+        copies[index].start()
+    for copy in copies:
+        copy.wait()
 
 
 def solve_body(inverse, *refs):
@@ -181,11 +186,13 @@
     scratch = [pltpu.VMEM((depth, cols), jnp.float32)]
     if step == 0:
         scratch += [pltpu.VMEM((rows, cols), jnp.float32), pltpu.SemaphoreType.DMA]
+    else:
+        scratch += [pltpu.VMEM((2, rows // 2, cols), jnp.float32), pltpu.SemaphoreType.DMA((2,))]
     return pl.pallas_call(
         first_body if step == 0 else second_body,
         out_shape=[jax.ShapeDtypeStruct((count, cols), jnp.float32) for count in counts],
         in_specs=[smem, smem] + [vmem] * 10 + ([pl.BlockSpec(memory_space=pl.ANY)] if step == 0 else [vmem] * 2),
-        out_specs=[vmem] * len(counts),
+        out_specs=[vmem] * 2 if step == 0 else [pl.BlockSpec(memory_space=pl.ANY)],
         scratch_shapes=scratch,
         compiler_params=pltpu.CompilerParams(vmem_limit_bytes=UPDATE_BYTES),
         cost_estimate=pl.CostEstimate(flops=6 * rows * depth * cols, bytes_accessed=4 * rows * (depth + 3 * cols), transcendentals=0),
@@ -243,9 +250,11 @@
         y, inverse, *first = tie(y, diag_inverse, *first)
         pieces = far(*first)
         beside = swap(y, "row", 1, rows)
-        beside, y, *second = tie(beside, y, *second)
-        other, last = swap(y, "row", 0, rows), swap(beside, "row", 0, rows)
-        x = solve(inverse[step], [y, beside, other, last])
+        y, *second = tie(y, *second)
+        other = swap(y, "row", 0, rows)
+        beside, inverse = tie(beside, inverse[step])
+        last = swap(beside, "row", 0, rows)
+        x = solve(inverse, [y, beside, other, last])
         x2, x1 = swap(x, "row", 2, rows), swap(x, "row", 1, rows)
         x2, x1, *pieces = tie(x2, x1, *pieces)
         high, low = prepare([*block, *first, *second, *pieces])
@@ -254,9 +263,9 @@
         x3, high, low, *across = tie(x3, high, low, *across)
         return [x, x1, x2, x3, *across, swap(x3, "row", 0, rows)], (high, low)
 
-    keep, send = halves(rhs[0], core)
-    got = swap(send, "row", 0, rows)
-    keep, send = tie(keep, send)
+    got = swap(halves(rhs[0], 1 - core)[0], "row", 0, rows)
+    kept, owner = tie(rhs, owner)
+    keep, owner = tie(halves(kept[0], core)[0], owner)
     y = jnp.where(bit(owner, 0) == core, keep, got)
     blocks, pair = solved(0, y, panel, owner)
     keep, send = update(0, flags, slot_block, pair, blocks, [rhs])

time: 114 us -> 116 us (1.018)
  starting transfers between devices: 40.4 us -> 46.2 us
  waiting for transfers between devices: 50.1 us -> 46.7 us
    ppermute x38, starting transfers between devices: 40.4 us -> 46.2 us  [swap(): return lax.ppermute(x, axis, [(i, i ^ 1 << b) for i in range(size)])]
    ppermute x38, waiting for transfers between devices: 50.1 us -> 46.7 us  [swap(): return lax.ppermute(x, axis, [(i, i ^ 1 << b) for i in range(size)])]
    dynamic_slice x0 -> x2, local copies, waits for them, and re-layouts: none -> 3.09 us  [halves(): lax.dynamic_slice_in_dim(x, b * half, half)]
    dynamic_slice x3 -> x2, local copies, waits for them, and re-layouts: 2.26 us -> 0.05 us  [halves(): lax.dynamic_slice_in_dim(x, (1 - b) * half, half)]
    select_n x2, other arithmetic: 1.96 us -> 0.07 us  [cross_step(): return jnp.where(bit(owner, b) == bit(me, b), x, swap(x, 'row', b, size))]
  transfers between devices with their start and end apart: 38 -> 38, of which waited for: 18 -> 21; matrix products, arithmetic and copies ran while one was open for 6% -> 6% of each run, Pallas kernels for 3% -> 3%
where the time goes in v6:
time: 116 us
  waiting for transfers between devices  46.7 us (40%)
  starting transfers between devices  46.2 us (40%)
  Pallas kernels  9.96 us (9%)
  local copies, waits for them, and re-layouts  6.69 us (6%)
  between operations  4.24 us (4%)
  other arithmetic  2.37 us (2%)
    ppermute x38, waiting for transfers between devices, swap(): return lax.ppermute(x, axis, [(i, i ^ 1 << b) for i in range(size)])  46.7 us
    ppermute x38, starting transfers between devices, swap(): return lax.ppermute(x, axis, [(i, i ^ 1 << b) for i in range(size)])  46.2 us
    pallas_call x2, Pallas kernels, update(): pl.pallas_call(first_body if step == 0 else second_body, out_shape=[jax.S...  6.09 us
    dynamic_slice x2, local copies, waits for them, and re-layouts, halves(): lax.dynamic_slice_in_dim(x, b * half, half)  3.09 us
    pallas_call x2, Pallas kernels, prepare(): pl.pallas_call(prepare_body, out_shape=[jax.ShapeDtypeStruct((depth, dept...  2.91 us
  transfers between devices with their start and end apart: 38, of which 21 were waited for; matrix products, arithmetic and copies ran while one was open for 6% of the time, Pallas kernels for 3%

profile of v6, /device:TPU:0, one launch (start us, length us, event | category | flops | bytes accessed | tf_op | source)
XLA Modules:
  0.0 116.2 jit_solution(14587675762550581507)
XLA Ops:
  0.0 2.0 %dynamic-slice_bitcast_fusion = f32[512,256]{1,0:T(8,128)} fusion(f32[1,1024,256]{2,1,0:T(8,128)} %refs_8_.1, s32[]{:T(128)S(6)} %select_n.67), kind=kLoop, calls=%fused_computation.6 | loop fusion | bytes 1048580 | tf_op jit(solution)/shard_map/dynamic_slice | solution.py:33
  2.5 1.4 %compare_reduce_fusion = (pred[]{:T(512)}, s32[]{:T(128)}) fusion(s32[8]{0:T(128)} %slot_block.3), kind=kLoop, calls=%fused_computation.14 | loop fusion | flops 57 | bytes 37 | tf_op jit(solution)/shard_map/paced/reduce | solution.py:229
  3.9 1.1 dynamic-slice_bitcast_fusion.1
  6.3 2.6 %collective-permute-start.1 = (f32[256,256]{1,0:T(8,128)S(1)}, f32[256,256]{1,0:T(8,128)S(1)}, u32[]{:S(2)}, u32[]{:S(2)}) collective-permute-start(f32[256,256]{1,0:T(8,128)S(1)} %constant_dynamic-slice_fusion.1), channel_id=1, source_target_pairs={{0,8},{4,12},{8,0},{12,4},{16,24},{20,28},{24,16},{28,20},{1,9},{5... | collective-permute-start | bytes 786440 | tf_op jit(solution)/shard_map/ppermute | solution.py:20
  9.1 1.6 %collective-permute-start.3 = (f32[128,1024]{1,0:T(8,128)S(1)}, f32[128,1024]{1,0:T(8,128)S(1)}, u32[]{:S(2)}, u32[]{:S(2)}) collective-permute-start(f32[128,1024]{1,0:T(8,128)S(1)} %get-tuple-element.84.own_top), channel_id=1, source_target_pairs={{0,1},{1,0},{2,3},{3,2},{4,5},{5,4},{6,7},{7,6},{8,9},{9,8},{10,11... | collective-permute-start | bytes 1572872 | tf_op jit(solution)/shard_map/ppermute | solution.py:20
  10.6 1.5 %collective-permute-start.4 = (f32[128,1024]{1,0:T(8,128)S(1)}, f32[128,1024]{1,0:T(8,128)S(1)}, u32[]{:S(2)}, u32[]{:S(2)}) collective-permute-start(f32[128,1024]{1,0:T(8,128)S(1)} %get-tuple-element.83.own_bottom), channel_id=1, source_target_pairs={{0,2},{1,3},{2,0},{3,1},{4,6},{5,7},{6,4},{7,5},{8,10},{9,11},{10,... | collective-permute-start | bytes 1572872 | tf_op jit(solution)/shard_map/ppermute | solution.py:20
  12.2 3.8 %collective-permute-done.1 = f32[256,256]{1,0:T(8,128)S(1)} collective-permute-done((f32[256,256]{1,0:T(8,128)S(1)}, f32[256,256]{1,0:T(8,128)S(1)}, u32[]{:S(2)}, u32[]{:S(2)}) %collective-permute-start.1) | collective-permute-done | bytes 262176 | tf_op jit(solution)/shard_map/ppermute | solution.py:20
  16.0 2.8 %collective-permute-start.2 = (f32[256,256]{1,0:T(8,128)S(1)}, f32[256,256]{1,0:T(8,128)}, u32[]{:S(2)}, u32[]{:S(2)}) collective-permute-start(f32[256,256]{1,0:T(8,128)S(1)} %dynamic-slice_select_fusion.1), channel_id=1, source_target_pairs={{0,16},{4,20},{8,24},{12,28},{16,0},{20,4},{24,8},{28,12},{1,17},{... | collective-permute-start | bytes 786440 | tf_op jit(solution)/shard_map/ppermute | solution.py:20
  18.8 1.5 %collective-permute-start.6 = (f32[128,1024]{1,0:T(8,128)S(1)}, f32[128,1024]{1,0:T(8,128)S(1)}, u32[]{:S(2)}, u32[]{:S(2)}) collective-permute-start(f32[128,1024]{1,0:T(8,128)S(1)} %get-tuple-element.83.own_bottom), channel_id=1, source_target_pairs={{0,1},{1,0},{2,3},{3,2},{4,5},{5,4},{6,7},{7,6},{8,9},{9,8},{10,11... | collective-permute-start | bytes 1572872 | tf_op jit(solution)/shard_map/ppermute | solution.py:20
  20.3 1.5 %collective-permute-start.7 = (f32[128,1024]{1,0:T(8,128)S(1)}, f32[128,1024]{1,0:T(8,128)S(1)}, u32[]{:S(2)}, u32[]{:S(2)}) collective-permute-start(f32[128,1024]{1,0:T(8,128)S(1)} %get-tuple-element.84.own_top), channel_id=1, source_target_pairs={{0,2},{1,3},{2,0},{3,1},{4,6},{5,7},{6,4},{7,5},{8,10},{9,11},{10,... | collective-permute-start | bytes 1572872 | tf_op jit(solution)/shard_map/ppermute | solution.py:20
  22.5 8.3 %collective-permute-done.2 = f32[256,256]{1,0:T(8,128)} collective-permute-done((f32[256,256]{1,0:T(8,128)S(1)}, f32[256,256]{1,0:T(8,128)}, u32[]{:S(2)}, u32[]{:S(2)}) %collective-permute-start.2) | collective-permute-done | bytes 262176 | tf_op jit(solution)/shard_map/ppermute | solution.py:20
  31.5 1.5 %collective-permute-start.12 = (f32[128,1024]{1,0:T(8,128)S(1)}, f32[128,1024]{1,0:T(8,128)S(1)}, u32[]{:S(2)}, u32[]{:S(2)}) collective-permute-start(f32[128,1024]{1,0:T(8,128)S(1)} %collective-permute-done.3.refs_0_), channel_id=1, source_target_pairs={{0,2},{1,3},{2,0},{3,1},{4,6},{5,7},{6,4},{7,5},{8,10},{9,11},{10,... | collective-permute-start | bytes 1572872 | tf_op jit(solution)/shard_map/ppermute | solution.py:20
  33.0 1.5 %collective-permute-start.13 = (f32[128,1024]{1,0:T(8,128)S(1)}, f32[128,1024]{1,0:T(8,128)S(1)}, u32[]{:S(2)}, u32[]{:S(2)}) collective-permute-start(f32[128,1024]{1,0:T(8,128)S(1)} %collective-permute-done.4.refs_1_), channel_id=1, source_target_pairs={{0,1},{1,0},{2,3},{3,2},{4,5},{5,4},{6,7},{7,6},{8,9},{9,8},{10,11... | collective-permute-start | bytes 1572872 | tf_op jit(solution)/shard_map/ppermute | solution.py:20
  34.5 1.1 slice_bitcast_fusion.3.inverse
  35.6 1.1 collective-permute-done.7.refs_3_
  36.7 1.6 %collective-permute-done.5.refs_1_ = f32[256,256]{1,0:T(8,128)S(1)} collective-permute-done((f32[256,256]{1,0:T(8,128)S(1)}, f32[256,256]{1,0:T(8,128)S(1)}, u32[]{:S(2)}, u32[]{:S(2)}) %collective-permute-start.5) | collective-permute-done | bytes 262176 | tf_op jit(solution)/shard_map/ppermute | solution.py:20
  38.2 1.5 %collective-permute-done.9.refs_3_ = f32[256,256]{1,0:T(8,128)S(1)} collective-permute-done((f32[256,256]{1,0:T(8,128)S(1)}, f32[256,256]{1,0:T(8,128)S(1)}, u32[]{:S(2)}, u32[]{:S(2)}) %collective-permute-start.9) | collective-permute-done | bytes 262176 | tf_op jit(solution)/shard_map/ppermute | solution.py:20
  40.3 4.2 %collective-permute-start.10 = (f32[128,256]{1,0:T(8,128)S(1)}, f32[128,256]{1,0:T(8,128)S(1)}, u32[]{:S(2)}, u32[]{:S(2)}) collective-permute-start(f32[128,256]{1,0:T(8,128)S(1)} %solve.2.refs_0_), channel_id=1, source_target_pairs={{0,16},{4,20},{8,24},{12,28},{16,0},{20,4},{24,8},{28,12},{1,17},{... | collective-permute-start | bytes 393224 | tf_op jit(solution)/shard_map/ppermute | solution.py:20
  44.5 1.7 %collective-permute-start.11 = (f32[128,256]{1,0:T(8,128)S(1)}, f32[128,256]{1,0:T(8,128)S(1)}, u32[]{:S(2)}, u32[]{:S(2)}) collective-permute-start(f32[128,256]{1,0:T(8,128)S(1)} %solve.2.refs_0_), channel_id=1, source_target_pairs={{0,8},{4,12},{8,0},{12,4},{16,24},{20,28},{24,16},{28,20},{1,9},{5... | collective-permute-start | bytes 393224 | tf_op jit(solution)/shard_map/ppermute | solution.py:20
  46.9 4.3 %collective-permute-done.10.refs_2_ = f32[128,256]{1,0:T(8,128)S(1)} collective-permute-done((f32[128,256]{1,0:T(8,128)S(1)}, f32[128,256]{1,0:T(8,128)S(1)}, u32[]{:S(2)}, u32[]{:S(2)}) %collective-permute-start.10) | collective-permute-done | bytes 131104 | tf_op jit(solution)/shard_map/ppermute | solution.py:20
  51.3 1.6 %collective-permute-start.14 = (f32[128,256]{1,0:T(8,128)S(1)}, f32[128,256]{1,0:T(8,128)S(1)}, u32[]{:S(2)}, u32[]{:S(2)}) collective-permute-start(f32[128,256]{1,0:T(8,128)S(1)} %collective-permute-done.10.refs_2_), channel_id=1, source_target_pairs={{0,8},{4,12},{8,0},{12,4},{16,24},{20,28},{24,16},{28,20},{1,9},{5... | collective-permute-start | bytes 393224 | tf_op jit(solution)/shard_map/ppermute | solution.py:20
  53.4 1.1 prepare.2
  54.5 1.8 %collective-permute-done.14.refs_3_ = f32[128,256]{1,0:T(8,128)S(1)} collective-permute-done((f32[128,256]{1,0:T(8,128)S(1)}, f32[128,256]{1,0:T(8,128)S(1)}, u32[]{:S(2)}, u32[]{:S(2)}) %collective-permute-start.14) | collective-permute-done | bytes 131104 | tf_op jit(solution)/shard_map/ppermute | solution.py:20
  56.3 1.3 %collective-permute-done.18.refs_7_ = f32[128,256]{1,0:T(8,128)S(1)} collective-permute-done((f32[128,256]{1,0:T(8,128)S(1)}, f32[128,256]{1,0:T(8,128)S(1)}, u32[]{:S(2)}, u32[]{:S(2)}) %collective-permute-start.18) | collective-permute-done | bytes 131104 | tf_op jit(solution)/shard_map/ppermute | solution.py:20
  57.6 2.7 %update.2 = (f32[512,256]{1,0:T(8,128)S(1)}, f32[512,256]{1,0:T(8,128)S(1)}) custom-call(s32[1,2]{1,0:T(1,128)S(1)} %copy-done.1, s32[8]{0:T(128)S(1)} %copy-done.2, bf16[1024,1024]{1,0:T(8,128)(2,1)S(1)} %get-tuple-element.97.high, bf16[1024,1024]{1,0:T(8,128)(2,1)S(1)} %get-tuple-element.98.low, f32[128,256]{1,0:T(8,128)S(1)} %solve.2.refs_0_, ...), custom_call_target="tpu_custom_call" | custom-call | flops 1610612736 | bytes 7340032 | tf_op jit(solution)/shard_map/update/pallas_call | solution.py:191
  62.7 1.7 %collective-permute-start.20 = (f32[256,256]{1,0:T(8,128)S(1)}, f32[256,256]{1,0:T(8,128)S(1)}, u32[]{:S(2)}, u32[]{:S(2)}) collective-permute-start(f32[256,256]{1,0:T(8,128)S(1)} %constant_dynamic-slice_fusion), channel_id=1, source_target_pairs={{0,8},{4,12},{8,0},{12,4},{16,24},{20,28},{24,16},{28,20},{1,9},{5... | collective-permute-start | bytes 786440 | tf_op jit(solution)/shard_map/ppermute | solution.py:20
  64.4 1.3 %slice_bitcast_fusion.1 = (f32[128,1024]{1,0:T(8,128)S(1)}, f32[128,1024]{1,0:T(8,128)S(1)}) fusion(f32[1,2,256,1024]{3,2,1,0:T(8,128)} %param.6), kind=kLoop, calls=%fused_computation.1 | loop fusion | bytes 2097152 | tf_op jit(solution)/shard_map/squeeze | solution.py:240
  65.7 1.6 %collective-permute-start.22 = (f32[128,1024]{1,0:T(8,128)S(1)}, f32[128,1024]{1,0:T(8,128)S(1)}, u32[]{:S(2)}, u32[]{:S(2)}) collective-permute-start(f32[128,1024]{1,0:T(8,128)S(1)} %get-tuple-element.114.own_top), channel_id=1, source_target_pairs={{0,1},{1,0},{2,3},{3,2},{4,5},{5,4},{6,7},{7,6},{8,9},{9,8},{10,11... | collective-permute-start | bytes 1572872 | tf_op jit(solution)/shard_map/ppermute | solution.py:20
  67.2 1.5 %collective-permute-start.23 = (f32[128,1024]{1,0:T(8,128)S(1)}, f32[128,1024]{1,0:T(8,128)S(1)}, u32[]{:S(2)}, u32[]{:S(2)}) collective-permute-start(f32[128,1024]{1,0:T(8,128)S(1)} %get-tuple-element.113.own_bottom), channel_id=1, source_target_pairs={{0,2},{1,3},{2,0},{3,1},{4,6},{5,7},{6,4},{7,5},{8,10},{9,11},{10,... | collective-permute-start | bytes 1572872 | tf_op jit(solution)/shard_map/ppermute | solution.py:20
  68.7 2.6 %collective-permute-done.20 = f32[256,256]{1,0:T(8,128)S(1)} collective-permute-done((f32[256,256]{1,0:T(8,128)S(1)}, f32[256,256]{1,0:T(8,128)S(1)}, u32[]{:S(2)}, u32[]{:S(2)}) %collective-permute-start.20) | collective-permute-done | bytes 262176 | tf_op jit(solution)/shard_map/ppermute | solution.py:20
  71.4 2.7 %collective-permute-start.21 = (f32[256,256]{1,0:T(8,128)S(1)}, f32[256,256]{1,0:T(8,128)}, u32[]{:S(2)}, u32[]{:S(2)}) collective-permute-start(f32[256,256]{1,0:T(8,128)S(1)} %dynamic-slice_select_fusion), channel_id=1, source_target_pairs={{0,16},{4,20},{8,24},{12,28},{16,0},{20,4},{24,8},{28,12},{1,17},{... | collective-permute-start | bytes 786440 | tf_op jit(solution)/shard_map/ppermute | solution.py:20
  74.1 1.5 %collective-permute-start.25 = (f32[128,1024]{1,0:T(8,128)S(1)}, f32[128,1024]{1,0:T(8,128)}, u32[]{:S(2)}, u32[]{:S(2)}) collective-permute-start(f32[128,1024]{1,0:T(8,128)S(1)} %get-tuple-element.113.own_bottom), channel_id=1, source_target_pairs={{0,1},{1,0},{2,3},{3,2},{4,5},{5,4},{6,7},{7,6},{8,9},{9,8},{10,11... | collective-permute-start | bytes 1572872 | tf_op jit(solution)/shard_map/ppermute | solution.py:20
  75.6 1.5 %collective-permute-start.26 = (f32[128,1024]{1,0:T(8,128)S(1)}, f32[128,1024]{1,0:T(8,128)}, u32[]{:S(2)}, u32[]{:S(2)}) collective-permute-start(f32[128,1024]{1,0:T(8,128)S(1)} %get-tuple-element.114.own_top), channel_id=1, source_target_pairs={{0,2},{1,3},{2,0},{3,1},{4,6},{5,7},{6,4},{7,5},{8,10},{9,11},{10,... | collective-permute-start | bytes 1572872 | tf_op jit(solution)/shard_map/ppermute | solution.py:20
  77.8 8.1 %collective-permute-done.21 = f32[256,256]{1,0:T(8,128)} collective-permute-done((f32[256,256]{1,0:T(8,128)S(1)}, f32[256,256]{1,0:T(8,128)}, u32[]{:S(2)}, u32[]{:S(2)}) %collective-permute-start.21) | collective-permute-done | bytes 262176 | tf_op jit(solution)/shard_map/ppermute | solution.py:20
  86.6 1.5 %collective-permute-start.31 = (f32[128,1024]{1,0:T(8,128)S(1)}, f32[128,1024]{1,0:T(8,128)S(1)}, u32[]{:S(2)}, u32[]{:S(2)}) collective-permute-start(f32[128,1024]{1,0:T(8,128)S(1)} %collective-permute-done.22.refs_0_), channel_id=1, source_target_pairs={{0,2},{1,3},{2,0},{3,1},{4,6},{5,7},{6,4},{7,5},{8,10},{9,11},{10,... | collective-permute-start | bytes 1572872 | tf_op jit(solution)/shard_map/ppermute | solution.py:20
  88.1 1.5 %collective-permute-start.32 = (f32[128,1024]{1,0:T(8,128)S(1)}, f32[128,1024]{1,0:T(8,128)S(1)}, u32[]{:S(2)}, u32[]{:S(2)}) collective-permute-start(f32[128,1024]{1,0:T(8,128)S(1)} %collective-permute-done.23.refs_1_), channel_id=1, source_target_pairs={{0,1},{1,0},{2,3},{3,2},{4,5},{5,4},{6,7},{7,6},{8,9},{9,8},{10,11... | collective-permute-start | bytes 1572872 | tf_op jit(solution)/shard_map/ppermute | solution.py:20
  89.6 1.1 slice_bitcast_fusion.inverse
  91.6 1.8 %collective-permute-done.26.refs_3_ = f32[128,1024]{1,0:T(8,128)} collective-permute-done((f32[128,1024]{1,0:T(8,128)S(1)}, f32[128,1024]{1,0:T(8,128)}, u32[]{:S(2)}, u32[]{:S(2)}) %collective-permute-start.26) | collective-permute-done | bytes 524320 | tf_op jit(solution)/shard_map/ppermute | solution.py:20
  93.9 1.0 collective-permute-done.27.refs_2_
  95.8 3.8 %collective-permute-start.29 = (f32[128,256]{1,0:T(8,128)S(1)}, f32[128,256]{1,0:T(8,128)S(1)}, u32[]{:S(2)}, u32[]{:S(2)}) collective-permute-start(f32[128,256]{1,0:T(8,128)S(1)} %solve.3.refs_0_), channel_id=1, source_target_pairs={{0,16},{4,20},{8,24},{12,28},{16,0},{20,4},{24,8},{28,12},{1,17},{... | collective-permute-start | bytes 393224 | tf_op jit(solution)/shard_map/ppermute | solution.py:20
  99.6 1.7 %collective-permute-start.30 = (f32[128,256]{1,0:T(8,128)S(1)}, f32[128,256]{1,0:T(8,128)S(1)}, u32[]{:S(2)}, u32[]{:S(2)}) collective-permute-start(f32[128,256]{1,0:T(8,128)S(1)} %solve.3.refs_0_), channel_id=1, source_target_pairs={{0,8},{4,12},{8,0},{12,4},{16,24},{20,28},{24,16},{28,20},{1,9},{5... | collective-permute-start | bytes 393224 | tf_op jit(solution)/shard_map/ppermute | solution.py:20
  101.4 1.9 %collective-permute-done.31.refs_4_ = f32[128,1024]{1,0:T(8,128)S(1)} collective-permute-done((f32[128,1024]{1,0:T(8,128)S(1)}, f32[128,1024]{1,0:T(8,128)S(1)}, u32[]{:S(2)}, u32[]{:S(2)}) %collective-permute-start.31) | collective-permute-done | bytes 524320 | tf_op jit(solution)/shard_map/ppermute | solution.py:20
  103.3 3.0 %collective-permute-done.29.refs_2_ = f32[128,256]{1,0:T(8,128)S(1)} collective-permute-done((f32[128,256]{1,0:T(8,128)S(1)}, f32[128,256]{1,0:T(8,128)S(1)}, u32[]{:S(2)}, u32[]{:S(2)}) %collective-permute-start.29) | collective-permute-done | bytes 131104 | tf_op jit(solution)/shard_map/ppermute | solution.py:20
  106.4 1.6 %collective-permute-start.33 = (f32[128,256]{1,0:T(8,128)S(1)}, f32[128,256]{1,0:T(8,128)S(1)}, u32[]{:S(2)}, u32[]{:S(2)}) collective-permute-start(f32[128,256]{1,0:T(8,128)S(1)} %collective-permute-done.29.refs_2_), channel_id=1, source_target_pairs={{0,8},{4,12},{8,0},{12,4},{16,24},{20,28},{24,16},{28,20},{1,9},{5... | collective-permute-start | bytes 393224 | tf_op jit(solution)/shard_map/ppermute | solution.py:20
  108.5 1.8 %prepare.3 = (bf16[1024,1024]{1,0:T(8,128)(2,1)S(1)}, bf16[1024,1024]{1,0:T(8,128)(2,1)S(1)}) custom-call(f32[128,1024]{1,0:T(8,128)S(1)} %get-tuple-element.114.own_top, f32[128,1024]{1,0:T(8,128)S(1)} %get-tuple-element.113.own_bottom, f32[128,1024]{1,0:T(8,128)S(1)} %collective-permute-done.22.refs_0_, f32[128,1024]{1,0:T(8,128)S(1)} %collective-permute-done.23.refs_1_, ...), custom_call_target="tpu_custom_call" | custom-call | bytes 16777216 | tf_op jit(solution)/shard_map/prepare/pallas_call | solution.py:98
  110.4 1.0 collective-permute-done.33.refs_3_
  111.4 1.3 %collective-permute-done.37.refs_7_ = f32[128,256]{1,0:T(8,128)S(1)} collective-permute-done((f32[128,256]{1,0:T(8,128)S(1)}, f32[128,256]{1,0:T(8,128)S(1)}, u32[]{:S(2)}, u32[]{:S(2)}) %collective-permute-start.37) | collective-permute-done | bytes 131104 | tf_op jit(solution)/shard_map/ppermute | solution.py:20
  112.7 3.4 %update.3 = f32[1024,256]{1,0:T(8,128)} custom-call(s32[1,2]{1,0:T(1,128)S(1)} %copy-done.1, s32[8]{0:T(128)S(1)} %copy-done.2, bf16[1024,1024]{1,0:T(8,128)(2,1)S(1)} %get-tuple-element.127.high, bf16[1024,1024]{1,0:T(8,128)(2,1)S(1)} %get-tuple-element.128.low, f32[128,256]{1,0:T(8,128)S(1)} %solve.3.refs_0_, ...), custom_call_target="tpu_custom_call" | custom-call | flops 1610612736 | bytes 7340032 | tf_op jit(solution)/shard_map/update/pallas_call | solution.py:191
  (58 shorter events, 7.7 us)
Async XLA Ops:
  0.0 9.0 %copy-start.3 = (f32[1,2,256,1024]{3,2,1,0:T(8,128)S(1)}, f32[1,2,256,1024]{3,2,1,0:T(8,128)}, u32[]{:S(2)}) copy-start(f32[1,2,256,1024]{3,2,1,0:T(8,128)} %param.6) | copy-start | bytes 6291460
  2.0 4.2 %collective-permute-start = (f32[512,256]{1,0:T(8,128)}, f32[512,256]{1,0:T(8,128)S(1)}, u32[]{:S(2)}, u32[]{:S(2)}) collective-permute-start(f32[512,256]{1,0:T(8,128)} %dynamic-slice_bitcast_fusion), channel_id=1, source_target_pairs={{0,4},{4,0},{8,12},{12,8},{16,20},{20,16},{24,28},{28,24},{1,5},{5... | collective-permute-start | bytes 1572872 | tf_op jit(solution)/shard_map/ppermute | solution.py:20
  6.3 9.6 %collective-permute-start.1 = (f32[256,256]{1,0:T(8,128)S(1)}, f32[256,256]{1,0:T(8,128)S(1)}, u32[]{:S(2)}, u32[]{:S(2)}) collective-permute-start(f32[256,256]{1,0:T(8,128)S(1)} %constant_dynamic-slice_fusion.1), channel_id=1, source_target_pairs={{0,8},{4,12},{8,0},{12,4},{16,24},{20,28},{24,16},{28,20},{1,9},{5... | collective-permute-start | bytes 786440 | tf_op jit(solution)/shard_map/ppermute | solution.py:20
  9.1 21.8 %collective-permute-start.3 = (f32[128,1024]{1,0:T(8,128)S(1)}, f32[128,1024]{1,0:T(8,128)S(1)}, u32[]{:S(2)}, u32[]{:S(2)}) collective-permute-start(f32[128,1024]{1,0:T(8,128)S(1)} %get-tuple-element.84.own_top), channel_id=1, source_target_pairs={{0,1},{1,0},{2,3},{3,2},{4,5},{5,4},{6,7},{7,6},{8,9},{9,8},{10,11... | collective-permute-start | bytes 1572872 | tf_op jit(solution)/shard_map/ppermute | solution.py:20
  10.6 20.2 %collective-permute-start.4 = (f32[128,1024]{1,0:T(8,128)S(1)}, f32[128,1024]{1,0:T(8,128)S(1)}, u32[]{:S(2)}, u32[]{:S(2)}) collective-permute-start(f32[128,1024]{1,0:T(8,128)S(1)} %get-tuple-element.83.own_bottom), channel_id=1, source_target_pairs={{0,2},{1,3},{2,0},{3,1},{4,6},{5,7},{6,4},{7,5},{8,10},{9,11},{10,... | collective-permute-start | bytes 1572872 | tf_op jit(solution)/shard_map/ppermute | solution.py:20
  16.0 14.8 %collective-permute-start.2 = (f32[256,256]{1,0:T(8,128)S(1)}, f32[256,256]{1,0:T(8,128)}, u32[]{:S(2)}, u32[]{:S(2)}) collective-permute-start(f32[256,256]{1,0:T(8,128)S(1)} %dynamic-slice_select_fusion.1), channel_id=1, source_target_pairs={{0,16},{4,20},{8,24},{12,28},{16,0},{20,4},{24,8},{28,12},{1,17},{... | collective-permute-start | bytes 786440 | tf_op jit(solution)/shard_map/ppermute | solution.py:20
  18.8 16.8 %collective-permute-start.6 = (f32[128,1024]{1,0:T(8,128)S(1)}, f32[128,1024]{1,0:T(8,128)S(1)}, u32[]{:S(2)}, u32[]{:S(2)}) collective-permute-start(f32[128,1024]{1,0:T(8,128)S(1)} %get-tuple-element.83.own_bottom), channel_id=1, source_target_pairs={{0,1},{1,0},{2,3},{3,2},{4,5},{5,4},{6,7},{7,6},{8,9},{9,8},{10,11... | collective-permute-start | bytes 1572872 | tf_op jit(solution)/shard_map/ppermute | solution.py:20
  20.3 16.4 %collective-permute-start.7 = (f32[128,1024]{1,0:T(8,128)S(1)}, f32[128,1024]{1,0:T(8,128)S(1)}, u32[]{:S(2)}, u32[]{:S(2)}) collective-permute-start(f32[128,1024]{1,0:T(8,128)S(1)} %get-tuple-element.84.own_top), channel_id=1, source_target_pairs={{0,2},{1,3},{2,0},{3,1},{4,6},{5,7},{6,4},{7,5},{8,10},{9,11},{10,... | collective-permute-start | bytes 1572872 | tf_op jit(solution)/shard_map/ppermute | solution.py:20
  30.9 7.4 %collective-permute-start.5 = (f32[256,256]{1,0:T(8,128)S(1)}, f32[256,256]{1,0:T(8,128)S(1)}, u32[]{:S(2)}, u32[]{:S(2)}) collective-permute-start(f32[256,256]{1,0:T(8,128)S(1)} %broadcast_select_fusion.2.refs_0_), channel_id=1, source_target_pairs={{0,8},{4,12},{8,0},{12,4},{16,24},{20,28},{24,16},{28,20},{1,9},{5... | collective-permute-start | bytes 786440 | tf_op jit(solution)/shard_map/ppermute | solution.py:20
  31.5 15.4 %collective-permute-start.12 = (f32[128,1024]{1,0:T(8,128)S(1)}, f32[128,1024]{1,0:T(8,128)S(1)}, u32[]{:S(2)}, u32[]{:S(2)}) collective-permute-start(f32[128,1024]{1,0:T(8,128)S(1)} %collective-permute-done.3.refs_0_), channel_id=1, source_target_pairs={{0,2},{1,3},{2,0},{3,1},{4,6},{5,7},{6,4},{7,5},{8,10},{9,11},{10,... | collective-permute-start | bytes 1572872 | tf_op jit(solution)/shard_map/ppermute | solution.py:20
  33.0 13.9 %collective-permute-start.13 = (f32[128,1024]{1,0:T(8,128)S(1)}, f32[128,1024]{1,0:T(8,128)S(1)}, u32[]{:S(2)}, u32[]{:S(2)}) collective-permute-start(f32[128,1024]{1,0:T(8,128)S(1)} %collective-permute-done.4.refs_1_), channel_id=1, source_target_pairs={{0,1},{1,0},{2,3},{3,2},{4,5},{5,4},{6,7},{7,6},{8,9},{9,8},{10,11... | collective-permute-start | bytes 1572872 | tf_op jit(solution)/shard_map/ppermute | solution.py:20
  36.7 1.6 %collective-permute-start.8 = (f32[256,256]{1,0:T(8,128)S(1)}, f32[256,256]{1,0:T(8,128)S(1)}, u32[]{:S(2)}, u32[]{:S(2)}) collective-permute-start(f32[256,256]{1,0:T(8,128)S(1)} %broadcast_select_fusion.2.refs_0_), channel_id=1, source_target_pairs={{0,4},{4,0},{8,12},{12,8},{16,20},{20,16},{24,28},{28,24},{1,5},{5... | collective-permute-start | bytes 786440 | tf_op jit(solution)/shard_map/ppermute | solution.py:20
  38.2 1.5 %collective-permute-start.9 = (f32[256,256]{1,0:T(8,128)S(1)}, f32[256,256]{1,0:T(8,128)S(1)}, u32[]{:S(2)}, u32[]{:S(2)}) collective-permute-start(f32[256,256]{1,0:T(8,128)S(1)} %collective-permute-done.5.refs_1_), channel_id=1, source_target_pairs={{0,4},{4,0},{8,12},{12,8},{16,20},{20,16},{24,28},{28,24},{1,5},{5... | collective-permute-start | bytes 786440 | tf_op jit(solution)/shard_map/ppermute | solution.py:20
  40.3 17.4 %copy-start = (f32[1,1024,256]{2,1,0:T(8,128)S(1)}, f32[1,1024,256]{2,1,0:T(8,128)}, u32[]{:S(2)}) copy-start(f32[1,1024,256]{2,1,0:T(8,128)} %refs_8_.1) | copy-start | bytes 3145732
  40.3 17.4 %copy-start.1 = (s32[1,2]{1,0:T(1,128)S(1)}, s32[1,2]{1,0:T(1,128)}, u32[]{:S(2)}) copy-start(s32[1,2]{1,0:T(1,128)} %flags.3) | copy-start | bytes 28
  40.3 17.4 %copy-start.2 = (s32[8]{0:T(128)S(1)}, s32[8]{0:T(128)}, u32[]{:S(2)}) copy-start(s32[8]{0:T(128)} %slot_block.3) | copy-start | bytes 100
  40.3 10.9 %collective-permute-start.10 = (f32[128,256]{1,0:T(8,128)S(1)}, f32[128,256]{1,0:T(8,128)S(1)}, u32[]{:S(2)}, u32[]{:S(2)}) collective-permute-start(f32[128,256]{1,0:T(8,128)S(1)} %solve.2.refs_0_), channel_id=1, source_target_pairs={{0,16},{4,20},{8,24},{12,28},{16,0},{20,4},{24,8},{28,12},{1,17},{... | collective-permute-start | bytes 393224 | tf_op jit(solution)/shard_map/ppermute | solution.py:20
  44.5 6.8 %collective-permute-start.11 = (f32[128,256]{1,0:T(8,128)S(1)}, f32[128,256]{1,0:T(8,128)S(1)}, u32[]{:S(2)}, u32[]{:S(2)}) collective-permute-start(f32[128,256]{1,0:T(8,128)S(1)} %solve.2.refs_0_), channel_id=1, source_target_pairs={{0,8},{4,12},{8,0},{12,4},{16,24},{20,28},{24,16},{28,20},{1,9},{5... | collective-permute-start | bytes 393224 | tf_op jit(solution)/shard_map/ppermute | solution.py:20
  46.3 8.2 %collective-permute-start.15 = (f32[128,256]{1,0:T(8,128)S(1)}, f32[128,256]{1,0:T(8,128)S(1)}, u32[]{:S(2)}, u32[]{:S(2)}) collective-permute-start(f32[128,256]{1,0:T(8,128)S(1)} %solve.2.refs_0_), channel_id=1, source_target_pairs={{0,4},{4,0},{8,12},{12,8},{16,20},{20,16},{24,28},{28,24},{1,5},{5... | collective-permute-start | bytes 393224 | tf_op jit(solution)/shard_map/ppermute | solution.py:20
  51.3 5.0 %collective-permute-start.14 = (f32[128,256]{1,0:T(8,128)S(1)}, f32[128,256]{1,0:T(8,128)S(1)}, u32[]{:S(2)}, u32[]{:S(2)}) collective-permute-start(f32[128,256]{1,0:T(8,128)S(1)} %collective-permute-done.10.refs_2_), channel_id=1, source_target_pairs={{0,8},{4,12},{8,0},{12,4},{16,24},{20,28},{24,16},{28,20},{1,9},{5... | collective-permute-start | bytes 393224 | tf_op jit(solution)/shard_map/ppermute | solution.py:20
  52.9 3.4 %collective-permute-start.16 = (f32[128,256]{1,0:T(8,128)S(1)}, f32[128,256]{1,0:T(8,128)S(1)}, u32[]{:S(2)}, u32[]{:S(2)}) collective-permute-start(f32[128,256]{1,0:T(8,128)S(1)} %collective-permute-done.11.refs_1_), channel_id=1, source_target_pairs={{0,4},{4,0},{8,12},{12,8},{16,20},{20,16},{24,28},{28,24},{1,5},{5... | collective-permute-start | bytes 393224 | tf_op jit(solution)/shard_map/ppermute | solution.py:20
  52.9 3.4 %collective-permute-start.17 = (f32[128,256]{1,0:T(8,128)S(1)}, f32[128,256]{1,0:T(8,128)S(1)}, u32[]{:S(2)}, u32[]{:S(2)}) collective-permute-start(f32[128,256]{1,0:T(8,128)S(1)} %collective-permute-done.10.refs_2_), channel_id=1, source_target_pairs={{0,4},{4,0},{8,12},{12,8},{16,20},{20,16},{24,28},{28,24},{1,5},{5... | collective-permute-start | bytes 393224 | tf_op jit(solution)/shard_map/ppermute | solution.py:20
  56.3 1.4 %collective-permute-start.18 = (f32[128,256]{1,0:T(8,128)S(1)}, f32[128,256]{1,0:T(8,128)S(1)}, u32[]{:S(2)}, u32[]{:S(2)}) collective-permute-start(f32[128,256]{1,0:T(8,128)S(1)} %collective-permute-done.14.refs_3_), channel_id=1, source_target_pairs={{0,4},{4,0},{8,12},{12,8},{16,20},{20,16},{24,28},{28,24},{1,5},{5... | collective-permute-start | bytes 393224 | tf_op jit(solution)/shard_map/ppermute | solution.py:20
  60.3 2.3 %collective-permute-start.19 = (f32[512,256]{1,0:T(8,128)S(1)}, f32[512,256]{1,0:T(8,128)S(1)}, u32[]{:S(2)}, u32[]{:S(2)}) collective-permute-start(f32[512,256]{1,0:T(8,128)S(1)} %get-tuple-element.104.refs_9_), channel_id=1, source_target_pairs={{0,4},{4,0},{8,12},{12,8},{16,20},{20,16},{24,28},{28,24},{1,5},{5... | collective-permute-start | bytes 1572872 | tf_op jit(solution)/shard_map/ppermute | solution.py:20
  62.7 8.6 %collective-permute-start.20 = (f32[256,256]{1,0:T(8,128)S(1)}, f32[256,256]{1,0:T(8,128)S(1)}, u32[]{:S(2)}, u32[]{:S(2)}) collective-permute-start(f32[256,256]{1,0:T(8,128)S(1)} %constant_dynamic-slice_fusion), channel_id=1, source_target_pairs={{0,8},{4,12},{8,0},{12,4},{16,24},{20,28},{24,16},{28,20},{1,9},{5... | collective-permute-start | bytes 786440 | tf_op jit(solution)/shard_map/ppermute | solution.py:20
  65.7 20.3 %collective-permute-start.22 = (f32[128,1024]{1,0:T(8,128)S(1)}, f32[128,1024]{1,0:T(8,128)S(1)}, u32[]{:S(2)}, u32[]{:S(2)}) collective-permute-start(f32[128,1024]{1,0:T(8,128)S(1)} %get-tuple-element.114.own_top), channel_id=1, source_target_pairs={{0,1},{1,0},{2,3},{3,2},{4,5},{5,4},{6,7},{7,6},{8,9},{9,8},{10,11... | collective-permute-start | bytes 1572872 | tf_op jit(solution)/shard_map/ppermute | solution.py:20
  67.2 18.7 %collective-permute-start.23 = (f32[128,1024]{1,0:T(8,128)S(1)}, f32[128,1024]{1,0:T(8,128)S(1)}, u32[]{:S(2)}, u32[]{:S(2)}) collective-permute-start(f32[128,1024]{1,0:T(8,128)S(1)} %get-tuple-element.113.own_bottom), channel_id=1, source_target_pairs={{0,2},{1,3},{2,0},{3,1},{4,6},{5,7},{6,4},{7,5},{8,10},{9,11},{10,... | collective-permute-start | bytes 1572872 | tf_op jit(solution)/shard_map/ppermute | solution.py:20
  71.4 14.5 %collective-permute-start.21 = (f32[256,256]{1,0:T(8,128)S(1)}, f32[256,256]{1,0:T(8,128)}, u32[]{:S(2)}, u32[]{:S(2)}) collective-permute-start(f32[256,256]{1,0:T(8,128)S(1)} %dynamic-slice_select_fusion), channel_id=1, source_target_pairs={{0,16},{4,20},{8,24},{12,28},{16,0},{20,4},{24,8},{28,12},{1,17},{... | collective-permute-start | bytes 786440 | tf_op jit(solution)/shard_map/ppermute | solution.py:20
  74.1 17.5 %collective-permute-start.25 = (f32[128,1024]{1,0:T(8,128)S(1)}, f32[128,1024]{1,0:T(8,128)}, u32[]{:S(2)}, u32[]{:S(2)}) collective-permute-start(f32[128,1024]{1,0:T(8,128)S(1)} %get-tuple-element.113.own_bottom), channel_id=1, source_target_pairs={{0,1},{1,0},{2,3},{3,2},{4,5},{5,4},{6,7},{7,6},{8,9},{9,8},{10,11... | collective-permute-start | bytes 1572872 | tf_op jit(solution)/shard_map/ppermute | solution.py:20
  75.6 17.8 %collective-permute-start.26 = (f32[128,1024]{1,0:T(8,128)S(1)}, f32[128,1024]{1,0:T(8,128)}, u32[]{:S(2)}, u32[]{:S(2)}) collective-permute-start(f32[128,1024]{1,0:T(8,128)S(1)} %get-tuple-element.114.own_top), channel_id=1, source_target_pairs={{0,2},{1,3},{2,0},{3,1},{4,6},{5,7},{6,4},{7,5},{8,10},{9,11},{10,... | collective-permute-start | bytes 1572872 | tf_op jit(solution)/shard_map/ppermute | solution.py:20
  85.9 7.5 %collective-permute-start.24 = (f32[256,256]{1,0:T(8,128)S(1)}, f32[256,256]{1,0:T(8,128)S(1)}, u32[]{:S(2)}, u32[]{:S(2)}) collective-permute-start(f32[256,256]{1,0:T(8,128)S(1)} %broadcast_select_fusion.3.refs_0_), channel_id=1, source_target_pairs={{0,8},{4,12},{8,0},{12,4},{16,24},{20,28},{24,16},{28,20},{1,9},{5... | collective-permute-start | bytes 786440 | tf_op jit(solution)/shard_map/ppermute | solution.py:20
  86.6 16.7 %collective-permute-start.31 = (f32[128,1024]{1,0:T(8,128)S(1)}, f32[128,1024]{1,0:T(8,128)S(1)}, u32[]{:S(2)}, u32[]{:S(2)}) collective-permute-start(f32[128,1024]{1,0:T(8,128)S(1)} %collective-permute-done.22.refs_0_), channel_id=1, source_target_pairs={{0,2},{1,3},{2,0},{3,1},{4,6},{5,7},{6,4},{7,5},{8,10},{9,11},{10,... | collective-permute-start | bytes 1572872 | tf_op jit(solution)/shard_map/ppermute | solution.py:20
  88.1 15.2 %collective-permute-start.32 = (f32[128,1024]{1,0:T(8,128)S(1)}, f32[128,1024]{1,0:T(8,128)S(1)}, u32[]{:S(2)}, u32[]{:S(2)}) collective-permute-start(f32[128,1024]{1,0:T(8,128)S(1)} %collective-permute-done.23.refs_1_), channel_id=1, source_target_pairs={{0,1},{1,0},{2,3},{3,2},{4,5},{5,4},{6,7},{7,6},{8,9},{9,8},{10,11... | collective-permute-start | bytes 1572872 | tf_op jit(solution)/shard_map/ppermute | solution.py:20
  93.4 1.5 %collective-permute-start.27 = (f32[256,256]{1,0:T(8,128)S(1)}, f32[256,256]{1,0:T(8,128)S(1)}, u32[]{:S(2)}, u32[]{:S(2)}) collective-permute-start(f32[256,256]{1,0:T(8,128)S(1)} %broadcast_select_fusion.3.refs_0_), channel_id=1, source_target_pairs={{0,4},{4,0},{8,12},{12,8},{16,20},{20,16},{24,28},{28,24},{1,5},{5... | collective-permute-start | bytes 786440 | tf_op jit(solution)/shard_map/ppermute | solution.py:20
  93.4 1.9 %collective-permute-start.28 = (f32[256,256]{1,0:T(8,128)S(1)}, f32[256,256]{1,0:T(8,128)S(1)}, u32[]{:S(2)}, u32[]{:S(2)}) collective-permute-start(f32[256,256]{1,0:T(8,128)S(1)} %collective-permute-done.24.refs_1_), channel_id=1, source_target_pairs={{0,4},{4,0},{8,12},{12,8},{16,20},{20,16},{24,28},{28,24},{1,5},{5... | collective-permute-start | bytes 786440 | tf_op jit(solution)/shard_map/ppermute | solution.py:20
  95.8 10.6 %collective-permute-start.29 = (f32[128,256]{1,0:T(8,128)S(1)}, f32[128,256]{1,0:T(8,128)S(1)}, u32[]{:S(2)}, u32[]{:S(2)}) collective-permute-start(f32[128,256]{1,0:T(8,128)S(1)} %solve.3.refs_0_), channel_id=1, source_target_pairs={{0,16},{4,20},{8,24},{12,28},{16,0},{20,4},{24,8},{28,12},{1,17},{... | collective-permute-start | bytes 393224 | tf_op jit(solution)/shard_map/ppermute | solution.py:20
  99.6 6.8 %collective-permute-start.30 = (f32[128,256]{1,0:T(8,128)S(1)}, f32[128,256]{1,0:T(8,128)S(1)}, u32[]{:S(2)}, u32[]{:S(2)}) collective-permute-start(f32[128,256]{1,0:T(8,128)S(1)} %solve.3.refs_0_), channel_id=1, source_target_pairs={{0,8},{4,12},{8,0},{12,4},{16,24},{20,28},{24,16},{28,20},{1,9},{5... | collective-permute-start | bytes 393224 | tf_op jit(solution)/shard_map/ppermute | solution.py:20
  101.4 9.0 %collective-permute-start.34 = (f32[128,256]{1,0:T(8,128)S(1)}, f32[128,256]{1,0:T(8,128)S(1)}, u32[]{:S(2)}, u32[]{:S(2)}) collective-permute-start(f32[128,256]{1,0:T(8,128)S(1)} %solve.3.refs_0_), channel_id=1, source_target_pairs={{0,4},{4,0},{8,12},{12,8},{16,20},{20,16},{24,28},{28,24},{1,5},{5... | collective-permute-start | bytes 393224 | tf_op jit(solution)/shard_map/ppermute | solution.py:20
  106.4 5.0 %collective-permute-start.33 = (f32[128,256]{1,0:T(8,128)S(1)}, f32[128,256]{1,0:T(8,128)S(1)}, u32[]{:S(2)}, u32[]{:S(2)}) collective-permute-start(f32[128,256]{1,0:T(8,128)S(1)} %collective-permute-done.29.refs_2_), channel_id=1, source_target_pairs={{0,8},{4,12},{8,0},{12,4},{16,24},{20,28},{24,16},{28,20},{1,9},{5... | collective-permute-start | bytes 393224 | tf_op jit(solution)/shard_map/ppermute | solution.py:20
  108.0 3.4 %collective-permute-start.35 = (f32[128,256]{1,0:T(8,128)S(1)}, f32[128,256]{1,0:T(8,128)S(1)}, u32[]{:S(2)}, u32[]{:S(2)}) collective-permute-start(f32[128,256]{1,0:T(8,128)S(1)} %collective-permute-done.30.refs_1_), channel_id=1, source_target_pairs={{0,4},{4,0},{8,12},{12,8},{16,20},{20,16},{24,28},{28,24},{1,5},{5... | collective-permute-start | bytes 393224 | tf_op jit(solution)/shard_map/ppermute | solution.py:20
  108.0 3.4 %collective-permute-start.36 = (f32[128,256]{1,0:T(8,128)S(1)}, f32[128,256]{1,0:T(8,128)S(1)}, u32[]{:S(2)}, u32[]{:S(2)}) collective-permute-start(f32[128,256]{1,0:T(8,128)S(1)} %collective-permute-done.29.refs_2_), channel_id=1, source_target_pairs={{0,4},{4,0},{8,12},{12,8},{16,20},{20,16},{24,28},{28,24},{1,5},{5... | collective-permute-start | bytes 393224 | tf_op jit(solution)/shard_map/ppermute | solution.py:20
  111.4 1.4 %collective-permute-start.37 = (f32[128,256]{1,0:T(8,128)S(1)}, f32[128,256]{1,0:T(8,128)S(1)}, u32[]{:S(2)}, u32[]{:S(2)}) collective-permute-start(f32[128,256]{1,0:T(8,128)S(1)} %collective-permute-done.33.refs_3_), channel_id=1, source_target_pairs={{0,4},{4,0},{8,12},{12,8},{16,20},{20,16},{24,28},{28,24},{1,5},{5... | collective-permute-start | bytes 393224 | tf_op jit(solution)/shard_map/ppermute | solution.py:20

commit v7 on v4

--- a/solution.py
+++ b/solution.py
@@ -105,6 +105,32 @@
         cost_estimate=pl.CostEstimate(flops=0, bytes_accessed=16 * depth * depth, transcendentals=0),
         name="prepare",
     )(*pieces)
+
+
+def cut_body(block, send, keep, sems):
+    core = bit(lax.axis_index("row"), 0)
+    size = send.shape[0]
+    copies = []
+    for index, (out, part) in enumerate(((send, 1 - core), (keep, core))):
+        rows = pl.ds(pl.multiple_of(part * size, size), size)
+        copies.append(pltpu.make_async_copy(block.at[0, rows], out, sems.at[index]))
+        copies[index].start()
+    for copy in copies:
+        copy.wait()
+
+
+def cut(block):
+    _, rows, cols = block.shape
+    return pl.pallas_call(
+        cut_body,
+        out_shape=[jax.ShapeDtypeStruct((rows // 2, cols), jnp.float32)] * 2,
+        in_specs=[pl.BlockSpec(memory_space=pl.ANY)],
+        out_specs=[pl.BlockSpec(memory_space=pltpu.VMEM)] * 2,
+        scratch_shapes=[pltpu.SemaphoreType.DMA((2,))],
+        compiler_params=pltpu.CompilerParams(vmem_limit_bytes=PREPARE_BYTES),
+        cost_estimate=pl.CostEstimate(flops=0, bytes_accessed=8 * rows * cols, transcendentals=0),
+        name="cut",
+    )(block)
 
 
 def assemble(x, blocks, rank):
@@ -243,9 +269,11 @@
         y, inverse, *first = tie(y, diag_inverse, *first)
         pieces = far(*first)
         beside = swap(y, "row", 1, rows)
-        beside, y, *second = tie(beside, y, *second)
-        other, last = swap(y, "row", 0, rows), swap(beside, "row", 0, rows)
-        x = solve(inverse[step], [y, beside, other, last])
+        y, *second = tie(y, *second)
+        other = swap(y, "row", 0, rows)
+        beside, inverse = tie(beside, inverse[step])
+        last = swap(beside, "row", 0, rows)
+        x = solve(inverse, [y, beside, other, last])
         x2, x1 = swap(x, "row", 2, rows), swap(x, "row", 1, rows)
         x2, x1, *pieces = tie(x2, x1, *pieces)
         high, low = prepare([*block, *first, *second, *pieces])
@@ -254,9 +282,8 @@
         x3, high, low, *across = tie(x3, high, low, *across)
         return [x, x1, x2, x3, *across, swap(x3, "row", 0, rows)], (high, low)
 
-    keep, send = halves(rhs[0], core)
+    send, keep = cut(rhs)
     got = swap(send, "row", 0, rows)
-    keep, send = tie(keep, send)
     y = jnp.where(bit(owner, 0) == core, keep, got)
     blocks, pair = solved(0, y, panel, owner)
     keep, send = update(0, flags, slot_block, pair, blocks, [rhs])

time: 114 us -> 115 us (level)
  starting transfers between devices: 40.4 us -> 44.7 us
  waiting for transfers between devices: 50.1 us -> 47.4 us
    ppermute x38, starting transfers between devices: 40.4 us -> 44.7 us  [swap(): return lax.ppermute(x, axis, [(i, i ^ 1 << b) for i in range(size)])]
    ppermute x38, waiting for transfers between devices: 50.1 us -> 47.4 us  [swap(): return lax.ppermute(x, axis, [(i, i ^ 1 << b) for i in range(size)])]
    dynamic_slice x3 -> x2, local copies, waits for them, and re-layouts: 2.26 us -> 0.05 us  [halves(): lax.dynamic_slice_in_dim(x, (1 - b) * half, half)]
    unnamed x8 -> x10, local copies, waits for them, and re-layouts: 0.02 us -> 1.25 us
  transfers between devices with their start and end apart: 38 -> 38, of which waited for: 18 -> 20; matrix products, arithmetic and copies ran while one was open for 6% -> 6% of each run, Pallas kernels for 3% -> 3%
where the time goes in v7:
time: 115 us
  waiting for transfers between devices  47.4 us (41%)
  starting transfers between devices  44.7 us (39%)
  Pallas kernels  10.1 us (9%)
  local copies, waits for them, and re-layouts  4.82 us (4%)
  between operations  4.24 us (4%)
  other arithmetic  3.37 us (3%)
    ppermute x38, waiting for transfers between devices, swap(): return lax.ppermute(x, axis, [(i, i ^ 1 << b) for i in range(size)])  47.4 us
    ppermute x38, starting transfers between devices, swap(): return lax.ppermute(x, axis, [(i, i ^ 1 << b) for i in range(size)])  44.7 us
    pallas_call x2, Pallas kernels, update(): pl.pallas_call(first_body if step == 0 else second_body, out_shape=[jax.S...  6.1 us
    pallas_call x2, Pallas kernels, prepare(): pl.pallas_call(prepare_body, out_shape=[jax.ShapeDtypeStruct((depth, dept...  2.91 us
  transfers between devices with their start and end apart: 38, of which 20 were waited for; matrix products, arithmetic and copies ran while one was open for 6% of the time, Pallas kernels for 3%

profile of v7, /device:TPU:0, one launch (start us, length us, event | category | flops | bytes accessed | tf_op | source)
XLA Modules:
  0.0 114.6 jit_solution(17823615969669681302)
XLA Ops:
  0.0 1.2 %copy-done = f32[1,1024,256]{2,1,0:T(8,128)S(1)} copy-done((f32[1,1024,256]{2,1,0:T(8,128)S(1)}, f32[1,1024,256]{2,1,0:T(8,128)}, u32[]{:S(2)}) %copy-start) | copy-done | bytes 1048600
  1.8 1.4 %compare_reduce_fusion = (pred[]{:T(512)}, s32[]{:T(128)}) fusion(s32[8]{0:T(128)} %slot_block.3), kind=kLoop, calls=%fused_computation.12 | loop fusion | flops 57 | bytes 37 | tf_op jit(solution)/shard_map/paced/reduce | solution.py:248
  4.8 2.7 %collective-permute-start.1 = (f32[256,256]{1,0:T(8,128)S(1)}, f32[256,256]{1,0:T(8,128)S(1)}, u32[]{:S(2)}, u32[]{:S(2)}) collective-permute-start(f32[256,256]{1,0:T(8,128)S(1)} %constant_dynamic-slice_fusion.1), channel_id=1, source_target_pairs={{0,8},{4,12},{8,0},{12,4},{16,24},{20,28},{24,16},{28,20},{1,9},{5... | collective-permute-start | bytes 786440 | tf_op jit(solution)/shard_map/ppermute | solution.py:20
  7.6 1.6 %collective-permute-start.3 = (f32[128,1024]{1,0:T(8,128)S(1)}, f32[128,1024]{1,0:T(8,128)S(1)}, u32[]{:S(2)}, u32[]{:S(2)}) collective-permute-start(f32[128,1024]{1,0:T(8,128)S(1)} %get-tuple-element.80.own_top), channel_id=1, source_target_pairs={{0,1},{1,0},{2,3},{3,2},{4,5},{5,4},{6,7},{7,6},{8,9},{9,8},{10,11... | collective-permute-start | bytes 1572872 | tf_op jit(solution)/shard_map/ppermute | solution.py:20
  9.2 1.5 %collective-permute-start.4 = (f32[128,1024]{1,0:T(8,128)S(1)}, f32[128,1024]{1,0:T(8,128)S(1)}, u32[]{:S(2)}, u32[]{:S(2)}) collective-permute-start(f32[128,1024]{1,0:T(8,128)S(1)} %get-tuple-element.79.own_bottom), channel_id=1, source_target_pairs={{0,2},{1,3},{2,0},{3,1},{4,6},{5,7},{6,4},{7,5},{8,10},{9,11},{10,... | collective-permute-start | bytes 1572872 | tf_op jit(solution)/shard_map/ppermute | solution.py:20
  10.7 3.3 %collective-permute-done.1 = f32[256,256]{1,0:T(8,128)S(1)} collective-permute-done((f32[256,256]{1,0:T(8,128)S(1)}, f32[256,256]{1,0:T(8,128)S(1)}, u32[]{:S(2)}, u32[]{:S(2)}) %collective-permute-start.1) | collective-permute-done | bytes 262176 | tf_op jit(solution)/shard_map/ppermute | solution.py:20
  14.0 3.4 %collective-permute-start.2 = (f32[256,256]{1,0:T(8,128)S(1)}, f32[256,256]{1,0:T(8,128)}, u32[]{:S(2)}, u32[]{:S(2)}) collective-permute-start(f32[256,256]{1,0:T(8,128)S(1)} %dynamic-slice_select_fusion.1), channel_id=1, source_target_pairs={{0,16},{4,20},{8,24},{12,28},{16,0},{20,4},{24,8},{28,12},{1,17},{... | collective-permute-start | bytes 786440 | tf_op jit(solution)/shard_map/ppermute | solution.py:20
  17.4 1.5 %collective-permute-start.6 = (f32[128,1024]{1,0:T(8,128)S(1)}, f32[128,1024]{1,0:T(8,128)S(1)}, u32[]{:S(2)}, u32[]{:S(2)}) collective-permute-start(f32[128,1024]{1,0:T(8,128)S(1)} %get-tuple-element.79.own_bottom), channel_id=1, source_target_pairs={{0,1},{1,0},{2,3},{3,2},{4,5},{5,4},{6,7},{7,6},{8,9},{9,8},{10,11... | collective-permute-start | bytes 1572872 | tf_op jit(solution)/shard_map/ppermute | solution.py:20
  18.9 1.5 %collective-permute-start.7 = (f32[128,1024]{1,0:T(8,128)S(1)}, f32[128,1024]{1,0:T(8,128)S(1)}, u32[]{:S(2)}, u32[]{:S(2)}) collective-permute-start(f32[128,1024]{1,0:T(8,128)S(1)} %get-tuple-element.80.own_top), channel_id=1, source_target_pairs={{0,2},{1,3},{2,0},{3,1},{4,6},{5,7},{6,4},{7,5},{8,10},{9,11},{10,... | collective-permute-start | bytes 1572872 | tf_op jit(solution)/shard_map/ppermute | solution.py:20
  21.1 9.0 %collective-permute-done.2 = f32[256,256]{1,0:T(8,128)} collective-permute-done((f32[256,256]{1,0:T(8,128)S(1)}, f32[256,256]{1,0:T(8,128)}, u32[]{:S(2)}, u32[]{:S(2)}) %collective-permute-start.2) | collective-permute-done | bytes 262176 | tf_op jit(solution)/shard_map/ppermute | solution.py:20
  30.2 0.7 collective-permute-start.5
  30.9 1.5 %collective-permute-start.12 = (f32[128,1024]{1,0:T(8,128)S(1)}, f32[128,1024]{1,0:T(8,128)S(1)}, u32[]{:S(2)}, u32[]{:S(2)}) collective-permute-start(f32[128,1024]{1,0:T(8,128)S(1)} %collective-permute-done.3.refs_0_), channel_id=1, source_target_pairs={{0,2},{1,3},{2,0},{3,1},{4,6},{5,7},{6,4},{7,5},{8,10},{9,11},{10,... | collective-permute-start | bytes 1572872 | tf_op jit(solution)/shard_map/ppermute | solution.py:20
  32.4 1.5 %collective-permute-start.13 = (f32[128,1024]{1,0:T(8,128)S(1)}, f32[128,1024]{1,0:T(8,128)S(1)}, u32[]{:S(2)}, u32[]{:S(2)}) collective-permute-start(f32[128,1024]{1,0:T(8,128)S(1)} %collective-permute-done.4.refs_1_), channel_id=1, source_target_pairs={{0,1},{1,0},{2,3},{3,2},{4,5},{5,4},{6,7},{7,6},{8,9},{9,8},{10,11... | collective-permute-start | bytes 1572872 | tf_op jit(solution)/shard_map/ppermute | solution.py:20
  33.9 1.1 slice_bitcast_fusion.3.inverse
  35.2 3.2 %collective-permute-done.5.refs_1_ = f32[256,256]{1,0:T(8,128)S(1)} collective-permute-done((f32[256,256]{1,0:T(8,128)S(1)}, f32[256,256]{1,0:T(8,128)S(1)}, u32[]{:S(2)}, u32[]{:S(2)}) %collective-permute-start.5) | collective-permute-done | bytes 262176 | tf_op jit(solution)/shard_map/ppermute | solution.py:20
  38.4 1.5 %collective-permute-done.9.refs_3_ = f32[256,256]{1,0:T(8,128)S(1)} collective-permute-done((f32[256,256]{1,0:T(8,128)S(1)}, f32[256,256]{1,0:T(8,128)S(1)}, u32[]{:S(2)}, u32[]{:S(2)}) %collective-permute-start.9) | collective-permute-done | bytes 262176 | tf_op jit(solution)/shard_map/ppermute | solution.py:20
  40.4 3.5 %collective-permute-start.10 = (f32[128,256]{1,0:T(8,128)S(1)}, f32[128,256]{1,0:T(8,128)S(1)}, u32[]{:S(2)}, u32[]{:S(2)}) collective-permute-start(f32[128,256]{1,0:T(8,128)S(1)} %solve.2.refs_0_), channel_id=1, source_target_pairs={{0,16},{4,20},{8,24},{12,28},{16,0},{20,4},{24,8},{28,12},{1,17},{... | collective-permute-start | bytes 393224 | tf_op jit(solution)/shard_map/ppermute | solution.py:20
  44.0 1.7 %collective-permute-start.11 = (f32[128,256]{1,0:T(8,128)S(1)}, f32[128,256]{1,0:T(8,128)S(1)}, u32[]{:S(2)}, u32[]{:S(2)}) collective-permute-start(f32[128,256]{1,0:T(8,128)S(1)} %solve.2.refs_0_), channel_id=1, source_target_pairs={{0,8},{4,12},{8,0},{12,4},{16,24},{20,28},{24,16},{28,20},{1,9},{5... | collective-permute-start | bytes 393224 | tf_op jit(solution)/shard_map/ppermute | solution.py:20
  46.3 4.4 %collective-permute-done.10.refs_2_ = f32[128,256]{1,0:T(8,128)S(1)} collective-permute-done((f32[128,256]{1,0:T(8,128)S(1)}, f32[128,256]{1,0:T(8,128)S(1)}, u32[]{:S(2)}, u32[]{:S(2)}) %collective-permute-start.10) | collective-permute-done | bytes 131104 | tf_op jit(solution)/shard_map/ppermute | solution.py:20
  50.8 1.6 %collective-permute-start.14 = (f32[128,256]{1,0:T(8,128)S(1)}, f32[128,256]{1,0:T(8,128)S(1)}, u32[]{:S(2)}, u32[]{:S(2)}) collective-permute-start(f32[128,256]{1,0:T(8,128)S(1)} %collective-permute-done.10.refs_2_), channel_id=1, source_target_pairs={{0,8},{4,12},{8,0},{12,4},{16,24},{20,28},{24,16},{28,20},{1,9},{5... | collective-permute-start | bytes 393224 | tf_op jit(solution)/shard_map/ppermute | solution.py:20
  52.9 1.1 prepare.2
  53.9 1.8 %collective-permute-done.14.refs_3_ = f32[128,256]{1,0:T(8,128)S(1)} collective-permute-done((f32[128,256]{1,0:T(8,128)S(1)}, f32[128,256]{1,0:T(8,128)S(1)}, u32[]{:S(2)}, u32[]{:S(2)}) %collective-permute-start.14) | collective-permute-done | bytes 131104 | tf_op jit(solution)/shard_map/ppermute | solution.py:20
  55.7 1.3 %collective-permute-done.18.refs_7_ = f32[128,256]{1,0:T(8,128)S(1)} collective-permute-done((f32[128,256]{1,0:T(8,128)S(1)}, f32[128,256]{1,0:T(8,128)S(1)}, u32[]{:S(2)}, u32[]{:S(2)}) %collective-permute-start.18) | collective-permute-done | bytes 131104 | tf_op jit(solution)/shard_map/ppermute | solution.py:20
  57.1 2.7 %update.2 = (f32[512,256]{1,0:T(8,128)S(1)}, f32[512,256]{1,0:T(8,128)S(1)}) custom-call(s32[1,2]{1,0:T(1,128)S(1)} %copy-done.2, s32[8]{0:T(128)S(1)} %copy-done.3, bf16[1024,1024]{1,0:T(8,128)(2,1)S(1)} %get-tuple-element.93.high, bf16[1024,1024]{1,0:T(8,128)(2,1)S(1)} %get-tuple-element.94.low, f32[128,256]{1,0:T(8,128)S(1)} %solve.2.refs_0_, ...), custom_call_target="tpu_custom_call" | custom-call | flops 1610612736 | bytes 7340032 | tf_op jit(solution)/shard_map/update/pallas_call | solution.py:210
  62.1 1.7 %collective-permute-start.20 = (f32[256,256]{1,0:T(8,128)S(1)}, f32[256,256]{1,0:T(8,128)S(1)}, u32[]{:S(2)}, u32[]{:S(2)}) collective-permute-start(f32[256,256]{1,0:T(8,128)S(1)} %constant_dynamic-slice_fusion), channel_id=1, source_target_pairs={{0,8},{4,12},{8,0},{12,4},{16,24},{20,28},{24,16},{28,20},{1,9},{5... | collective-permute-start | bytes 786440 | tf_op jit(solution)/shard_map/ppermute | solution.py:20
  63.7 1.3 %slice_bitcast_fusion.1 = (f32[128,1024]{1,0:T(8,128)S(1)}, f32[128,1024]{1,0:T(8,128)S(1)}) fusion(f32[1,2,256,1024]{3,2,1,0:T(8,128)} %param.6), kind=kLoop, calls=%fused_computation.1 | loop fusion | bytes 2097152 | tf_op jit(solution)/shard_map/squeeze | solution.py:259
  65.0 1.6 %collective-permute-start.22 = (f32[128,1024]{1,0:T(8,128)S(1)}, f32[128,1024]{1,0:T(8,128)S(1)}, u32[]{:S(2)}, u32[]{:S(2)}) collective-permute-start(f32[128,1024]{1,0:T(8,128)S(1)} %get-tuple-element.110.own_top), channel_id=1, source_target_pairs={{0,1},{1,0},{2,3},{3,2},{4,5},{5,4},{6,7},{7,6},{8,9},{9,8},{10,11... | collective-permute-start | bytes 1572872 | tf_op jit(solution)/shard_map/ppermute | solution.py:20
  66.6 1.5 %collective-permute-start.23 = (f32[128,1024]{1,0:T(8,128)S(1)}, f32[128,1024]{1,0:T(8,128)S(1)}, u32[]{:S(2)}, u32[]{:S(2)}) collective-permute-start(f32[128,1024]{1,0:T(8,128)S(1)} %get-tuple-element.109.own_bottom), channel_id=1, source_target_pairs={{0,2},{1,3},{2,0},{3,1},{4,6},{5,7},{6,4},{7,5},{8,10},{9,11},{10,... | collective-permute-start | bytes 1572872 | tf_op jit(solution)/shard_map/ppermute | solution.py:20
  68.1 2.6 %collective-permute-done.20 = f32[256,256]{1,0:T(8,128)S(1)} collective-permute-done((f32[256,256]{1,0:T(8,128)S(1)}, f32[256,256]{1,0:T(8,128)S(1)}, u32[]{:S(2)}, u32[]{:S(2)}) %collective-permute-start.20) | collective-permute-done | bytes 262176 | tf_op jit(solution)/shard_map/ppermute | solution.py:20
  70.8 2.7 %collective-permute-start.21 = (f32[256,256]{1,0:T(8,128)S(1)}, f32[256,256]{1,0:T(8,128)}, u32[]{:S(2)}, u32[]{:S(2)}) collective-permute-start(f32[256,256]{1,0:T(8,128)S(1)} %dynamic-slice_select_fusion), channel_id=1, source_target_pairs={{0,16},{4,20},{8,24},{12,28},{16,0},{20,4},{24,8},{28,12},{1,17},{... | collective-permute-start | bytes 786440 | tf_op jit(solution)/shard_map/ppermute | solution.py:20
  73.5 1.5 %collective-permute-start.25 = (f32[128,1024]{1,0:T(8,128)S(1)}, f32[128,1024]{1,0:T(8,128)}, u32[]{:S(2)}, u32[]{:S(2)}) collective-permute-start(f32[128,1024]{1,0:T(8,128)S(1)} %get-tuple-element.109.own_bottom), channel_id=1, source_target_pairs={{0,1},{1,0},{2,3},{3,2},{4,5},{5,4},{6,7},{7,6},{8,9},{9,8},{10,11... | collective-permute-start | bytes 1572872 | tf_op jit(solution)/shard_map/ppermute | solution.py:20
  75.0 1.5 %collective-permute-start.26 = (f32[128,1024]{1,0:T(8,128)S(1)}, f32[128,1024]{1,0:T(8,128)}, u32[]{:S(2)}, u32[]{:S(2)}) collective-permute-start(f32[128,1024]{1,0:T(8,128)S(1)} %get-tuple-element.110.own_top), channel_id=1, source_target_pairs={{0,2},{1,3},{2,0},{3,1},{4,6},{5,7},{6,4},{7,5},{8,10},{9,11},{10,... | collective-permute-start | bytes 1572872 | tf_op jit(solution)/shard_map/ppermute | solution.py:20
  77.1 8.1 %collective-permute-done.21 = f32[256,256]{1,0:T(8,128)} collective-permute-done((f32[256,256]{1,0:T(8,128)S(1)}, f32[256,256]{1,0:T(8,128)}, u32[]{:S(2)}, u32[]{:S(2)}) %collective-permute-start.21) | collective-permute-done | bytes 262176 | tf_op jit(solution)/shard_map/ppermute | solution.py:20
  85.2 1.0 broadcast_select_fusion.3.refs_0_
  86.9 1.5 %collective-permute-start.31 = (f32[128,1024]{1,0:T(8,128)S(1)}, f32[128,1024]{1,0:T(8,128)S(1)}, u32[]{:S(2)}, u32[]{:S(2)}) collective-permute-start(f32[128,1024]{1,0:T(8,128)S(1)} %collective-permute-done.22.refs_0_), channel_id=1, source_target_pairs={{0,2},{1,3},{2,0},{3,1},{4,6},{5,7},{6,4},{7,5},{8,10},{9,11},{10,... | collective-permute-start | bytes 1572872 | tf_op jit(solution)/shard_map/ppermute | solution.py:20
  88.5 1.5 %collective-permute-start.32 = (f32[128,1024]{1,0:T(8,128)S(1)}, f32[128,1024]{1,0:T(8,128)S(1)}, u32[]{:S(2)}, u32[]{:S(2)}) collective-permute-start(f32[128,1024]{1,0:T(8,128)S(1)} %collective-permute-done.23.refs_1_), channel_id=1, source_target_pairs={{0,1},{1,0},{2,3},{3,2},{4,5},{5,4},{6,7},{7,6},{8,9},{9,8},{10,11... | collective-permute-start | bytes 1572872 | tf_op jit(solution)/shard_map/ppermute | solution.py:20
  89.9 1.1 slice_bitcast_fusion.inverse
  91.0 1.7 %collective-permute-done.26.refs_3_ = f32[128,1024]{1,0:T(8,128)} collective-permute-done((f32[128,1024]{1,0:T(8,128)S(1)}, f32[128,1024]{1,0:T(8,128)}, u32[]{:S(2)}, u32[]{:S(2)}) %collective-permute-start.26) | collective-permute-done | bytes 524320 | tf_op jit(solution)/shard_map/ppermute | solution.py:20
  93.4 0.8 collective-permute-done.27.refs_2_
  95.4 2.6 %collective-permute-start.29 = (f32[128,256]{1,0:T(8,128)S(1)}, f32[128,256]{1,0:T(8,128)S(1)}, u32[]{:S(2)}, u32[]{:S(2)}) collective-permute-start(f32[128,256]{1,0:T(8,128)S(1)} %solve.3.refs_0_), channel_id=1, source_target_pairs={{0,16},{4,20},{8,24},{12,28},{16,0},{20,4},{24,8},{28,12},{1,17},{... | collective-permute-start | bytes 393224 | tf_op jit(solution)/shard_map/ppermute | solution.py:20
  98.1 1.7 %collective-permute-start.30 = (f32[128,256]{1,0:T(8,128)S(1)}, f32[128,256]{1,0:T(8,128)S(1)}, u32[]{:S(2)}, u32[]{:S(2)}) collective-permute-start(f32[128,256]{1,0:T(8,128)S(1)} %solve.3.refs_0_), channel_id=1, source_target_pairs={{0,8},{4,12},{8,0},{12,4},{16,24},{20,28},{24,16},{28,20},{1,9},{5... | collective-permute-start | bytes 393224 | tf_op jit(solution)/shard_map/ppermute | solution.py:20
  99.8 2.9 %collective-permute-done.31.refs_4_ = f32[128,1024]{1,0:T(8,128)S(1)} collective-permute-done((f32[128,1024]{1,0:T(8,128)S(1)}, f32[128,1024]{1,0:T(8,128)S(1)}, u32[]{:S(2)}, u32[]{:S(2)}) %collective-permute-start.31) | collective-permute-done | bytes 524320 | tf_op jit(solution)/shard_map/ppermute | solution.py:20
  102.7 2.2 %collective-permute-done.29.refs_2_ = f32[128,256]{1,0:T(8,128)S(1)} collective-permute-done((f32[128,256]{1,0:T(8,128)S(1)}, f32[128,256]{1,0:T(8,128)S(1)}, u32[]{:S(2)}, u32[]{:S(2)}) %collective-permute-start.29) | collective-permute-done | bytes 131104 | tf_op jit(solution)/shard_map/ppermute | solution.py:20
  104.8 1.6 %collective-permute-start.33 = (f32[128,256]{1,0:T(8,128)S(1)}, f32[128,256]{1,0:T(8,128)S(1)}, u32[]{:S(2)}, u32[]{:S(2)}) collective-permute-start(f32[128,256]{1,0:T(8,128)S(1)} %collective-permute-done.29.refs_2_), channel_id=1, source_target_pairs={{0,8},{4,12},{8,0},{12,4},{16,24},{20,28},{24,16},{28,20},{1,9},{5... | collective-permute-start | bytes 393224 | tf_op jit(solution)/shard_map/ppermute | solution.py:20
  106.9 1.8 %prepare.3 = (bf16[1024,1024]{1,0:T(8,128)(2,1)S(1)}, bf16[1024,1024]{1,0:T(8,128)(2,1)S(1)}) custom-call(f32[128,1024]{1,0:T(8,128)S(1)} %get-tuple-element.110.own_top, f32[128,1024]{1,0:T(8,128)S(1)} %get-tuple-element.109.own_bottom, f32[128,1024]{1,0:T(8,128)S(1)} %collective-permute-done.22.refs_0_, f32[128,1024]{1,0:T(8,128)S(1)} %collective-permute-done.23.refs_1_, ...), custom_call_target="tpu_custom_call" | custom-call | bytes 16777216 | tf_op jit(solution)/shard_map/prepare/pallas_call | solution.py:98
  108.8 1.0 collective-permute-done.33.refs_3_
  109.8 1.3 %collective-permute-done.37.refs_7_ = f32[128,256]{1,0:T(8,128)S(1)} collective-permute-done((f32[128,256]{1,0:T(8,128)S(1)}, f32[128,256]{1,0:T(8,128)S(1)}, u32[]{:S(2)}, u32[]{:S(2)}) %collective-permute-start.37) | collective-permute-done | bytes 131104 | tf_op jit(solution)/shard_map/ppermute | solution.py:20
  111.2 3.4 %update.3 = f32[1024,256]{1,0:T(8,128)} custom-call(s32[1,2]{1,0:T(1,128)S(1)} %copy-done.2, s32[8]{0:T(128)S(1)} %copy-done.3, bf16[1024,1024]{1,0:T(8,128)(2,1)S(1)} %get-tuple-element.123.high, bf16[1024,1024]{1,0:T(8,128)(2,1)S(1)} %get-tuple-element.124.low, f32[128,256]{1,0:T(8,128)S(1)} %solve.3.refs_0_, ...), custom_call_target="tpu_custom_call" | custom-call | flops 1610612736 | bytes 7340032 | tf_op jit(solution)/shard_map/update/pallas_call | solution.py:210
  (59 shorter events, 7.0 us)
Async XLA Ops:
  0.0 1.2 %copy-start = (f32[1,1024,256]{2,1,0:T(8,128)S(1)}, f32[1,1024,256]{2,1,0:T(8,128)}, u32[]{:S(2)}) copy-start(f32[1,1024,256]{2,1,0:T(8,128)} %refs_8_.1) | copy-start | bytes 3145732
  1.2 6.3 %copy-start.4 = (f32[1,2,256,1024]{3,2,1,0:T(8,128)S(1)}, f32[1,2,256,1024]{3,2,1,0:T(8,128)}, u32[]{:S(2)}) copy-start(f32[1,2,256,1024]{3,2,1,0:T(8,128)} %param.6) | copy-start | bytes 6291460
  1.3 3.3 %collective-permute-start = (f32[512,256]{1,0:T(8,128)S(1)}, f32[512,256]{1,0:T(8,128)}, u32[]{:S(2)}, u32[]{:S(2)}) collective-permute-start(f32[512,256]{1,0:T(8,128)S(1)} %get-tuple-element.70), channel_id=1, source_target_pairs={{0,4},{4,0},{8,12},{12,8},{16,20},{20,16},{24,28},{28,24},{1,5},{5... | collective-permute-start | bytes 1572872 | tf_op jit(solution)/shard_map/ppermute | solution.py:20
  4.8 9.2 %collective-permute-start.1 = (f32[256,256]{1,0:T(8,128)S(1)}, f32[256,256]{1,0:T(8,128)S(1)}, u32[]{:S(2)}, u32[]{:S(2)}) collective-permute-start(f32[256,256]{1,0:T(8,128)S(1)} %constant_dynamic-slice_fusion.1), channel_id=1, source_target_pairs={{0,8},{4,12},{8,0},{12,4},{16,24},{20,28},{24,16},{28,20},{1,9},{5... | collective-permute-start | bytes 786440 | tf_op jit(solution)/shard_map/ppermute | solution.py:20
  7.6 22.6 %collective-permute-start.3 = (f32[128,1024]{1,0:T(8,128)S(1)}, f32[128,1024]{1,0:T(8,128)S(1)}, u32[]{:S(2)}, u32[]{:S(2)}) collective-permute-start(f32[128,1024]{1,0:T(8,128)S(1)} %get-tuple-element.80.own_top), channel_id=1, source_target_pairs={{0,1},{1,0},{2,3},{3,2},{4,5},{5,4},{6,7},{7,6},{8,9},{9,8},{10,11... | collective-permute-start | bytes 1572872 | tf_op jit(solution)/shard_map/ppermute | solution.py:20
  9.2 21.0 %collective-permute-start.4 = (f32[128,1024]{1,0:T(8,128)S(1)}, f32[128,1024]{1,0:T(8,128)S(1)}, u32[]{:S(2)}, u32[]{:S(2)}) collective-permute-start(f32[128,1024]{1,0:T(8,128)S(1)} %get-tuple-element.79.own_bottom), channel_id=1, source_target_pairs={{0,2},{1,3},{2,0},{3,1},{4,6},{5,7},{6,4},{7,5},{8,10},{9,11},{10,... | collective-permute-start | bytes 1572872 | tf_op jit(solution)/shard_map/ppermute | solution.py:20
  14.0 16.1 %collective-permute-start.2 = (f32[256,256]{1,0:T(8,128)S(1)}, f32[256,256]{1,0:T(8,128)}, u32[]{:S(2)}, u32[]{:S(2)}) collective-permute-start(f32[256,256]{1,0:T(8,128)S(1)} %dynamic-slice_select_fusion.1), channel_id=1, source_target_pairs={{0,16},{4,20},{8,24},{12,28},{16,0},{20,4},{24,8},{28,12},{1,17},{... | collective-permute-start | bytes 786440 | tf_op jit(solution)/shard_map/ppermute | solution.py:20
  17.4 17.5 %collective-permute-start.6 = (f32[128,1024]{1,0:T(8,128)S(1)}, f32[128,1024]{1,0:T(8,128)S(1)}, u32[]{:S(2)}, u32[]{:S(2)}) collective-permute-start(f32[128,1024]{1,0:T(8,128)S(1)} %get-tuple-element.79.own_bottom), channel_id=1, source_target_pairs={{0,1},{1,0},{2,3},{3,2},{4,5},{5,4},{6,7},{7,6},{8,9},{9,8},{10,11... | collective-permute-start | bytes 1572872 | tf_op jit(solution)/shard_map/ppermute | solution.py:20
  18.9 16.3 %collective-permute-start.7 = (f32[128,1024]{1,0:T(8,128)S(1)}, f32[128,1024]{1,0:T(8,128)S(1)}, u32[]{:S(2)}, u32[]{:S(2)}) collective-permute-start(f32[128,1024]{1,0:T(8,128)S(1)} %get-tuple-element.80.own_top), channel_id=1, source_target_pairs={{0,2},{1,3},{2,0},{3,1},{4,6},{5,7},{6,4},{7,5},{8,10},{9,11},{10,... | collective-permute-start | bytes 1572872 | tf_op jit(solution)/shard_map/ppermute | solution.py:20
  30.2 8.2 %collective-permute-start.5 = (f32[256,256]{1,0:T(8,128)S(1)}, f32[256,256]{1,0:T(8,128)S(1)}, u32[]{:S(2)}, u32[]{:S(2)}) collective-permute-start(f32[256,256]{1,0:T(8,128)S(1)} %broadcast_select_fusion.2.refs_0_), channel_id=1, source_target_pairs={{0,8},{4,12},{8,0},{12,4},{16,24},{20,28},{24,16},{28,20},{1,9},{5... | collective-permute-start | bytes 786440 | tf_op jit(solution)/shard_map/ppermute | solution.py:20
  30.9 15.4 %collective-permute-start.12 = (f32[128,1024]{1,0:T(8,128)S(1)}, f32[128,1024]{1,0:T(8,128)S(1)}, u32[]{:S(2)}, u32[]{:S(2)}) collective-permute-start(f32[128,1024]{1,0:T(8,128)S(1)} %collective-permute-done.3.refs_0_), channel_id=1, source_target_pairs={{0,2},{1,3},{2,0},{3,1},{4,6},{5,7},{6,4},{7,5},{8,10},{9,11},{10,... | collective-permute-start | bytes 1572872 | tf_op jit(solution)/shard_map/ppermute | solution.py:20
  32.4 13.9 %collective-permute-start.13 = (f32[128,1024]{1,0:T(8,128)S(1)}, f32[128,1024]{1,0:T(8,128)S(1)}, u32[]{:S(2)}, u32[]{:S(2)}) collective-permute-start(f32[128,1024]{1,0:T(8,128)S(1)} %collective-permute-done.4.refs_1_), channel_id=1, source_target_pairs={{0,1},{1,0},{2,3},{3,2},{4,5},{5,4},{6,7},{7,6},{8,9},{9,8},{10,11... | collective-permute-start | bytes 1572872 | tf_op jit(solution)/shard_map/ppermute | solution.py:20
  35.2 3.2 %collective-permute-start.8 = (f32[256,256]{1,0:T(8,128)S(1)}, f32[256,256]{1,0:T(8,128)S(1)}, u32[]{:S(2)}, u32[]{:S(2)}) collective-permute-start(f32[256,256]{1,0:T(8,128)S(1)} %broadcast_select_fusion.2.refs_0_), channel_id=1, source_target_pairs={{0,4},{4,0},{8,12},{12,8},{16,20},{20,16},{24,28},{28,24},{1,5},{5... | collective-permute-start | bytes 786440 | tf_op jit(solution)/shard_map/ppermute | solution.py:20
  38.4 1.5 %collective-permute-start.9 = (f32[256,256]{1,0:T(8,128)S(1)}, f32[256,256]{1,0:T(8,128)S(1)}, u32[]{:S(2)}, u32[]{:S(2)}) collective-permute-start(f32[256,256]{1,0:T(8,128)S(1)} %collective-permute-done.5.refs_1_), channel_id=1, source_target_pairs={{0,4},{4,0},{8,12},{12,8},{16,20},{20,16},{24,28},{28,24},{1,5},{5... | collective-permute-start | bytes 786440 | tf_op jit(solution)/shard_map/ppermute | solution.py:20
  40.4 16.7 %copy-start.1 = (f32[1,1024,256]{2,1,0:T(8,128)S(1)}, f32[1,1024,256]{2,1,0:T(8,128)}, u32[]{:S(2)}) copy-start(f32[1,1024,256]{2,1,0:T(8,128)} %refs_8_.1) | copy-start | bytes 3145732
  40.4 16.7 %copy-start.2 = (s32[1,2]{1,0:T(1,128)S(1)}, s32[1,2]{1,0:T(1,128)}, u32[]{:S(2)}) copy-start(s32[1,2]{1,0:T(1,128)} %flags.3) | copy-start | bytes 28
  40.4 16.7 %copy-start.3 = (s32[8]{0:T(128)S(1)}, s32[8]{0:T(128)}, u32[]{:S(2)}) copy-start(s32[8]{0:T(128)} %slot_block.3) | copy-start | bytes 100
  40.4 10.3 %collective-permute-start.10 = (f32[128,256]{1,0:T(8,128)S(1)}, f32[128,256]{1,0:T(8,128)S(1)}, u32[]{:S(2)}, u32[]{:S(2)}) collective-permute-start(f32[128,256]{1,0:T(8,128)S(1)} %solve.2.refs_0_), channel_id=1, source_target_pairs={{0,16},{4,20},{8,24},{12,28},{16,0},{20,4},{24,8},{28,12},{1,17},{... | collective-permute-start | bytes 393224 | tf_op jit(solution)/shard_map/ppermute | solution.py:20
  44.0 6.8 %collective-permute-start.11 = (f32[128,256]{1,0:T(8,128)S(1)}, f32[128,256]{1,0:T(8,128)S(1)}, u32[]{:S(2)}, u32[]{:S(2)}) collective-permute-start(f32[128,256]{1,0:T(8,128)S(1)} %solve.2.refs_0_), channel_id=1, source_target_pairs={{0,8},{4,12},{8,0},{12,4},{16,24},{20,28},{24,16},{28,20},{1,9},{5... | collective-permute-start | bytes 393224 | tf_op jit(solution)/shard_map/ppermute | solution.py:20
  45.7 8.2 %collective-permute-start.15 = (f32[128,256]{1,0:T(8,128)S(1)}, f32[128,256]{1,0:T(8,128)S(1)}, u32[]{:S(2)}, u32[]{:S(2)}) collective-permute-start(f32[128,256]{1,0:T(8,128)S(1)} %solve.2.refs_0_), channel_id=1, source_target_pairs={{0,4},{4,0},{8,12},{12,8},{16,20},{20,16},{24,28},{28,24},{1,5},{5... | collective-permute-start | bytes 393224 | tf_op jit(solution)/shard_map/ppermute | solution.py:20
  50.8 5.0 %collective-permute-start.14 = (f32[128,256]{1,0:T(8,128)S(1)}, f32[128,256]{1,0:T(8,128)S(1)}, u32[]{:S(2)}, u32[]{:S(2)}) collective-permute-start(f32[128,256]{1,0:T(8,128)S(1)} %collective-permute-done.10.refs_2_), channel_id=1, source_target_pairs={{0,8},{4,12},{8,0},{12,4},{16,24},{20,28},{24,16},{28,20},{1,9},{5... | collective-permute-start | bytes 393224 | tf_op jit(solution)/shard_map/ppermute | solution.py:20
  52.3 3.4 %collective-permute-start.16 = (f32[128,256]{1,0:T(8,128)S(1)}, f32[128,256]{1,0:T(8,128)S(1)}, u32[]{:S(2)}, u32[]{:S(2)}) collective-permute-start(f32[128,256]{1,0:T(8,128)S(1)} %collective-permute-done.11.refs_1_), channel_id=1, source_target_pairs={{0,4},{4,0},{8,12},{12,8},{16,20},{20,16},{24,28},{28,24},{1,5},{5... | collective-permute-start | bytes 393224 | tf_op jit(solution)/shard_map/ppermute | solution.py:20
  52.4 3.4 %collective-permute-start.17 = (f32[128,256]{1,0:T(8,128)S(1)}, f32[128,256]{1,0:T(8,128)S(1)}, u32[]{:S(2)}, u32[]{:S(2)}) collective-permute-start(f32[128,256]{1,0:T(8,128)S(1)} %collective-permute-done.10.refs_2_), channel_id=1, source_target_pairs={{0,4},{4,0},{8,12},{12,8},{16,20},{20,16},{24,28},{28,24},{1,5},{5... | collective-permute-start | bytes 393224 | tf_op jit(solution)/shard_map/ppermute | solution.py:20
  55.7 1.4 %collective-permute-start.18 = (f32[128,256]{1,0:T(8,128)S(1)}, f32[128,256]{1,0:T(8,128)S(1)}, u32[]{:S(2)}, u32[]{:S(2)}) collective-permute-start(f32[128,256]{1,0:T(8,128)S(1)} %collective-permute-done.14.refs_3_), channel_id=1, source_target_pairs={{0,4},{4,0},{8,12},{12,8},{16,20},{20,16},{24,28},{28,24},{1,5},{5... | collective-permute-start | bytes 393224 | tf_op jit(solution)/shard_map/ppermute | solution.py:20
  59.8 2.2 %collective-permute-start.19 = (f32[512,256]{1,0:T(8,128)S(1)}, f32[512,256]{1,0:T(8,128)S(1)}, u32[]{:S(2)}, u32[]{:S(2)}) collective-permute-start(f32[512,256]{1,0:T(8,128)S(1)} %get-tuple-element.100.refs_9_), channel_id=1, source_target_pairs={{0,4},{4,0},{8,12},{12,8},{16,20},{20,16},{24,28},{28,24},{1,5},{5... | collective-permute-start | bytes 1572872 | tf_op jit(solution)/shard_map/ppermute | solution.py:20
  62.1 8.6 %collective-permute-start.20 = (f32[256,256]{1,0:T(8,128)S(1)}, f32[256,256]{1,0:T(8,128)S(1)}, u32[]{:S(2)}, u32[]{:S(2)}) collective-permute-start(f32[256,256]{1,0:T(8,128)S(1)} %constant_dynamic-slice_fusion), channel_id=1, source_target_pairs={{0,8},{4,12},{8,0},{12,4},{16,24},{20,28},{24,16},{28,20},{1,9},{5... | collective-permute-start | bytes 786440 | tf_op jit(solution)/shard_map/ppermute | solution.py:20
  65.0 21.2 %collective-permute-start.22 = (f32[128,1024]{1,0:T(8,128)S(1)}, f32[128,1024]{1,0:T(8,128)S(1)}, u32[]{:S(2)}, u32[]{:S(2)}) collective-permute-start(f32[128,1024]{1,0:T(8,128)S(1)} %get-tuple-element.110.own_top), channel_id=1, source_target_pairs={{0,1},{1,0},{2,3},{3,2},{4,5},{5,4},{6,7},{7,6},{8,9},{9,8},{10,11... | collective-permute-start | bytes 1572872 | tf_op jit(solution)/shard_map/ppermute | solution.py:20
  66.6 19.7 %collective-permute-start.23 = (f32[128,1024]{1,0:T(8,128)S(1)}, f32[128,1024]{1,0:T(8,128)S(1)}, u32[]{:S(2)}, u32[]{:S(2)}) collective-permute-start(f32[128,1024]{1,0:T(8,128)S(1)} %get-tuple-element.109.own_bottom), channel_id=1, source_target_pairs={{0,2},{1,3},{2,0},{3,1},{4,6},{5,7},{6,4},{7,5},{8,10},{9,11},{10,... | collective-permute-start | bytes 1572872 | tf_op jit(solution)/shard_map/ppermute | solution.py:20
  70.8 14.5 %collective-permute-start.21 = (f32[256,256]{1,0:T(8,128)S(1)}, f32[256,256]{1,0:T(8,128)}, u32[]{:S(2)}, u32[]{:S(2)}) collective-permute-start(f32[256,256]{1,0:T(8,128)S(1)} %dynamic-slice_select_fusion), channel_id=1, source_target_pairs={{0,16},{4,20},{8,24},{12,28},{16,0},{20,4},{24,8},{28,12},{1,17},{... | collective-permute-start | bytes 786440 | tf_op jit(solution)/shard_map/ppermute | solution.py:20
  73.5 17.5 %collective-permute-start.25 = (f32[128,1024]{1,0:T(8,128)S(1)}, f32[128,1024]{1,0:T(8,128)}, u32[]{:S(2)}, u32[]{:S(2)}) collective-permute-start(f32[128,1024]{1,0:T(8,128)S(1)} %get-tuple-element.109.own_bottom), channel_id=1, source_target_pairs={{0,1},{1,0},{2,3},{3,2},{4,5},{5,4},{6,7},{7,6},{8,9},{9,8},{10,11... | collective-permute-start | bytes 1572872 | tf_op jit(solution)/shard_map/ppermute | solution.py:20
  75.0 17.8 %collective-permute-start.26 = (f32[128,1024]{1,0:T(8,128)S(1)}, f32[128,1024]{1,0:T(8,128)}, u32[]{:S(2)}, u32[]{:S(2)}) collective-permute-start(f32[128,1024]{1,0:T(8,128)S(1)} %get-tuple-element.110.own_top), channel_id=1, source_target_pairs={{0,2},{1,3},{2,0},{3,1},{4,6},{5,7},{6,4},{7,5},{8,10},{9,11},{10,... | collective-permute-start | bytes 1572872 | tf_op jit(solution)/shard_map/ppermute | solution.py:20
  86.3 7.2 %collective-permute-start.24 = (f32[256,256]{1,0:T(8,128)S(1)}, f32[256,256]{1,0:T(8,128)S(1)}, u32[]{:S(2)}, u32[]{:S(2)}) collective-permute-start(f32[256,256]{1,0:T(8,128)S(1)} %broadcast_select_fusion.3.refs_0_), channel_id=1, source_target_pairs={{0,8},{4,12},{8,0},{12,4},{16,24},{20,28},{24,16},{28,20},{1,9},{5... | collective-permute-start | bytes 786440 | tf_op jit(solution)/shard_map/ppermute | solution.py:20
  86.9 15.7 %collective-permute-start.31 = (f32[128,1024]{1,0:T(8,128)S(1)}, f32[128,1024]{1,0:T(8,128)S(1)}, u32[]{:S(2)}, u32[]{:S(2)}) collective-permute-start(f32[128,1024]{1,0:T(8,128)S(1)} %collective-permute-done.22.refs_0_), channel_id=1, source_target_pairs={{0,2},{1,3},{2,0},{3,1},{4,6},{5,7},{6,4},{7,5},{8,10},{9,11},{10,... | collective-permute-start | bytes 1572872 | tf_op jit(solution)/shard_map/ppermute | solution.py:20
  88.5 14.2 %collective-permute-start.32 = (f32[128,1024]{1,0:T(8,128)S(1)}, f32[128,1024]{1,0:T(8,128)S(1)}, u32[]{:S(2)}, u32[]{:S(2)}) collective-permute-start(f32[128,1024]{1,0:T(8,128)S(1)} %collective-permute-done.23.refs_1_), channel_id=1, source_target_pairs={{0,1},{1,0},{2,3},{3,2},{4,5},{5,4},{6,7},{7,6},{8,9},{9,8},{10,11... | collective-permute-start | bytes 1572872 | tf_op jit(solution)/shard_map/ppermute | solution.py:20
  92.7 1.5 %collective-permute-start.27 = (f32[256,256]{1,0:T(8,128)S(1)}, f32[256,256]{1,0:T(8,128)S(1)}, u32[]{:S(2)}, u32[]{:S(2)}) collective-permute-start(f32[256,256]{1,0:T(8,128)S(1)} %broadcast_select_fusion.3.refs_0_), channel_id=1, source_target_pairs={{0,4},{4,0},{8,12},{12,8},{16,20},{20,16},{24,28},{28,24},{1,5},{5... | collective-permute-start | bytes 786440 | tf_op jit(solution)/shard_map/ppermute | solution.py:20
  93.4 1.5 %collective-permute-start.28 = (f32[256,256]{1,0:T(8,128)S(1)}, f32[256,256]{1,0:T(8,128)S(1)}, u32[]{:S(2)}, u32[]{:S(2)}) collective-permute-start(f32[256,256]{1,0:T(8,128)S(1)} %collective-permute-done.24.refs_1_), channel_id=1, source_target_pairs={{0,4},{4,0},{8,12},{12,8},{16,20},{20,16},{24,28},{28,24},{1,5},{5... | collective-permute-start | bytes 786440 | tf_op jit(solution)/shard_map/ppermute | solution.py:20
  95.4 9.4 %collective-permute-start.29 = (f32[128,256]{1,0:T(8,128)S(1)}, f32[128,256]{1,0:T(8,128)S(1)}, u32[]{:S(2)}, u32[]{:S(2)}) collective-permute-start(f32[128,256]{1,0:T(8,128)S(1)} %solve.3.refs_0_), channel_id=1, source_target_pairs={{0,16},{4,20},{8,24},{12,28},{16,0},{20,4},{24,8},{28,12},{1,17},{... | collective-permute-start | bytes 393224 | tf_op jit(solution)/shard_map/ppermute | solution.py:20
  98.1 6.8 %collective-permute-start.30 = (f32[128,256]{1,0:T(8,128)S(1)}, f32[128,256]{1,0:T(8,128)S(1)}, u32[]{:S(2)}, u32[]{:S(2)}) collective-permute-start(f32[128,256]{1,0:T(8,128)S(1)} %solve.3.refs_0_), channel_id=1, source_target_pairs={{0,8},{4,12},{8,0},{12,4},{16,24},{20,28},{24,16},{28,20},{1,9},{5... | collective-permute-start | bytes 393224 | tf_op jit(solution)/shard_map/ppermute | solution.py:20
  99.8 9.0 %collective-permute-start.34 = (f32[128,256]{1,0:T(8,128)S(1)}, f32[128,256]{1,0:T(8,128)S(1)}, u32[]{:S(2)}, u32[]{:S(2)}) collective-permute-start(f32[128,256]{1,0:T(8,128)S(1)} %solve.3.refs_0_), channel_id=1, source_target_pairs={{0,4},{4,0},{8,12},{12,8},{16,20},{20,16},{24,28},{28,24},{1,5},{5... | collective-permute-start | bytes 393224 | tf_op jit(solution)/shard_map/ppermute | solution.py:20
  104.8 5.0 %collective-permute-start.33 = (f32[128,256]{1,0:T(8,128)S(1)}, f32[128,256]{1,0:T(8,128)S(1)}, u32[]{:S(2)}, u32[]{:S(2)}) collective-permute-start(f32[128,256]{1,0:T(8,128)S(1)} %collective-permute-done.29.refs_2_), channel_id=1, source_target_pairs={{0,8},{4,12},{8,0},{12,4},{16,24},{20,28},{24,16},{28,20},{1,9},{5... | collective-permute-start | bytes 393224 | tf_op jit(solution)/shard_map/ppermute | solution.py:20
  106.4 3.4 %collective-permute-start.35 = (f32[128,256]{1,0:T(8,128)S(1)}, f32[128,256]{1,0:T(8,128)S(1)}, u32[]{:S(2)}, u32[]{:S(2)}) collective-permute-start(f32[128,256]{1,0:T(8,128)S(1)} %collective-permute-done.30.refs_1_), channel_id=1, source_target_pairs={{0,4},{4,0},{8,12},{12,8},{16,20},{20,16},{24,28},{28,24},{1,5},{5... | collective-permute-start | bytes 393224 | tf_op jit(solution)/shard_map/ppermute | solution.py:20
  106.4 3.4 %collective-permute-start.36 = (f32[128,256]{1,0:T(8,128)S(1)}, f32[128,256]{1,0:T(8,128)S(1)}, u32[]{:S(2)}, u32[]{:S(2)}) collective-permute-start(f32[128,256]{1,0:T(8,128)S(1)} %collective-permute-done.29.refs_2_), channel_id=1, source_target_pairs={{0,4},{4,0},{8,12},{12,8},{16,20},{20,16},{24,28},{28,24},{1,5},{5... | collective-permute-start | bytes 393224 | tf_op jit(solution)/shard_map/ppermute | solution.py:20
  109.8 1.4 %collective-permute-start.37 = (f32[128,256]{1,0:T(8,128)S(1)}, f32[128,256]{1,0:T(8,128)S(1)}, u32[]{:S(2)}, u32[]{:S(2)}) collective-permute-start(f32[128,256]{1,0:T(8,128)S(1)} %collective-permute-done.33.refs_3_), channel_id=1, source_target_pairs={{0,4},{4,0},{8,12},{12,8},{16,20},{20,16},{24,28},{28,24},{1,5},{5... | collective-permute-start | bytes 393224 | tf_op jit(solution)/shard_map/ppermute | solution.py:20

commit v8 on v4

--- a/solution.py
+++ b/solution.py
@@ -243,9 +243,11 @@
         y, inverse, *first = tie(y, diag_inverse, *first)
         pieces = far(*first)
         beside = swap(y, "row", 1, rows)
-        beside, y, *second = tie(beside, y, *second)
-        other, last = swap(y, "row", 0, rows), swap(beside, "row", 0, rows)
-        x = solve(inverse[step], [y, beside, other, last])
+        y, *second = tie(y, *second)
+        other = swap(y, "row", 0, rows)
+        beside, inverse = tie(beside, inverse[step])
+        last = swap(beside, "row", 0, rows)
+        x = solve(inverse, [y, beside, other, last])
         x2, x1 = swap(x, "row", 2, rows), swap(x, "row", 1, rows)
         x2, x1, *pieces = tie(x2, x1, *pieces)
         high, low = prepare([*block, *first, *second, *pieces])

time: 114 us -> 114 us (level)
  starting transfers between devices: 40.4 us -> 46.2 us
  waiting for transfers between devices: 50.1 us -> 46.6 us
  other arithmetic: 3.46 us -> 1.56 us
    ppermute x38, starting transfers between devices: 40.4 us -> 46.2 us  [swap(): return lax.ppermute(x, axis, [(i, i ^ 1 << b) for i in range(size)])]
    ppermute x38, waiting for transfers between devices: 50.1 us -> 46.6 us  [swap(): return lax.ppermute(x, axis, [(i, i ^ 1 << b) for i in range(size)])]
    select_n x2, other arithmetic: 1.96 us -> 0.06 us  [cross_step(): return jnp.where(bit(owner, b) == bit(me, b), x, swap(x, 'row', b, size))]
  transfers between devices with their start and end apart: 38 -> 38, of which waited for: 18 -> 22; matrix products, arithmetic and copies ran while one was open for 6% -> 4% of each run, Pallas kernels for 3% -> 3%
where the time goes in v8:
time: 114 us
  waiting for transfers between devices  46.6 us (41%)
  starting transfers between devices  46.2 us (41%)
  Pallas kernels  9.98 us (9%)
  local copies, waits for them, and re-layouts  5.8 us (5%)
  between operations  3.67 us (3%)
  other arithmetic  1.56 us (1%)
    ppermute x38, waiting for transfers between devices, swap(): return lax.ppermute(x, axis, [(i, i ^ 1 << b) for i in range(size)])  46.6 us
    ppermute x38, starting transfers between devices, swap(): return lax.ppermute(x, axis, [(i, i ^ 1 << b) for i in range(size)])  46.2 us
    pallas_call x2, Pallas kernels, update(): pl.pallas_call(first_body if step == 0 else second_body, out_shape=[jax.S...  6.11 us
    pallas_call x2, Pallas kernels, prepare(): pl.pallas_call(prepare_body, out_shape=[jax.ShapeDtypeStruct((depth, dept...  2.91 us
  transfers between devices with their start and end apart: 38, of which 22 were waited for; matrix products, arithmetic and copies ran while one was open for 4% of the time, Pallas kernels for 3%

profile of v8, /device:TPU:0, one launch (start us, length us, event | category | flops | bytes accessed | tf_op | source)
XLA Modules:
  0.0 113.8 jit_solution(11822280749226605246)
XLA Ops:
  0.0 2.2 %dynamic-slice_bitcast_fusion = (f32[512,256]{1,0:T(8,128)}, f32[512,256]{1,0:T(8,128)S(1)}) fusion(f32[1,1024,256]{2,1,0:T(8,128)} %refs_8_.1, s32[]{:T(128)S(6)} %select_n.67, s32[]{:T(128)S(6)} %select_n.66), kind=kLoop, calls=%fused_computation.6 | loop fusion | bytes 2097160 | tf_op jit(solution)/shard_map/dynamic_slice | solution.py:33
  4.6 2.9 %collective-permute-start.1 = (f32[256,256]{1,0:T(8,128)S(1)}, f32[256,256]{1,0:T(8,128)S(1)}, u32[]{:S(2)}, u32[]{:S(2)}) collective-permute-start(f32[256,256]{1,0:T(8,128)S(1)} %constant_dynamic-slice_fusion.1), channel_id=1, source_target_pairs={{0,8},{4,12},{8,0},{12,4},{16,24},{20,28},{24,16},{28,20},{1,9},{5... | collective-permute-start | bytes 786440 | tf_op jit(solution)/shard_map/ppermute | solution.py:20
  7.6 1.6 %collective-permute-start.3 = (f32[128,1024]{1,0:T(8,128)S(1)}, f32[128,1024]{1,0:T(8,128)S(1)}, u32[]{:S(2)}, u32[]{:S(2)}) collective-permute-start(f32[128,1024]{1,0:T(8,128)S(1)} %get-tuple-element.78.own_top), channel_id=1, source_target_pairs={{0,1},{1,0},{2,3},{3,2},{4,5},{5,4},{6,7},{7,6},{8,9},{9,8},{10,11... | collective-permute-start | bytes 1572872 | tf_op jit(solution)/shard_map/ppermute | solution.py:20
  9.2 1.5 %collective-permute-start.4 = (f32[128,1024]{1,0:T(8,128)S(1)}, f32[128,1024]{1,0:T(8,128)S(1)}, u32[]{:S(2)}, u32[]{:S(2)}) collective-permute-start(f32[128,1024]{1,0:T(8,128)S(1)} %get-tuple-element.77.own_bottom), channel_id=1, source_target_pairs={{0,2},{1,3},{2,0},{3,1},{4,6},{5,7},{6,4},{7,5},{8,10},{9,11},{10,... | collective-permute-start | bytes 1572872 | tf_op jit(solution)/shard_map/ppermute | solution.py:20
  10.7 3.5 %collective-permute-done.1 = f32[256,256]{1,0:T(8,128)S(1)} collective-permute-done((f32[256,256]{1,0:T(8,128)S(1)}, f32[256,256]{1,0:T(8,128)S(1)}, u32[]{:S(2)}, u32[]{:S(2)}) %collective-permute-start.1) | collective-permute-done | bytes 262176 | tf_op jit(solution)/shard_map/ppermute | solution.py:20
  14.3 2.8 %collective-permute-start.2 = (f32[256,256]{1,0:T(8,128)S(1)}, f32[256,256]{1,0:T(8,128)}, u32[]{:S(2)}, u32[]{:S(2)}) collective-permute-start(f32[256,256]{1,0:T(8,128)S(1)} %dynamic-slice_select_fusion.1), channel_id=1, source_target_pairs={{0,16},{4,20},{8,24},{12,28},{16,0},{20,4},{24,8},{28,12},{1,17},{... | collective-permute-start | bytes 786440 | tf_op jit(solution)/shard_map/ppermute | solution.py:20
  17.1 1.5 %collective-permute-start.6 = (f32[128,1024]{1,0:T(8,128)S(1)}, f32[128,1024]{1,0:T(8,128)S(1)}, u32[]{:S(2)}, u32[]{:S(2)}) collective-permute-start(f32[128,1024]{1,0:T(8,128)S(1)} %get-tuple-element.77.own_bottom), channel_id=1, source_target_pairs={{0,1},{1,0},{2,3},{3,2},{4,5},{5,4},{6,7},{7,6},{8,9},{9,8},{10,11... | collective-permute-start | bytes 1572872 | tf_op jit(solution)/shard_map/ppermute | solution.py:20
  18.6 1.5 %collective-permute-start.7 = (f32[128,1024]{1,0:T(8,128)S(1)}, f32[128,1024]{1,0:T(8,128)S(1)}, u32[]{:S(2)}, u32[]{:S(2)}) collective-permute-start(f32[128,1024]{1,0:T(8,128)S(1)} %get-tuple-element.78.own_top), channel_id=1, source_target_pairs={{0,2},{1,3},{2,0},{3,1},{4,6},{5,7},{6,4},{7,5},{8,10},{9,11},{10,... | collective-permute-start | bytes 1572872 | tf_op jit(solution)/shard_map/ppermute | solution.py:20
  20.7 8.2 %collective-permute-done.2 = f32[256,256]{1,0:T(8,128)} collective-permute-done((f32[256,256]{1,0:T(8,128)S(1)}, f32[256,256]{1,0:T(8,128)}, u32[]{:S(2)}, u32[]{:S(2)}) %collective-permute-start.2) | collective-permute-done | bytes 262176 | tf_op jit(solution)/shard_map/ppermute | solution.py:20
  29.4 1.5 %collective-permute-start.12 = (f32[128,1024]{1,0:T(8,128)S(1)}, f32[128,1024]{1,0:T(8,128)S(1)}, u32[]{:S(2)}, u32[]{:S(2)}) collective-permute-start(f32[128,1024]{1,0:T(8,128)S(1)} %collective-permute-done.3.refs_0_), channel_id=1, source_target_pairs={{0,2},{1,3},{2,0},{3,1},{4,6},{5,7},{6,4},{7,5},{8,10},{9,11},{10,... | collective-permute-start | bytes 1572872 | tf_op jit(solution)/shard_map/ppermute | solution.py:20
  31.0 1.5 %collective-permute-start.13 = (f32[128,1024]{1,0:T(8,128)S(1)}, f32[128,1024]{1,0:T(8,128)S(1)}, u32[]{:S(2)}, u32[]{:S(2)}) collective-permute-start(f32[128,1024]{1,0:T(8,128)S(1)} %collective-permute-done.4.refs_1_), channel_id=1, source_target_pairs={{0,1},{1,0},{2,3},{3,2},{4,5},{5,4},{6,7},{7,6},{8,9},{9,8},{10,11... | collective-permute-start | bytes 1572872 | tf_op jit(solution)/shard_map/ppermute | solution.py:20
  32.4 1.1 slice_bitcast_fusion.3.inverse
  33.5 1.7 %collective-permute-done.7.refs_3_ = f32[128,1024]{1,0:T(8,128)S(1)} collective-permute-done((f32[128,1024]{1,0:T(8,128)S(1)}, f32[128,1024]{1,0:T(8,128)S(1)}, u32[]{:S(2)}, u32[]{:S(2)}) %collective-permute-start.7) | collective-permute-done | bytes 524320 | tf_op jit(solution)/shard_map/ppermute | solution.py:20
  35.3 1.1 collective-permute-done.5.refs_1_
  36.8 1.1 collective-permute-done.9.refs_3_
  38.4 4.1 %collective-permute-start.10 = (f32[128,256]{1,0:T(8,128)S(1)}, f32[128,256]{1,0:T(8,128)S(1)}, u32[]{:S(2)}, u32[]{:S(2)}) collective-permute-start(f32[128,256]{1,0:T(8,128)S(1)} %solve.2.refs_0_), channel_id=1, source_target_pairs={{0,16},{4,20},{8,24},{12,28},{16,0},{20,4},{24,8},{28,12},{1,17},{... | collective-permute-start | bytes 393224 | tf_op jit(solution)/shard_map/ppermute | solution.py:20
  42.5 1.7 %collective-permute-start.11 = (f32[128,256]{1,0:T(8,128)S(1)}, f32[128,256]{1,0:T(8,128)S(1)}, u32[]{:S(2)}, u32[]{:S(2)}) collective-permute-start(f32[128,256]{1,0:T(8,128)S(1)} %solve.2.refs_0_), channel_id=1, source_target_pairs={{0,8},{4,12},{8,0},{12,4},{16,24},{20,28},{24,16},{28,20},{1,9},{5... | collective-permute-start | bytes 393224 | tf_op jit(solution)/shard_map/ppermute | solution.py:20
  44.2 1.0 collective-permute-done.12.refs_4_
  45.2 4.0 %collective-permute-done.10.refs_2_ = f32[128,256]{1,0:T(8,128)S(1)} collective-permute-done((f32[128,256]{1,0:T(8,128)S(1)}, f32[128,256]{1,0:T(8,128)S(1)}, u32[]{:S(2)}, u32[]{:S(2)}) %collective-permute-start.10) | collective-permute-done | bytes 131104 | tf_op jit(solution)/shard_map/ppermute | solution.py:20
  49.3 1.6 %collective-permute-start.14 = (f32[128,256]{1,0:T(8,128)S(1)}, f32[128,256]{1,0:T(8,128)S(1)}, u32[]{:S(2)}, u32[]{:S(2)}) collective-permute-start(f32[128,256]{1,0:T(8,128)S(1)} %collective-permute-done.10.refs_2_), channel_id=1, source_target_pairs={{0,8},{4,12},{8,0},{12,4},{16,24},{20,28},{24,16},{28,20},{1,9},{5... | collective-permute-start | bytes 393224 | tf_op jit(solution)/shard_map/ppermute | solution.py:20
  51.4 1.1 prepare.2
  52.4 1.8 %collective-permute-done.14.refs_3_ = f32[128,256]{1,0:T(8,128)S(1)} collective-permute-done((f32[128,256]{1,0:T(8,128)S(1)}, f32[128,256]{1,0:T(8,128)S(1)}, u32[]{:S(2)}, u32[]{:S(2)}) %collective-permute-start.14) | collective-permute-done | bytes 131104 | tf_op jit(solution)/shard_map/ppermute | solution.py:20
  54.2 1.3 %collective-permute-done.18.refs_7_ = f32[128,256]{1,0:T(8,128)S(1)} collective-permute-done((f32[128,256]{1,0:T(8,128)S(1)}, f32[128,256]{1,0:T(8,128)S(1)}, u32[]{:S(2)}, u32[]{:S(2)}) %collective-permute-start.18) | collective-permute-done | bytes 131104 | tf_op jit(solution)/shard_map/ppermute | solution.py:20
  55.6 2.7 %update.2 = (f32[512,256]{1,0:T(8,128)S(1)}, f32[512,256]{1,0:T(8,128)S(1)}) custom-call(s32[1,2]{1,0:T(1,128)S(1)} %copy-done.1, s32[8]{0:T(128)S(1)} %copy-done.2, bf16[1024,1024]{1,0:T(8,128)(2,1)S(1)} %get-tuple-element.91.high, bf16[1024,1024]{1,0:T(8,128)(2,1)S(1)} %get-tuple-element.92.low, f32[128,256]{1,0:T(8,128)S(1)} %solve.2.refs_0_, ...), custom_call_target="tpu_custom_call" | custom-call | flops 1610612736 | bytes 7340032 | tf_op jit(solution)/shard_map/update/pallas_call | solution.py:184
  60.4 1.7 %collective-permute-start.20 = (f32[256,256]{1,0:T(8,128)S(1)}, f32[256,256]{1,0:T(8,128)S(1)}, u32[]{:S(2)}, u32[]{:S(2)}) collective-permute-start(f32[256,256]{1,0:T(8,128)S(1)} %constant_dynamic-slice_fusion), channel_id=1, source_target_pairs={{0,8},{4,12},{8,0},{12,4},{16,24},{20,28},{24,16},{28,20},{1,9},{5... | collective-permute-start | bytes 786440 | tf_op jit(solution)/shard_map/ppermute | solution.py:20
  62.0 1.3 %slice_bitcast_fusion.1 = (f32[128,1024]{1,0:T(8,128)S(1)}, f32[128,1024]{1,0:T(8,128)S(1)}) fusion(f32[1,2,256,1024]{3,2,1,0:T(8,128)} %param.6), kind=kLoop, calls=%fused_computation.1 | loop fusion | bytes 2097152 | tf_op jit(solution)/shard_map/squeeze | solution.py:233
  63.3 1.6 %collective-permute-start.22 = (f32[128,1024]{1,0:T(8,128)S(1)}, f32[128,1024]{1,0:T(8,128)S(1)}, u32[]{:S(2)}, u32[]{:S(2)}) collective-permute-start(f32[128,1024]{1,0:T(8,128)S(1)} %get-tuple-element.108.own_top), channel_id=1, source_target_pairs={{0,1},{1,0},{2,3},{3,2},{4,5},{5,4},{6,7},{7,6},{8,9},{9,8},{10,11... | collective-permute-start | bytes 1572872 | tf_op jit(solution)/shard_map/ppermute | solution.py:20
  64.9 1.5 %collective-permute-start.23 = (f32[128,1024]{1,0:T(8,128)S(1)}, f32[128,1024]{1,0:T(8,128)S(1)}, u32[]{:S(2)}, u32[]{:S(2)}) collective-permute-start(f32[128,1024]{1,0:T(8,128)S(1)} %get-tuple-element.107.own_bottom), channel_id=1, source_target_pairs={{0,2},{1,3},{2,0},{3,1},{4,6},{5,7},{6,4},{7,5},{8,10},{9,11},{10,... | collective-permute-start | bytes 1572872 | tf_op jit(solution)/shard_map/ppermute | solution.py:20
  66.4 2.6 %collective-permute-done.20 = f32[256,256]{1,0:T(8,128)S(1)} collective-permute-done((f32[256,256]{1,0:T(8,128)S(1)}, f32[256,256]{1,0:T(8,128)S(1)}, u32[]{:S(2)}, u32[]{:S(2)}) %collective-permute-start.20) | collective-permute-done | bytes 262176 | tf_op jit(solution)/shard_map/ppermute | solution.py:20
  69.0 2.7 %collective-permute-start.21 = (f32[256,256]{1,0:T(8,128)S(1)}, f32[256,256]{1,0:T(8,128)}, u32[]{:S(2)}, u32[]{:S(2)}) collective-permute-start(f32[256,256]{1,0:T(8,128)S(1)} %dynamic-slice_select_fusion), channel_id=1, source_target_pairs={{0,16},{4,20},{8,24},{12,28},{16,0},{20,4},{24,8},{28,12},{1,17},{... | collective-permute-start | bytes 786440 | tf_op jit(solution)/shard_map/ppermute | solution.py:20
  71.8 1.5 %collective-permute-start.25 = (f32[128,1024]{1,0:T(8,128)S(1)}, f32[128,1024]{1,0:T(8,128)}, u32[]{:S(2)}, u32[]{:S(2)}) collective-permute-start(f32[128,1024]{1,0:T(8,128)S(1)} %get-tuple-element.107.own_bottom), channel_id=1, source_target_pairs={{0,1},{1,0},{2,3},{3,2},{4,5},{5,4},{6,7},{7,6},{8,9},{9,8},{10,11... | collective-permute-start | bytes 1572872 | tf_op jit(solution)/shard_map/ppermute | solution.py:20
  73.3 1.5 %collective-permute-start.26 = (f32[128,1024]{1,0:T(8,128)S(1)}, f32[128,1024]{1,0:T(8,128)}, u32[]{:S(2)}, u32[]{:S(2)}) collective-permute-start(f32[128,1024]{1,0:T(8,128)S(1)} %get-tuple-element.108.own_top), channel_id=1, source_target_pairs={{0,2},{1,3},{2,0},{3,1},{4,6},{5,7},{6,4},{7,5},{8,10},{9,11},{10,... | collective-permute-start | bytes 1572872 | tf_op jit(solution)/shard_map/ppermute | solution.py:20
  75.3 8.2 %collective-permute-done.21 = f32[256,256]{1,0:T(8,128)} collective-permute-done((f32[256,256]{1,0:T(8,128)S(1)}, f32[256,256]{1,0:T(8,128)}, u32[]{:S(2)}, u32[]{:S(2)}) %collective-permute-start.21) | collective-permute-done | bytes 262176 | tf_op jit(solution)/shard_map/ppermute | solution.py:20
  84.2 1.5 %collective-permute-start.31 = (f32[128,1024]{1,0:T(8,128)S(1)}, f32[128,1024]{1,0:T(8,128)S(1)}, u32[]{:S(2)}, u32[]{:S(2)}) collective-permute-start(f32[128,1024]{1,0:T(8,128)S(1)} %collective-permute-done.22.refs_0_), channel_id=1, source_target_pairs={{0,2},{1,3},{2,0},{3,1},{4,6},{5,7},{6,4},{7,5},{8,10},{9,11},{10,... | collective-permute-start | bytes 1572872 | tf_op jit(solution)/shard_map/ppermute | solution.py:20
  85.8 1.5 %collective-permute-start.32 = (f32[128,1024]{1,0:T(8,128)S(1)}, f32[128,1024]{1,0:T(8,128)S(1)}, u32[]{:S(2)}, u32[]{:S(2)}) collective-permute-start(f32[128,1024]{1,0:T(8,128)S(1)} %collective-permute-done.23.refs_1_), channel_id=1, source_target_pairs={{0,1},{1,0},{2,3},{3,2},{4,5},{5,4},{6,7},{7,6},{8,9},{9,8},{10,11... | collective-permute-start | bytes 1572872 | tf_op jit(solution)/shard_map/ppermute | solution.py:20
  87.2 1.1 slice_bitcast_fusion.inverse
  88.3 0.9 collective-permute-done.25.refs_2_
  89.2 1.8 %collective-permute-done.26.refs_3_ = f32[128,1024]{1,0:T(8,128)} collective-permute-done((f32[128,1024]{1,0:T(8,128)S(1)}, f32[128,1024]{1,0:T(8,128)}, u32[]{:S(2)}, u32[]{:S(2)}) %collective-permute-start.26) | collective-permute-done | bytes 524320 | tf_op jit(solution)/shard_map/ppermute | solution.py:20
  91.5 1.0 collective-permute-done.27.refs_2_
  93.4 3.8 %collective-permute-start.29 = (f32[128,256]{1,0:T(8,128)S(1)}, f32[128,256]{1,0:T(8,128)S(1)}, u32[]{:S(2)}, u32[]{:S(2)}) collective-permute-start(f32[128,256]{1,0:T(8,128)S(1)} %solve.3.refs_0_), channel_id=1, source_target_pairs={{0,16},{4,20},{8,24},{12,28},{16,0},{20,4},{24,8},{28,12},{1,17},{... | collective-permute-start | bytes 393224 | tf_op jit(solution)/shard_map/ppermute | solution.py:20
  97.2 1.7 %collective-permute-start.30 = (f32[128,256]{1,0:T(8,128)S(1)}, f32[128,256]{1,0:T(8,128)S(1)}, u32[]{:S(2)}, u32[]{:S(2)}) collective-permute-start(f32[128,256]{1,0:T(8,128)S(1)} %solve.3.refs_0_), channel_id=1, source_target_pairs={{0,8},{4,12},{8,0},{12,4},{16,24},{20,28},{24,16},{28,20},{1,9},{5... | collective-permute-start | bytes 393224 | tf_op jit(solution)/shard_map/ppermute | solution.py:20
  99.0 2.0 %collective-permute-done.31.refs_4_ = f32[128,1024]{1,0:T(8,128)S(1)} collective-permute-done((f32[128,1024]{1,0:T(8,128)S(1)}, f32[128,1024]{1,0:T(8,128)S(1)}, u32[]{:S(2)}, u32[]{:S(2)}) %collective-permute-start.31) | collective-permute-done | bytes 524320 | tf_op jit(solution)/shard_map/ppermute | solution.py:20
  100.9 3.0 %collective-permute-done.29.refs_2_ = f32[128,256]{1,0:T(8,128)S(1)} collective-permute-done((f32[128,256]{1,0:T(8,128)S(1)}, f32[128,256]{1,0:T(8,128)S(1)}, u32[]{:S(2)}, u32[]{:S(2)}) %collective-permute-start.29) | collective-permute-done | bytes 131104 | tf_op jit(solution)/shard_map/ppermute | solution.py:20
  104.0 1.6 %collective-permute-start.33 = (f32[128,256]{1,0:T(8,128)S(1)}, f32[128,256]{1,0:T(8,128)S(1)}, u32[]{:S(2)}, u32[]{:S(2)}) collective-permute-start(f32[128,256]{1,0:T(8,128)S(1)} %collective-permute-done.29.refs_2_), channel_id=1, source_target_pairs={{0,8},{4,12},{8,0},{12,4},{16,24},{20,28},{24,16},{28,20},{1,9},{5... | collective-permute-start | bytes 393224 | tf_op jit(solution)/shard_map/ppermute | solution.py:20
  106.1 1.8 %prepare.3 = (bf16[1024,1024]{1,0:T(8,128)(2,1)S(1)}, bf16[1024,1024]{1,0:T(8,128)(2,1)S(1)}) custom-call(f32[128,1024]{1,0:T(8,128)S(1)} %get-tuple-element.108.own_top, f32[128,1024]{1,0:T(8,128)S(1)} %get-tuple-element.107.own_bottom, f32[128,1024]{1,0:T(8,128)S(1)} %collective-permute-done.22.refs_0_, f32[128,1024]{1,0:T(8,128)S(1)} %collective-permute-done.23.refs_1_, ...), custom_call_target="tpu_custom_call" | custom-call | bytes 16777216 | tf_op jit(solution)/shard_map/prepare/pallas_call | solution.py:98
  108.0 1.0 collective-permute-done.33.refs_3_
  109.0 1.3 %collective-permute-done.37.refs_7_ = f32[128,256]{1,0:T(8,128)S(1)} collective-permute-done((f32[128,256]{1,0:T(8,128)S(1)}, f32[128,256]{1,0:T(8,128)S(1)}, u32[]{:S(2)}, u32[]{:S(2)}) %collective-permute-start.37) | collective-permute-done | bytes 131104 | tf_op jit(solution)/shard_map/ppermute | solution.py:20
  110.4 3.4 %update.3 = f32[1024,256]{1,0:T(8,128)} custom-call(s32[1,2]{1,0:T(1,128)S(1)} %copy-done.1, s32[8]{0:T(128)S(1)} %copy-done.2, bf16[1024,1024]{1,0:T(8,128)(2,1)S(1)} %get-tuple-element.121.high, bf16[1024,1024]{1,0:T(8,128)(2,1)S(1)} %get-tuple-element.122.low, f32[128,256]{1,0:T(8,128)S(1)} %solve.3.refs_0_, ...), custom_call_target="tpu_custom_call" | custom-call | flops 1610612736 | bytes 7340032 | tf_op jit(solution)/shard_map/update/pallas_call | solution.py:184
  (57 shorter events, 7.1 us)
Async XLA Ops:
  0.0 2.7 %copy-start.2 = (s32[8]{0:T(128)S(1)}, s32[8]{0:T(128)}, u32[]{:S(2)}) copy-start(s32[8]{0:T(128)} %slot_block.3) | copy-start | bytes 100
  0.0 7.5 %copy-start.3 = (f32[1,2,256,1024]{3,2,1,0:T(8,128)S(1)}, f32[1,2,256,1024]{3,2,1,0:T(8,128)}, u32[]{:S(2)}) copy-start(f32[1,2,256,1024]{3,2,1,0:T(8,128)} %param.6) | copy-start | bytes 6291460
  2.2 2.3 %collective-permute-start = (f32[512,256]{1,0:T(8,128)}, f32[512,256]{1,0:T(8,128)S(1)}, u32[]{:S(2)}, u32[]{:S(2)}) collective-permute-start(f32[512,256]{1,0:T(8,128)} %get-tuple-element.131), channel_id=1, source_target_pairs={{0,4},{4,0},{8,12},{12,8},{16,20},{20,16},{24,28},{28,24},{1,5},{5... | collective-permute-start | bytes 1572872 | tf_op jit(solution)/shard_map/ppermute | solution.py:20
  4.6 9.6 %collective-permute-start.1 = (f32[256,256]{1,0:T(8,128)S(1)}, f32[256,256]{1,0:T(8,128)S(1)}, u32[]{:S(2)}, u32[]{:S(2)}) collective-permute-start(f32[256,256]{1,0:T(8,128)S(1)} %constant_dynamic-slice_fusion.1), channel_id=1, source_target_pairs={{0,8},{4,12},{8,0},{12,4},{16,24},{20,28},{24,16},{28,20},{1,9},{5... | collective-permute-start | bytes 786440 | tf_op jit(solution)/shard_map/ppermute | solution.py:20
  7.6 21.3 %collective-permute-start.3 = (f32[128,1024]{1,0:T(8,128)S(1)}, f32[128,1024]{1,0:T(8,128)S(1)}, u32[]{:S(2)}, u32[]{:S(2)}) collective-permute-start(f32[128,1024]{1,0:T(8,128)S(1)} %get-tuple-element.78.own_top), channel_id=1, source_target_pairs={{0,1},{1,0},{2,3},{3,2},{4,5},{5,4},{6,7},{7,6},{8,9},{9,8},{10,11... | collective-permute-start | bytes 1572872 | tf_op jit(solution)/shard_map/ppermute | solution.py:20
  9.2 19.8 %collective-permute-start.4 = (f32[128,1024]{1,0:T(8,128)S(1)}, f32[128,1024]{1,0:T(8,128)S(1)}, u32[]{:S(2)}, u32[]{:S(2)}) collective-permute-start(f32[128,1024]{1,0:T(8,128)S(1)} %get-tuple-element.77.own_bottom), channel_id=1, source_target_pairs={{0,2},{1,3},{2,0},{3,1},{4,6},{5,7},{6,4},{7,5},{8,10},{9,11},{10,... | collective-permute-start | bytes 1572872 | tf_op jit(solution)/shard_map/ppermute | solution.py:20
  14.3 14.6 %collective-permute-start.2 = (f32[256,256]{1,0:T(8,128)S(1)}, f32[256,256]{1,0:T(8,128)}, u32[]{:S(2)}, u32[]{:S(2)}) collective-permute-start(f32[256,256]{1,0:T(8,128)S(1)} %dynamic-slice_select_fusion.1), channel_id=1, source_target_pairs={{0,16},{4,20},{8,24},{12,28},{16,0},{20,4},{24,8},{28,12},{1,17},{... | collective-permute-start | bytes 786440 | tf_op jit(solution)/shard_map/ppermute | solution.py:20
  17.1 16.4 %collective-permute-start.6 = (f32[128,1024]{1,0:T(8,128)S(1)}, f32[128,1024]{1,0:T(8,128)S(1)}, u32[]{:S(2)}, u32[]{:S(2)}) collective-permute-start(f32[128,1024]{1,0:T(8,128)S(1)} %get-tuple-element.77.own_bottom), channel_id=1, source_target_pairs={{0,1},{1,0},{2,3},{3,2},{4,5},{5,4},{6,7},{7,6},{8,9},{9,8},{10,11... | collective-permute-start | bytes 1572872 | tf_op jit(solution)/shard_map/ppermute | solution.py:20
  18.6 16.7 %collective-permute-start.7 = (f32[128,1024]{1,0:T(8,128)S(1)}, f32[128,1024]{1,0:T(8,128)S(1)}, u32[]{:S(2)}, u32[]{:S(2)}) collective-permute-start(f32[128,1024]{1,0:T(8,128)S(1)} %get-tuple-element.78.own_top), channel_id=1, source_target_pairs={{0,2},{1,3},{2,0},{3,1},{4,6},{5,7},{6,4},{7,5},{8,10},{9,11},{10,... | collective-permute-start | bytes 1572872 | tf_op jit(solution)/shard_map/ppermute | solution.py:20
  29.0 7.4 %collective-permute-start.5 = (f32[256,256]{1,0:T(8,128)S(1)}, f32[256,256]{1,0:T(8,128)S(1)}, u32[]{:S(2)}, u32[]{:S(2)}) collective-permute-start(f32[256,256]{1,0:T(8,128)S(1)} %broadcast_select_fusion.2.refs_0_), channel_id=1, source_target_pairs={{0,8},{4,12},{8,0},{12,4},{16,24},{20,28},{24,16},{28,20},{1,9},{5... | collective-permute-start | bytes 786440 | tf_op jit(solution)/shard_map/ppermute | solution.py:20
  29.4 15.7 %collective-permute-start.12 = (f32[128,1024]{1,0:T(8,128)S(1)}, f32[128,1024]{1,0:T(8,128)S(1)}, u32[]{:S(2)}, u32[]{:S(2)}) collective-permute-start(f32[128,1024]{1,0:T(8,128)S(1)} %collective-permute-done.3.refs_0_), channel_id=1, source_target_pairs={{0,2},{1,3},{2,0},{3,1},{4,6},{5,7},{6,4},{7,5},{8,10},{9,11},{10,... | collective-permute-start | bytes 1572872 | tf_op jit(solution)/shard_map/ppermute | solution.py:20
  31.0 14.2 %collective-permute-start.13 = (f32[128,1024]{1,0:T(8,128)S(1)}, f32[128,1024]{1,0:T(8,128)S(1)}, u32[]{:S(2)}, u32[]{:S(2)}) collective-permute-start(f32[128,1024]{1,0:T(8,128)S(1)} %collective-permute-done.4.refs_1_), channel_id=1, source_target_pairs={{0,1},{1,0},{2,3},{3,2},{4,5},{5,4},{6,7},{7,6},{8,9},{9,8},{10,11... | collective-permute-start | bytes 1572872 | tf_op jit(solution)/shard_map/ppermute | solution.py:20
  35.3 1.5 %collective-permute-start.8 = (f32[256,256]{1,0:T(8,128)S(1)}, f32[256,256]{1,0:T(8,128)S(1)}, u32[]{:S(2)}, u32[]{:S(2)}) collective-permute-start(f32[256,256]{1,0:T(8,128)S(1)} %broadcast_select_fusion.2.refs_0_), channel_id=1, source_target_pairs={{0,4},{4,0},{8,12},{12,8},{16,20},{20,16},{24,28},{28,24},{1,5},{5... | collective-permute-start | bytes 786440 | tf_op jit(solution)/shard_map/ppermute | solution.py:20
  36.4 1.5 %collective-permute-start.9 = (f32[256,256]{1,0:T(8,128)S(1)}, f32[256,256]{1,0:T(8,128)S(1)}, u32[]{:S(2)}, u32[]{:S(2)}) collective-permute-start(f32[256,256]{1,0:T(8,128)S(1)} %collective-permute-done.5.refs_1_), channel_id=1, source_target_pairs={{0,4},{4,0},{8,12},{12,8},{16,20},{20,16},{24,28},{28,24},{1,5},{5... | collective-permute-start | bytes 786440 | tf_op jit(solution)/shard_map/ppermute | solution.py:20
  38.4 17.2 %copy-start = (f32[1,1024,256]{2,1,0:T(8,128)S(1)}, f32[1,1024,256]{2,1,0:T(8,128)}, u32[]{:S(2)}) copy-start(f32[1,1024,256]{2,1,0:T(8,128)} %refs_8_.1) | copy-start | bytes 3145732
  38.4 17.2 %copy-start.1 = (s32[1,2]{1,0:T(1,128)S(1)}, s32[1,2]{1,0:T(1,128)}, u32[]{:S(2)}) copy-start(s32[1,2]{1,0:T(1,128)} %flags.3) | copy-start | bytes 28
  38.4 10.8 %collective-permute-start.10 = (f32[128,256]{1,0:T(8,128)S(1)}, f32[128,256]{1,0:T(8,128)S(1)}, u32[]{:S(2)}, u32[]{:S(2)}) collective-permute-start(f32[128,256]{1,0:T(8,128)S(1)} %solve.2.refs_0_), channel_id=1, source_target_pairs={{0,16},{4,20},{8,24},{12,28},{16,0},{20,4},{24,8},{28,12},{1,17},{... | collective-permute-start | bytes 393224 | tf_op jit(solution)/shard_map/ppermute | solution.py:20
  42.5 6.8 %collective-permute-start.11 = (f32[128,256]{1,0:T(8,128)S(1)}, f32[128,256]{1,0:T(8,128)S(1)}, u32[]{:S(2)}, u32[]{:S(2)}) collective-permute-start(f32[128,256]{1,0:T(8,128)S(1)} %solve.2.refs_0_), channel_id=1, source_target_pairs={{0,8},{4,12},{8,0},{12,4},{16,24},{20,28},{24,16},{28,20},{1,9},{5... | collective-permute-start | bytes 393224 | tf_op jit(solution)/shard_map/ppermute | solution.py:20
  44.2 8.2 %collective-permute-start.15 = (f32[128,256]{1,0:T(8,128)S(1)}, f32[128,256]{1,0:T(8,128)S(1)}, u32[]{:S(2)}, u32[]{:S(2)}) collective-permute-start(f32[128,256]{1,0:T(8,128)S(1)} %solve.2.refs_0_), channel_id=1, source_target_pairs={{0,4},{4,0},{8,12},{12,8},{16,20},{20,16},{24,28},{28,24},{1,5},{5... | collective-permute-start | bytes 393224 | tf_op jit(solution)/shard_map/ppermute | solution.py:20
  49.3 5.0 %collective-permute-start.14 = (f32[128,256]{1,0:T(8,128)S(1)}, f32[128,256]{1,0:T(8,128)S(1)}, u32[]{:S(2)}, u32[]{:S(2)}) collective-permute-start(f32[128,256]{1,0:T(8,128)S(1)} %collective-permute-done.10.refs_2_), channel_id=1, source_target_pairs={{0,8},{4,12},{8,0},{12,4},{16,24},{20,28},{24,16},{28,20},{1,9},{5... | collective-permute-start | bytes 393224 | tf_op jit(solution)/shard_map/ppermute | solution.py:20
  50.8 3.4 %collective-permute-start.16 = (f32[128,256]{1,0:T(8,128)S(1)}, f32[128,256]{1,0:T(8,128)S(1)}, u32[]{:S(2)}, u32[]{:S(2)}) collective-permute-start(f32[128,256]{1,0:T(8,128)S(1)} %collective-permute-done.11.refs_1_), channel_id=1, source_target_pairs={{0,4},{4,0},{8,12},{12,8},{16,20},{20,16},{24,28},{28,24},{1,5},{5... | collective-permute-start | bytes 393224 | tf_op jit(solution)/shard_map/ppermute | solution.py:20
  50.8 3.4 %collective-permute-start.17 = (f32[128,256]{1,0:T(8,128)S(1)}, f32[128,256]{1,0:T(8,128)S(1)}, u32[]{:S(2)}, u32[]{:S(2)}) collective-permute-start(f32[128,256]{1,0:T(8,128)S(1)} %collective-permute-done.10.refs_2_), channel_id=1, source_target_pairs={{0,4},{4,0},{8,12},{12,8},{16,20},{20,16},{24,28},{28,24},{1,5},{5... | collective-permute-start | bytes 393224 | tf_op jit(solution)/shard_map/ppermute | solution.py:20
  54.2 1.4 %collective-permute-start.18 = (f32[128,256]{1,0:T(8,128)S(1)}, f32[128,256]{1,0:T(8,128)S(1)}, u32[]{:S(2)}, u32[]{:S(2)}) collective-permute-start(f32[128,256]{1,0:T(8,128)S(1)} %collective-permute-done.14.refs_3_), channel_id=1, source_target_pairs={{0,4},{4,0},{8,12},{12,8},{16,20},{20,16},{24,28},{28,24},{1,5},{5... | collective-permute-start | bytes 393224 | tf_op jit(solution)/shard_map/ppermute | solution.py:20
  58.3 2.0 %collective-permute-start.19 = (f32[512,256]{1,0:T(8,128)S(1)}, f32[512,256]{1,0:T(8,128)S(1)}, u32[]{:S(2)}, u32[]{:S(2)}) collective-permute-start(f32[512,256]{1,0:T(8,128)S(1)} %get-tuple-element.98.refs_9_), channel_id=1, source_target_pairs={{0,4},{4,0},{8,12},{12,8},{16,20},{20,16},{24,28},{28,24},{1,5},{5... | collective-permute-start | bytes 1572872 | tf_op jit(solution)/shard_map/ppermute | solution.py:20
  60.4 8.6 %collective-permute-start.20 = (f32[256,256]{1,0:T(8,128)S(1)}, f32[256,256]{1,0:T(8,128)S(1)}, u32[]{:S(2)}, u32[]{:S(2)}) collective-permute-start(f32[256,256]{1,0:T(8,128)S(1)} %constant_dynamic-slice_fusion), channel_id=1, source_target_pairs={{0,8},{4,12},{8,0},{12,4},{16,24},{20,28},{24,16},{28,20},{1,9},{5... | collective-permute-start | bytes 786440 | tf_op jit(solution)/shard_map/ppermute | solution.py:20
  63.3 20.2 %collective-permute-start.22 = (f32[128,1024]{1,0:T(8,128)S(1)}, f32[128,1024]{1,0:T(8,128)S(1)}, u32[]{:S(2)}, u32[]{:S(2)}) collective-permute-start(f32[128,1024]{1,0:T(8,128)S(1)} %get-tuple-element.108.own_top), channel_id=1, source_target_pairs={{0,1},{1,0},{2,3},{3,2},{4,5},{5,4},{6,7},{7,6},{8,9},{9,8},{10,11... | collective-permute-start | bytes 1572872 | tf_op jit(solution)/shard_map/ppermute | solution.py:20
  64.9 18.7 %collective-permute-start.23 = (f32[128,1024]{1,0:T(8,128)S(1)}, f32[128,1024]{1,0:T(8,128)S(1)}, u32[]{:S(2)}, u32[]{:S(2)}) collective-permute-start(f32[128,1024]{1,0:T(8,128)S(1)} %get-tuple-element.107.own_bottom), channel_id=1, source_target_pairs={{0,2},{1,3},{2,0},{3,1},{4,6},{5,7},{6,4},{7,5},{8,10},{9,11},{10,... | collective-permute-start | bytes 1572872 | tf_op jit(solution)/shard_map/ppermute | solution.py:20
  69.0 14.5 %collective-permute-start.21 = (f32[256,256]{1,0:T(8,128)S(1)}, f32[256,256]{1,0:T(8,128)}, u32[]{:S(2)}, u32[]{:S(2)}) collective-permute-start(f32[256,256]{1,0:T(8,128)S(1)} %dynamic-slice_select_fusion), channel_id=1, source_target_pairs={{0,16},{4,20},{8,24},{12,28},{16,0},{20,4},{24,8},{28,12},{1,17},{... | collective-permute-start | bytes 786440 | tf_op jit(solution)/shard_map/ppermute | solution.py:20
  71.8 17.5 %collective-permute-start.25 = (f32[128,1024]{1,0:T(8,128)S(1)}, f32[128,1024]{1,0:T(8,128)}, u32[]{:S(2)}, u32[]{:S(2)}) collective-permute-start(f32[128,1024]{1,0:T(8,128)S(1)} %get-tuple-element.107.own_bottom), channel_id=1, source_target_pairs={{0,1},{1,0},{2,3},{3,2},{4,5},{5,4},{6,7},{7,6},{8,9},{9,8},{10,11... | collective-permute-start | bytes 1572872 | tf_op jit(solution)/shard_map/ppermute | solution.py:20
  73.3 17.8 %collective-permute-start.26 = (f32[128,1024]{1,0:T(8,128)S(1)}, f32[128,1024]{1,0:T(8,128)}, u32[]{:S(2)}, u32[]{:S(2)}) collective-permute-start(f32[128,1024]{1,0:T(8,128)S(1)} %get-tuple-element.108.own_top), channel_id=1, source_target_pairs={{0,2},{1,3},{2,0},{3,1},{4,6},{5,7},{6,4},{7,5},{8,10},{9,11},{10,... | collective-permute-start | bytes 1572872 | tf_op jit(solution)/shard_map/ppermute | solution.py:20
  83.6 7.5 %collective-permute-start.24 = (f32[256,256]{1,0:T(8,128)S(1)}, f32[256,256]{1,0:T(8,128)S(1)}, u32[]{:S(2)}, u32[]{:S(2)}) collective-permute-start(f32[256,256]{1,0:T(8,128)S(1)} %broadcast_select_fusion.3.refs_0_), channel_id=1, source_target_pairs={{0,8},{4,12},{8,0},{12,4},{16,24},{20,28},{24,16},{28,20},{1,9},{5... | collective-permute-start | bytes 786440 | tf_op jit(solution)/shard_map/ppermute | solution.py:20
  84.2 16.7 %collective-permute-start.31 = (f32[128,1024]{1,0:T(8,128)S(1)}, f32[128,1024]{1,0:T(8,128)S(1)}, u32[]{:S(2)}, u32[]{:S(2)}) collective-permute-start(f32[128,1024]{1,0:T(8,128)S(1)} %collective-permute-done.22.refs_0_), channel_id=1, source_target_pairs={{0,2},{1,3},{2,0},{3,1},{4,6},{5,7},{6,4},{7,5},{8,10},{9,11},{10,... | collective-permute-start | bytes 1572872 | tf_op jit(solution)/shard_map/ppermute | solution.py:20
  85.8 15.2 %collective-permute-start.32 = (f32[128,1024]{1,0:T(8,128)S(1)}, f32[128,1024]{1,0:T(8,128)S(1)}, u32[]{:S(2)}, u32[]{:S(2)}) collective-permute-start(f32[128,1024]{1,0:T(8,128)S(1)} %collective-permute-done.23.refs_1_), channel_id=1, source_target_pairs={{0,1},{1,0},{2,3},{3,2},{4,5},{5,4},{6,7},{7,6},{8,9},{9,8},{10,11... | collective-permute-start | bytes 1572872 | tf_op jit(solution)/shard_map/ppermute | solution.py:20
  91.0 1.5 %collective-permute-start.27 = (f32[256,256]{1,0:T(8,128)S(1)}, f32[256,256]{1,0:T(8,128)S(1)}, u32[]{:S(2)}, u32[]{:S(2)}) collective-permute-start(f32[256,256]{1,0:T(8,128)S(1)} %broadcast_select_fusion.3.refs_0_), channel_id=1, source_target_pairs={{0,4},{4,0},{8,12},{12,8},{16,20},{20,16},{24,28},{28,24},{1,5},{5... | collective-permute-start | bytes 786440 | tf_op jit(solution)/shard_map/ppermute | solution.py:20
  91.0 1.9 %collective-permute-start.28 = (f32[256,256]{1,0:T(8,128)S(1)}, f32[256,256]{1,0:T(8,128)S(1)}, u32[]{:S(2)}, u32[]{:S(2)}) collective-permute-start(f32[256,256]{1,0:T(8,128)S(1)} %collective-permute-done.24.refs_1_), channel_id=1, source_target_pairs={{0,4},{4,0},{8,12},{12,8},{16,20},{20,16},{24,28},{28,24},{1,5},{5... | collective-permute-start | bytes 786440 | tf_op jit(solution)/shard_map/ppermute | solution.py:20
  93.4 10.5 %collective-permute-start.29 = (f32[128,256]{1,0:T(8,128)S(1)}, f32[128,256]{1,0:T(8,128)S(1)}, u32[]{:S(2)}, u32[]{:S(2)}) collective-permute-start(f32[128,256]{1,0:T(8,128)S(1)} %solve.3.refs_0_), channel_id=1, source_target_pairs={{0,16},{4,20},{8,24},{12,28},{16,0},{20,4},{24,8},{28,12},{1,17},{... | collective-permute-start | bytes 393224 | tf_op jit(solution)/shard_map/ppermute | solution.py:20
  97.2 6.8 %collective-permute-start.30 = (f32[128,256]{1,0:T(8,128)S(1)}, f32[128,256]{1,0:T(8,128)S(1)}, u32[]{:S(2)}, u32[]{:S(2)}) collective-permute-start(f32[128,256]{1,0:T(8,128)S(1)} %solve.3.refs_0_), channel_id=1, source_target_pairs={{0,8},{4,12},{8,0},{12,4},{16,24},{20,28},{24,16},{28,20},{1,9},{5... | collective-permute-start | bytes 393224 | tf_op jit(solution)/shard_map/ppermute | solution.py:20
  99.0 9.0 %collective-permute-start.34 = (f32[128,256]{1,0:T(8,128)S(1)}, f32[128,256]{1,0:T(8,128)S(1)}, u32[]{:S(2)}, u32[]{:S(2)}) collective-permute-start(f32[128,256]{1,0:T(8,128)S(1)} %solve.3.refs_0_), channel_id=1, source_target_pairs={{0,4},{4,0},{8,12},{12,8},{16,20},{20,16},{24,28},{28,24},{1,5},{5... | collective-permute-start | bytes 393224 | tf_op jit(solution)/shard_map/ppermute | solution.py:20
  104.0 5.0 %collective-permute-start.33 = (f32[128,256]{1,0:T(8,128)S(1)}, f32[128,256]{1,0:T(8,128)S(1)}, u32[]{:S(2)}, u32[]{:S(2)}) collective-permute-start(f32[128,256]{1,0:T(8,128)S(1)} %collective-permute-done.29.refs_2_), channel_id=1, source_target_pairs={{0,8},{4,12},{8,0},{12,4},{16,24},{20,28},{24,16},{28,20},{1,9},{5... | collective-permute-start | bytes 393224 | tf_op jit(solution)/shard_map/ppermute | solution.py:20
  105.6 3.4 %collective-permute-start.35 = (f32[128,256]{1,0:T(8,128)S(1)}, f32[128,256]{1,0:T(8,128)S(1)}, u32[]{:S(2)}, u32[]{:S(2)}) collective-permute-start(f32[128,256]{1,0:T(8,128)S(1)} %collective-permute-done.30.refs_1_), channel_id=1, source_target_pairs={{0,4},{4,0},{8,12},{12,8},{16,20},{20,16},{24,28},{28,24},{1,5},{5... | collective-permute-start | bytes 393224 | tf_op jit(solution)/shard_map/ppermute | solution.py:20
  105.6 3.4 %collective-permute-start.36 = (f32[128,256]{1,0:T(8,128)S(1)}, f32[128,256]{1,0:T(8,128)S(1)}, u32[]{:S(2)}, u32[]{:S(2)}) collective-permute-start(f32[128,256]{1,0:T(8,128)S(1)} %collective-permute-done.29.refs_2_), channel_id=1, source_target_pairs={{0,4},{4,0},{8,12},{12,8},{16,20},{20,16},{24,28},{28,24},{1,5},{5... | collective-permute-start | bytes 393224 | tf_op jit(solution)/shard_map/ppermute | solution.py:20
  109.0 1.4 %collective-permute-start.37 = (f32[128,256]{1,0:T(8,128)S(1)}, f32[128,256]{1,0:T(8,128)S(1)}, u32[]{:S(2)}, u32[]{:S(2)}) collective-permute-start(f32[128,256]{1,0:T(8,128)S(1)} %collective-permute-done.33.refs_3_), channel_id=1, source_target_pairs={{0,4},{4,0},{8,12},{12,8},{16,20},{20,16},{24,28},{28,24},{1,5},{5... | collective-permute-start | bytes 393224 | tf_op jit(solution)/shard_map/ppermute | solution.py:20

commit v9 on v8

--- a/solution.py
+++ b/solution.py
@@ -256,10 +256,8 @@
         x3, high, low, *across = tie(x3, high, low, *across)
         return [x, x1, x2, x3, *across, swap(x3, "row", 0, rows)], (high, low)
 
-    keep, send = halves(rhs[0], core)
-    got = swap(send, "row", 0, rows)
-    keep, send = tie(keep, send)
-    y = jnp.where(bit(owner, 0) == core, keep, got)
+    got = swap(rhs, "row", 0, rows)
+    y = jnp.where(bit(owner, 0) == core, halves(rhs[0], core)[0], halves(got[0], core)[0])
     blocks, pair = solved(0, y, panel, owner)
     keep, send = update(0, flags, slot_block, pair, blocks, [rhs])
     got = swap(send, "row", 0, rows)

time: 114 us -> 114 us (level)
  starting transfers between devices: 46.2 us -> 39.1 us
  other arithmetic: 1.56 us -> 5.49 us
  waiting for transfers between devices: 46.6 us -> 50.3 us
  local copies, waits for them, and re-layouts: 5.8 us -> 3.6 us
    ppermute x38, starting transfers between devices: 46.2 us -> 39.1 us  [swap(): return lax.ppermute(x, axis, [(i, i ^ 1 << b) for i in range(size)])]
    ppermute x38, waiting for transfers between devices: 46.6 us -> 50.3 us  [swap(): return lax.ppermute(x, axis, [(i, i ^ 1 << b) for i in range(size)])]
    dynamic_slice x3 -> x2, local copies, waits for them, and re-layouts: 2.26 us -> 0.05 us  [halves(): lax.dynamic_slice_in_dim(x, (1 - b) * half, half)]
    select_n x2, other arithmetic: 0.06 us -> 2 us  [cross_step(): return jnp.where(bit(owner, b) == bit(me, b), x, swap(x, 'row', b, size))]
  transfers between devices with their start and end apart: 38 -> 38, of which waited for: 22 -> 20; matrix products, arithmetic and copies ran while one was open for 4% -> 7% of each run, Pallas kernels for 3% -> 3%
where the time goes in v9:
time: 114 us; the launch traced here: 113 us
  waiting for transfers between devices  50.3 us (44%)
  starting transfers between devices  39.1 us (34%)
  Pallas kernels  9.97 us (9%)
  other arithmetic  5.49 us (5%)
  between operations  4.24 us (4%)
  local copies, waits for them, and re-layouts  3.6 us (3%)
    ppermute x38, waiting for transfers between devices, swap(): return lax.ppermute(x, axis, [(i, i ^ 1 << b) for i in range(size)])  50.3 us
    ppermute x38, starting transfers between devices, swap(): return lax.ppermute(x, axis, [(i, i ^ 1 << b) for i in range(size)])  39.1 us
    pallas_call x2, Pallas kernels, update(): pl.pallas_call(first_body if step == 0 else second_body, out_shape=[jax.S...  6.1 us
    pallas_call x2, Pallas kernels, prepare(): pl.pallas_call(prepare_body, out_shape=[jax.ShapeDtypeStruct((depth, dept...  2.91 us
  transfers between devices with their start and end apart: 38, of which 20 were waited for; matrix products, arithmetic and copies ran while one was open for 7% of the time, Pallas kernels for 3%

profile of v9, /device:TPU:0, one launch (start us, length us, event | category | flops | bytes accessed | tf_op | source)
XLA Modules:
  0.0 112.7 jit_solution(3179621206016916034)
XLA Ops:
  0.5 1.5 %compare_reduce_fusion = (pred[]{:T(512)}, s32[]{:T(128)}) fusion(s32[8]{0:T(128)} %slot_block.3), kind=kLoop, calls=%fused_computation.12 | loop fusion | flops 57 | bytes 37 | tf_op jit(solution)/shard_map/paced/reduce | solution.py:222
  3.3 1.1 %select_bitcast_fusion = f32[512,256]{1,0:T(8,128)S(1)} fusion(f32[1,1024,256]{2,1,0:T(8,128)S(1)} %collective-permute-done, s32[]{:T(128)S(6)} %select_n.67, f32[1,1024,256]{2,1,0:T(8,128)} %refs_8_.1, pred[]{:T(512)S(6)} %eq.34), kind=kLoop, calls=%fused_computation.6 | loop fusion | flops 131072 | bytes 1572869 | tf_op jit(solution)/shard_map/jit(_where)/select_n | solution.py:260
  4.4 2.7 %collective-permute-start.1 = (f32[256,256]{1,0:T(8,128)S(1)}, f32[256,256]{1,0:T(8,128)S(1)}, u32[]{:S(2)}, u32[]{:S(2)}) collective-permute-start(f32[256,256]{1,0:T(8,128)S(1)} %constant_dynamic-slice_fusion), channel_id=1, source_target_pairs={{0,8},{4,12},{8,0},{12,4},{16,24},{20,28},{24,16},{28,20},{1,9},{5... | collective-permute-start | bytes 786440 | tf_op jit(solution)/shard_map/ppermute | solution.py:20
  7.2 1.6 %collective-permute-start.3 = (f32[128,1024]{1,0:T(8,128)S(1)}, f32[128,1024]{1,0:T(8,128)S(1)}, u32[]{:S(2)}, u32[]{:S(2)}) collective-permute-start(f32[128,1024]{1,0:T(8,128)S(1)} %get-tuple-element.76.own_top), channel_id=1, source_target_pairs={{0,1},{1,0},{2,3},{3,2},{4,5},{5,4},{6,7},{7,6},{8,9},{9,8},{10,11... | collective-permute-start | bytes 1572872 | tf_op jit(solution)/shard_map/ppermute | solution.py:20
  8.8 1.5 %collective-permute-start.4 = (f32[128,1024]{1,0:T(8,128)S(1)}, f32[128,1024]{1,0:T(8,128)S(1)}, u32[]{:S(2)}, u32[]{:S(2)}) collective-permute-start(f32[128,1024]{1,0:T(8,128)S(1)} %get-tuple-element.75.own_bottom), channel_id=1, source_target_pairs={{0,2},{1,3},{2,0},{3,1},{4,6},{5,7},{6,4},{7,5},{8,10},{9,11},{10,... | collective-permute-start | bytes 1572872 | tf_op jit(solution)/shard_map/ppermute | solution.py:20
  10.3 3.6 %collective-permute-done.1 = f32[256,256]{1,0:T(8,128)S(1)} collective-permute-done((f32[256,256]{1,0:T(8,128)S(1)}, f32[256,256]{1,0:T(8,128)S(1)}, u32[]{:S(2)}, u32[]{:S(2)}) %collective-permute-start.1) | collective-permute-done | bytes 262176 | tf_op jit(solution)/shard_map/ppermute | solution.py:20
  13.9 2.8 %collective-permute-start.2 = (f32[256,256]{1,0:T(8,128)S(1)}, f32[256,256]{1,0:T(8,128)}, u32[]{:S(2)}, u32[]{:S(2)}) collective-permute-start(f32[256,256]{1,0:T(8,128)S(1)} %dynamic-slice_select_fusion.1), channel_id=1, source_target_pairs={{0,16},{4,20},{8,24},{12,28},{16,0},{20,4},{24,8},{28,12},{1,17},{... | collective-permute-start | bytes 786440 | tf_op jit(solution)/shard_map/ppermute | solution.py:20
  16.7 1.5 %collective-permute-start.6 = (f32[128,1024]{1,0:T(8,128)S(1)}, f32[128,1024]{1,0:T(8,128)S(1)}, u32[]{:S(2)}, u32[]{:S(2)}) collective-permute-start(f32[128,1024]{1,0:T(8,128)S(1)} %get-tuple-element.75.own_bottom), channel_id=1, source_target_pairs={{0,1},{1,0},{2,3},{3,2},{4,5},{5,4},{6,7},{7,6},{8,9},{9,8},{10,11... | collective-permute-start | bytes 1572872 | tf_op jit(solution)/shard_map/ppermute | solution.py:20
  18.2 1.5 %collective-permute-start.7 = (f32[128,1024]{1,0:T(8,128)S(1)}, f32[128,1024]{1,0:T(8,128)S(1)}, u32[]{:S(2)}, u32[]{:S(2)}) collective-permute-start(f32[128,1024]{1,0:T(8,128)S(1)} %get-tuple-element.76.own_top), channel_id=1, source_target_pairs={{0,2},{1,3},{2,0},{3,1},{4,6},{5,7},{6,4},{7,5},{8,10},{9,11},{10,... | collective-permute-start | bytes 1572872 | tf_op jit(solution)/shard_map/ppermute | solution.py:20
  20.4 8.2 %collective-permute-done.2 = f32[256,256]{1,0:T(8,128)} collective-permute-done((f32[256,256]{1,0:T(8,128)S(1)}, f32[256,256]{1,0:T(8,128)}, u32[]{:S(2)}, u32[]{:S(2)}) %collective-permute-start.2) | collective-permute-done | bytes 262176 | tf_op jit(solution)/shard_map/ppermute | solution.py:20
  28.6 1.0 broadcast_select_fusion.1.refs_0_
  30.1 1.5 %collective-permute-start.12 = (f32[128,1024]{1,0:T(8,128)S(1)}, f32[128,1024]{1,0:T(8,128)S(1)}, u32[]{:S(2)}, u32[]{:S(2)}) collective-permute-start(f32[128,1024]{1,0:T(8,128)S(1)} %collective-permute-done.3.refs_0_), channel_id=1, source_target_pairs={{0,2},{1,3},{2,0},{3,1},{4,6},{5,7},{6,4},{7,5},{8,10},{9,11},{10,... | collective-permute-start | bytes 1572872 | tf_op jit(solution)/shard_map/ppermute | solution.py:20
  31.6 1.5 %collective-permute-start.13 = (f32[128,1024]{1,0:T(8,128)S(1)}, f32[128,1024]{1,0:T(8,128)S(1)}, u32[]{:S(2)}, u32[]{:S(2)}) collective-permute-start(f32[128,1024]{1,0:T(8,128)S(1)} %collective-permute-done.4.refs_1_), channel_id=1, source_target_pairs={{0,1},{1,0},{2,3},{3,2},{4,5},{5,4},{6,7},{7,6},{8,9},{9,8},{10,11... | collective-permute-start | bytes 1572872 | tf_op jit(solution)/shard_map/ppermute | solution.py:20
  33.1 1.1 slice_bitcast_fusion.3.inverse
  34.7 2.4 %collective-permute-done.5.refs_1_ = f32[256,256]{1,0:T(8,128)S(1)} collective-permute-done((f32[256,256]{1,0:T(8,128)S(1)}, f32[256,256]{1,0:T(8,128)S(1)}, u32[]{:S(2)}, u32[]{:S(2)}) %collective-permute-start.5) | collective-permute-done | bytes 262176 | tf_op jit(solution)/shard_map/ppermute | solution.py:20
  37.0 1.5 %collective-permute-done.9.refs_3_ = f32[256,256]{1,0:T(8,128)S(1)} collective-permute-done((f32[256,256]{1,0:T(8,128)S(1)}, f32[256,256]{1,0:T(8,128)S(1)}, u32[]{:S(2)}, u32[]{:S(2)}) %collective-permute-start.9) | collective-permute-done | bytes 262176 | tf_op jit(solution)/shard_map/ppermute | solution.py:20
  39.1 2.2 %collective-permute-start.10 = (f32[128,256]{1,0:T(8,128)S(1)}, f32[128,256]{1,0:T(8,128)S(1)}, u32[]{:S(2)}, u32[]{:S(2)}) collective-permute-start(f32[128,256]{1,0:T(8,128)S(1)} %solve.2.refs_0_), channel_id=1, source_target_pairs={{0,16},{4,20},{8,24},{12,28},{16,0},{20,4},{24,8},{28,12},{1,17},{... | collective-permute-start | bytes 393224 | tf_op jit(solution)/shard_map/ppermute | solution.py:20
  41.3 1.7 %collective-permute-start.11 = (f32[128,256]{1,0:T(8,128)S(1)}, f32[128,256]{1,0:T(8,128)S(1)}, u32[]{:S(2)}, u32[]{:S(2)}) collective-permute-start(f32[128,256]{1,0:T(8,128)S(1)} %solve.2.refs_0_), channel_id=1, source_target_pairs={{0,8},{4,12},{8,0},{12,4},{16,24},{20,28},{24,16},{28,20},{1,9},{5... | collective-permute-start | bytes 393224 | tf_op jit(solution)/shard_map/ppermute | solution.py:20
  43.0 1.8 %collective-permute-done.12.refs_4_ = f32[128,1024]{1,0:T(8,128)S(1)} collective-permute-done((f32[128,1024]{1,0:T(8,128)S(1)}, f32[128,1024]{1,0:T(8,128)S(1)}, u32[]{:S(2)}, u32[]{:S(2)}) %collective-permute-start.12) | collective-permute-done | bytes 524320 | tf_op jit(solution)/shard_map/ppermute | solution.py:20
  44.9 3.6 %collective-permute-done.10.refs_2_ = f32[128,256]{1,0:T(8,128)S(1)} collective-permute-done((f32[128,256]{1,0:T(8,128)S(1)}, f32[128,256]{1,0:T(8,128)S(1)}, u32[]{:S(2)}, u32[]{:S(2)}) %collective-permute-start.10) | collective-permute-done | bytes 131104 | tf_op jit(solution)/shard_map/ppermute | solution.py:20
  48.5 1.1 %collective-permute-start.14 = (f32[128,256]{1,0:T(8,128)S(1)}, f32[128,256]{1,0:T(8,128)S(1)}, u32[]{:S(2)}, u32[]{:S(2)}) collective-permute-start(f32[128,256]{1,0:T(8,128)S(1)} %collective-permute-done.10.refs_2_), channel_id=1, source_target_pairs={{0,8},{4,12},{8,0},{12,4},{16,24},{20,28},{24,16},{28,20},{1,9},{5... | collective-permute-start | bytes 393224 | tf_op jit(solution)/shard_map/ppermute | solution.py:20
  50.1 1.1 prepare.2
  51.2 2.2 %collective-permute-done.14.refs_3_ = f32[128,256]{1,0:T(8,128)S(1)} collective-permute-done((f32[128,256]{1,0:T(8,128)S(1)}, f32[128,256]{1,0:T(8,128)S(1)}, u32[]{:S(2)}, u32[]{:S(2)}) %collective-permute-start.14) | collective-permute-done | bytes 131104 | tf_op jit(solution)/shard_map/ppermute | solution.py:20
  53.5 1.3 %collective-permute-done.18.refs_7_ = f32[128,256]{1,0:T(8,128)S(1)} collective-permute-done((f32[128,256]{1,0:T(8,128)S(1)}, f32[128,256]{1,0:T(8,128)S(1)}, u32[]{:S(2)}, u32[]{:S(2)}) %collective-permute-start.18) | collective-permute-done | bytes 131104 | tf_op jit(solution)/shard_map/ppermute | solution.py:20
  54.8 2.7 %update.2 = (f32[512,256]{1,0:T(8,128)S(1)}, f32[512,256]{1,0:T(8,128)S(1)}) custom-call(s32[1,2]{1,0:T(1,128)S(1)} %copy-done.1, s32[8]{0:T(128)S(1)} %copy-done.2, bf16[1024,1024]{1,0:T(8,128)(2,1)S(1)} %get-tuple-element.89.high, bf16[1024,1024]{1,0:T(8,128)(2,1)S(1)} %get-tuple-element.90.low, f32[128,256]{1,0:T(8,128)S(1)} %solve.2.refs_0_, ...), custom_call_target="tpu_custom_call" | custom-call | flops 1610612736 | bytes 7340032 | tf_op jit(solution)/shard_map/update/pallas_call | solution.py:184
  59.9 1.2 %collective-permute-start.20 = (f32[256,256]{1,0:T(8,128)S(1)}, f32[256,256]{1,0:T(8,128)S(1)}, u32[]{:S(2)}, u32[]{:S(2)}) collective-permute-start(f32[256,256]{1,0:T(8,128)S(1)} %constant_dynamic-slice_fusion.1), channel_id=1, source_target_pairs={{0,8},{4,12},{8,0},{12,4},{16,24},{20,28},{24,16},{28,20},{1,9},{5... | collective-permute-start | bytes 786440 | tf_op jit(solution)/shard_map/ppermute | solution.py:20
  61.1 1.3 %slice_bitcast_fusion.1 = (f32[128,1024]{1,0:T(8,128)S(1)}, f32[128,1024]{1,0:T(8,128)S(1)}) fusion(f32[1,2,256,1024]{3,2,1,0:T(8,128)} %param.6), kind=kLoop, calls=%fused_computation.1 | loop fusion | bytes 2097152 | tf_op jit(solution)/shard_map/squeeze | solution.py:233
  62.4 1.6 %collective-permute-start.22 = (f32[128,1024]{1,0:T(8,128)S(1)}, f32[128,1024]{1,0:T(8,128)S(1)}, u32[]{:S(2)}, u32[]{:S(2)}) collective-permute-start(f32[128,1024]{1,0:T(8,128)S(1)} %get-tuple-element.106.own_top), channel_id=1, source_target_pairs={{0,1},{1,0},{2,3},{3,2},{4,5},{5,4},{6,7},{7,6},{8,9},{9,8},{10,11... | collective-permute-start | bytes 1572872 | tf_op jit(solution)/shard_map/ppermute | solution.py:20
  64.0 1.5 %collective-permute-start.23 = (f32[128,1024]{1,0:T(8,128)S(1)}, f32[128,1024]{1,0:T(8,128)S(1)}, u32[]{:S(2)}, u32[]{:S(2)}) collective-permute-start(f32[128,1024]{1,0:T(8,128)S(1)} %get-tuple-element.105.own_bottom), channel_id=1, source_target_pairs={{0,2},{1,3},{2,0},{3,1},{4,6},{5,7},{6,4},{7,5},{8,10},{9,11},{10,... | collective-permute-start | bytes 1572872 | tf_op jit(solution)/shard_map/ppermute | solution.py:20
  65.5 3.1 %collective-permute-done.20 = f32[256,256]{1,0:T(8,128)S(1)} collective-permute-done((f32[256,256]{1,0:T(8,128)S(1)}, f32[256,256]{1,0:T(8,128)S(1)}, u32[]{:S(2)}, u32[]{:S(2)}) %collective-permute-start.20) | collective-permute-done | bytes 262176 | tf_op jit(solution)/shard_map/ppermute | solution.py:20
  68.6 2.3 %collective-permute-start.21 = (f32[256,256]{1,0:T(8,128)S(1)}, f32[256,256]{1,0:T(8,128)}, u32[]{:S(2)}, u32[]{:S(2)}) collective-permute-start(f32[256,256]{1,0:T(8,128)S(1)} %dynamic-slice_select_fusion), channel_id=1, source_target_pairs={{0,16},{4,20},{8,24},{12,28},{16,0},{20,4},{24,8},{28,12},{1,17},{... | collective-permute-start | bytes 786440 | tf_op jit(solution)/shard_map/ppermute | solution.py:20
  70.9 1.5 %collective-permute-start.25 = (f32[128,1024]{1,0:T(8,128)S(1)}, f32[128,1024]{1,0:T(8,128)}, u32[]{:S(2)}, u32[]{:S(2)}) collective-permute-start(f32[128,1024]{1,0:T(8,128)S(1)} %get-tuple-element.105.own_bottom), channel_id=1, source_target_pairs={{0,1},{1,0},{2,3},{3,2},{4,5},{5,4},{6,7},{7,6},{8,9},{9,8},{10,11... | collective-permute-start | bytes 1572872 | tf_op jit(solution)/shard_map/ppermute | solution.py:20
  72.4 1.5 %collective-permute-start.26 = (f32[128,1024]{1,0:T(8,128)S(1)}, f32[128,1024]{1,0:T(8,128)}, u32[]{:S(2)}, u32[]{:S(2)}) collective-permute-start(f32[128,1024]{1,0:T(8,128)S(1)} %get-tuple-element.106.own_top), channel_id=1, source_target_pairs={{0,2},{1,3},{2,0},{3,1},{4,6},{5,7},{6,4},{7,5},{8,10},{9,11},{10,... | collective-permute-start | bytes 1572872 | tf_op jit(solution)/shard_map/ppermute | solution.py:20
  74.6 8.5 %collective-permute-done.21 = f32[256,256]{1,0:T(8,128)} collective-permute-done((f32[256,256]{1,0:T(8,128)S(1)}, f32[256,256]{1,0:T(8,128)}, u32[]{:S(2)}, u32[]{:S(2)}) %collective-permute-start.21) | collective-permute-done | bytes 262176 | tf_op jit(solution)/shard_map/ppermute | solution.py:20
  84.3 1.5 %collective-permute-start.31 = (f32[128,1024]{1,0:T(8,128)S(1)}, f32[128,1024]{1,0:T(8,128)S(1)}, u32[]{:S(2)}, u32[]{:S(2)}) collective-permute-start(f32[128,1024]{1,0:T(8,128)S(1)} %collective-permute-done.22.refs_0_), channel_id=1, source_target_pairs={{0,2},{1,3},{2,0},{3,1},{4,6},{5,7},{6,4},{7,5},{8,10},{9,11},{10,... | collective-permute-start | bytes 1572872 | tf_op jit(solution)/shard_map/ppermute | solution.py:20
  85.9 1.5 %collective-permute-start.32 = (f32[128,1024]{1,0:T(8,128)S(1)}, f32[128,1024]{1,0:T(8,128)S(1)}, u32[]{:S(2)}, u32[]{:S(2)}) collective-permute-start(f32[128,1024]{1,0:T(8,128)S(1)} %collective-permute-done.23.refs_1_), channel_id=1, source_target_pairs={{0,1},{1,0},{2,3},{3,2},{4,5},{5,4},{6,7},{7,6},{8,9},{9,8},{10,11... | collective-permute-start | bytes 1572872 | tf_op jit(solution)/shard_map/ppermute | solution.py:20
  87.3 1.1 slice_bitcast_fusion.inverse
  88.4 1.7 %collective-permute-done.26.refs_3_ = f32[128,1024]{1,0:T(8,128)} collective-permute-done((f32[128,1024]{1,0:T(8,128)S(1)}, f32[128,1024]{1,0:T(8,128)}, u32[]{:S(2)}, u32[]{:S(2)}) %collective-permute-start.26) | collective-permute-done | bytes 524320 | tf_op jit(solution)/shard_map/ppermute | solution.py:20
  90.1 1.4 %collective-permute-done.24.refs_1_ = f32[256,256]{1,0:T(8,128)S(1)} collective-permute-done((f32[256,256]{1,0:T(8,128)S(1)}, f32[256,256]{1,0:T(8,128)S(1)}, u32[]{:S(2)}, u32[]{:S(2)}) %collective-permute-start.24) | collective-permute-done | bytes 262176 | tf_op jit(solution)/shard_map/ppermute | solution.py:20
  91.7 1.4 %collective-permute-done.28.refs_3_ = f32[256,256]{1,0:T(8,128)S(1)} collective-permute-done((f32[256,256]{1,0:T(8,128)S(1)}, f32[256,256]{1,0:T(8,128)S(1)}, u32[]{:S(2)}, u32[]{:S(2)}) %collective-permute-start.28) | collective-permute-done | bytes 262176 | tf_op jit(solution)/shard_map/ppermute | solution.py:20
  93.6 1.9 %collective-permute-start.29 = (f32[128,256]{1,0:T(8,128)S(1)}, f32[128,256]{1,0:T(8,128)S(1)}, u32[]{:S(2)}, u32[]{:S(2)}) collective-permute-start(f32[128,256]{1,0:T(8,128)S(1)} %solve.3.refs_0_), channel_id=1, source_target_pairs={{0,16},{4,20},{8,24},{12,28},{16,0},{20,4},{24,8},{28,12},{1,17},{... | collective-permute-start | bytes 393224 | tf_op jit(solution)/shard_map/ppermute | solution.py:20
  95.4 1.7 %collective-permute-start.30 = (f32[128,256]{1,0:T(8,128)S(1)}, f32[128,256]{1,0:T(8,128)S(1)}, u32[]{:S(2)}, u32[]{:S(2)}) collective-permute-start(f32[128,256]{1,0:T(8,128)S(1)} %solve.3.refs_0_), channel_id=1, source_target_pairs={{0,8},{4,12},{8,0},{12,4},{16,24},{20,28},{24,16},{28,20},{1,9},{5... | collective-permute-start | bytes 393224 | tf_op jit(solution)/shard_map/ppermute | solution.py:20
  97.2 2.9 %collective-permute-done.31.refs_4_ = f32[128,1024]{1,0:T(8,128)S(1)} collective-permute-done((f32[128,1024]{1,0:T(8,128)S(1)}, f32[128,1024]{1,0:T(8,128)S(1)}, u32[]{:S(2)}, u32[]{:S(2)}) %collective-permute-start.31) | collective-permute-done | bytes 524320 | tf_op jit(solution)/shard_map/ppermute | solution.py:20
  100.1 2.9 %collective-permute-done.29.refs_2_ = f32[128,256]{1,0:T(8,128)S(1)} collective-permute-done((f32[128,256]{1,0:T(8,128)S(1)}, f32[128,256]{1,0:T(8,128)S(1)}, u32[]{:S(2)}, u32[]{:S(2)}) %collective-permute-start.29) | collective-permute-done | bytes 131104 | tf_op jit(solution)/shard_map/ppermute | solution.py:20
  104.3 1.8 %prepare.3 = (bf16[1024,1024]{1,0:T(8,128)(2,1)S(1)}, bf16[1024,1024]{1,0:T(8,128)(2,1)S(1)}) custom-call(f32[128,1024]{1,0:T(8,128)S(1)} %get-tuple-element.106.own_top, f32[128,1024]{1,0:T(8,128)S(1)} %get-tuple-element.105.own_bottom, f32[128,1024]{1,0:T(8,128)S(1)} %collective-permute-done.22.refs_0_, f32[128,1024]{1,0:T(8,128)S(1)} %collective-permute-done.23.refs_1_, ...), custom_call_target="tpu_custom_call" | custom-call | bytes 16777216 | tf_op jit(solution)/shard_map/prepare/pallas_call | solution.py:98
  106.2 1.8 %collective-permute-done.33.refs_3_ = f32[128,256]{1,0:T(8,128)S(1)} collective-permute-done((f32[128,256]{1,0:T(8,128)S(1)}, f32[128,256]{1,0:T(8,128)S(1)}, u32[]{:S(2)}, u32[]{:S(2)}) %collective-permute-start.33) | collective-permute-done | bytes 131104 | tf_op jit(solution)/shard_map/ppermute | solution.py:20
  108.0 1.3 %collective-permute-done.37.refs_7_ = f32[128,256]{1,0:T(8,128)S(1)} collective-permute-done((f32[128,256]{1,0:T(8,128)S(1)}, f32[128,256]{1,0:T(8,128)S(1)}, u32[]{:S(2)}, u32[]{:S(2)}) %collective-permute-start.37) | collective-permute-done | bytes 131104 | tf_op jit(solution)/shard_map/ppermute | solution.py:20
  109.3 3.4 %update.3 = f32[1024,256]{1,0:T(8,128)} custom-call(s32[1,2]{1,0:T(1,128)S(1)} %copy-done.1, s32[8]{0:T(128)S(1)} %copy-done.2, bf16[1024,1024]{1,0:T(8,128)(2,1)S(1)} %get-tuple-element.119.high, bf16[1024,1024]{1,0:T(8,128)(2,1)S(1)} %get-tuple-element.120.low, f32[128,256]{1,0:T(8,128)S(1)} %solve.3.refs_0_, ...), custom_call_target="tpu_custom_call" | custom-call | flops 1610612736 | bytes 7340032 | tf_op jit(solution)/shard_map/update/pallas_call | solution.py:184
  (56 shorter events, 7.0 us)
Async XLA Ops:
  0.0 7.1 %copy-start.3 = (f32[1,2,256,1024]{3,2,1,0:T(8,128)S(1)}, f32[1,2,256,1024]{3,2,1,0:T(8,128)}, u32[]{:S(2)}) copy-start(f32[1,2,256,1024]{3,2,1,0:T(8,128)} %param.6) | copy-start | bytes 6291460
  0.0 3.3 %collective-permute-start = (f32[1,1024,256]{2,1,0:T(8,128)}, f32[1,1024,256]{2,1,0:T(8,128)S(1)}, u32[]{:S(2)}, u32[]{:S(2)}) collective-permute-start(f32[1,1024,256]{2,1,0:T(8,128)} %refs_8_.1), channel_id=1, source_target_pairs={{0,4},{4,0},{8,12},{12,8},{16,20},{20,16},{24,28},{28,24},{1,5},{5... | collective-permute-start | bytes 3145736 | tf_op jit(solution)/shard_map/ppermute | solution.py:20
  4.4 9.4 %collective-permute-start.1 = (f32[256,256]{1,0:T(8,128)S(1)}, f32[256,256]{1,0:T(8,128)S(1)}, u32[]{:S(2)}, u32[]{:S(2)}) collective-permute-start(f32[256,256]{1,0:T(8,128)S(1)} %constant_dynamic-slice_fusion), channel_id=1, source_target_pairs={{0,8},{4,12},{8,0},{12,4},{16,24},{20,28},{24,16},{28,20},{1,9},{5... | collective-permute-start | bytes 786440 | tf_op jit(solution)/shard_map/ppermute | solution.py:20
  7.2 22.4 %collective-permute-start.3 = (f32[128,1024]{1,0:T(8,128)S(1)}, f32[128,1024]{1,0:T(8,128)S(1)}, u32[]{:S(2)}, u32[]{:S(2)}) collective-permute-start(f32[128,1024]{1,0:T(8,128)S(1)} %get-tuple-element.76.own_top), channel_id=1, source_target_pairs={{0,1},{1,0},{2,3},{3,2},{4,5},{5,4},{6,7},{7,6},{8,9},{9,8},{10,11... | collective-permute-start | bytes 1572872 | tf_op jit(solution)/shard_map/ppermute | solution.py:20
  8.8 20.8 %collective-permute-start.4 = (f32[128,1024]{1,0:T(8,128)S(1)}, f32[128,1024]{1,0:T(8,128)S(1)}, u32[]{:S(2)}, u32[]{:S(2)}) collective-permute-start(f32[128,1024]{1,0:T(8,128)S(1)} %get-tuple-element.75.own_bottom), channel_id=1, source_target_pairs={{0,2},{1,3},{2,0},{3,1},{4,6},{5,7},{6,4},{7,5},{8,10},{9,11},{10,... | collective-permute-start | bytes 1572872 | tf_op jit(solution)/shard_map/ppermute | solution.py:20
  13.9 14.7 %collective-permute-start.2 = (f32[256,256]{1,0:T(8,128)S(1)}, f32[256,256]{1,0:T(8,128)}, u32[]{:S(2)}, u32[]{:S(2)}) collective-permute-start(f32[256,256]{1,0:T(8,128)S(1)} %dynamic-slice_select_fusion.1), channel_id=1, source_target_pairs={{0,16},{4,20},{8,24},{12,28},{16,0},{20,4},{24,8},{28,12},{1,17},{... | collective-permute-start | bytes 786440 | tf_op jit(solution)/shard_map/ppermute | solution.py:20
  16.7 17.5 %collective-permute-start.6 = (f32[128,1024]{1,0:T(8,128)S(1)}, f32[128,1024]{1,0:T(8,128)S(1)}, u32[]{:S(2)}, u32[]{:S(2)}) collective-permute-start(f32[128,1024]{1,0:T(8,128)S(1)} %get-tuple-element.75.own_bottom), channel_id=1, source_target_pairs={{0,1},{1,0},{2,3},{3,2},{4,5},{5,4},{6,7},{7,6},{8,9},{9,8},{10,11... | collective-permute-start | bytes 1572872 | tf_op jit(solution)/shard_map/ppermute | solution.py:20
  18.2 16.4 %collective-permute-start.7 = (f32[128,1024]{1,0:T(8,128)S(1)}, f32[128,1024]{1,0:T(8,128)S(1)}, u32[]{:S(2)}, u32[]{:S(2)}) collective-permute-start(f32[128,1024]{1,0:T(8,128)S(1)} %get-tuple-element.76.own_top), channel_id=1, source_target_pairs={{0,2},{1,3},{2,0},{3,1},{4,6},{5,7},{6,4},{7,5},{8,10},{9,11},{10,... | collective-permute-start | bytes 1572872 | tf_op jit(solution)/shard_map/ppermute | solution.py:20
  29.6 7.4 %collective-permute-start.5 = (f32[256,256]{1,0:T(8,128)S(1)}, f32[256,256]{1,0:T(8,128)S(1)}, u32[]{:S(2)}, u32[]{:S(2)}) collective-permute-start(f32[256,256]{1,0:T(8,128)S(1)} %broadcast_select_fusion.1.refs_0_), channel_id=1, source_target_pairs={{0,8},{4,12},{8,0},{12,4},{16,24},{20,28},{24,16},{28,20},{1,9},{5... | collective-permute-start | bytes 786440 | tf_op jit(solution)/shard_map/ppermute | solution.py:20
  30.1 14.7 %collective-permute-start.12 = (f32[128,1024]{1,0:T(8,128)S(1)}, f32[128,1024]{1,0:T(8,128)S(1)}, u32[]{:S(2)}, u32[]{:S(2)}) collective-permute-start(f32[128,1024]{1,0:T(8,128)S(1)} %collective-permute-done.3.refs_0_), channel_id=1, source_target_pairs={{0,2},{1,3},{2,0},{3,1},{4,6},{5,7},{6,4},{7,5},{8,10},{9,11},{10,... | collective-permute-start | bytes 1572872 | tf_op jit(solution)/shard_map/ppermute | solution.py:20
  31.6 13.3 %collective-permute-start.13 = (f32[128,1024]{1,0:T(8,128)S(1)}, f32[128,1024]{1,0:T(8,128)S(1)}, u32[]{:S(2)}, u32[]{:S(2)}) collective-permute-start(f32[128,1024]{1,0:T(8,128)S(1)} %collective-permute-done.4.refs_1_), channel_id=1, source_target_pairs={{0,1},{1,0},{2,3},{3,2},{4,5},{5,4},{6,7},{7,6},{8,9},{9,8},{10,11... | collective-permute-start | bytes 1572872 | tf_op jit(solution)/shard_map/ppermute | solution.py:20
  34.7 2.4 %collective-permute-start.8 = (f32[256,256]{1,0:T(8,128)S(1)}, f32[256,256]{1,0:T(8,128)S(1)}, u32[]{:S(2)}, u32[]{:S(2)}) collective-permute-start(f32[256,256]{1,0:T(8,128)S(1)} %broadcast_select_fusion.1.refs_0_), channel_id=1, source_target_pairs={{0,4},{4,0},{8,12},{12,8},{16,20},{20,16},{24,28},{28,24},{1,5},{5... | collective-permute-start | bytes 786440 | tf_op jit(solution)/shard_map/ppermute | solution.py:20
  37.0 1.5 %collective-permute-start.9 = (f32[256,256]{1,0:T(8,128)S(1)}, f32[256,256]{1,0:T(8,128)S(1)}, u32[]{:S(2)}, u32[]{:S(2)}) collective-permute-start(f32[256,256]{1,0:T(8,128)S(1)} %collective-permute-done.5.refs_1_), channel_id=1, source_target_pairs={{0,4},{4,0},{8,12},{12,8},{16,20},{20,16},{24,28},{28,24},{1,5},{5... | collective-permute-start | bytes 786440 | tf_op jit(solution)/shard_map/ppermute | solution.py:20
  39.1 15.8 %copy-start = (f32[1,1024,256]{2,1,0:T(8,128)S(1)}, f32[1,1024,256]{2,1,0:T(8,128)}, u32[]{:S(2)}) copy-start(f32[1,1024,256]{2,1,0:T(8,128)} %refs_8_.1) | copy-start | bytes 3145732
  39.1 15.8 %copy-start.1 = (s32[1,2]{1,0:T(1,128)S(1)}, s32[1,2]{1,0:T(1,128)}, u32[]{:S(2)}) copy-start(s32[1,2]{1,0:T(1,128)} %flags.3) | copy-start | bytes 28
  39.1 15.7 %copy-start.2 = (s32[8]{0:T(128)S(1)}, s32[8]{0:T(128)}, u32[]{:S(2)}) copy-start(s32[8]{0:T(128)} %slot_block.3) | copy-start | bytes 100
  39.1 9.4 %collective-permute-start.10 = (f32[128,256]{1,0:T(8,128)S(1)}, f32[128,256]{1,0:T(8,128)S(1)}, u32[]{:S(2)}, u32[]{:S(2)}) collective-permute-start(f32[128,256]{1,0:T(8,128)S(1)} %solve.2.refs_0_), channel_id=1, source_target_pairs={{0,16},{4,20},{8,24},{12,28},{16,0},{20,4},{24,8},{28,12},{1,17},{... | collective-permute-start | bytes 393224 | tf_op jit(solution)/shard_map/ppermute | solution.py:20
  41.3 7.2 %collective-permute-start.11 = (f32[128,256]{1,0:T(8,128)S(1)}, f32[128,256]{1,0:T(8,128)S(1)}, u32[]{:S(2)}, u32[]{:S(2)}) collective-permute-start(f32[128,256]{1,0:T(8,128)S(1)} %solve.2.refs_0_), channel_id=1, source_target_pairs={{0,8},{4,12},{8,0},{12,4},{16,24},{20,28},{24,16},{28,20},{1,9},{5... | collective-permute-start | bytes 393224 | tf_op jit(solution)/shard_map/ppermute | solution.py:20
  43.0 8.2 %collective-permute-start.15 = (f32[128,256]{1,0:T(8,128)S(1)}, f32[128,256]{1,0:T(8,128)S(1)}, u32[]{:S(2)}, u32[]{:S(2)}) collective-permute-start(f32[128,256]{1,0:T(8,128)S(1)} %solve.2.refs_0_), channel_id=1, source_target_pairs={{0,4},{4,0},{8,12},{12,8},{16,20},{20,16},{24,28},{28,24},{1,5},{5... | collective-permute-start | bytes 393224 | tf_op jit(solution)/shard_map/ppermute | solution.py:20
  48.5 5.0 %collective-permute-start.14 = (f32[128,256]{1,0:T(8,128)S(1)}, f32[128,256]{1,0:T(8,128)S(1)}, u32[]{:S(2)}, u32[]{:S(2)}) collective-permute-start(f32[128,256]{1,0:T(8,128)S(1)} %collective-permute-done.10.refs_2_), channel_id=1, source_target_pairs={{0,8},{4,12},{8,0},{12,4},{16,24},{20,28},{24,16},{28,20},{1,9},{5... | collective-permute-start | bytes 393224 | tf_op jit(solution)/shard_map/ppermute | solution.py:20
  49.6 3.8 %collective-permute-start.16 = (f32[128,256]{1,0:T(8,128)S(1)}, f32[128,256]{1,0:T(8,128)S(1)}, u32[]{:S(2)}, u32[]{:S(2)}) collective-permute-start(f32[128,256]{1,0:T(8,128)S(1)} %collective-permute-done.11.refs_1_), channel_id=1, source_target_pairs={{0,4},{4,0},{8,12},{12,8},{16,20},{20,16},{24,28},{28,24},{1,5},{5... | collective-permute-start | bytes 393224 | tf_op jit(solution)/shard_map/ppermute | solution.py:20
  49.6 3.8 %collective-permute-start.17 = (f32[128,256]{1,0:T(8,128)S(1)}, f32[128,256]{1,0:T(8,128)S(1)}, u32[]{:S(2)}, u32[]{:S(2)}) collective-permute-start(f32[128,256]{1,0:T(8,128)S(1)} %collective-permute-done.10.refs_2_), channel_id=1, source_target_pairs={{0,4},{4,0},{8,12},{12,8},{16,20},{20,16},{24,28},{28,24},{1,5},{5... | collective-permute-start | bytes 393224 | tf_op jit(solution)/shard_map/ppermute | solution.py:20
  53.5 1.4 %collective-permute-start.18 = (f32[128,256]{1,0:T(8,128)S(1)}, f32[128,256]{1,0:T(8,128)S(1)}, u32[]{:S(2)}, u32[]{:S(2)}) collective-permute-start(f32[128,256]{1,0:T(8,128)S(1)} %collective-permute-done.14.refs_3_), channel_id=1, source_target_pairs={{0,4},{4,0},{8,12},{12,8},{16,20},{20,16},{24,28},{28,24},{1,5},{5... | collective-permute-start | bytes 393224 | tf_op jit(solution)/shard_map/ppermute | solution.py:20
  57.5 2.3 %collective-permute-start.19 = (f32[512,256]{1,0:T(8,128)S(1)}, f32[512,256]{1,0:T(8,128)S(1)}, u32[]{:S(2)}, u32[]{:S(2)}) collective-permute-start(f32[512,256]{1,0:T(8,128)S(1)} %get-tuple-element.96.refs_9_), channel_id=1, source_target_pairs={{0,4},{4,0},{8,12},{12,8},{16,20},{20,16},{24,28},{28,24},{1,5},{5... | collective-permute-start | bytes 1572872 | tf_op jit(solution)/shard_map/ppermute | solution.py:20
  59.9 8.6 %collective-permute-start.20 = (f32[256,256]{1,0:T(8,128)S(1)}, f32[256,256]{1,0:T(8,128)S(1)}, u32[]{:S(2)}, u32[]{:S(2)}) collective-permute-start(f32[256,256]{1,0:T(8,128)S(1)} %constant_dynamic-slice_fusion.1), channel_id=1, source_target_pairs={{0,8},{4,12},{8,0},{12,4},{16,24},{20,28},{24,16},{28,20},{1,9},{5... | collective-permute-start | bytes 786440 | tf_op jit(solution)/shard_map/ppermute | solution.py:20
  62.4 21.6 %collective-permute-start.22 = (f32[128,1024]{1,0:T(8,128)S(1)}, f32[128,1024]{1,0:T(8,128)S(1)}, u32[]{:S(2)}, u32[]{:S(2)}) collective-permute-start(f32[128,1024]{1,0:T(8,128)S(1)} %get-tuple-element.106.own_top), channel_id=1, source_target_pairs={{0,1},{1,0},{2,3},{3,2},{4,5},{5,4},{6,7},{7,6},{8,9},{9,8},{10,11... | collective-permute-start | bytes 1572872 | tf_op jit(solution)/shard_map/ppermute | solution.py:20
  64.0 20.1 %collective-permute-start.23 = (f32[128,1024]{1,0:T(8,128)S(1)}, f32[128,1024]{1,0:T(8,128)S(1)}, u32[]{:S(2)}, u32[]{:S(2)}) collective-permute-start(f32[128,1024]{1,0:T(8,128)S(1)} %get-tuple-element.105.own_bottom), channel_id=1, source_target_pairs={{0,2},{1,3},{2,0},{3,1},{4,6},{5,7},{6,4},{7,5},{8,10},{9,11},{10,... | collective-permute-start | bytes 1572872 | tf_op jit(solution)/shard_map/ppermute | solution.py:20
  68.6 14.4 %collective-permute-start.21 = (f32[256,256]{1,0:T(8,128)S(1)}, f32[256,256]{1,0:T(8,128)}, u32[]{:S(2)}, u32[]{:S(2)}) collective-permute-start(f32[256,256]{1,0:T(8,128)S(1)} %dynamic-slice_select_fusion), channel_id=1, source_target_pairs={{0,16},{4,20},{8,24},{12,28},{16,0},{20,4},{24,8},{28,12},{1,17},{... | collective-permute-start | bytes 786440 | tf_op jit(solution)/shard_map/ppermute | solution.py:20
  70.9 17.5 %collective-permute-start.25 = (f32[128,1024]{1,0:T(8,128)S(1)}, f32[128,1024]{1,0:T(8,128)}, u32[]{:S(2)}, u32[]{:S(2)}) collective-permute-start(f32[128,1024]{1,0:T(8,128)S(1)} %get-tuple-element.105.own_bottom), channel_id=1, source_target_pairs={{0,1},{1,0},{2,3},{3,2},{4,5},{5,4},{6,7},{7,6},{8,9},{9,8},{10,11... | collective-permute-start | bytes 1572872 | tf_op jit(solution)/shard_map/ppermute | solution.py:20
  72.4 17.8 %collective-permute-start.26 = (f32[128,1024]{1,0:T(8,128)S(1)}, f32[128,1024]{1,0:T(8,128)}, u32[]{:S(2)}, u32[]{:S(2)}) collective-permute-start(f32[128,1024]{1,0:T(8,128)S(1)} %get-tuple-element.106.own_top), channel_id=1, source_target_pairs={{0,2},{1,3},{2,0},{3,1},{4,6},{5,7},{6,4},{7,5},{8,10},{9,11},{10,... | collective-permute-start | bytes 1572872 | tf_op jit(solution)/shard_map/ppermute | solution.py:20
  84.1 7.5 %collective-permute-start.24 = (f32[256,256]{1,0:T(8,128)S(1)}, f32[256,256]{1,0:T(8,128)S(1)}, u32[]{:S(2)}, u32[]{:S(2)}) collective-permute-start(f32[256,256]{1,0:T(8,128)S(1)} %broadcast_select_fusion.2.refs_0_), channel_id=1, source_target_pairs={{0,8},{4,12},{8,0},{12,4},{16,24},{20,28},{24,16},{28,20},{1,9},{5... | collective-permute-start | bytes 786440 | tf_op jit(solution)/shard_map/ppermute | solution.py:20
  84.3 15.7 %collective-permute-start.31 = (f32[128,1024]{1,0:T(8,128)S(1)}, f32[128,1024]{1,0:T(8,128)S(1)}, u32[]{:S(2)}, u32[]{:S(2)}) collective-permute-start(f32[128,1024]{1,0:T(8,128)S(1)} %collective-permute-done.22.refs_0_), channel_id=1, source_target_pairs={{0,2},{1,3},{2,0},{3,1},{4,6},{5,7},{6,4},{7,5},{8,10},{9,11},{10,... | collective-permute-start | bytes 1572872 | tf_op jit(solution)/shard_map/ppermute | solution.py:20
  85.9 14.2 %collective-permute-start.32 = (f32[128,1024]{1,0:T(8,128)S(1)}, f32[128,1024]{1,0:T(8,128)S(1)}, u32[]{:S(2)}, u32[]{:S(2)}) collective-permute-start(f32[128,1024]{1,0:T(8,128)S(1)} %collective-permute-done.23.refs_1_), channel_id=1, source_target_pairs={{0,1},{1,0},{2,3},{3,2},{4,5},{5,4},{6,7},{7,6},{8,9},{9,8},{10,11... | collective-permute-start | bytes 1572872 | tf_op jit(solution)/shard_map/ppermute | solution.py:20
  90.1 1.5 %collective-permute-start.27 = (f32[256,256]{1,0:T(8,128)S(1)}, f32[256,256]{1,0:T(8,128)S(1)}, u32[]{:S(2)}, u32[]{:S(2)}) collective-permute-start(f32[256,256]{1,0:T(8,128)S(1)} %broadcast_select_fusion.2.refs_0_), channel_id=1, source_target_pairs={{0,4},{4,0},{8,12},{12,8},{16,20},{20,16},{24,28},{28,24},{1,5},{5... | collective-permute-start | bytes 786440 | tf_op jit(solution)/shard_map/ppermute | solution.py:20
  91.6 1.5 %collective-permute-start.28 = (f32[256,256]{1,0:T(8,128)S(1)}, f32[256,256]{1,0:T(8,128)S(1)}, u32[]{:S(2)}, u32[]{:S(2)}) collective-permute-start(f32[256,256]{1,0:T(8,128)S(1)} %collective-permute-done.24.refs_1_), channel_id=1, source_target_pairs={{0,4},{4,0},{8,12},{12,8},{16,20},{20,16},{24,28},{28,24},{1,5},{5... | collective-permute-start | bytes 786440 | tf_op jit(solution)/shard_map/ppermute | solution.py:20
  93.6 9.4 %collective-permute-start.29 = (f32[128,256]{1,0:T(8,128)S(1)}, f32[128,256]{1,0:T(8,128)S(1)}, u32[]{:S(2)}, u32[]{:S(2)}) collective-permute-start(f32[128,256]{1,0:T(8,128)S(1)} %solve.3.refs_0_), channel_id=1, source_target_pairs={{0,16},{4,20},{8,24},{12,28},{16,0},{20,4},{24,8},{28,12},{1,17},{... | collective-permute-start | bytes 393224 | tf_op jit(solution)/shard_map/ppermute | solution.py:20
  95.4 7.5 %collective-permute-start.30 = (f32[128,256]{1,0:T(8,128)S(1)}, f32[128,256]{1,0:T(8,128)S(1)}, u32[]{:S(2)}, u32[]{:S(2)}) collective-permute-start(f32[128,256]{1,0:T(8,128)S(1)} %solve.3.refs_0_), channel_id=1, source_target_pairs={{0,8},{4,12},{8,0},{12,4},{16,24},{20,28},{24,16},{28,20},{1,9},{5... | collective-permute-start | bytes 393224 | tf_op jit(solution)/shard_map/ppermute | solution.py:20
  97.2 9.0 %collective-permute-start.34 = (f32[128,256]{1,0:T(8,128)S(1)}, f32[128,256]{1,0:T(8,128)S(1)}, u32[]{:S(2)}, u32[]{:S(2)}) collective-permute-start(f32[128,256]{1,0:T(8,128)S(1)} %solve.3.refs_0_), channel_id=1, source_target_pairs={{0,4},{4,0},{8,12},{12,8},{16,20},{20,16},{24,28},{28,24},{1,5},{5... | collective-permute-start | bytes 393224 | tf_op jit(solution)/shard_map/ppermute | solution.py:20
  103.0 5.0 %collective-permute-start.33 = (f32[128,256]{1,0:T(8,128)S(1)}, f32[128,256]{1,0:T(8,128)S(1)}, u32[]{:S(2)}, u32[]{:S(2)}) collective-permute-start(f32[128,256]{1,0:T(8,128)S(1)} %collective-permute-done.29.refs_2_), channel_id=1, source_target_pairs={{0,8},{4,12},{8,0},{12,4},{16,24},{20,28},{24,16},{28,20},{1,9},{5... | collective-permute-start | bytes 393224 | tf_op jit(solution)/shard_map/ppermute | solution.py:20
  103.8 4.1 %collective-permute-start.35 = (f32[128,256]{1,0:T(8,128)S(1)}, f32[128,256]{1,0:T(8,128)S(1)}, u32[]{:S(2)}, u32[]{:S(2)}) collective-permute-start(f32[128,256]{1,0:T(8,128)S(1)} %collective-permute-done.30.refs_1_), channel_id=1, source_target_pairs={{0,4},{4,0},{8,12},{12,8},{16,20},{20,16},{24,28},{28,24},{1,5},{5... | collective-permute-start | bytes 393224 | tf_op jit(solution)/shard_map/ppermute | solution.py:20
  103.8 4.1 %collective-permute-start.36 = (f32[128,256]{1,0:T(8,128)S(1)}, f32[128,256]{1,0:T(8,128)S(1)}, u32[]{:S(2)}, u32[]{:S(2)}) collective-permute-start(f32[128,256]{1,0:T(8,128)S(1)} %collective-permute-done.29.refs_2_), channel_id=1, source_target_pairs={{0,4},{4,0},{8,12},{12,8},{16,20},{20,16},{24,28},{28,24},{1,5},{5... | collective-permute-start | bytes 393224 | tf_op jit(solution)/shard_map/ppermute | solution.py:20
  108.0 1.4 %collective-permute-start.37 = (f32[128,256]{1,0:T(8,128)S(1)}, f32[128,256]{1,0:T(8,128)S(1)}, u32[]{:S(2)}, u32[]{:S(2)}) collective-permute-start(f32[128,256]{1,0:T(8,128)S(1)} %collective-permute-done.33.refs_3_), channel_id=1, source_target_pairs={{0,4},{4,0},{8,12},{12,8},{16,20},{20,16},{24,28},{28,24},{1,5},{5... | collective-permute-start | bytes 393224 | tf_op jit(solution)/shard_map/ppermute | solution.py:20

commit v10 on v9

--- a/solution.py
+++ b/solution.py
@@ -257,7 +257,9 @@
         return [x, x1, x2, x3, *across, swap(x3, "row", 0, rows)], (high, low)
 
     got = swap(rhs, "row", 0, rows)
-    y = jnp.where(bit(owner, 0) == core, halves(rhs[0], core)[0], halves(got[0], core)[0])
+    kept, owner = tie(rhs, owner)
+    keep, owner = tie(halves(kept[0], core)[0], owner)
+    y = jnp.where(bit(owner, 0) == core, keep, halves(got[0], core)[0])
     blocks, pair = solved(0, y, panel, owner)
     keep, send = update(0, flags, slot_block, pair, blocks, [rhs])
     got = swap(send, "row", 0, rows)

time: 114 us -> 114 us (level); the launches traced: 113 us -> 114 us
  starting transfers between devices: 39.1 us -> 42.9 us
  waiting for transfers between devices: 50.3 us -> 47.7 us
    ppermute x38, starting transfers between devices: 39.1 us -> 42.9 us  [swap(): return lax.ppermute(x, axis, [(i, i ^ 1 << b) for i in range(size)])]
    ppermute x38, waiting for transfers between devices: 50.3 us -> 47.7 us  [swap(): return lax.ppermute(x, axis, [(i, i ^ 1 << b) for i in range(size)])]
  transfers between devices with their start and end apart: 38 -> 38, of which waited for: 20 -> 22; matrix products, arithmetic and copies ran while one was open for 7% -> 7% of each run, Pallas kernels for 3% -> 3%
where the time goes in v10:
time: 114 us
  waiting for transfers between devices  47.7 us (42%)
  starting transfers between devices  42.9 us (38%)
  Pallas kernels  9.97 us (9%)
  local copies, waits for them, and re-layouts  4.67 us (4%)
  other arithmetic  4.54 us (4%)
  between operations  4.18 us (4%)
    ppermute x38, waiting for transfers between devices, swap(): return lax.ppermute(x, axis, [(i, i ^ 1 << b) for i in range(size)])  47.7 us
    ppermute x38, starting transfers between devices, swap(): return lax.ppermute(x, axis, [(i, i ^ 1 << b) for i in range(size)])  42.9 us
    pallas_call x2, Pallas kernels, update(): pl.pallas_call(first_body if step == 0 else second_body, out_shape=[jax.S...  6.1 us
    pallas_call x2, Pallas kernels, prepare(): pl.pallas_call(prepare_body, out_shape=[jax.ShapeDtypeStruct((depth, dept...  2.91 us
  transfers between devices with their start and end apart: 38, of which 22 were waited for; matrix products, arithmetic and copies ran while one was open for 7% of the time, Pallas kernels for 3%

profile of v10, /device:TPU:0, one launch (start us, length us, event | category | flops | bytes accessed | tf_op | source)
XLA Modules:
  0.0 114.0 jit_solution(8916482041332450165)
XLA Ops:
  0.5 1.5 %compare_reduce_fusion = (pred[]{:T(512)}, s32[]{:T(128)}) fusion(s32[8]{0:T(128)} %slot_block.3), kind=kLoop, calls=%fused_computation.13 | loop fusion | flops 57 | bytes 37 | tf_op jit(solution)/shard_map/paced/reduce | solution.py:222
  2.0 1.1 dynamic-slice_bitcast_fusion
  4.3 1.1 %bitcast_select_fusion = f32[512,256]{1,0:T(8,128)S(1)} fusion(f32[512,256]{1,0:T(8,128)S(1)} %dynamic-slice_bitcast_fusion, f32[1,1024,256]{2,1,0:T(8,128)} %collective-permute-done, s32[]{:T(128)S(6)} %select_n.61, pred[]{:T(512)S(6)} %eq.34), kind=kLoop, calls=%fused_computation | loop fusion | flops 131072 | bytes 1572869 | tf_op jit(solution)/shard_map/jit(_where)/select_n | solution.py:262
  5.5 2.6 %collective-permute-start.1 = (f32[256,256]{1,0:T(8,128)S(1)}, f32[256,256]{1,0:T(8,128)S(1)}, u32[]{:S(2)}, u32[]{:S(2)}) collective-permute-start(f32[256,256]{1,0:T(8,128)S(1)} %constant_dynamic-slice_fusion.1), channel_id=1, source_target_pairs={{0,8},{4,12},{8,0},{12,4},{16,24},{20,28},{24,16},{28,20},{1,9},{5... | collective-permute-start | bytes 786440 | tf_op jit(solution)/shard_map/ppermute | solution.py:20
  8.2 1.6 %collective-permute-start.3 = (f32[128,1024]{1,0:T(8,128)S(1)}, f32[128,1024]{1,0:T(8,128)S(1)}, u32[]{:S(2)}, u32[]{:S(2)}) collective-permute-start(f32[128,1024]{1,0:T(8,128)S(1)} %get-tuple-element.84.own_top), channel_id=1, source_target_pairs={{0,1},{1,0},{2,3},{3,2},{4,5},{5,4},{6,7},{7,6},{8,9},{9,8},{10,11... | collective-permute-start | bytes 1572872 | tf_op jit(solution)/shard_map/ppermute | solution.py:20
  9.8 1.5 %collective-permute-start.4 = (f32[128,1024]{1,0:T(8,128)S(1)}, f32[128,1024]{1,0:T(8,128)S(1)}, u32[]{:S(2)}, u32[]{:S(2)}) collective-permute-start(f32[128,1024]{1,0:T(8,128)S(1)} %get-tuple-element.83.own_bottom), channel_id=1, source_target_pairs={{0,2},{1,3},{2,0},{3,1},{4,6},{5,7},{6,4},{7,5},{8,10},{9,11},{10,... | collective-permute-start | bytes 1572872 | tf_op jit(solution)/shard_map/ppermute | solution.py:20
  11.3 3.6 %collective-permute-done.1 = f32[256,256]{1,0:T(8,128)S(1)} collective-permute-done((f32[256,256]{1,0:T(8,128)S(1)}, f32[256,256]{1,0:T(8,128)S(1)}, u32[]{:S(2)}, u32[]{:S(2)}) %collective-permute-start.1) | collective-permute-done | bytes 262176 | tf_op jit(solution)/shard_map/ppermute | solution.py:20
  15.0 2.8 %collective-permute-start.2 = (f32[256,256]{1,0:T(8,128)S(1)}, f32[256,256]{1,0:T(8,128)}, u32[]{:S(2)}, u32[]{:S(2)}) collective-permute-start(f32[256,256]{1,0:T(8,128)S(1)} %dynamic-slice_select_fusion.1), channel_id=1, source_target_pairs={{0,16},{4,20},{8,24},{12,28},{16,0},{20,4},{24,8},{28,12},{1,17},{... | collective-permute-start | bytes 786440 | tf_op jit(solution)/shard_map/ppermute | solution.py:20
  17.8 1.5 %collective-permute-start.6 = (f32[128,1024]{1,0:T(8,128)S(1)}, f32[128,1024]{1,0:T(8,128)S(1)}, u32[]{:S(2)}, u32[]{:S(2)}) collective-permute-start(f32[128,1024]{1,0:T(8,128)S(1)} %get-tuple-element.83.own_bottom), channel_id=1, source_target_pairs={{0,1},{1,0},{2,3},{3,2},{4,5},{5,4},{6,7},{7,6},{8,9},{9,8},{10,11... | collective-permute-start | bytes 1572872 | tf_op jit(solution)/shard_map/ppermute | solution.py:20
  19.3 1.5 %collective-permute-start.7 = (f32[128,1024]{1,0:T(8,128)S(1)}, f32[128,1024]{1,0:T(8,128)S(1)}, u32[]{:S(2)}, u32[]{:S(2)}) collective-permute-start(f32[128,1024]{1,0:T(8,128)S(1)} %get-tuple-element.84.own_top), channel_id=1, source_target_pairs={{0,2},{1,3},{2,0},{3,1},{4,6},{5,7},{6,4},{7,5},{8,10},{9,11},{10,... | collective-permute-start | bytes 1572872 | tf_op jit(solution)/shard_map/ppermute | solution.py:20
  21.4 8.2 %collective-permute-done.2 = f32[256,256]{1,0:T(8,128)} collective-permute-done((f32[256,256]{1,0:T(8,128)S(1)}, f32[256,256]{1,0:T(8,128)}, u32[]{:S(2)}, u32[]{:S(2)}) %collective-permute-start.2) | collective-permute-done | bytes 262176 | tf_op jit(solution)/shard_map/ppermute | solution.py:20
  31.2 1.5 %collective-permute-start.12 = (f32[128,1024]{1,0:T(8,128)S(1)}, f32[128,1024]{1,0:T(8,128)S(1)}, u32[]{:S(2)}, u32[]{:S(2)}) collective-permute-start(f32[128,1024]{1,0:T(8,128)S(1)} %collective-permute-done.3.refs_0_), channel_id=1, source_target_pairs={{0,2},{1,3},{2,0},{3,1},{4,6},{5,7},{6,4},{7,5},{8,10},{9,11},{10,... | collective-permute-start | bytes 1572872 | tf_op jit(solution)/shard_map/ppermute | solution.py:20
  32.7 1.5 %collective-permute-start.13 = (f32[128,1024]{1,0:T(8,128)S(1)}, f32[128,1024]{1,0:T(8,128)S(1)}, u32[]{:S(2)}, u32[]{:S(2)}) collective-permute-start(f32[128,1024]{1,0:T(8,128)S(1)} %collective-permute-done.4.refs_1_), channel_id=1, source_target_pairs={{0,1},{1,0},{2,3},{3,2},{4,5},{5,4},{6,7},{7,6},{8,9},{9,8},{10,11... | collective-permute-start | bytes 1572872 | tf_op jit(solution)/shard_map/ppermute | solution.py:20
  34.2 1.1 slice_bitcast_fusion.3.inverse
  35.6 2.4 %collective-permute-done.5.refs_1_ = f32[256,256]{1,0:T(8,128)S(1)} collective-permute-done((f32[256,256]{1,0:T(8,128)S(1)}, f32[256,256]{1,0:T(8,128)S(1)}, u32[]{:S(2)}, u32[]{:S(2)}) %collective-permute-start.5) | collective-permute-done | bytes 262176 | tf_op jit(solution)/shard_map/ppermute | solution.py:20
  38.0 1.5 %collective-permute-done.9.refs_3_ = f32[256,256]{1,0:T(8,128)S(1)} collective-permute-done((f32[256,256]{1,0:T(8,128)S(1)}, f32[256,256]{1,0:T(8,128)S(1)}, u32[]{:S(2)}, u32[]{:S(2)}) %collective-permute-start.9) | collective-permute-done | bytes 262176 | tf_op jit(solution)/shard_map/ppermute | solution.py:20
  40.1 2.3 %collective-permute-start.10 = (f32[128,256]{1,0:T(8,128)S(1)}, f32[128,256]{1,0:T(8,128)S(1)}, u32[]{:S(2)}, u32[]{:S(2)}) collective-permute-start(f32[128,256]{1,0:T(8,128)S(1)} %solve.2.refs_0_), channel_id=1, source_target_pairs={{0,16},{4,20},{8,24},{12,28},{16,0},{20,4},{24,8},{28,12},{1,17},{... | collective-permute-start | bytes 393224 | tf_op jit(solution)/shard_map/ppermute | solution.py:20
  42.4 1.7 %collective-permute-start.11 = (f32[128,256]{1,0:T(8,128)S(1)}, f32[128,256]{1,0:T(8,128)S(1)}, u32[]{:S(2)}, u32[]{:S(2)}) collective-permute-start(f32[128,256]{1,0:T(8,128)S(1)} %solve.2.refs_0_), channel_id=1, source_target_pairs={{0,8},{4,12},{8,0},{12,4},{16,24},{20,28},{24,16},{28,20},{1,9},{5... | collective-permute-start | bytes 393224 | tf_op jit(solution)/shard_map/ppermute | solution.py:20
  44.1 1.7 %collective-permute-done.12.refs_4_ = f32[128,1024]{1,0:T(8,128)S(1)} collective-permute-done((f32[128,1024]{1,0:T(8,128)S(1)}, f32[128,1024]{1,0:T(8,128)S(1)}, u32[]{:S(2)}, u32[]{:S(2)}) %collective-permute-start.12) | collective-permute-done | bytes 524320 | tf_op jit(solution)/shard_map/ppermute | solution.py:20
  46.0 3.4 %collective-permute-done.10.refs_2_ = f32[128,256]{1,0:T(8,128)S(1)} collective-permute-done((f32[128,256]{1,0:T(8,128)S(1)}, f32[128,256]{1,0:T(8,128)S(1)}, u32[]{:S(2)}, u32[]{:S(2)}) %collective-permute-start.10) | collective-permute-done | bytes 131104 | tf_op jit(solution)/shard_map/ppermute | solution.py:20
  49.5 1.3 %collective-permute-start.14 = (f32[128,256]{1,0:T(8,128)S(1)}, f32[128,256]{1,0:T(8,128)S(1)}, u32[]{:S(2)}, u32[]{:S(2)}) collective-permute-start(f32[128,256]{1,0:T(8,128)S(1)} %collective-permute-done.10.refs_2_), channel_id=1, source_target_pairs={{0,8},{4,12},{8,0},{12,4},{16,24},{20,28},{24,16},{28,20},{1,9},{5... | collective-permute-start | bytes 393224 | tf_op jit(solution)/shard_map/ppermute | solution.py:20
  51.3 1.1 prepare.2
  52.3 2.1 %collective-permute-done.14.refs_3_ = f32[128,256]{1,0:T(8,128)S(1)} collective-permute-done((f32[128,256]{1,0:T(8,128)S(1)}, f32[128,256]{1,0:T(8,128)S(1)}, u32[]{:S(2)}, u32[]{:S(2)}) %collective-permute-start.14) | collective-permute-done | bytes 131104 | tf_op jit(solution)/shard_map/ppermute | solution.py:20
  54.4 1.3 %collective-permute-done.18.refs_7_ = f32[128,256]{1,0:T(8,128)S(1)} collective-permute-done((f32[128,256]{1,0:T(8,128)S(1)}, f32[128,256]{1,0:T(8,128)S(1)}, u32[]{:S(2)}, u32[]{:S(2)}) %collective-permute-start.18) | collective-permute-done | bytes 131104 | tf_op jit(solution)/shard_map/ppermute | solution.py:20
  55.8 2.7 %update.2 = (f32[512,256]{1,0:T(8,128)S(1)}, f32[512,256]{1,0:T(8,128)S(1)}) custom-call(s32[1,2]{1,0:T(1,128)S(1)} %copy-done.1, s32[8]{0:T(128)S(1)} %copy-done.2, bf16[1024,1024]{1,0:T(8,128)(2,1)S(1)} %get-tuple-element.97.high, bf16[1024,1024]{1,0:T(8,128)(2,1)S(1)} %get-tuple-element.98.low, f32[128,256]{1,0:T(8,128)S(1)} %solve.2.refs_0_, ...), custom_call_target="tpu_custom_call" | custom-call | flops 1610612736 | bytes 7340032 | tf_op jit(solution)/shard_map/update/pallas_call | solution.py:184
  60.9 1.4 %collective-permute-start.20 = (f32[256,256]{1,0:T(8,128)S(1)}, f32[256,256]{1,0:T(8,128)S(1)}, u32[]{:S(2)}, u32[]{:S(2)}) collective-permute-start(f32[256,256]{1,0:T(8,128)S(1)} %constant_dynamic-slice_fusion), channel_id=1, source_target_pairs={{0,8},{4,12},{8,0},{12,4},{16,24},{20,28},{24,16},{28,20},{1,9},{5... | collective-permute-start | bytes 786440 | tf_op jit(solution)/shard_map/ppermute | solution.py:20
  62.3 1.3 %slice_bitcast_fusion.1 = (f32[128,1024]{1,0:T(8,128)S(1)}, f32[128,1024]{1,0:T(8,128)S(1)}) fusion(f32[1,2,256,1024]{3,2,1,0:T(8,128)} %param.6), kind=kLoop, calls=%fused_computation.2 | loop fusion | bytes 2097152 | tf_op jit(solution)/shard_map/squeeze | solution.py:233
  63.5 1.6 %collective-permute-start.22 = (f32[128,1024]{1,0:T(8,128)S(1)}, f32[128,1024]{1,0:T(8,128)S(1)}, u32[]{:S(2)}, u32[]{:S(2)}) collective-permute-start(f32[128,1024]{1,0:T(8,128)S(1)} %get-tuple-element.114.own_top), channel_id=1, source_target_pairs={{0,1},{1,0},{2,3},{3,2},{4,5},{5,4},{6,7},{7,6},{8,9},{9,8},{10,11... | collective-permute-start | bytes 1572872 | tf_op jit(solution)/shard_map/ppermute | solution.py:20
  65.1 1.5 %collective-permute-start.23 = (f32[128,1024]{1,0:T(8,128)S(1)}, f32[128,1024]{1,0:T(8,128)S(1)}, u32[]{:S(2)}, u32[]{:S(2)}) collective-permute-start(f32[128,1024]{1,0:T(8,128)S(1)} %get-tuple-element.113.own_bottom), channel_id=1, source_target_pairs={{0,2},{1,3},{2,0},{3,1},{4,6},{5,7},{6,4},{7,5},{8,10},{9,11},{10,... | collective-permute-start | bytes 1572872 | tf_op jit(solution)/shard_map/ppermute | solution.py:20
  66.6 2.9 %collective-permute-done.20 = f32[256,256]{1,0:T(8,128)S(1)} collective-permute-done((f32[256,256]{1,0:T(8,128)S(1)}, f32[256,256]{1,0:T(8,128)S(1)}, u32[]{:S(2)}, u32[]{:S(2)}) %collective-permute-start.20) | collective-permute-done | bytes 262176 | tf_op jit(solution)/shard_map/ppermute | solution.py:20
  69.6 2.4 %collective-permute-start.21 = (f32[256,256]{1,0:T(8,128)S(1)}, f32[256,256]{1,0:T(8,128)}, u32[]{:S(2)}, u32[]{:S(2)}) collective-permute-start(f32[256,256]{1,0:T(8,128)S(1)} %dynamic-slice_select_fusion), channel_id=1, source_target_pairs={{0,16},{4,20},{8,24},{12,28},{16,0},{20,4},{24,8},{28,12},{1,17},{... | collective-permute-start | bytes 786440 | tf_op jit(solution)/shard_map/ppermute | solution.py:20
  72.0 1.5 %collective-permute-start.25 = (f32[128,1024]{1,0:T(8,128)S(1)}, f32[128,1024]{1,0:T(8,128)}, u32[]{:S(2)}, u32[]{:S(2)}) collective-permute-start(f32[128,1024]{1,0:T(8,128)S(1)} %get-tuple-element.113.own_bottom), channel_id=1, source_target_pairs={{0,1},{1,0},{2,3},{3,2},{4,5},{5,4},{6,7},{7,6},{8,9},{9,8},{10,11... | collective-permute-start | bytes 1572872 | tf_op jit(solution)/shard_map/ppermute | solution.py:20
  73.5 1.5 %collective-permute-start.26 = (f32[128,1024]{1,0:T(8,128)S(1)}, f32[128,1024]{1,0:T(8,128)}, u32[]{:S(2)}, u32[]{:S(2)}) collective-permute-start(f32[128,1024]{1,0:T(8,128)S(1)} %get-tuple-element.114.own_top), channel_id=1, source_target_pairs={{0,2},{1,3},{2,0},{3,1},{4,6},{5,7},{6,4},{7,5},{8,10},{9,11},{10,... | collective-permute-start | bytes 1572872 | tf_op jit(solution)/shard_map/ppermute | solution.py:20
  75.7 8.3 %collective-permute-done.21 = f32[256,256]{1,0:T(8,128)} collective-permute-done((f32[256,256]{1,0:T(8,128)S(1)}, f32[256,256]{1,0:T(8,128)}, u32[]{:S(2)}, u32[]{:S(2)}) %collective-permute-start.21) | collective-permute-done | bytes 262176 | tf_op jit(solution)/shard_map/ppermute | solution.py:20
  84.5 1.5 %collective-permute-start.31 = (f32[128,1024]{1,0:T(8,128)S(1)}, f32[128,1024]{1,0:T(8,128)S(1)}, u32[]{:S(2)}, u32[]{:S(2)}) collective-permute-start(f32[128,1024]{1,0:T(8,128)S(1)} %collective-permute-done.22.refs_0_), channel_id=1, source_target_pairs={{0,2},{1,3},{2,0},{3,1},{4,6},{5,7},{6,4},{7,5},{8,10},{9,11},{10,... | collective-permute-start | bytes 1572872 | tf_op jit(solution)/shard_map/ppermute | solution.py:20
  86.0 1.5 %collective-permute-start.32 = (f32[128,1024]{1,0:T(8,128)S(1)}, f32[128,1024]{1,0:T(8,128)S(1)}, u32[]{:S(2)}, u32[]{:S(2)}) collective-permute-start(f32[128,1024]{1,0:T(8,128)S(1)} %collective-permute-done.23.refs_1_), channel_id=1, source_target_pairs={{0,1},{1,0},{2,3},{3,2},{4,5},{5,4},{6,7},{7,6},{8,9},{9,8},{10,11... | collective-permute-start | bytes 1572872 | tf_op jit(solution)/shard_map/ppermute | solution.py:20
  87.5 1.1 slice_bitcast_fusion.inverse
  89.4 1.8 %collective-permute-done.26.refs_3_ = f32[128,1024]{1,0:T(8,128)} collective-permute-done((f32[128,1024]{1,0:T(8,128)S(1)}, f32[128,1024]{1,0:T(8,128)}, u32[]{:S(2)}, u32[]{:S(2)}) %collective-permute-start.26) | collective-permute-done | bytes 524320 | tf_op jit(solution)/shard_map/ppermute | solution.py:20
  91.8 1.0 collective-permute-done.27.refs_2_
  93.6 3.9 %collective-permute-start.29 = (f32[128,256]{1,0:T(8,128)S(1)}, f32[128,256]{1,0:T(8,128)S(1)}, u32[]{:S(2)}, u32[]{:S(2)}) collective-permute-start(f32[128,256]{1,0:T(8,128)S(1)} %solve.3.refs_0_), channel_id=1, source_target_pairs={{0,16},{4,20},{8,24},{12,28},{16,0},{20,4},{24,8},{28,12},{1,17},{... | collective-permute-start | bytes 393224 | tf_op jit(solution)/shard_map/ppermute | solution.py:20
  97.5 1.7 %collective-permute-start.30 = (f32[128,256]{1,0:T(8,128)S(1)}, f32[128,256]{1,0:T(8,128)S(1)}, u32[]{:S(2)}, u32[]{:S(2)}) collective-permute-start(f32[128,256]{1,0:T(8,128)S(1)} %solve.3.refs_0_), channel_id=1, source_target_pairs={{0,8},{4,12},{8,0},{12,4},{16,24},{20,28},{24,16},{28,20},{1,9},{5... | collective-permute-start | bytes 393224 | tf_op jit(solution)/shard_map/ppermute | solution.py:20
  99.2 1.9 %collective-permute-done.31.refs_4_ = f32[128,1024]{1,0:T(8,128)S(1)} collective-permute-done((f32[128,1024]{1,0:T(8,128)S(1)}, f32[128,1024]{1,0:T(8,128)S(1)}, u32[]{:S(2)}, u32[]{:S(2)}) %collective-permute-start.31) | collective-permute-done | bytes 524320 | tf_op jit(solution)/shard_map/ppermute | solution.py:20
  101.2 3.0 %collective-permute-done.29.refs_2_ = f32[128,256]{1,0:T(8,128)S(1)} collective-permute-done((f32[128,256]{1,0:T(8,128)S(1)}, f32[128,256]{1,0:T(8,128)S(1)}, u32[]{:S(2)}, u32[]{:S(2)}) %collective-permute-start.29) | collective-permute-done | bytes 131104 | tf_op jit(solution)/shard_map/ppermute | solution.py:20
  104.3 1.6 %collective-permute-start.33 = (f32[128,256]{1,0:T(8,128)S(1)}, f32[128,256]{1,0:T(8,128)S(1)}, u32[]{:S(2)}, u32[]{:S(2)}) collective-permute-start(f32[128,256]{1,0:T(8,128)S(1)} %collective-permute-done.29.refs_2_), channel_id=1, source_target_pairs={{0,8},{4,12},{8,0},{12,4},{16,24},{20,28},{24,16},{28,20},{1,9},{5... | collective-permute-start | bytes 393224 | tf_op jit(solution)/shard_map/ppermute | solution.py:20
  106.4 1.8 %prepare.3 = (bf16[1024,1024]{1,0:T(8,128)(2,1)S(1)}, bf16[1024,1024]{1,0:T(8,128)(2,1)S(1)}) custom-call(f32[128,1024]{1,0:T(8,128)S(1)} %get-tuple-element.114.own_top, f32[128,1024]{1,0:T(8,128)S(1)} %get-tuple-element.113.own_bottom, f32[128,1024]{1,0:T(8,128)S(1)} %collective-permute-done.22.refs_0_, f32[128,1024]{1,0:T(8,128)S(1)} %collective-permute-done.23.refs_1_, ...), custom_call_target="tpu_custom_call" | custom-call | bytes 16777216 | tf_op jit(solution)/shard_map/prepare/pallas_call | solution.py:98
  108.2 1.0 collective-permute-done.33.refs_3_
  109.3 1.3 %collective-permute-done.37.refs_7_ = f32[128,256]{1,0:T(8,128)S(1)} collective-permute-done((f32[128,256]{1,0:T(8,128)S(1)}, f32[128,256]{1,0:T(8,128)S(1)}, u32[]{:S(2)}, u32[]{:S(2)}) %collective-permute-start.37) | collective-permute-done | bytes 131104 | tf_op jit(solution)/shard_map/ppermute | solution.py:20
  110.6 3.4 %update.3 = f32[1024,256]{1,0:T(8,128)} custom-call(s32[1,2]{1,0:T(1,128)S(1)} %copy-done.1, s32[8]{0:T(128)S(1)} %copy-done.2, bf16[1024,1024]{1,0:T(8,128)(2,1)S(1)} %get-tuple-element.127.high, bf16[1024,1024]{1,0:T(8,128)(2,1)S(1)} %get-tuple-element.128.low, f32[128,256]{1,0:T(8,128)S(1)} %solve.3.refs_0_, ...), custom_call_target="tpu_custom_call" | custom-call | flops 1610612736 | bytes 7340032 | tf_op jit(solution)/shard_map/update/pallas_call | solution.py:184
  (57 shorter events, 8.0 us)
Async XLA Ops:
  0.0 8.1 %copy-start.3 = (f32[1,2,256,1024]{3,2,1,0:T(8,128)S(1)}, f32[1,2,256,1024]{3,2,1,0:T(8,128)}, u32[]{:S(2)}) copy-start(f32[1,2,256,1024]{3,2,1,0:T(8,128)} %param.6) | copy-start | bytes 6291460
  0.0 4.3 %collective-permute-start = (f32[1,1024,256]{2,1,0:T(8,128)}, f32[1,1024,256]{2,1,0:T(8,128)}, u32[]{:S(2)}, u32[]{:S(2)}) collective-permute-start(f32[1,1024,256]{2,1,0:T(8,128)} %refs_8_.1), channel_id=1, source_target_pairs={{0,4},{4,0},{8,12},{12,8},{16,20},{20,16},{24,28},{28,24},{1,5},{5... | collective-permute-start | bytes 3145736 | tf_op jit(solution)/shard_map/ppermute | solution.py:20
  5.5 9.4 %collective-permute-start.1 = (f32[256,256]{1,0:T(8,128)S(1)}, f32[256,256]{1,0:T(8,128)S(1)}, u32[]{:S(2)}, u32[]{:S(2)}) collective-permute-start(f32[256,256]{1,0:T(8,128)S(1)} %constant_dynamic-slice_fusion.1), channel_id=1, source_target_pairs={{0,8},{4,12},{8,0},{12,4},{16,24},{20,28},{24,16},{28,20},{1,9},{5... | collective-permute-start | bytes 786440 | tf_op jit(solution)/shard_map/ppermute | solution.py:20
  8.2 22.4 %collective-permute-start.3 = (f32[128,1024]{1,0:T(8,128)S(1)}, f32[128,1024]{1,0:T(8,128)S(1)}, u32[]{:S(2)}, u32[]{:S(2)}) collective-permute-start(f32[128,1024]{1,0:T(8,128)S(1)} %get-tuple-element.84.own_top), channel_id=1, source_target_pairs={{0,1},{1,0},{2,3},{3,2},{4,5},{5,4},{6,7},{7,6},{8,9},{9,8},{10,11... | collective-permute-start | bytes 1572872 | tf_op jit(solution)/shard_map/ppermute | solution.py:20
  9.8 20.9 %collective-permute-start.4 = (f32[128,1024]{1,0:T(8,128)S(1)}, f32[128,1024]{1,0:T(8,128)S(1)}, u32[]{:S(2)}, u32[]{:S(2)}) collective-permute-start(f32[128,1024]{1,0:T(8,128)S(1)} %get-tuple-element.83.own_bottom), channel_id=1, source_target_pairs={{0,2},{1,3},{2,0},{3,1},{4,6},{5,7},{6,4},{7,5},{8,10},{9,11},{10,... | collective-permute-start | bytes 1572872 | tf_op jit(solution)/shard_map/ppermute | solution.py:20
  15.0 14.7 %collective-permute-start.2 = (f32[256,256]{1,0:T(8,128)S(1)}, f32[256,256]{1,0:T(8,128)}, u32[]{:S(2)}, u32[]{:S(2)}) collective-permute-start(f32[256,256]{1,0:T(8,128)S(1)} %dynamic-slice_select_fusion.1), channel_id=1, source_target_pairs={{0,16},{4,20},{8,24},{12,28},{16,0},{20,4},{24,8},{28,12},{1,17},{... | collective-permute-start | bytes 786440 | tf_op jit(solution)/shard_map/ppermute | solution.py:20
  17.8 17.5 %collective-permute-start.6 = (f32[128,1024]{1,0:T(8,128)S(1)}, f32[128,1024]{1,0:T(8,128)S(1)}, u32[]{:S(2)}, u32[]{:S(2)}) collective-permute-start(f32[128,1024]{1,0:T(8,128)S(1)} %get-tuple-element.83.own_bottom), channel_id=1, source_target_pairs={{0,1},{1,0},{2,3},{3,2},{4,5},{5,4},{6,7},{7,6},{8,9},{9,8},{10,11... | collective-permute-start | bytes 1572872 | tf_op jit(solution)/shard_map/ppermute | solution.py:20
  19.3 16.4 %collective-permute-start.7 = (f32[128,1024]{1,0:T(8,128)S(1)}, f32[128,1024]{1,0:T(8,128)S(1)}, u32[]{:S(2)}, u32[]{:S(2)}) collective-permute-start(f32[128,1024]{1,0:T(8,128)S(1)} %get-tuple-element.84.own_top), channel_id=1, source_target_pairs={{0,2},{1,3},{2,0},{3,1},{4,6},{5,7},{6,4},{7,5},{8,10},{9,11},{10,... | collective-permute-start | bytes 1572872 | tf_op jit(solution)/shard_map/ppermute | solution.py:20
  30.7 7.3 %collective-permute-start.5 = (f32[256,256]{1,0:T(8,128)S(1)}, f32[256,256]{1,0:T(8,128)S(1)}, u32[]{:S(2)}, u32[]{:S(2)}) collective-permute-start(f32[256,256]{1,0:T(8,128)S(1)} %broadcast_select_fusion.1.refs_0_), channel_id=1, source_target_pairs={{0,8},{4,12},{8,0},{12,4},{16,24},{20,28},{24,16},{28,20},{1,9},{5... | collective-permute-start | bytes 786440 | tf_op jit(solution)/shard_map/ppermute | solution.py:20
  31.2 14.6 %collective-permute-start.12 = (f32[128,1024]{1,0:T(8,128)S(1)}, f32[128,1024]{1,0:T(8,128)S(1)}, u32[]{:S(2)}, u32[]{:S(2)}) collective-permute-start(f32[128,1024]{1,0:T(8,128)S(1)} %collective-permute-done.3.refs_0_), channel_id=1, source_target_pairs={{0,2},{1,3},{2,0},{3,1},{4,6},{5,7},{6,4},{7,5},{8,10},{9,11},{10,... | collective-permute-start | bytes 1572872 | tf_op jit(solution)/shard_map/ppermute | solution.py:20
  32.7 13.3 %collective-permute-start.13 = (f32[128,1024]{1,0:T(8,128)S(1)}, f32[128,1024]{1,0:T(8,128)S(1)}, u32[]{:S(2)}, u32[]{:S(2)}) collective-permute-start(f32[128,1024]{1,0:T(8,128)S(1)} %collective-permute-done.4.refs_1_), channel_id=1, source_target_pairs={{0,1},{1,0},{2,3},{3,2},{4,5},{5,4},{6,7},{7,6},{8,9},{9,8},{10,11... | collective-permute-start | bytes 1572872 | tf_op jit(solution)/shard_map/ppermute | solution.py:20
  35.6 2.4 %collective-permute-start.8 = (f32[256,256]{1,0:T(8,128)S(1)}, f32[256,256]{1,0:T(8,128)S(1)}, u32[]{:S(2)}, u32[]{:S(2)}) collective-permute-start(f32[256,256]{1,0:T(8,128)S(1)} %broadcast_select_fusion.1.refs_0_), channel_id=1, source_target_pairs={{0,4},{4,0},{8,12},{12,8},{16,20},{20,16},{24,28},{28,24},{1,5},{5... | collective-permute-start | bytes 786440 | tf_op jit(solution)/shard_map/ppermute | solution.py:20
  38.0 1.5 %collective-permute-start.9 = (f32[256,256]{1,0:T(8,128)S(1)}, f32[256,256]{1,0:T(8,128)S(1)}, u32[]{:S(2)}, u32[]{:S(2)}) collective-permute-start(f32[256,256]{1,0:T(8,128)S(1)} %collective-permute-done.5.refs_1_), channel_id=1, source_target_pairs={{0,4},{4,0},{8,12},{12,8},{16,20},{20,16},{24,28},{28,24},{1,5},{5... | collective-permute-start | bytes 786440 | tf_op jit(solution)/shard_map/ppermute | solution.py:20
  40.0 15.8 %copy-start = (f32[1,1024,256]{2,1,0:T(8,128)S(1)}, f32[1,1024,256]{2,1,0:T(8,128)}, u32[]{:S(2)}) copy-start(f32[1,1024,256]{2,1,0:T(8,128)} %refs_8_.1) | copy-start | bytes 3145732
  40.0 15.8 %copy-start.1 = (s32[1,2]{1,0:T(1,128)S(1)}, s32[1,2]{1,0:T(1,128)}, u32[]{:S(2)}) copy-start(s32[1,2]{1,0:T(1,128)} %flags.3) | copy-start | bytes 28
  40.0 15.7 %copy-start.2 = (s32[8]{0:T(128)S(1)}, s32[8]{0:T(128)}, u32[]{:S(2)}) copy-start(s32[8]{0:T(128)} %slot_block.3) | copy-start | bytes 100
  40.1 9.4 %collective-permute-start.10 = (f32[128,256]{1,0:T(8,128)S(1)}, f32[128,256]{1,0:T(8,128)S(1)}, u32[]{:S(2)}, u32[]{:S(2)}) collective-permute-start(f32[128,256]{1,0:T(8,128)S(1)} %solve.2.refs_0_), channel_id=1, source_target_pairs={{0,16},{4,20},{8,24},{12,28},{16,0},{20,4},{24,8},{28,12},{1,17},{... | collective-permute-start | bytes 393224 | tf_op jit(solution)/shard_map/ppermute | solution.py:20
  42.4 7.1 %collective-permute-start.11 = (f32[128,256]{1,0:T(8,128)S(1)}, f32[128,256]{1,0:T(8,128)S(1)}, u32[]{:S(2)}, u32[]{:S(2)}) collective-permute-start(f32[128,256]{1,0:T(8,128)S(1)} %solve.2.refs_0_), channel_id=1, source_target_pairs={{0,8},{4,12},{8,0},{12,4},{16,24},{20,28},{24,16},{28,20},{1,9},{5... | collective-permute-start | bytes 393224 | tf_op jit(solution)/shard_map/ppermute | solution.py:20
  44.1 8.2 %collective-permute-start.15 = (f32[128,256]{1,0:T(8,128)S(1)}, f32[128,256]{1,0:T(8,128)S(1)}, u32[]{:S(2)}, u32[]{:S(2)}) collective-permute-start(f32[128,256]{1,0:T(8,128)S(1)} %solve.2.refs_0_), channel_id=1, source_target_pairs={{0,4},{4,0},{8,12},{12,8},{16,20},{20,16},{24,28},{28,24},{1,5},{5... | collective-permute-start | bytes 393224 | tf_op jit(solution)/shard_map/ppermute | solution.py:20
  49.5 5.0 %collective-permute-start.14 = (f32[128,256]{1,0:T(8,128)S(1)}, f32[128,256]{1,0:T(8,128)S(1)}, u32[]{:S(2)}, u32[]{:S(2)}) collective-permute-start(f32[128,256]{1,0:T(8,128)S(1)} %collective-permute-done.10.refs_2_), channel_id=1, source_target_pairs={{0,8},{4,12},{8,0},{12,4},{16,24},{20,28},{24,16},{28,20},{1,9},{5... | collective-permute-start | bytes 393224 | tf_op jit(solution)/shard_map/ppermute | solution.py:20
  50.7 3.7 %collective-permute-start.16 = (f32[128,256]{1,0:T(8,128)S(1)}, f32[128,256]{1,0:T(8,128)S(1)}, u32[]{:S(2)}, u32[]{:S(2)}) collective-permute-start(f32[128,256]{1,0:T(8,128)S(1)} %collective-permute-done.11.refs_1_), channel_id=1, source_target_pairs={{0,4},{4,0},{8,12},{12,8},{16,20},{20,16},{24,28},{28,24},{1,5},{5... | collective-permute-start | bytes 393224 | tf_op jit(solution)/shard_map/ppermute | solution.py:20
  50.7 3.7 %collective-permute-start.17 = (f32[128,256]{1,0:T(8,128)S(1)}, f32[128,256]{1,0:T(8,128)S(1)}, u32[]{:S(2)}, u32[]{:S(2)}) collective-permute-start(f32[128,256]{1,0:T(8,128)S(1)} %collective-permute-done.10.refs_2_), channel_id=1, source_target_pairs={{0,4},{4,0},{8,12},{12,8},{16,20},{20,16},{24,28},{28,24},{1,5},{5... | collective-permute-start | bytes 393224 | tf_op jit(solution)/shard_map/ppermute | solution.py:20
  54.4 1.4 %collective-permute-start.18 = (f32[128,256]{1,0:T(8,128)S(1)}, f32[128,256]{1,0:T(8,128)S(1)}, u32[]{:S(2)}, u32[]{:S(2)}) collective-permute-start(f32[128,256]{1,0:T(8,128)S(1)} %collective-permute-done.14.refs_3_), channel_id=1, source_target_pairs={{0,4},{4,0},{8,12},{12,8},{16,20},{20,16},{24,28},{28,24},{1,5},{5... | collective-permute-start | bytes 393224 | tf_op jit(solution)/shard_map/ppermute | solution.py:20
  58.5 2.3 %collective-permute-start.19 = (f32[512,256]{1,0:T(8,128)S(1)}, f32[512,256]{1,0:T(8,128)S(1)}, u32[]{:S(2)}, u32[]{:S(2)}) collective-permute-start(f32[512,256]{1,0:T(8,128)S(1)} %get-tuple-element.104.refs_9_), channel_id=1, source_target_pairs={{0,4},{4,0},{8,12},{12,8},{16,20},{20,16},{24,28},{28,24},{1,5},{5... | collective-permute-start | bytes 1572872 | tf_op jit(solution)/shard_map/ppermute | solution.py:20
  60.9 8.6 %collective-permute-start.20 = (f32[256,256]{1,0:T(8,128)S(1)}, f32[256,256]{1,0:T(8,128)S(1)}, u32[]{:S(2)}, u32[]{:S(2)}) collective-permute-start(f32[256,256]{1,0:T(8,128)S(1)} %constant_dynamic-slice_fusion), channel_id=1, source_target_pairs={{0,8},{4,12},{8,0},{12,4},{16,24},{20,28},{24,16},{28,20},{1,9},{5... | collective-permute-start | bytes 786440 | tf_op jit(solution)/shard_map/ppermute | solution.py:20
  63.5 20.5 %collective-permute-start.22 = (f32[128,1024]{1,0:T(8,128)S(1)}, f32[128,1024]{1,0:T(8,128)S(1)}, u32[]{:S(2)}, u32[]{:S(2)}) collective-permute-start(f32[128,1024]{1,0:T(8,128)S(1)} %get-tuple-element.114.own_top), channel_id=1, source_target_pairs={{0,1},{1,0},{2,3},{3,2},{4,5},{5,4},{6,7},{7,6},{8,9},{9,8},{10,11... | collective-permute-start | bytes 1572872 | tf_op jit(solution)/shard_map/ppermute | solution.py:20
  65.1 19.0 %collective-permute-start.23 = (f32[128,1024]{1,0:T(8,128)S(1)}, f32[128,1024]{1,0:T(8,128)S(1)}, u32[]{:S(2)}, u32[]{:S(2)}) collective-permute-start(f32[128,1024]{1,0:T(8,128)S(1)} %get-tuple-element.113.own_bottom), channel_id=1, source_target_pairs={{0,2},{1,3},{2,0},{3,1},{4,6},{5,7},{6,4},{7,5},{8,10},{9,11},{10,... | collective-permute-start | bytes 1572872 | tf_op jit(solution)/shard_map/ppermute | solution.py:20
  69.6 14.5 %collective-permute-start.21 = (f32[256,256]{1,0:T(8,128)S(1)}, f32[256,256]{1,0:T(8,128)}, u32[]{:S(2)}, u32[]{:S(2)}) collective-permute-start(f32[256,256]{1,0:T(8,128)S(1)} %dynamic-slice_select_fusion), channel_id=1, source_target_pairs={{0,16},{4,20},{8,24},{12,28},{16,0},{20,4},{24,8},{28,12},{1,17},{... | collective-permute-start | bytes 786440 | tf_op jit(solution)/shard_map/ppermute | solution.py:20
  72.0 17.4 %collective-permute-start.25 = (f32[128,1024]{1,0:T(8,128)S(1)}, f32[128,1024]{1,0:T(8,128)}, u32[]{:S(2)}, u32[]{:S(2)}) collective-permute-start(f32[128,1024]{1,0:T(8,128)S(1)} %get-tuple-element.113.own_bottom), channel_id=1, source_target_pairs={{0,1},{1,0},{2,3},{3,2},{4,5},{5,4},{6,7},{7,6},{8,9},{9,8},{10,11... | collective-permute-start | bytes 1572872 | tf_op jit(solution)/shard_map/ppermute | solution.py:20
  73.5 17.8 %collective-permute-start.26 = (f32[128,1024]{1,0:T(8,128)S(1)}, f32[128,1024]{1,0:T(8,128)}, u32[]{:S(2)}, u32[]{:S(2)}) collective-permute-start(f32[128,1024]{1,0:T(8,128)S(1)} %get-tuple-element.114.own_top), channel_id=1, source_target_pairs={{0,2},{1,3},{2,0},{3,1},{4,6},{5,7},{6,4},{7,5},{8,10},{9,11},{10,... | collective-permute-start | bytes 1572872 | tf_op jit(solution)/shard_map/ppermute | solution.py:20
  84.1 7.3 %collective-permute-start.24 = (f32[256,256]{1,0:T(8,128)S(1)}, f32[256,256]{1,0:T(8,128)S(1)}, u32[]{:S(2)}, u32[]{:S(2)}) collective-permute-start(f32[256,256]{1,0:T(8,128)S(1)} %broadcast_select_fusion.2.refs_0_), channel_id=1, source_target_pairs={{0,8},{4,12},{8,0},{12,4},{16,24},{20,28},{24,16},{28,20},{1,9},{5... | collective-permute-start | bytes 786440 | tf_op jit(solution)/shard_map/ppermute | solution.py:20
  84.5 16.7 %collective-permute-start.31 = (f32[128,1024]{1,0:T(8,128)S(1)}, f32[128,1024]{1,0:T(8,128)S(1)}, u32[]{:S(2)}, u32[]{:S(2)}) collective-permute-start(f32[128,1024]{1,0:T(8,128)S(1)} %collective-permute-done.22.refs_0_), channel_id=1, source_target_pairs={{0,2},{1,3},{2,0},{3,1},{4,6},{5,7},{6,4},{7,5},{8,10},{9,11},{10,... | collective-permute-start | bytes 1572872 | tf_op jit(solution)/shard_map/ppermute | solution.py:20
  86.0 15.2 %collective-permute-start.32 = (f32[128,1024]{1,0:T(8,128)S(1)}, f32[128,1024]{1,0:T(8,128)S(1)}, u32[]{:S(2)}, u32[]{:S(2)}) collective-permute-start(f32[128,1024]{1,0:T(8,128)S(1)} %collective-permute-done.23.refs_1_), channel_id=1, source_target_pairs={{0,1},{1,0},{2,3},{3,2},{4,5},{5,4},{6,7},{7,6},{8,9},{9,8},{10,11... | collective-permute-start | bytes 1572872 | tf_op jit(solution)/shard_map/ppermute | solution.py:20
  91.2 1.5 %collective-permute-start.27 = (f32[256,256]{1,0:T(8,128)S(1)}, f32[256,256]{1,0:T(8,128)S(1)}, u32[]{:S(2)}, u32[]{:S(2)}) collective-permute-start(f32[256,256]{1,0:T(8,128)S(1)} %broadcast_select_fusion.2.refs_0_), channel_id=1, source_target_pairs={{0,4},{4,0},{8,12},{12,8},{16,20},{20,16},{24,28},{28,24},{1,5},{5... | collective-permute-start | bytes 786440 | tf_op jit(solution)/shard_map/ppermute | solution.py:20
  91.5 1.7 %collective-permute-start.28 = (f32[256,256]{1,0:T(8,128)S(1)}, f32[256,256]{1,0:T(8,128)S(1)}, u32[]{:S(2)}, u32[]{:S(2)}) collective-permute-start(f32[256,256]{1,0:T(8,128)S(1)} %collective-permute-done.24.refs_1_), channel_id=1, source_target_pairs={{0,4},{4,0},{8,12},{12,8},{16,20},{20,16},{24,28},{28,24},{1,5},{5... | collective-permute-start | bytes 786440 | tf_op jit(solution)/shard_map/ppermute | solution.py:20
  93.6 10.6 %collective-permute-start.29 = (f32[128,256]{1,0:T(8,128)S(1)}, f32[128,256]{1,0:T(8,128)S(1)}, u32[]{:S(2)}, u32[]{:S(2)}) collective-permute-start(f32[128,256]{1,0:T(8,128)S(1)} %solve.3.refs_0_), channel_id=1, source_target_pairs={{0,16},{4,20},{8,24},{12,28},{16,0},{20,4},{24,8},{28,12},{1,17},{... | collective-permute-start | bytes 393224 | tf_op jit(solution)/shard_map/ppermute | solution.py:20
  97.5 6.8 %collective-permute-start.30 = (f32[128,256]{1,0:T(8,128)S(1)}, f32[128,256]{1,0:T(8,128)S(1)}, u32[]{:S(2)}, u32[]{:S(2)}) collective-permute-start(f32[128,256]{1,0:T(8,128)S(1)} %solve.3.refs_0_), channel_id=1, source_target_pairs={{0,8},{4,12},{8,0},{12,4},{16,24},{20,28},{24,16},{28,20},{1,9},{5... | collective-permute-start | bytes 393224 | tf_op jit(solution)/shard_map/ppermute | solution.py:20
  99.2 9.0 %collective-permute-start.34 = (f32[128,256]{1,0:T(8,128)S(1)}, f32[128,256]{1,0:T(8,128)S(1)}, u32[]{:S(2)}, u32[]{:S(2)}) collective-permute-start(f32[128,256]{1,0:T(8,128)S(1)} %solve.3.refs_0_), channel_id=1, source_target_pairs={{0,4},{4,0},{8,12},{12,8},{16,20},{20,16},{24,28},{28,24},{1,5},{5... | collective-permute-start | bytes 393224 | tf_op jit(solution)/shard_map/ppermute | solution.py:20
  104.3 5.0 %collective-permute-start.33 = (f32[128,256]{1,0:T(8,128)S(1)}, f32[128,256]{1,0:T(8,128)S(1)}, u32[]{:S(2)}, u32[]{:S(2)}) collective-permute-start(f32[128,256]{1,0:T(8,128)S(1)} %collective-permute-done.29.refs_2_), channel_id=1, source_target_pairs={{0,8},{4,12},{8,0},{12,4},{16,24},{20,28},{24,16},{28,20},{1,9},{5... | collective-permute-start | bytes 393224 | tf_op jit(solution)/shard_map/ppermute | solution.py:20
  105.9 3.4 %collective-permute-start.35 = (f32[128,256]{1,0:T(8,128)S(1)}, f32[128,256]{1,0:T(8,128)S(1)}, u32[]{:S(2)}, u32[]{:S(2)}) collective-permute-start(f32[128,256]{1,0:T(8,128)S(1)} %collective-permute-done.30.refs_1_), channel_id=1, source_target_pairs={{0,4},{4,0},{8,12},{12,8},{16,20},{20,16},{24,28},{28,24},{1,5},{5... | collective-permute-start | bytes 393224 | tf_op jit(solution)/shard_map/ppermute | solution.py:20
  105.9 3.4 %collective-permute-start.36 = (f32[128,256]{1,0:T(8,128)S(1)}, f32[128,256]{1,0:T(8,128)S(1)}, u32[]{:S(2)}, u32[]{:S(2)}) collective-permute-start(f32[128,256]{1,0:T(8,128)S(1)} %collective-permute-done.29.refs_2_), channel_id=1, source_target_pairs={{0,4},{4,0},{8,12},{12,8},{16,20},{20,16},{24,28},{28,24},{1,5},{5... | collective-permute-start | bytes 393224 | tf_op jit(solution)/shard_map/ppermute | solution.py:20
  109.3 1.4 %collective-permute-start.37 = (f32[128,256]{1,0:T(8,128)S(1)}, f32[128,256]{1,0:T(8,128)S(1)}, u32[]{:S(2)}, u32[]{:S(2)}) collective-permute-start(f32[128,256]{1,0:T(8,128)S(1)} %collective-permute-done.33.refs_3_), channel_id=1, source_target_pairs={{0,4},{4,0},{8,12},{12,8},{16,20},{20,16},{24,28},{28,24},{1,5},{5... | collective-permute-start | bytes 393224 | tf_op jit(solution)/shard_map/ppermute | solution.py:20
